TPU v7x, 32 devices: a whole 2x2x4 slice. The times are simulated.
32 devices in a mesh: groups: 2 (over y), replica: 4 (over x, core), mp: 4 (over z).
Axes of the slice: x: 2, y: 2, z: 4, core: 2. Of those that a mesh axis runs over, the one named last changes fastest.
Arguments:
- layer_input: bfloat16 [2, 64, 8192], P(None, ('groups', 'replica'), 'mp'), parts along dimension 1, may hold values from -6 to 6
- kv_weight: bfloat16 [8192, 1024], P('mp'), may hold values from -0.0625 to 0.0625
- queries: bfloat16 [2, 64, 4096], P(None, ('groups', 'replica'), 'mp'), parts along dimension 1, may hold values from -15 to 15
- kv_pool: bfloat16 [8, 4, 8, 128, 1024], P(('groups', 'replica'), 'mp'), parts along dimension 0, may hold values from -6 to 6
- lengths: int32 [64], P(('groups', 'replica')), parts along dimension 0, may hold values from 1 to 510, 4096 in all
- block_table: int32 [64, 4], P(('groups', 'replica')), parts along dimension 0, may hold values from 0 to 31, as said below
- new_table: int32 [64, 4], P(('groups', 'replica')), parts along dimension 0, may hold values from 0 to 31, as said below
- migrations: int32 [16, 2], P('groups'), parts along dimension 0, may hold values from 0 to 31, as said below
Outputs:
- attn_first: bfloat16 [64, 4096], P(('groups', 'replica'), 'mp'), parts along dimension 0
- attn_second: bfloat16 [64, 4096], P(('groups', 'replica'), 'mp'), parts along dimension 0
- pool_after: bfloat16 [8, 4, 8, 128, 1024], P(('groups', 'replica'), 'mp'), parts along dimension 0
There are 2 independent parts, one for each index of `groups`. A program takes and returns all parts, laid end to end along the dimension named above; an argument that names none is the same for every part. Nothing has to cross between parts.
Inputs may be any that keep to these rules, and one draw needn't show every extreme that they name: block_table[r, p] = m * 8 + s names slot s of device m along mp in row r's replica, holding tokens 128 * p to 128 * p + 127 of row r; every slot of a replica is named once, and every row has exactly 1 page on each device along mp. `new_table`: as block_table, for the rows after migration; a row that keeps its request keeps its entries, and every page of a migrating request keeps its device index along mp. `migrations`: each row (b, a): the request in row b moves to row a of another replica. Each replica sends exactly 2 requests, to 2 different replicas, and receives exactly 2, into the rows that it sends from.
All inputs are finite; a program needn't handle non-finite values. No bound on the sum of `lengths` on one device may be relied on, other than what follows from the above.
Results may differ from a plain program's by a relative error of at most 0.0052.
Values may be sent and summed in bfloat16 or wider, within the bound.
No kernel may reach another device: no remote copies, remote signals or barrier semaphores. Data moves between devices by JAX's collectives and lax.ppermute only.
A program may use at most 64 MiB of HBM per device.

v0:
```python
import math

import jax
import jax.numpy as jnp
from jax import lax
from jax.sharding import PartitionSpec as P

H = 32
KVH = 4
HD = 128
PPD = 1


CAP = 20.0


def project(row_block, kv_weight):
    partial_value = jnp.dot(row_block, kv_weight, preferred_element_type=jnp.float32)
    return lax.psum(partial_value, "mp").astype(jnp.bfloat16)


def write_token(cache_pages, new_rows, table_rows, positions, my_column, slot_count):
    page_size = cache_pages.shape[1]
    page_of = positions // page_size
    global_slot = jnp.take_along_axis(table_rows, page_of[:, None], axis=1)[:, 0]
    target = jnp.where(global_slot // slot_count == my_column, global_slot % slot_count, slot_count)
    return cache_pages.at[target, positions % page_size].set(new_rows, mode="drop")


def device_slots(table_rows, my_column, slot_count):
    on_device = table_rows // slot_count == my_column
    ranking = jnp.cumsum(on_device.astype(jnp.int32), axis=1) - 1
    chosen_mask = on_device[:, :, None] & (
        ranking[:, :, None] == jnp.arange(PPD, dtype=jnp.int32)[None, None, :]
    )
    return jnp.sum(jnp.where(chosen_mask, (table_rows % slot_count)[:, :, None], 0), axis=1)


def attend(query_rows, cache_pages, table_rows, positions, my_column, slot_count):
    row_count = table_rows.shape[0]
    page_size = cache_pages.shape[1]
    group_size = H // KVH
    targets = my_column * slot_count + jnp.arange(slot_count, dtype=jnp.int32)
    matches = table_rows[:, :, None] == targets[None, None, :]
    holder_mask = jnp.any(matches, axis=1)
    page_index = jnp.sum(
        jnp.where(matches, jnp.arange(table_rows.shape[1], dtype=jnp.int32)[None, :, None], 0),
        axis=(0, 1),
    )
    holder_length = jnp.sum(jnp.where(holder_mask, positions[:, None], 0), axis=0)
    slot_queries = jnp.dot(
        holder_mask.T.astype(jnp.bfloat16), query_rows, preferred_element_type=jnp.float32
    ).astype(jnp.bfloat16)
    slot_queries = slot_queries.reshape(slot_count, KVH, group_size, HD)
    key_rows = cache_pages[:, :, : KVH * HD].reshape(slot_count, page_size, KVH, HD)
    value_rows = cache_pages[:, :, KVH * HD :].reshape(slot_count, page_size, KVH, HD)
    scores = jnp.einsum(
        "skge,stke->skgt", slot_queries, key_rows, preferred_element_type=jnp.float32
    ) * (1.0 / math.sqrt(HD))
    capped = CAP * jnp.tanh(scores / CAP)
    token_position = (
        page_index[:, None] * page_size + jnp.arange(page_size, dtype=jnp.int32)[None, :]
    )
    inside = token_position <= holder_length[:, None]
    weight = jnp.where(inside[:, None, None, :], jnp.exp(capped), 0.0)
    numerator = jnp.einsum(
        "skgt,stke->skge",
        weight.astype(jnp.bfloat16),
        value_rows,
        preferred_element_type=jnp.float32,
    )
    numerator = numerator.reshape(slot_count, H * HD)
    denominator = jnp.sum(weight, axis=3).reshape(slot_count, H)
    holder_float = holder_mask.astype(jnp.float32)
    numerator_rows = jnp.dot(holder_float, numerator, precision=lax.Precision.HIGHEST)
    denominator_rows = jnp.dot(holder_float, denominator, precision=lax.Precision.HIGHEST)
    numerator_mine, denominator_mine = (
        lax.psum_scatter(numerator_rows, "mp", scatter_dimension=1, tiled=True),
        lax.psum_scatter(denominator_rows, "mp", scatter_dimension=1, tiled=True),
    )
    local_heads = denominator_mine.shape[1]
    result = numerator_mine.reshape(row_count, local_heads, HD) / denominator_mine[:, :, None]
    return result.reshape(row_count, local_heads * HD).astype(jnp.bfloat16)


def body(layer_input, kv_weight, queries, kv_pool, lengths, block_table, new_table, migrations):
    replica_count = lax.axis_size("replica")
    my_replica = lax.axis_index("replica")
    my_column = lax.axis_index("mp")
    slot_count = kv_pool.shape[2]
    row_count = lengths.shape[0]
    page_size = kv_pool.shape[3]
    all_queries = lax.all_gather(queries, "mp", axis=2, tiled=True)
    kv_first = project(layer_input[0], kv_weight)
    cache_one = write_token(kv_pool[0, 0], kv_first, block_table, lengths, my_column, slot_count)
    attn_first = attend(all_queries[0], cache_one, block_table, lengths, my_column, slot_count)
    moved_from = migrations[:, 0]
    moved_to = migrations[:, 1]
    per_replica = migrations.shape[0] // replica_count
    leaving = moved_from // row_count == my_replica
    counter = jnp.cumsum(leaving.astype(jnp.int32)) - 1
    select = leaving[None, :] & (
        counter[None, :] == jnp.arange(per_replica, dtype=jnp.int32)[:, None]
    )
    out_rows = jnp.sum(jnp.where(select, moved_from[None, :] % row_count, 0), axis=1)
    out_target = jnp.sum(jnp.where(select, moved_to[None, :], 0), axis=1)
    out_slots = device_slots(block_table[out_rows], my_column, slot_count)
    out_pages = cache_one[out_slots]
    out_lengths = lengths[out_rows]
    got_pages, got_target, got_lengths = (
        lax.all_gather(out_pages, "replica", axis=0, tiled=True),
        lax.all_gather(out_target, "replica", axis=0, tiled=True),
        lax.all_gather(out_lengths, "replica", axis=0, tiled=True),
    )
    has_source = got_target // row_count == my_replica
    got_rows = got_target % row_count
    in_slots = device_slots(new_table[got_rows], my_column, slot_count)
    in_slots = jnp.where(has_source[:, None], in_slots, slot_count)
    cache_two = cache_one.at[in_slots.reshape(-1)].set(
        got_pages.reshape(-1, page_size, cache_one.shape[2]), mode="drop"
    )
    arrival_index = jnp.where(has_source, got_rows, row_count)
    carried = jnp.zeros((row_count,), jnp.int32).at[arrival_index].set(got_lengths, mode="drop")
    is_arrival = jnp.zeros((row_count,), bool).at[arrival_index].set(True, mode="drop")
    lengths_after = jnp.where(is_arrival, carried, lengths) + 1
    kv_second = project(layer_input[1], kv_weight)
    pool_after = write_token(cache_two, kv_second, new_table, lengths_after, my_column, slot_count)
    attn_second = attend(
        all_queries[1], pool_after, new_table, lengths_after, my_column, slot_count
    )
    return (attn_first, attn_second, pool_after[None, None])


def solution(mesh):
    return jax.shard_map(
        body,
        mesh=mesh,
        in_specs=(
            P(None, ("groups", "replica"), "mp"),
            P("mp", None),
            P(None, ("groups", "replica"), "mp"),
            P(("groups", "replica"), "mp", None, None, None),
            P(("groups", "replica")),
            P(("groups", "replica"), None),
            P(("groups", "replica"), None),
            P("groups", None),
        ),
        out_specs=(
            P(("groups", "replica"), "mp"),
            P(("groups", "replica"), "mp"),
            P(("groups", "replica"), "mp", None, None, None),
        ),
        check_vma=False,
    )
```

profile of v0, /device:TPU:0, one launch (start us, length us, event | category | flops | bytes accessed | tf_op | source)
XLA Modules:
  0.0 119.6 jit_solution(17754205701085553100)
XLA Ops:
  8.1 2.2 %copy-done.5 = bf16[2048,1024]{1,0:T(8,128)(2,1)S(1)} copy-done((bf16[2048,1024]{1,0:T(8,128)(2,1)S(1)}, bf16[2048,1024]{1,0:T(8,128)(2,1)}, u32[]{:S(2)}) %copy-start.5) | copy-done | bytes 4194328
  10.2 1.5 %fusion.22 = f32[8,1024]{1,0:T(8,128)S(1)} fusion(bf16[2048,1024]{1,0:T(8,128)(2,1)S(1)} %copy-done.5, bf16[2,8,2048]{2,1,0:T(8,128)(2,1)} %param.10), kind=kOutput, calls=%fused_computation.43 | convolution fusion | flops 33554432 | bytes 4259840 | tf_op jit(solution)/shard_map/dot_general | solution.py:18
  11.8 0.7 fusion.19
  12.8 0.6 dynamic-slice
  14.1 0.6 gather_fusion
  15.1 6.4 %all-reduce.4 = (s32[8]{0:T(128)S(1)}, s32[8]{0:T(128)S(1)}) all-reduce(s32[8]{0:T(128)S(1)} %dynamic-update-slice, s32[8]{0:T(128)S(1)} %dynamic-update-slice.1), channel_id=1, replica_groups=mesh['groups'=2,'replica'=4,'mp'=4] {'replica'}, use_global_device_ids=true, to_apply=%add | all-reduce | flops 16 | bytes 128
  21.5 0.6 scatter_custom_fusion.1
  22.1 0.6 scatter_custom_fusion.2
  22.9 0.7 gather_fusion.4
  24.5 19.9 %all-reduce.6 = (bf16[8,1024]{1,0:T(8,128)(2,1)S(1)}, bf16[8,1024]{1,0:T(8,128)(2,1)S(1)}) all-reduce(f32[8,1024]{1,0:T(8,128)S(1)} %fusion.22, f32[8,1024]{1,0:T(8,128)S(1)} %fusion.19), channel_id=1, replica_groups=mesh['groups'=2,'replica'=4,'mp'=4] {'mp'}, use_global_device_ids=true, to_apply=%region_3.5 | all-reduce | flops 16384 | bytes 98304 | tf_op jit(solution)/shard_map/psum | solution.py:19
  44.4 1.0 scatter_fusion
  45.4 1.4 %gather_fusion.3 = bf16[2,128,1024]{2,1,0:T(8,128)(2,1)} fusion(bf16[8,128,1024]{2,1,0:T(8,128)(2,1)S(1)} %scatter_fusion, s32[1024]{0:T(1024)S(1)} %pad_clamp_fusion), kind=kCustom, calls=%fused_computation.5 | custom fusion | bytes 1048584 | tf_op jit(solution)/shard_map/gather | solution.py:108
  46.9 1.5 %fusion.57 = (bf16[8,128,512]{2,1,0:T(8,128)(2,1)}, bf16[8,128,512]{2,1,0:T(8,128)(2,1)}) fusion(bf16[8,128,1024]{2,1,0:T(8,128)(2,1)S(1)} %scatter_fusion), kind=kLoop, calls=%fused_computation.177 | loop fusion | bytes 4194304 | tf_op jit(solution)/shard_map/slice | solution.py:55
  48.4 1.6 %copy.68 = bf16[8,128,512]{1,2,0:T(8,128)(2,1)S(1)} copy(bf16[8,128,512]{2,1,0:T(8,128)(2,1)} %get-tuple-element.31) | data formatting | bytes 2097152 | tf_op jit(solution)/shard_map/slice | solution.py:56
  50.0 2.3 %copy.65 = bf16[8,128,512]{1,2,0:T(8,128)(2,1)} copy(bf16[8,128,512]{2,1,0:T(8,128)(2,1)} %get-tuple-element.30) | data formatting | bytes 2097152 | tf_op jit(solution)/shard_map/slice | solution.py:55
  52.4 13.5 %all_gather.12 = bf16[2,8,4096]{2,1,0:T(8,128)(2,1)S(1)} all-gather(bf16[2,8,1024]{2,1,0:T(8,128)(2,1)S(1)} %copy-done.7), channel_id=1, replica_groups=mesh['groups'=2,'replica'=4,'mp'=4] {'mp'}, dimensions={2}, use_global_device_ids=true | all-gather | bytes 163840 | tf_op jit(solution)/shard_map/all_gather | solution.py:93
  66.4 1.7 %fusion.58 = (f32[8,4,8]{2,1,0:T(4,128)S(1)}, bf16[8,4,8,128]{3,2,1,0:T(8,128)(2,1)S(1)}) fusion(bf16[8,128,4,128]{1,3,2,0:T(8,128)(2,1)} %bitcast.143, bf16[8,4,8,128]{3,0,2,1:T(8,128)(2,1)S(1)} %bitcast.147, pred[8,128]{1,0:T(8,128)(4,1)S(1)} %add_compare_fusion.2), kind=kOutput, calls=%fused_computation.178 | convolution fusion | flops 8552192 | bytes 1181696 | tf_op jit(solution)/shard_map/skge,stke->skgt/dot_general | solution.py:57
  68.1 0.6 convolution_bitcast_fusion.1
  68.8 0.9 fusion.11
  71.0 0.7 gather_fusion.5
  72.0 0.6 dynamic-slice.2
  73.3 3.2 %scatter_fusion.1 = bf16[8,128,1024]{2,1,0:T(8,128)(2,1)S(1)} fusion(bf16[8,128,1024]{2,1,0:T(8,128)(2,1)S(1)} %scatter_fusion, s32[8]{0:T(128)S(1)} %compare_select_fusion.7, bf16[8,128,1024]{2,1,0:T(8,128)(2,1)} %all-gather.4.cloned.1.call-done), kind=kCustom, calls=%fused_computation.9 | custom fusion | bytes 6291488 | tf_op jit(solution)/shard_map/scatter | solution.py:119
  76.6 1.0 scatter_fusion.2
  77.6 1.2 %fusion.56 = (bf16[8,128,512]{2,1,0:T(8,128)(2,1)S(1)}, bf16[8,128,512]{2,1,0:T(8,128)(2,1)}) fusion(bf16[8,128,1024]{2,1,0:T(8,128)(2,1)S(1)} %scatter_fusion.2), kind=kLoop, calls=%fused_computation.176 | loop fusion | bytes 4194304 | tf_op jit(solution)/shard_map/slice | solution.py:56
  79.3 1.6 %copy.73 = bf16[8,128,512]{1,2,0:T(8,128)(2,1)S(1)} copy(bf16[8,128,512]{2,1,0:T(8,128)(2,1)} %get-tuple-element.29) | data formatting | bytes 2097152 | tf_op jit(solution)/shard_map/slice | solution.py:55
  81.6 0.7 copy.76
  82.3 8.9 %all-reduce.5 = (f32[8,32]{1,0:T(8,128)S(1)}, f32[8,32]{1,0:T(8,128)S(1)}) all-reduce(f32[8,32]{1,0:T(8,128)S(1)} %fusion.60, f32[8,32]{1,0:T(8,128)S(1)} %fusion.61), channel_id=5, replica_groups=mesh['groups'=2,'replica'=4,'mp'=4] {'mp'}, use_global_device_ids=true, to_apply=%region_7.9.clone | all-reduce | flops 512 | bytes 4096
  91.1 0.6 convolution_bitcast_fusion
  91.9 0.9 fusion.8
  93.0 1.4 %fusion.21 = bf16[8,1024]{1,0:T(8,128)(2,1)} fusion(f32[8,1024]{1,0:T(8,128)} %reduce-scatter.5.cloned.1.call-done, f32[8,8]{0,1:T(8,128)S(1)} %copy.70), kind=kLoop, calls=%fused_computation.42 | loop fusion | flops 16384 | bytes 49408 | tf_op jit(solution)/shard_map/convert_element_type | solution.py:83
  94.5 16.2 %reduce-scatter.7.cloned.1.call-done = f32[8,1024]{1,0:T(8,128)} async-done(((f32[8,4096]{1,0:T(8,128)}), f32[8,1024]{1,0:T(8,128)}) %reduce-scatter.7.cloned.1.call-update) | async-done | bytes 32784 | tf_op jit(solution)/shard_map/reduce_scatter | solution.py:78
  110.7 1.4 %fusion.18 = bf16[8,1024]{1,0:T(8,128)(2,1)} fusion(f32[8,1024]{1,0:T(8,128)} %reduce-scatter.7.cloned.1.call-done, f32[8,8]{0,1:T(8,128)S(1)} %copy.78), kind=kLoop, calls=%fused_computation.38 | loop fusion | flops 16384 | bytes 49408 | tf_op jit(solution)/shard_map/convert_element_type | solution.py:83
  (84 shorter events, 5.6 us)
Async XLA Ops:
  8.0 65.3 %all-gather.4.cloned.1.call-start = ((), (), s32[]{:S(2)}) async-start(), calls=%async_computation.4 | async-start | bytes 2621440 | tf_op jit(solution)/shard_map/all_gather | solution.py:111
  8.0 2.2 %copy-start.5 = (bf16[2048,1024]{1,0:T(8,128)(2,1)S(1)}, bf16[2048,1024]{1,0:T(8,128)(2,1)}, u32[]{:S(2)}) copy-start(bf16[2048,1024]{1,0:T(8,128)(2,1)} %param.11) | copy-start | bytes 12582916
  10.2 1.5 %copy-start.6 = (bf16[2,8,2048]{2,1,0:T(8,128)(2,1)S(1)}, bf16[2,8,2048]{2,1,0:T(8,128)(2,1)}, u32[]{:S(2)}) copy-start(bf16[2,8,2048]{2,1,0:T(8,128)(2,1)} %param.10) | copy-start | bytes 196612
  11.7 0.7 copy-start.8
  11.7 1.1 copy-start.10
  11.7 2.4 %copy-start = (s32[8]{0:T(128)S(1)}, s32[8]{0:T(128)}, u32[]{:S(2)}) copy-start(s32[8]{0:T(128)} %param.14) | copy-start | bytes 100
  11.7 11.0 %copy-start.1 = (s32[8,4]{0,1:T(4,128)S(1)}, s32[8,4]{0,1:T(4,128)}, u32[]{:S(2)}) copy-start(s32[8,4]{0,1:T(4,128)} %param.15) | copy-start | bytes 388
  11.7 32.6 %copy-start.4 = (bf16[1,1,8,128,1024]{4,3,2,1,0:T(8,128)(2,1)S(1)}, bf16[1,1,8,128,1024]{4,3,2,1,0:T(8,128)(2,1)}, u32[]{:S(2)}) copy-start(bf16[1,1,8,128,1024]{4,3,2,1,0:T(8,128)(2,1)} %param.13) | copy-start | bytes 6291460
  46.8 46.2 %reduce-scatter.5.cloned.1.call-start = ((), (), s32[]{:S(2)}) async-start(), calls=%async_computation.2 | async-start | bytes 163840 | tf_op jit(solution)/shard_map/reduce_scatter | solution.py:78
  48.4 3.9 %copy-start.7 = (bf16[2,8,1024]{2,1,0:T(8,128)(2,1)S(1)}, bf16[2,8,1024]{2,1,0:T(8,128)(2,1)}, u32[]{:S(2)}) copy-start(bf16[2,8,1024]{2,1,0:T(8,128)(2,1)} %param.12) | copy-start | bytes 98308
  48.4 17.5 %copy-start.2 = (s32[8,4]{0,1:T(4,128)S(1)}, s32[8,4]{0,1:T(4,128)}, u32[]{:S(2)}) copy-start(s32[8,4]{0,1:T(4,128)} %param.16) | copy-start | bytes 388
  52.4 19.7 %copy-start.9 = (u32[32]{0:T(128)S(1)}, u32[32]{0:T(128)}, u32[]{:S(2)}) copy-start(u32[32]{0:T(128)} %constant.273) | copy-start | bytes 388
  69.7 40.9 %reduce-scatter.7.cloned.1.call-start = ((), (), s32[]{:S(2)}) async-start(), calls=%async_computation.3 | async-start | bytes 163840 | tf_op jit(solution)/shard_map/reduce_scatter | solution.py:78
  77.6 1.7 %copy-start.3 = (bf16[8,128,1024]{2,1,0:T(8,128)(2,1)}, bf16[8,128,1024]{2,1,0:T(8,128)(2,1)S(1)}, u32[]{:S(2)}) copy-start(bf16[8,128,1024]{2,1,0:T(8,128)(2,1)S(1)} %scatter_fusion.2) | copy-start | bytes 6291460
Sparse Core Ops, SparseCore 0:
  46.9 20.2 all-gather.3
Sparse Core Ops, SparseCore 1:
  69.8 16.7 reduce-scatter.4
  92.9 17.7 reduce-scatter.6
where the time goes:
time: 120 us
  blocking collectives  48.7 us (41%)
  local copies, waits for them, and re-layouts  24.8 us (21%)
  between operations  17.1 us (14%)
  waiting for transfers between devices  16.3 us (14%)
  matrix products  8.09 us (7%)
  other arithmetic  4.53 us (4%)
    psum x1, blocking collectives, project(): return lax.psum(partial_value, 'mp').astype(jnp.bfloat16)  19.9 us
    reduce_scatter x2, waiting for transfers between devices, attend(): lax.psum_scatter(numerator_rows, 'mp', scatter_dimension=1, tiled=True)  16.2 us
    unnamed x2, blocking collectives  15.2 us
    all_gather x1, blocking collectives, body(): all_queries = lax.all_gather(queries, 'mp', axis=2, tiled=True)  13.5 us
    slice x3, local copies, waits for them, and re-layouts, attend(): cache_pages[:, :, :KVH * HD].reshape(slot_count, page_size, KVH, HD)  5.46 us
    unnamed x30, local copies, waits for them, and re-layouts  4.51 us
    slice x3, local copies, waits for them, and re-layouts, attend(): cache_pages[:, :, KVH * HD:].reshape(slot_count, page_size, KVH, HD)  3.54 us
    scatter x1, local copies, waits for them, and re-layouts, body(): cache_one.at[in_slots.reshape(-1)]  3.25 us
  transfers between devices with their start and end apart: 3, of which 1 were waited for; matrix products, arithmetic and copies ran while one was open for 20% of the time, Pallas kernels for 0%

commit v1 on v0

v1 whole, which is shorter than its diff:
```python
import functools
import math

import jax
import jax.numpy as jnp
from jax import lax
from jax.experimental import pallas as pl
from jax.experimental.pallas import tpu as pltpu
from jax.sharding import PartitionSpec as P

H = 32
KVH = 4
HD = 128
GROUP = H // KVH
CAP = 20.0
SCALE = 1.0 / math.sqrt(HD)
WINDOW = 32
KV_ROWS = 24

SMEM = pl.BlockSpec(memory_space=pltpu.SMEM)
VMEM = pl.BlockSpec(memory_space=pltpu.VMEM)
ANY = pl.BlockSpec(memory_space=pl.ANY)
SEND = jnp.bfloat16


def shift_by(value, axis, amount):
    size = lax.axis_size(axis)
    return lax.ppermute(value, axis, [(i, (i + amount) % size) for i in range(size)])


def exchange(messages, axis):
    return [shift_by(message, axis, s + 1) for s, message in enumerate(messages)]


def count_up(limit, step, start):
    return lax.fori_loop(0, limit, step, start)


def locate(table, row, column, slots):
    def step(p, found):
        entry = table[row, p]
        here = entry // slots == column
        return jnp.where(here, p, found[0]), jnp.where(here, entry % slots, found[1])

    return count_up(table.shape[1], step, (jnp.int32(0), jnp.int32(0)))


def pair_row(moves, source, target, rows, side):
    def step(j, found):
        match = (moves[j, 0] // rows == source) & (moves[j, 1] // rows == target)
        return (
            jnp.where(match, jnp.int32(1), found[0]),
            jnp.where(match, moves[j, side] % rows, found[1]),
        )

    return count_up(moves.shape[0], step, (jnp.int32(0), jnp.int32(0)))


def source_of(axis, shift):
    size = lax.axis_size(axis)
    return lax.rem(lax.axis_index(axis) + (size - shift), size)


def target_of(axis, shift):
    return lax.rem(lax.axis_index(axis) + shift, lax.axis_size(axis))


def head_columns(device, local_heads):
    return pl.ds(pl.multiple_of(device * local_heads // GROUP * HD, HD), HD)


def weight_of(score):
    return jnp.exp(CAP * jnp.tanh(score * (SCALE / CAP)))


def leave_kernel(rows, moves, table, pool, *refs):
    outs, sems = refs[:-1], refs[-1]
    me, column = lax.axis_index("replica"), lax.axis_index("mp")
    copies = []
    for s, out in enumerate(outs):
        _, row = pair_row(moves, me, target_of("replica", s + 1), rows, 0)
        _, slot = locate(table, row, column, pool.shape[0])
        copies.append(pltpu.make_async_copy(pool.at[slot], out, sems.at[s]))
        copies[-1].start()
    for copy in copies:
        copy.wait()


def project_kernel(count, local_heads, x, weight, q, *refs):
    outs, total = refs[:-1], refs[-1]
    step = pl.program_id(0)
    rows = q.shape[1]
    query_rows = 2 * local_heads * rows

    @pl.when(step == 0)
    def _():
        total[...] = jnp.zeros_like(total)
        wide = [q[i].astype(jnp.float32) for i in range(2)]
        blocks = [wide[i][:, h * HD : (h + 1) * HD] for i in range(2) for h in range(local_heads)]
        packed = jnp.concatenate(blocks, axis=0).astype(jnp.bfloat16)
        for out in outs:
            out[:query_rows, :] = packed

    total[...] += jnp.dot(x[...], weight[...], preferred_element_type=jnp.float32)

    @pl.when(step == pl.num_programs(0) - 1)
    def _():
        for s, out in enumerate(outs):
            columns = head_columns(target_of("mp", s), local_heads)
            parts = []
            for half in range(2):
                part = total.at[:, pl.ds(half * KVH * HD, KVH * HD)][:, columns]
                high = part.astype(jnp.bfloat16)
                parts += [high, (part - high.astype(jnp.float32)).astype(jnp.bfloat16)]
            out[query_rows:, :] = jnp.concatenate(parts, axis=0)


def token_kernel(count, replicas, rows, moves, lengths, *refs):
    messages, kv, outs = refs[:count], refs[count], refs[count + 1 :]
    tokens = 2 * rows
    base = messages[0].shape[0] - 4 * tokens
    me = lax.axis_index("replica")
    for half in range(2):
        total = jnp.zeros((tokens, HD), jnp.float32)
        for message in messages:
            start = base + 2 * half * tokens
            total += message[start : start + tokens, :].astype(jnp.float32)
            total += message[start + tokens : start + 2 * tokens, :].astype(jnp.float32)
        kv[half] = total.astype(jnp.bfloat16).astype(jnp.float32)
    for s, out in enumerate(outs):
        _, row = pair_row(moves, me, target_of("replica", s + 1), rows, 0)
        out[...] = jnp.zeros_like(out)
        out[0:1, :] = kv[0, pl.ds(row, 1), :]
        out[1:2, :] = kv[1, pl.ds(row, 1), :]
        out[2:3, :] = jnp.full((1, HD), lengths[row], jnp.int32).astype(jnp.float32)


def page_attention(q, keys, values, inside):
    scores = lax.dot_general(
        q, keys, (((1,), (1,)), ((), ())), preferred_element_type=jnp.float32
    )
    weight = jnp.where(inside, weight_of(scores), 0.0)
    numerator = jnp.dot(weight.astype(jnp.bfloat16), values, preferred_element_type=jnp.float32)
    return numerator, jnp.sum(weight, axis=1, keepdims=True)


def attend_kernel(count, local_heads, table, lengths, pool, *refs):
    messages = refs[:count]
    num, den, pool_out, pages, wide, in_sems, out_sems = refs[count:]
    column = lax.axis_index("mp")
    rows = lengths.shape[0]
    slots, page_size, width = pool.shape
    both = 2 * local_heads
    places = [locate(table, r, column, slots) for r in range(rows)]
    loads = [
        pltpu.make_async_copy(pool.at[places[r][1]], pages.at[r], in_sems.at[r]) for r in range(rows)
    ]
    stores = [
        pltpu.make_async_copy(pages.at[r], pool_out.at[places[r][1]], out_sems.at[r])
        for r in range(rows)
    ]
    for load in loads:
        load.start()
    for s, message in enumerate(messages):
        wide[s] = message[: both * rows, :].astype(jnp.float32)
    lane = lax.broadcasted_iota(jnp.int32, (both, HD), 1)
    token = lax.broadcasted_iota(jnp.int32, (both, page_size), 1)
    denominators = [jnp.zeros((both, HD), jnp.float32) for _ in range(count)]
    for r in range(rows):
        loads[r].wait()
        stores[r].start()
        inside = token < lengths[r] - places[r][0] * page_size
        for s in range(count):
            columns = head_columns(source_of("mp", s), local_heads)
            q = wide[s, pl.ds(r, both, stride=rows), :].astype(jnp.bfloat16)
            keys = pages.at[r, :, pl.ds(0, width // 2)][:, columns]
            values = pages.at[r, :, pl.ds(width // 2, width // 2)][:, columns]
            numerator, denominator = page_attention(q, keys, values, inside)
            num[s, pl.ds(r, both, stride=rows), :] = numerator
            denominators[s] += jnp.where(lane == r, denominator, 0.0)
    for s in range(count):
        den[s] = denominators[s]
    for store in stores:
        store.wait()


def arrive_kernel(count, replicas, local_heads, moves, table, kv, *refs):
    rows, slots = table.shape[0], table.shape[0]
    refs = list(refs)
    take = lambda n: [refs.pop(0) for _ in range(n)]
    pages_in, tokens_in, messages = take(replicas - 1), take(replicas - 1), take(count)
    num_in, den_in = take(2)
    outs = take(count - 1)
    own_num, own_den, num, den, pages, wide, sems = refs
    me, column = lax.axis_index("replica"), lax.axis_index("mp")
    page_size, width = pages_in[0].shape
    half_rows = local_heads * rows
    loads = [
        pltpu.make_async_copy(page, pages.at[s], sems.at[s]) for s, page in enumerate(pages_in)
    ]
    for load in loads:
        load.start()
    num[...] = num_in[...]
    den[...] = den_in[...]
    for s, message in enumerate(messages):
        wide[s] = message[half_rows : 2 * half_rows, :].astype(jnp.float32)
    lane = lax.broadcasted_iota(jnp.int32, (local_heads, HD), 1)
    token = lax.broadcasted_iota(jnp.int32, (local_heads, page_size), 1)
    for shift in range(1, replicas):
        loads[shift - 1].wait()
        valid, row = pair_row(moves, source_of("replica", shift), me, rows, 1)

        @pl.when(valid == 1)
        def _():
            index, _ = locate(table, row, column, slots)
            length = tokens_in[shift - 1][2:3, :]
            inside = (token + index * page_size).astype(jnp.float32) < length
            for s in range(count):
                columns = head_columns(source_of("mp", s), local_heads)
                q = wide[s, pl.ds(row, local_heads, stride=rows), :].astype(jnp.bfloat16)
                keys = pages.at[shift - 1, :, pl.ds(0, width // 2)][:, columns]
                values = pages.at[shift - 1, :, pl.ds(width // 2, width // 2)][:, columns]
                numerator, denominator = page_attention(q, keys, values, inside)
                num[s, pl.ds(half_rows + row, local_heads, stride=rows), :] = numerator
                old = den[s, pl.ds(local_heads, local_heads), :]
                den[s, pl.ds(local_heads, local_heads), :] = jnp.where(lane == row, denominator, old)

    own_num[...] = num[0]
    own_den[...] = den[0]
    filler = jnp.zeros((KV_ROWS - 2 * rows - (replicas - 1), HD), jnp.float32)
    all_kv = []
    for half in range(2):
        all_kv += [kv[half]] + [arrived[half : half + 1, :] for arrived in tokens_in] + [filler]
    all_kv = jnp.concatenate(all_kv, axis=0)
    for s, out in enumerate(outs):
        at = count - 1 - s
        parts = den[at]
        high = parts.astype(SEND).astype(jnp.float32)
        parts = high + pltpu.roll(parts - high, HD // 2, 1)
        out[...] = jnp.concatenate([num[at], parts, all_kv], axis=0).astype(SEND)


def finish_kernel(count, replicas, local_heads, moves, table, lengths, kv, q, num, den, *refs):
    refs = list(refs)
    take = lambda n: [refs.pop(0) for _ in range(n)]
    pages_in, tokens_in, messages = take(replicas - 1), take(replicas - 1), take(count - 1)
    pool_raw, _, first, second, pool = take(5)
    held, full, windows, page_sems, read_sems, write_sems = refs
    me, column = lax.axis_index("replica"), lax.axis_index("mp")
    rows = lengths.shape[0]
    slots, page_size, width = pool_raw.shape
    both = 2 * local_heads

    arrivals, copies = [], []
    for shift in range(1, replicas):
        valid, row = pair_row(moves, source_of("replica", shift), me, rows, 1)
        length = jnp.max(tokens_in[shift - 1][2:3, :]).astype(jnp.int32)
        _, slot = locate(table, row, column, slots)
        arrivals.append((valid == 1, row, length))
        copies.append(
            pltpu.make_async_copy(pages_in[shift - 1], pool.at[slot], page_sems.at[shift - 1])
        )
        pl.when(valid == 1)(copies[-1].start)

    plans = []
    for r in range(rows):
        origin, length = jnp.int32(0), lengths[r]
        for s, (valid, row, arrived) in enumerate(arrivals):
            here = valid & (row == r)
            origin = jnp.where(here, s + 1, origin)
            length = jnp.where(here, arrived, length)
        index, slot = locate(table, r, column, slots)
        at = length - index * page_size
        touched = (at >= -1) & (at < page_size)
        start = jnp.clip(at, 0, page_size - WINDOW) // 16 * 16
        start = pl.multiple_of(start, 16)
        span = pl.ds(start, WINDOW)
        sources = [pool_raw.at[slot]] + list(pages_in)
        for s, source in enumerate(sources):

            @pl.when(touched & (origin == s))
            def _(source=source, span=span, r=r):
                pltpu.make_async_copy(source.at[span], windows.at[r], read_sems.at[r]).start()

        plans.append((touched, origin, at - start, pool.at[slot, span], pool_raw.at[slot, span]))

    for half in range(2):
        held[half] = kv[half, :rows, :]
        for s, (valid, row, _) in enumerate(arrivals):

            @pl.when(valid)
            def _(half=half, s=s, row=row):
                held[half, pl.ds(row, 1), :] = tokens_in[s][half : half + 1, :]

    query_rows = both * rows
    kv_base = messages[0].shape[0] - 2 * KV_ROWS
    filler = jnp.zeros((KV_ROWS - 2 * rows - (replicas - 1), HD), jnp.float32)
    for s in range(count):
        device = source_of("mp", s)
        for half in range(2):
            if s == 0:
                chunk = jnp.concatenate(
                    [kv[half]] + [arrived[half : half + 1, :] for arrived in tokens_in] + [filler],
                    axis=0,
                )
            else:
                start = kv_base + half * KV_ROWS
                chunk = messages[s - 1][start : start + KV_ROWS, :].astype(jnp.float32)

            def place(half=half, device=device, chunk=chunk):
                columns = head_columns(device, local_heads)
                full.at[:, pl.ds(half * (width // 2), width // 2)][:, columns] = chunk

            if local_heads == GROUP:
                place()
            else:
                pl.when(lax.rem(device * local_heads, GROUP) == 0)(place)

    sums = den[...]
    for message in messages:
        part = message[query_rows : query_rows + both, :].astype(jnp.float32)
        sums += part + pltpu.roll(part, HD // 2, 1)
    sums = jnp.transpose(sums)[:rows, :]
    for step, out in enumerate((first, second)):
        results = []
        for h in range(local_heads):
            at = (step * local_heads + h) * rows
            query = q[at : at + rows, :].astype(jnp.float32)
            numerator = num[at : at + rows, :]
            for message in messages:
                numerator += message[at : at + rows, :].astype(jnp.float32)
            denominator = sums[:, step * local_heads + h : step * local_heads + h + 1]
            extra = [(kv[0, :rows, :], kv[1, :rows, :])]
            if step == 1:
                extra = [(held[0], held[1]), (kv[0, rows:, :], kv[1, rows:, :])]
            for key, value in extra:
                weight = weight_of(jnp.sum(query * key, axis=1, keepdims=True))
                numerator += weight.astype(jnp.bfloat16).astype(jnp.float32) * value
                denominator += weight
            results.append(numerator / denominator)
        out[...] = jnp.concatenate(results, axis=1).astype(out.dtype)

    for (valid, _, _), copy in zip(arrivals, copies):
        pl.when(valid)(copy.wait)
    place_ids = lax.broadcasted_iota(jnp.int32, (WINDOW, width), 0)
    for r, (touched, origin, offset, target, source) in enumerate(plans):

        @pl.when(touched)
        def _(r=r, origin=origin, offset=offset, target=target, source=source):
            pltpu.make_async_copy(source, windows.at[r], read_sems.at[r]).wait()
            row = jnp.where(origin == 0, r, 2 * rows + origin - 1)
            old = windows[r].astype(jnp.float32)
            new = jnp.where(place_ids == offset, full[pl.ds(row, 1), :], old)
            new = jnp.where(place_ids == offset + 1, full[rows + r : rows + r + 1, :], new)
            windows[r] = new.astype(jnp.bfloat16)
            pltpu.make_async_copy(windows.at[r], target, write_sems.at[r]).start()

    for r, (touched, _, _, target, _) in enumerate(plans):

        @pl.when(touched)
        def _(r=r, target=target):
            pltpu.make_async_copy(windows.at[r], target, write_sems.at[r]).wait()


def params(megabytes=32, **rest):
    return pltpu.CompilerParams(vmem_limit_bytes=megabytes << 20, **rest)


def body(layer_input, kv_weight, queries, kv_pool, lengths, block_table, new_table, migrations):
    replicas, count = lax.axis_size("replica"), lax.axis_size("mp")
    rows = lengths.shape[0]
    pool = kv_pool[0, 0]
    slots, page_size, width = pool.shape
    local_heads = queries.shape[2] // HD
    both = 2 * local_heads
    query_rows = both * rows
    depth = layer_input.shape[2]
    f32, bf16 = jnp.float32, jnp.bfloat16
    shape = jax.ShapeDtypeStruct

    leaving = pl.pallas_call(
        functools.partial(leave_kernel, rows),
        out_shape=[shape((page_size, width), bf16)] * (replicas - 1),
        in_specs=[SMEM, SMEM, ANY],
        out_specs=[ANY] * (replicas - 1),
        scratch_shapes=[pltpu.SemaphoreType.DMA((replicas - 1,))],
        compiler_params=params(),
        name="leave",
    )(migrations, block_table, pool)
    pages_in = exchange(leaving, "replica")

    block = math.gcd(depth, 512)
    message_rows = query_rows + 8 * rows
    sent = pl.pallas_call(
        functools.partial(project_kernel, count, local_heads),
        grid=(depth // block,),
        out_shape=[shape((message_rows, HD), bf16)] * count,
        in_specs=[
            pl.BlockSpec((2 * rows, block), lambda k: (0, k)),
            pl.BlockSpec((block, width), lambda k: (k, 0)),
            pl.BlockSpec(queries.shape, lambda k: (0, 0, 0)),
        ],
        out_specs=[pl.BlockSpec((message_rows, HD), lambda k: (0, 0))] * count,
        scratch_shapes=[pltpu.VMEM((2 * rows, width), f32)],
        compiler_params=params(),
        name="project",
    )(layer_input.reshape(2 * rows, depth), kv_weight, queries)
    messages = [sent[0]] + exchange(sent[1:], "mp")

    kv, *tokens = pl.pallas_call(
        functools.partial(token_kernel, count, replicas, rows),
        out_shape=[shape((2, 2 * rows, HD), f32)] + [shape((8, HD), f32)] * (replicas - 1),
        in_specs=[SMEM, SMEM] + [VMEM] * count,
        out_specs=[VMEM] * replicas,
        compiler_params=params(),
        name="token",
    )(migrations, lengths, *messages)
    tokens_in = exchange(tokens, "replica")

    num, den, pool_copy = pl.pallas_call(
        functools.partial(attend_kernel, count, local_heads),
        out_shape=[
            shape((count, query_rows, HD), f32),
            shape((count, both, HD), f32),
            shape(pool.shape, bf16),
        ],
        in_specs=[SMEM, SMEM, ANY] + [VMEM] * count,
        out_specs=[VMEM, VMEM, ANY],
        scratch_shapes=[
            pltpu.VMEM((rows, page_size, width), bf16),
            pltpu.VMEM((count, query_rows, HD), f32),
            pltpu.SemaphoreType.DMA((rows,)),
            pltpu.SemaphoreType.DMA((rows,)),
        ],
        compiler_params=params(),
        name="attend",
    )(block_table, lengths, pool, *messages)

    sum_rows = query_rows + both + 2 * KV_ROWS
    *sums, num, den = pl.pallas_call(
        functools.partial(arrive_kernel, count, replicas, local_heads),
        out_shape=[shape((sum_rows, HD), SEND)] * (count - 1)
        + [shape((query_rows, HD), f32), shape((both, HD), f32)],
        in_specs=[SMEM, SMEM, VMEM]
        + [ANY] * (replicas - 1)
        + [VMEM] * (replicas - 1)
        + [VMEM] * count
        + [VMEM] * 2,
        out_specs=[VMEM] * (count + 1),
        scratch_shapes=[
            pltpu.VMEM((count, query_rows, HD), f32),
            pltpu.VMEM((count, both, HD), f32),
            pltpu.VMEM((replicas - 1, page_size, width), bf16),
            pltpu.VMEM((count, query_rows // 2, HD), f32),
            pltpu.SemaphoreType.DMA((replicas - 1,)),
        ],
        compiler_params=params(),
        name="arrive",
    )(migrations, new_table, kv, *pages_in, *tokens_in, *messages, num, den)
    sums_in = exchange(sums, "mp")

    first, second, pool_after = pl.pallas_call(
        functools.partial(finish_kernel, count, replicas, local_heads),
        out_shape=[
            shape((rows, local_heads * HD), bf16),
            shape((rows, local_heads * HD), bf16),
            shape(pool.shape, bf16),
        ],
        in_specs=[SMEM, SMEM, SMEM]
        + [VMEM] * 4
        + [ANY] * (replicas - 1)
        + [VMEM] * (replicas - 1)
        + [VMEM] * (count - 1)
        + [ANY, ANY],
        out_specs=[VMEM, VMEM, ANY],
        scratch_shapes=[
            pltpu.VMEM((2, rows, HD), f32),
            pltpu.VMEM((KV_ROWS, width), f32),
            pltpu.VMEM((rows, WINDOW, width), bf16),
            pltpu.SemaphoreType.DMA((replicas - 1,)),
            pltpu.SemaphoreType.DMA((rows,)),
            pltpu.SemaphoreType.DMA((rows,)),
        ],
        input_output_aliases={7 + 2 * (replicas - 1) + (count - 1) + 1: 2},
        compiler_params=params(),
        name="finish",
    )(migrations, new_table, lengths, kv, messages[0], num, den, *pages_in, *tokens_in, *sums_in, pool, pool_copy)
    return first, second, pool_after[None, None]


def solution(mesh):
    return jax.shard_map(
        body,
        mesh=mesh,
        in_specs=(
            P(None, ("groups", "replica"), "mp"),
            P("mp", None),
            P(None, ("groups", "replica"), "mp"),
            P(("groups", "replica"), "mp", None, None, None),
            P(("groups", "replica")),
            P(("groups", "replica"), None),
            P(("groups", "replica"), None),
            P("groups", None),
        ),
        out_specs=(
            P(("groups", "replica"), "mp"),
            P(("groups", "replica"), "mp"),
            P(("groups", "replica"), "mp", None, None, None),
        ),
        check_vma=False,
    )
```

time: 120 us -> 51.7 us (0.43)
  blocking collectives: 48.7 us -> 0 us
  local copies, waits for them, and re-layouts: 24.8 us -> 5.39 us
  Pallas kernels: 0 us -> 18.6 us
  between operations: 17.1 us -> 0.74 us
  starting transfers between devices: 0.13 us -> 15.1 us
  matrix products: 8.09 us -> 0 us
  waiting for transfers between devices: 16.3 us -> 11.2 us
  other arithmetic: 4.53 us -> 0 us
    psum x1 -> x0, blocking collectives: 19.9 us -> none  [project(): return lax.psum(partial_value, 'mp').astype(jnp.bfloat16)]
    pallas_call x0 -> x6, Pallas kernels: none -> 18.6 us  [the longest x1 7.86 us: body(): pl.pallas_call(functools.partial(attend_kernel, count, local_heads), out_...]
    reduce_scatter x2 -> x0, waiting for transfers between devices: 16.2 us -> none  [attend(): lax.psum_scatter(numerator_rows, 'mp', scatter_dimension=1, tiled=True)]
    unnamed x2 -> x0, blocking collectives: 15.2 us -> none
    ppermute x0 -> x12, starting transfers between devices: none -> 15.1 us  [shift_by(): lax.ppermute(value, axis, [(i, (i + amount) % size) for i in range(size)])]
    all_gather x1 -> x0, blocking collectives: 13.5 us -> none  [body(): all_queries = lax.all_gather(queries, 'mp', axis=2, tiled=True)]
    ppermute x0 -> x12, waiting for transfers between devices: none -> 11.2 us  [shift_by(): lax.ppermute(value, axis, [(i, (i + amount) % size) for i in range(size)])]
    slice x6 -> x0, local copies, waits for them, and re-layouts: 8.99 us -> none  [the longest x3 5.46 us: attend(): cache_pages[:, :, :KVH * HD].reshape(slot_count, page_size, KVH, HD)]
  transfers between devices with their start and end apart: 3 -> 12, of which waited for: 1 -> 6; matrix products, arithmetic and copies ran while one was open for 20% -> 0% of each run, Pallas kernels for 0% -> 20%
where the time goes in v1:
time: 51.7 us; the launch traced here: 51.1 us
  Pallas kernels  18.6 us (36%)
  starting transfers between devices  15.1 us (29%)
  waiting for transfers between devices  11.2 us (22%)
  local copies, waits for them, and re-layouts  5.39 us (10%)
  between operations  0.74 us (1%)
    ppermute x12, starting transfers between devices, shift_by(): lax.ppermute(value, axis, [(i, (i + amount) % size) for i in range(size)])  15.1 us
    ppermute x12, waiting for transfers between devices, shift_by(): lax.ppermute(value, axis, [(i, (i + amount) % size) for i in range(size)])  11.2 us
    pallas_call x1, Pallas kernels, body(): pl.pallas_call(functools.partial(attend_kernel, count, local_heads), out_...  7.86 us
    unnamed x17, local copies, waits for them, and re-layouts  5.39 us
    pallas_call x1, Pallas kernels, body(): pl.pallas_call(functools.partial(finish_kernel, count, replicas, local_he...  3.86 us
    pallas_call x1, Pallas kernels, body(): pl.pallas_call(functools.partial(arrive_kernel, count, replicas, local_he...  2.9 us
    pallas_call x1, Pallas kernels, body(): pl.pallas_call(functools.partial(leave_kernel, rows), out_shape=[shape((p...  1.81 us
    pallas_call x1, Pallas kernels, body(): pl.pallas_call(functools.partial(project_kernel, count, local_heads), gri...  1.1 us
  transfers between devices with their start and end apart: 12, of which 6 were waited for; matrix products, arithmetic and copies ran while one was open for 0% of the time, Pallas kernels for 20%

profile of v1, /device:TPU:0, one launch (start us, length us, event | category | flops | bytes accessed | tf_op | source)
XLA Modules:
  0.0 51.1 jit_solution(5168132718499147488)
XLA Ops:
  0.6 0.8 %copy.18.moves = s32[8,2]{1,0:T(8,128)S(1)} copy(s32[8,2]{0,1:T(2,128)} %param.15) | data formatting | bytes 128 | tf_op args[7]
  1.4 0.8 %copy.14.table = s32[8,4]{1,0:T(8,128)S(1)} copy(s32[8,4]{0,1:T(4,128)} %param.13) | data formatting | bytes 256 | tf_op args[5]
  2.1 1.6 %copy-done = bf16[1,1,8,128,1024]{4,3,2,1,0:T(8,128)(2,1)S(1)} copy-done((bf16[1,1,8,128,1024]{4,3,2,1,0:T(8,128)(2,1)S(1)}, bf16[1,1,8,128,1024]{4,3,2,1,0:T(8,128)(2,1)}, u32[]{:S(2)}) %copy-start) | copy-done | bytes 2097176
  3.7 1.8 %leave.1 = (bf16[128,1024]{1,0:T(8,128)(2,1)}, bf16[128,1024]{1,0:T(8,128)(2,1)}, bf16[128,1024]{1,0:T(8,128)(2,1)S(1)}) custom-call(s32[8,2]{1,0:T(8,128)S(1)} %copy.18.moves, s32[8,4]{1,0:T(8,128)S(1)} %copy.14.table, bf16[8,128,1024]{2,1,0:T(8,128)(2,1)S(1)} %bitcast.3), custom_call_target="tpu_custom_call" | custom-call | tf_op jit(solution)/shard_map/leave/pallas_call | solution.py:381
  5.6 0.5 collective-permute-start.3
  6.1 2.6 %collective-permute-start.4 = (bf16[128,1024]{1,0:T(8,128)(2,1)}, bf16[128,1024]{1,0:T(8,128)(2,1)S(1)}, u32[]{:S(2)}, u32[]{:S(2)}) collective-permute-start(bf16[128,1024]{1,0:T(8,128)(2,1)} %get-tuple-element.31), channel_id=1, source_target_pairs={{0,8},{4,12},{8,0},{12,4},{1,9},{5,13},{9,1},{13,5},{2,10},{6,14},... | collective-permute-start | bytes 786440 | tf_op jit(solution)/shard_map/ppermute | solution.py:28
  8.6 1.4 %collective-permute-start.5 = (bf16[128,1024]{1,0:T(8,128)(2,1)S(1)}, bf16[128,1024]{1,0:T(8,128)(2,1)S(1)}, u32[]{:S(2)}, u32[]{:S(2)}) collective-permute-start(bf16[128,1024]{1,0:T(8,128)(2,1)S(1)} %get-tuple-element.32), channel_id=1, source_target_pairs={{0,12},{4,0},{8,4},{12,8},{1,13},{5,1},{9,5},{13,9},{2,14},{6,2},{... | collective-permute-start | bytes 786440 | tf_op jit(solution)/shard_map/ppermute | solution.py:28
  10.0 2.2 %copy-done.2 = bf16[2048,1024]{1,0:T(8,128)(2,1)S(1)} copy-done((bf16[2048,1024]{1,0:T(8,128)(2,1)S(1)}, bf16[2048,1024]{1,0:T(8,128)(2,1)}, u32[]{:S(2)}) %copy-start.2) | copy-done | bytes 4194328
  12.2 1.1 %project.1 = (bf16[192,128]{1,0:T(8,128)(2,1)S(1)}, bf16[192,128]{1,0:T(8,128)(2,1)S(1)}, bf16[192,128]{1,0:T(8,128)(2,1)S(1)}, bf16[192,128]{1,0:T(8,128)(2,1)S(1)}) custom-call(bf16[16,2048]{1,0:T(8,128)(2,1)S(1)} %bitcast.6, bf16[2048,1024]{1,0:T(8,128)(2,1)S(1)} %copy-done.2, bf16[2,8,1024]{2,1,0:T(8,128)(2,1)S(1)} %copy-done.4), custom_call_target="tpu_custom_call" | custom-call | tf_op jit(solution)/shard_map/project/pallas_call | solution.py:394
  13.3 1.6 %collective-permute-start = (bf16[192,128]{1,0:T(8,128)(2,1)S(1)}, bf16[192,128]{1,0:T(8,128)(2,1)S(1)}, u32[]{:S(2)}, u32[]{:S(2)}) collective-permute-start(bf16[192,128]{1,0:T(8,128)(2,1)S(1)} %get-tuple-element.26), channel_id=1, source_target_pairs={{0,1},{1,2},{2,3},{3,0},{4,5},{5,6},{6,7},{7,4},{8,9},{9,10},{10,1... | collective-permute-start | bytes 147464 | tf_op jit(solution)/shard_map/ppermute | solution.py:28
  15.0 2.6 %collective-permute-start.1 = (bf16[192,128]{1,0:T(8,128)(2,1)S(1)}, bf16[192,128]{1,0:T(8,128)(2,1)S(1)}, u32[]{:S(2)}, u32[]{:S(2)}) collective-permute-start(bf16[192,128]{1,0:T(8,128)(2,1)S(1)} %get-tuple-element.27), channel_id=1, source_target_pairs={{0,2},{1,3},{2,0},{3,1},{4,6},{5,7},{6,4},{7,5},{8,10},{9,11},{10,... | collective-permute-start | bytes 147464 | tf_op jit(solution)/shard_map/ppermute | solution.py:28
  17.5 1.8 %collective-permute-done.refs_1_.refs_7_ = bf16[192,128]{1,0:T(8,128)(2,1)S(1)} collective-permute-done((bf16[192,128]{1,0:T(8,128)(2,1)S(1)}, bf16[192,128]{1,0:T(8,128)(2,1)S(1)}, u32[]{:S(2)}, u32[]{:S(2)}) %collective-permute-start) | collective-permute-done | bytes 49184 | tf_op jit(solution)/shard_map/ppermute | solution.py:28
  19.4 1.7 %collective-permute-start.2 = (bf16[192,128]{1,0:T(8,128)(2,1)S(1)}, bf16[192,128]{1,0:T(8,128)(2,1)S(1)}, u32[]{:S(2)}, u32[]{:S(2)}) collective-permute-start(bf16[192,128]{1,0:T(8,128)(2,1)S(1)} %get-tuple-element.28), channel_id=1, source_target_pairs={{0,3},{1,0},{2,1},{3,2},{4,7},{5,4},{6,5},{7,6},{8,11},{9,8},{10,9... | collective-permute-start | bytes 147464 | tf_op jit(solution)/shard_map/ppermute | solution.py:28
  21.1 0.0 collective-permute-done.1.refs_2_.refs_8_
  21.1 2.4 %collective-permute-done.2.refs_3_.refs_9_ = bf16[192,128]{1,0:T(8,128)(2,1)S(1)} collective-permute-done((bf16[192,128]{1,0:T(8,128)(2,1)S(1)}, bf16[192,128]{1,0:T(8,128)(2,1)S(1)}, u32[]{:S(2)}, u32[]{:S(2)}) %collective-permute-start.2) | collective-permute-done | bytes 49184 | tf_op jit(solution)/shard_map/ppermute | solution.py:28
  23.4 1.1 %token_.1 = (f32[2,16,128]{2,1,0:T(8,128)S(1)}, f32[8,128]{1,0:T(8,128)S(1)}, f32[8,128]{1,0:T(8,128)S(1)}, f32[8,128]{1,0:T(8,128)S(1)}) custom-call(s32[8,2]{1,0:T(8,128)S(1)} %copy.18.moves, s32[8]{0:T(128)S(1)} %copy-done.5, bf16[192,128]{1,0:T(8,128)(2,1)S(1)} %get-tuple-element.25.refs_0_.refs_6_.q, ...), custom_call_target="tpu_custom_call" | custom-call | tf_op jit(solution)/shard_map/token/pallas_call | solution.py:410
  24.5 0.1 collective-permute-start.6
  24.6 0.4 collective-permute-start.7
  25.0 2.6 %collective-permute-done.6.refs_3_ = f32[8,128]{1,0:T(8,128)S(1)} collective-permute-done((f32[8,128]{1,0:T(8,128)S(1)}, f32[8,128]{1,0:T(8,128)S(1)}, u32[]{:S(2)}, u32[]{:S(2)}) %collective-permute-start.6) | collective-permute-done | bytes 4128 | tf_op jit(solution)/shard_map/ppermute | solution.py:28
  27.6 0.0 collective-permute-start.8
  27.6 0.1 copy.19.table
  27.7 7.9 %attend.1 = (f32[4,128,128]{2,1,0:T(8,128)S(1)}, f32[4,16,128]{2,1,0:T(8,128)S(1)}, bf16[8,128,1024]{2,1,0:T(8,128)(2,1)}) custom-call(s32[8,4]{1,0:T(8,128)S(1)} %copy.14.table, s32[8]{0:T(128)S(1)} %copy-done.5, bf16[8,128,1024]{2,1,0:T(8,128)(2,1)S(1)} %bitcast.4, bf16[192,128]{1,0:T(8,128)(2,1)S(1)} %get-tuple-element.25.refs_0_.refs_6_.q, ...), custom_call_target="tpu_custom_call" | custom-call | tf_op jit(solution)/shard_map/attend/pallas_call | solution.py:420
  35.5 0.0 collective-permute-done.7.refs_4_
  35.6 0.0 collective-permute-done.3.refs_0_
  35.6 2.9 %arrive.1 = (bf16[192,128]{1,0:T(8,128)(2,1)S(1)}, bf16[192,128]{1,0:T(8,128)(2,1)S(1)}, bf16[192,128]{1,0:T(8,128)(2,1)S(1)}, f32[128,128]{1,0:T(8,128)S(1)}, f32[16,128]{1,0:T(8,128)S(1)}) custom-call(s32[8,2]{1,0:T(8,128)S(1)} %copy.18.moves, s32[8,4]{1,0:T(8,128)S(1)} %copy.19.table, f32[2,16,128]{2,1,0:T(8,128)S(1)} %get-tuple-element.29.kv, ...), custom_call_target="tpu_custom_call" | custom-call | tf_op jit(solution)/shard_map/arrive/pallas_call | solution.py:440
  38.5 0.1 collective-permute-start.9
  38.6 4.1 %collective-permute-start.10 = (bf16[192,128]{1,0:T(8,128)(2,1)S(1)}, bf16[192,128]{1,0:T(8,128)(2,1)S(1)}, u32[]{:S(2)}, u32[]{:S(2)}) collective-permute-start(bf16[192,128]{1,0:T(8,128)(2,1)S(1)} %get-tuple-element.41), channel_id=1, source_target_pairs={{0,2},{1,3},{2,0},{3,1},{4,6},{5,7},{6,4},{7,5},{8,10},{9,11},{10,... | collective-permute-start | bytes 147464 | tf_op jit(solution)/shard_map/ppermute | solution.py:28
  42.6 0.1 collective-permute-start.11
  42.7 2.3 %collective-permute-done.9.refs_6_ = bf16[192,128]{1,0:T(8,128)(2,1)S(1)} collective-permute-done((bf16[192,128]{1,0:T(8,128)(2,1)S(1)}, bf16[192,128]{1,0:T(8,128)(2,1)S(1)}, u32[]{:S(2)}, u32[]{:S(2)}) %collective-permute-start.9) | collective-permute-done | bytes 49184 | tf_op jit(solution)/shard_map/ppermute | solution.py:28
  45.0 1.7 %collective-permute-done.10.refs_7_ = bf16[192,128]{1,0:T(8,128)(2,1)S(1)} collective-permute-done((bf16[192,128]{1,0:T(8,128)(2,1)S(1)}, bf16[192,128]{1,0:T(8,128)(2,1)S(1)}, u32[]{:S(2)}, u32[]{:S(2)}) %collective-permute-start.10) | collective-permute-done | bytes 49184 | tf_op jit(solution)/shard_map/ppermute | solution.py:28
  46.7 0.5 collective-permute-done.11.refs_8_
  47.2 3.9 %finish.1 = (bf16[8,1024]{1,0:T(8,128)(2,1)}, bf16[8,1024]{1,0:T(8,128)(2,1)}, bf16[8,128,1024]{2,1,0:T(8,128)(2,1)}) custom-call(s32[8,2]{1,0:T(8,128)S(1)} %copy.18.moves, s32[8,4]{1,0:T(8,128)S(1)} %copy.19.table, s32[8]{0:T(128)S(1)} %copy-done.5, f32[2,16,128]{2,1,0:T(8,128)S(1)} %get-tuple-element.29.kv, ...), custom_call_target="tpu_custom_call", output_to_operand_aliasing={{2}: (17, {})} | custom-call | tf_op jit(solution)/shard_map/finish/pallas_call | solution.py:462
  (15 shorter events, 0.0 us)
Async XLA Ops:
  2.1 1.6 %copy-start = (bf16[1,1,8,128,1024]{4,3,2,1,0:T(8,128)(2,1)S(1)}, bf16[1,1,8,128,1024]{4,3,2,1,0:T(8,128)(2,1)}, u32[]{:S(2)}) copy-start(bf16[1,1,8,128,1024]{4,3,2,1,0:T(8,128)(2,1)} %param.11) | copy-start | bytes 6291460
  3.7 6.3 %copy-start.3 = (bf16[2,8,2048]{2,1,0:T(8,128)(2,1)S(1)}, bf16[2,8,2048]{2,1,0:T(8,128)(2,1)}, u32[]{:S(2)}) copy-start(bf16[2,8,2048]{2,1,0:T(8,128)(2,1)} %param.8) | copy-start | bytes 196612
  3.7 6.3 %copy-start.4 = (bf16[2,8,1024]{2,1,0:T(8,128)(2,1)S(1)}, bf16[2,8,1024]{2,1,0:T(8,128)(2,1)}, u32[]{:S(2)}) copy-start(bf16[2,8,1024]{2,1,0:T(8,128)(2,1)} %q.1) | copy-start | bytes 98308
  5.6 30.0 %collective-permute-start.3 = (bf16[128,1024]{1,0:T(8,128)(2,1)}, bf16[128,1024]{1,0:T(8,128)(2,1)S(1)}, u32[]{:S(2)}, u32[]{:S(2)}) collective-permute-start(bf16[128,1024]{1,0:T(8,128)(2,1)} %get-tuple-element.30), channel_id=1, source_target_pairs={{0,4},{4,8},{8,12},{12,0},{1,5},{5,9},{9,13},{13,1},{2,6},{6,10},{... | collective-permute-start | bytes 786440 | tf_op jit(solution)/shard_map/ppermute | solution.py:28
  6.1 29.5 %collective-permute-start.4 = (bf16[128,1024]{1,0:T(8,128)(2,1)}, bf16[128,1024]{1,0:T(8,128)(2,1)S(1)}, u32[]{:S(2)}, u32[]{:S(2)}) collective-permute-start(bf16[128,1024]{1,0:T(8,128)(2,1)} %get-tuple-element.31), channel_id=1, source_target_pairs={{0,8},{4,12},{8,0},{12,4},{1,9},{5,13},{9,1},{13,5},{2,10},{6,14},... | collective-permute-start | bytes 786440 | tf_op jit(solution)/shard_map/ppermute | solution.py:28
  8.6 27.0 %collective-permute-start.5 = (bf16[128,1024]{1,0:T(8,128)(2,1)S(1)}, bf16[128,1024]{1,0:T(8,128)(2,1)S(1)}, u32[]{:S(2)}, u32[]{:S(2)}) collective-permute-start(bf16[128,1024]{1,0:T(8,128)(2,1)S(1)} %get-tuple-element.32), channel_id=1, source_target_pairs={{0,12},{4,0},{8,4},{12,8},{1,13},{5,1},{9,5},{13,9},{2,14},{6,2},{... | collective-permute-start | bytes 786440 | tf_op jit(solution)/shard_map/ppermute | solution.py:28
  10.0 2.2 %copy-start.2 = (bf16[2048,1024]{1,0:T(8,128)(2,1)S(1)}, bf16[2048,1024]{1,0:T(8,128)(2,1)}, u32[]{:S(2)}) copy-start(bf16[2048,1024]{1,0:T(8,128)(2,1)} %weight.1) | copy-start | bytes 12582916
  12.2 11.2 %copy-start.5 = (s32[8]{0:T(128)S(1)}, s32[8]{0:T(128)}, u32[]{:S(2)}) copy-start(s32[8]{0:T(128)} %lengths.5) | copy-start | bytes 100
  12.2 15.4 %copy-start.6 = (s32[8,4]{0,1:T(4,128)S(1)}, s32[8,4]{0,1:T(4,128)}, u32[]{:S(2)}) copy-start(s32[8,4]{0,1:T(4,128)} %param.14) | copy-start | bytes 388
  12.2 15.5 %copy-start.1 = (bf16[1,1,8,128,1024]{4,3,2,1,0:T(8,128)(2,1)S(1)}, bf16[1,1,8,128,1024]{4,3,2,1,0:T(8,128)(2,1)}, u32[]{:S(2)}) copy-start(bf16[1,1,8,128,1024]{4,3,2,1,0:T(8,128)(2,1)} %param.11) | copy-start | bytes 6291460
  13.3 6.0 %collective-permute-start = (bf16[192,128]{1,0:T(8,128)(2,1)S(1)}, bf16[192,128]{1,0:T(8,128)(2,1)S(1)}, u32[]{:S(2)}, u32[]{:S(2)}) collective-permute-start(bf16[192,128]{1,0:T(8,128)(2,1)S(1)} %get-tuple-element.26), channel_id=1, source_target_pairs={{0,1},{1,2},{2,3},{3,0},{4,5},{5,6},{6,7},{7,4},{8,9},{9,10},{10,1... | collective-permute-start | bytes 147464 | tf_op jit(solution)/shard_map/ppermute | solution.py:28
  15.0 6.1 %collective-permute-start.1 = (bf16[192,128]{1,0:T(8,128)(2,1)S(1)}, bf16[192,128]{1,0:T(8,128)(2,1)S(1)}, u32[]{:S(2)}, u32[]{:S(2)}) collective-permute-start(bf16[192,128]{1,0:T(8,128)(2,1)S(1)} %get-tuple-element.27), channel_id=1, source_target_pairs={{0,2},{1,3},{2,0},{3,1},{4,6},{5,7},{6,4},{7,5},{8,10},{9,11},{10,... | collective-permute-start | bytes 147464 | tf_op jit(solution)/shard_map/ppermute | solution.py:28
  19.4 4.1 %collective-permute-start.2 = (bf16[192,128]{1,0:T(8,128)(2,1)S(1)}, bf16[192,128]{1,0:T(8,128)(2,1)S(1)}, u32[]{:S(2)}, u32[]{:S(2)}) collective-permute-start(bf16[192,128]{1,0:T(8,128)(2,1)S(1)} %get-tuple-element.28), channel_id=1, source_target_pairs={{0,3},{1,0},{2,1},{3,2},{4,7},{5,4},{6,5},{7,6},{8,11},{9,8},{10,9... | collective-permute-start | bytes 147464 | tf_op jit(solution)/shard_map/ppermute | solution.py:28
  24.5 3.1 %collective-permute-start.6 = (f32[8,128]{1,0:T(8,128)S(1)}, f32[8,128]{1,0:T(8,128)S(1)}, u32[]{:S(2)}, u32[]{:S(2)}) collective-permute-start(f32[8,128]{1,0:T(8,128)S(1)} %get-tuple-element.33), channel_id=1, source_target_pairs={{0,4},{4,8},{8,12},{12,0},{1,5},{5,9},{9,13},{13,1},{2,6},{6,10},{... | collective-permute-start | bytes 12296 | tf_op jit(solution)/shard_map/ppermute | solution.py:28
  24.6 11.0 %collective-permute-start.7 = (f32[8,128]{1,0:T(8,128)S(1)}, f32[8,128]{1,0:T(8,128)S(1)}, u32[]{:S(2)}, u32[]{:S(2)}) collective-permute-start(f32[8,128]{1,0:T(8,128)S(1)} %get-tuple-element.34), channel_id=1, source_target_pairs={{0,8},{4,12},{8,0},{12,4},{1,9},{5,13},{9,1},{13,5},{2,10},{6,14},... | collective-permute-start | bytes 12296 | tf_op jit(solution)/shard_map/ppermute | solution.py:28
  27.6 8.0 %collective-permute-start.8 = (f32[8,128]{1,0:T(8,128)S(1)}, f32[8,128]{1,0:T(8,128)S(1)}, u32[]{:S(2)}, u32[]{:S(2)}) collective-permute-start(f32[8,128]{1,0:T(8,128)S(1)} %get-tuple-element.35), channel_id=1, source_target_pairs={{0,12},{4,0},{8,4},{12,8},{1,13},{5,1},{9,5},{13,9},{2,14},{6,2},{... | collective-permute-start | bytes 12296 | tf_op jit(solution)/shard_map/ppermute | solution.py:28
  38.5 6.5 %collective-permute-start.9 = (bf16[192,128]{1,0:T(8,128)(2,1)S(1)}, bf16[192,128]{1,0:T(8,128)(2,1)S(1)}, u32[]{:S(2)}, u32[]{:S(2)}) collective-permute-start(bf16[192,128]{1,0:T(8,128)(2,1)S(1)} %get-tuple-element.40), channel_id=1, source_target_pairs={{0,1},{1,2},{2,3},{3,0},{4,5},{5,6},{6,7},{7,4},{8,9},{9,10},{10,1... | collective-permute-start | bytes 147464 | tf_op jit(solution)/shard_map/ppermute | solution.py:28
  38.6 8.1 %collective-permute-start.10 = (bf16[192,128]{1,0:T(8,128)(2,1)S(1)}, bf16[192,128]{1,0:T(8,128)(2,1)S(1)}, u32[]{:S(2)}, u32[]{:S(2)}) collective-permute-start(bf16[192,128]{1,0:T(8,128)(2,1)S(1)} %get-tuple-element.41), channel_id=1, source_target_pairs={{0,2},{1,3},{2,0},{3,1},{4,6},{5,7},{6,4},{7,5},{8,10},{9,11},{10,... | collective-permute-start | bytes 147464 | tf_op jit(solution)/shard_map/ppermute | solution.py:28
  42.6 4.5 %collective-permute-start.11 = (bf16[192,128]{1,0:T(8,128)(2,1)S(1)}, bf16[192,128]{1,0:T(8,128)(2,1)S(1)}, u32[]{:S(2)}, u32[]{:S(2)}) collective-permute-start(bf16[192,128]{1,0:T(8,128)(2,1)S(1)} %get-tuple-element.42), channel_id=1, source_target_pairs={{0,3},{1,0},{2,1},{3,2},{4,7},{5,4},{6,5},{7,6},{8,11},{9,8},{10,9... | collective-permute-start | bytes 147464 | tf_op jit(solution)/shard_map/ppermute | solution.py:28

commit v2 on v1

v2 whole, which is shorter than its diff:
```python
import functools
import math

import jax
import jax.numpy as jnp
from jax import lax
from jax.experimental import pallas as pl
from jax.experimental.pallas import tpu as pltpu
from jax.sharding import PartitionSpec as P

H = 32
KVH = 4
HD = 128
GROUP = H // KVH
CAP = 20.0
SCALE = 1.0 / math.sqrt(HD)
WINDOW = 32
KV_ROWS = 24

SMEM = pl.BlockSpec(memory_space=pltpu.SMEM)
VMEM = pl.BlockSpec(memory_space=pltpu.VMEM)
ANY = pl.BlockSpec(memory_space=pl.ANY)
HBM = pl.BlockSpec(memory_space=pltpu.HBM)
SEND = jnp.bfloat16


def swap(value, axis, distance):
    size = lax.axis_size(axis)
    return lax.ppermute(value, axis, [(i, i ^ distance) for i in range(size)])


def exchange(messages, axis):
    return [swap(message, axis, d + 1) for d, message in enumerate(messages)]


def partner(axis, distance):
    return lax.axis_index(axis) ^ distance


def split(value, size):
    if size & (size - 1) == 0:
        return lax.shift_right_logical(value, size.bit_length() - 1), value & (size - 1)
    return lax.div(value, size), lax.rem(value, size)


def count_up(limit, step, state):
    if limit > 8:
        return lax.fori_loop(0, limit, step, state)
    for i in range(limit):
        state = step(i, state)
    return state


def locate(table, row, column, slots):
    def step(p, found):
        device, slot = split(table[p, row], slots)
        here = device == column
        return jnp.where(here, p, found[0]), jnp.where(here, slot, found[1])

    return count_up(table.shape[0], step, (jnp.int32(0), jnp.int32(0)))


def pair_row(moves, source, target, rows, side):
    def step(j, found):
        ends = [split(moves[i, j], rows) for i in range(2)]
        match = (ends[0][0] == source) & (ends[1][0] == target)
        return (
            jnp.where(match, jnp.int32(1), found[0]),
            jnp.where(match, ends[side][1], found[1]),
        )

    return count_up(moves.shape[1], step, (jnp.int32(0), jnp.int32(0)))


def head_columns(device, local_heads):
    return pl.ds(pl.multiple_of(split(device * local_heads, GROUP)[0] * HD, HD), HD)


def weight_of(score):
    return jnp.exp(CAP * jnp.tanh(score * (SCALE / CAP)))


def leave_kernel(rows, moves, table, pool, *refs):
    outs, sems = refs[:-1], refs[-1]
    me, column = lax.axis_index("replica"), lax.axis_index("mp")
    copies = []
    for s, out in enumerate(outs):
        _, row = pair_row(moves, me, partner("replica", s + 1), rows, 0)
        _, slot = locate(table, row, column, pool.shape[0])
        copies.append(pltpu.make_async_copy(pool.at[slot], out, sems.at[s]))
        copies[-1].start()
    for copy in copies:
        copy.wait()


def project_kernel(count, local_heads, x, weight, q, *refs):
    outs, total = refs[:-1], refs[-1]
    step = pl.program_id(0)
    rows = q.shape[1]
    query_rows = 2 * local_heads * rows

    @pl.when(step == 0)
    def _():
        total[...] = jnp.zeros_like(total)
        wide = [q[i].astype(jnp.float32) for i in range(2)]
        blocks = [wide[i][:, h * HD : (h + 1) * HD] for i in range(2) for h in range(local_heads)]
        packed = jnp.concatenate(blocks, axis=0).astype(jnp.bfloat16)
        for out in outs:
            out[:query_rows, :] = packed

    total[...] += jnp.dot(x[...], weight[...], preferred_element_type=jnp.float32)

    @pl.when(step == pl.num_programs(0) - 1)
    def _():
        for s, out in enumerate(outs):
            columns = head_columns(partner("mp", s), local_heads)
            parts = []
            for half in range(2):
                part = total.at[:, pl.ds(half * KVH * HD, KVH * HD)][:, columns]
                high = part.astype(jnp.bfloat16)
                parts += [high, (part - high.astype(jnp.float32)).astype(jnp.bfloat16)]
            out[query_rows:, :] = jnp.concatenate(parts, axis=0)


def token_kernel(count, replicas, rows, moves, lengths, *refs):
    messages, kv, outs = refs[:count], refs[count], refs[count + 1 :]
    tokens = 2 * rows
    base = messages[0].shape[0] - 4 * tokens
    me = lax.axis_index("replica")
    for half in range(2):
        total = jnp.zeros((tokens, HD), jnp.float32)
        for message in messages:
            start = base + 2 * half * tokens
            total += message[start : start + tokens, :].astype(jnp.float32)
            total += message[start + tokens : start + 2 * tokens, :].astype(jnp.float32)
        kv[half] = total.astype(jnp.bfloat16).astype(jnp.float32)
    for s, out in enumerate(outs):
        _, row = pair_row(moves, me, partner("replica", s + 1), rows, 0)
        out[...] = jnp.zeros_like(out)
        out[0:1, :] = kv[0, pl.ds(row, 1), :]
        out[1:2, :] = kv[1, pl.ds(row, 1), :]
        out[2:3, :] = jnp.full((1, HD), lengths[row], jnp.int32).astype(jnp.float32)


def scores_of(q, keys):
    return lax.dot_general(q, keys, (((1,), (1,)), ((), ())), preferred_element_type=jnp.float32)


def attend_kernel(count, local_heads, table, lengths, pool, *refs):
    messages = refs[:count]
    num, den, pool_out, wide, sem = refs[count:]
    column = lax.axis_index("mp")
    rows = lengths.shape[0]
    slots, page_size, width = pool.shape
    both = 2 * local_heads
    store = pltpu.make_async_copy(pool, pool_out, sem)
    store.start()
    for s, message in enumerate(messages):
        wide[s] = message[: both * rows, :].astype(jnp.float32)
    lane = lax.broadcasted_iota(jnp.int32, (both, HD), 1)
    token = lax.broadcasted_iota(jnp.int32, (both, page_size), 1)
    places = [locate(table, r, column, slots) for r in range(rows)]
    columns = [head_columns(partner("mp", s), local_heads) for s in range(count)]
    keys = pool.at[:, :, pl.ds(0, width // 2)]
    values = pool.at[:, :, pl.ds(width // 2, width // 2)]
    cases = [(r, s) for r in range(rows) for s in range(count)]
    scores = {}
    for r, s in cases:
        q = wide[s, pl.ds(r, both, stride=rows), :].astype(jnp.bfloat16)
        scores[r, s] = scores_of(q, keys[places[r][1], :, columns[s]])
    weights = {}
    denominators = [jnp.zeros((both, HD), jnp.float32) for _ in range(count)]
    for r, s in cases:
        inside = token < lengths[r] - places[r][0] * page_size
        weight = jnp.where(inside, weight_of(scores[r, s]), 0.0)
        weights[r, s] = weight.astype(jnp.bfloat16)
        total = jnp.sum(weight, axis=1, keepdims=True)
        denominators[s] += jnp.where(lane == r, total, 0.0)
    for r, s in cases:
        num[s, pl.ds(r, both, stride=rows), :] = jnp.dot(
            weights[r, s], values[places[r][1], :, columns[s]], preferred_element_type=jnp.float32
        )
    for s in range(count):
        den[s] = denominators[s]
    store.wait()


def arrive_kernel(count, replicas, local_heads, slots, moves, table, kv, *refs):
    rows = table.shape[1]
    refs = list(refs)
    take = lambda n: [refs.pop(0) for _ in range(n)]
    pages_in, tokens_in, messages = take(replicas - 1), take(replicas - 1), take(count)
    num_in, den_in = take(2)
    outs = take(count - 1)
    own_num, own_den, num, den, wide = refs
    me, column = lax.axis_index("replica"), lax.axis_index("mp")
    page_size, width = pages_in[0].shape
    half_rows = local_heads * rows
    num[...] = num_in[...]
    den[...] = den_in[...]
    for s, message in enumerate(messages):
        wide[s] = message[half_rows : 2 * half_rows, :].astype(jnp.float32)
    lane = lax.broadcasted_iota(jnp.int32, (local_heads, HD), 1)
    token = lax.broadcasted_iota(jnp.int32, (local_heads, page_size), 1)
    columns = [head_columns(partner("mp", s), local_heads) for s in range(count)]
    cases = [(d, s) for d in range(1, replicas) for s in range(count)]
    arrivals = [pair_row(moves, partner("replica", d), me, rows, 1) for d in range(1, replicas)]
    scores, weights, totals = {}, {}, {}
    for d, s in cases:
        row = arrivals[d - 1][1]
        q = wide[s, pl.ds(row, local_heads, stride=rows), :].astype(jnp.bfloat16)
        scores[d, s] = scores_of(q, pages_in[d - 1].at[:, pl.ds(0, width // 2)][:, columns[s]])
    for d, s in cases:
        index, _ = locate(table, arrivals[d - 1][1], column, slots)
        inside = (token + index * page_size).astype(jnp.float32) < tokens_in[d - 1][2:3, :]
        weight = jnp.where(inside, weight_of(scores[d, s]), 0.0)
        weights[d, s] = weight.astype(jnp.bfloat16)
        totals[d, s] = jnp.sum(weight, axis=1, keepdims=True)
    for d, s in cases:
        values = pages_in[d - 1].at[:, pl.ds(width // 2, width // 2)][:, columns[s]]
        scores[d, s] = jnp.dot(weights[d, s], values, preferred_element_type=jnp.float32)
    for d, (valid, row) in enumerate(arrivals, 1):

        @pl.when(valid == 1)
        def _(d=d, row=row):
            for s in range(count):
                num[s, pl.ds(half_rows + row, local_heads, stride=rows), :] = scores[d, s]
                old = den[s, pl.ds(local_heads, local_heads), :]
                den[s, pl.ds(local_heads, local_heads), :] = jnp.where(lane == row, totals[d, s], old)

    own_num[...] = num[0]
    own_den[...] = den[0]
    filler = jnp.zeros((KV_ROWS - 2 * rows - (replicas - 1), HD), jnp.float32)
    all_kv = []
    for half in range(2):
        all_kv += [kv[half]] + [arrived[half : half + 1, :] for arrived in tokens_in] + [filler]
    all_kv = jnp.concatenate(all_kv, axis=0)
    for s, out in enumerate(outs):
        at = s + 1
        parts = den[at]
        high = parts.astype(SEND).astype(jnp.float32)
        parts = high + pltpu.roll(parts - high, HD // 2, 1)
        out[...] = jnp.concatenate([num[at], parts, all_kv], axis=0).astype(SEND)


def finish_kernel(count, replicas, local_heads, moves, table, lengths, kv, q, num, den, *refs):
    refs = list(refs)
    take = lambda n: [refs.pop(0) for _ in range(n)]
    pages_in, tokens_in, messages = take(replicas - 1), take(replicas - 1), take(count - 1)
    pool_raw, _, first, second, pool = take(5)
    held, full, windows, page_sems, read_sems, write_sems = refs
    me, column = lax.axis_index("replica"), lax.axis_index("mp")
    rows = lengths.shape[0]
    slots, page_size, width = pool_raw.shape
    both = 2 * local_heads

    arrivals, copies, kept, plans = [], [], [jnp.bool_(True)] * rows, []

    def add_plan(active, row, length, first_token, source, r=None):
        index, slot = locate(table, row, column, slots)
        at = length - index * page_size
        touched = active & (at >= -1) & (at < page_size)
        start = jnp.clip(at, 0, page_size - WINDOW) & -16
        span = pl.ds(pl.multiple_of(start, 16), WINDOW)
        n = len(plans)
        source = source.at[slot] if r is not None else source
        read = pltpu.make_async_copy(source.at[span], windows.at[n], read_sems.at[n])
        write = pltpu.make_async_copy(windows.at[n], pool.at[slot, span], write_sems.at[n])
        plans.append((touched, read, write, first_token, rows + row, at - start))
        pl.when(touched)(read.start)
        return slot

    for s, page in enumerate(pages_in):
        valid, row = pair_row(moves, partner("replica", s + 1), me, rows, 1)
        valid = valid == 1
        length = jnp.max(tokens_in[s][2:3, :]).astype(jnp.int32)
        slot = add_plan(valid, row, length, 2 * rows + s, page)
        copies.append(pltpu.make_async_copy(page, pool.at[slot], page_sems.at[s]))
        pl.when(valid)(copies[-1].start)
        arrivals.append((valid, row))
        kept = [stays & ~(valid & (row == r)) for r, stays in enumerate(kept)]
    for r in range(rows):
        add_plan(kept[r], r, lengths[r], r, pool_raw, r)

    for half in range(2):
        held[half] = kv[half, :rows, :]
        for s, (valid, row) in enumerate(arrivals):

            @pl.when(valid)
            def _(half=half, s=s, row=row):
                held[half, pl.ds(row, 1), :] = tokens_in[s][half : half + 1, :]

    query_rows = both * rows
    kv_base = messages[0].shape[0] - 2 * KV_ROWS
    filler = jnp.zeros((KV_ROWS - 2 * rows - (replicas - 1), HD), jnp.float32)
    for s in range(count):
        device = partner("mp", s)
        for half in range(2):
            if s == 0:
                chunk = jnp.concatenate(
                    [kv[half]] + [arrived[half : half + 1, :] for arrived in tokens_in] + [filler],
                    axis=0,
                )
            else:
                start = kv_base + half * KV_ROWS
                chunk = messages[s - 1][start : start + KV_ROWS, :].astype(jnp.float32)

            def place(half=half, device=device, chunk=chunk):
                columns = head_columns(device, local_heads)
                full.at[:, pl.ds(half * (width // 2), width // 2)][:, columns] = chunk

            if local_heads == GROUP:
                place()
            else:
                pl.when(split(device * local_heads, GROUP)[1] == 0)(place)

    sums = den[...]
    for message in messages:
        part = message[query_rows : query_rows + both, :].astype(jnp.float32)
        sums += part + pltpu.roll(part, HD // 2, 1)
    sums = jnp.transpose(sums)[:rows, :]
    for step, out in enumerate((first, second)):
        results = []
        for h in range(local_heads):
            at = (step * local_heads + h) * rows
            query = q[at : at + rows, :].astype(jnp.float32)
            numerator = num[at : at + rows, :]
            for message in messages:
                numerator += message[at : at + rows, :].astype(jnp.float32)
            denominator = sums[:, step * local_heads + h : step * local_heads + h + 1]
            extra = [(kv[0, :rows, :], kv[1, :rows, :])]
            if step == 1:
                extra = [(held[0], held[1]), (kv[0, rows:, :], kv[1, rows:, :])]
            for key, value in extra:
                weight = weight_of(jnp.sum(query * key, axis=1, keepdims=True))
                numerator += weight.astype(jnp.bfloat16).astype(jnp.float32) * value
                denominator += weight
            results.append(numerator / denominator)
        out[...] = jnp.concatenate(results, axis=1).astype(out.dtype)

    for (valid, _), copy in zip(arrivals, copies):
        pl.when(valid)(copy.wait)
    place_ids = lax.broadcasted_iota(jnp.int32, (WINDOW, width), 0)
    for n, (touched, read, write, token, next_token, offset) in enumerate(plans):

        @pl.when(touched)
        def _(n=n, read=read, write=write, token=token, next_token=next_token, offset=offset):
            read.wait()
            old = windows[n].astype(jnp.float32)
            new = jnp.where(place_ids == offset, full[pl.ds(token, 1), :], old)
            new = jnp.where(place_ids == offset + 1, full[pl.ds(next_token, 1), :], new)
            windows[n] = new.astype(jnp.bfloat16)
            write.start()

    for touched, _, write, _, _, _ in plans:
        pl.when(touched)(write.wait)


def params(megabytes=32, **rest):
    return pltpu.CompilerParams(vmem_limit_bytes=megabytes << 20, **rest)


def body(layer_input, kv_weight, queries, kv_pool, lengths, block_table, new_table, migrations):
    replicas, count = lax.axis_size("replica"), lax.axis_size("mp")
    rows = lengths.shape[0]
    pool = kv_pool[0, 0]
    slots, page_size, width = pool.shape
    local_heads = queries.shape[2] // HD
    both = 2 * local_heads
    query_rows = both * rows
    depth = layer_input.shape[2]
    f32, bf16 = jnp.float32, jnp.bfloat16
    moves, old_table, table_after = migrations.T, block_table.T, new_table.T
    shape = jax.ShapeDtypeStruct

    leaving = pl.pallas_call(
        functools.partial(leave_kernel, rows),
        out_shape=[shape((page_size, width), bf16)] * (replicas - 1),
        in_specs=[SMEM, SMEM, HBM],
        out_specs=[ANY] * (replicas - 1),
        scratch_shapes=[pltpu.SemaphoreType.DMA((replicas - 1,))],
        compiler_params=params(),
        name="leave",
    )(moves, old_table, pool)
    pages_in = exchange(leaving, "replica")

    block = math.gcd(depth, 512)
    message_rows = query_rows + 8 * rows
    sent = pl.pallas_call(
        functools.partial(project_kernel, count, local_heads),
        grid=(depth // block,),
        out_shape=[shape((message_rows, HD), bf16)] * count,
        in_specs=[
            pl.BlockSpec((2 * rows, block), lambda k: (0, k)),
            pl.BlockSpec((block, width), lambda k: (k, 0), memory_space=pltpu.VMEM),
            pl.BlockSpec(queries.shape, lambda k: (0, 0, 0)),
        ],
        out_specs=[pl.BlockSpec((message_rows, HD), lambda k: (0, 0))] * count,
        scratch_shapes=[pltpu.VMEM((2 * rows, width), f32)],
        compiler_params=params(),
        name="project",
    )(layer_input.reshape(2 * rows, depth), kv_weight, queries)
    sent, pages_in[0] = lax.optimization_barrier((sent, pages_in[0]))
    messages = [sent[0]] + exchange(sent[1:], "mp")

    kv, *tokens = pl.pallas_call(
        functools.partial(token_kernel, count, replicas, rows),
        out_shape=[shape((2, 2 * rows, HD), f32)] + [shape((8, HD), f32)] * (replicas - 1),
        in_specs=[SMEM, SMEM] + [VMEM] * count,
        out_specs=[VMEM] * replicas,
        compiler_params=params(),
        name="token",
    )(moves, lengths, *messages)
    tokens_in = exchange(tokens, "replica")

    num, den, pool_copy = pl.pallas_call(
        functools.partial(attend_kernel, count, local_heads),
        out_shape=[
            shape((count, query_rows, HD), f32),
            shape((count, both, HD), f32),
            shape(pool.shape, bf16),
        ],
        in_specs=[SMEM, SMEM, VMEM] + [VMEM] * count,
        out_specs=[VMEM, VMEM, ANY],
        scratch_shapes=[
            pltpu.VMEM((count, query_rows, HD), f32),
            pltpu.SemaphoreType.DMA(()),
        ],
        compiler_params=params(),
        name="attend",
    )(old_table, lengths, pool, *messages)

    sum_rows = query_rows + both + 2 * KV_ROWS
    *sums, num, den = pl.pallas_call(
        functools.partial(arrive_kernel, count, replicas, local_heads, slots),
        out_shape=[shape((sum_rows, HD), SEND)] * (count - 1)
        + [shape((query_rows, HD), f32), shape((both, HD), f32)],
        in_specs=[SMEM, SMEM, VMEM]
        + [VMEM] * (replicas - 1)
        + [VMEM] * (replicas - 1)
        + [VMEM] * count
        + [VMEM] * 2,
        out_specs=[VMEM] * (count + 1),
        scratch_shapes=[
            pltpu.VMEM((count, query_rows, HD), f32),
            pltpu.VMEM((count, both, HD), f32),
            pltpu.VMEM((count, query_rows // 2, HD), f32),
        ],
        compiler_params=params(),
        name="arrive",
    )(moves, table_after, kv, *pages_in, *tokens_in, *messages, num, den)
    sums_in = exchange(sums, "mp")

    first, second, pool_after = pl.pallas_call(
        functools.partial(finish_kernel, count, replicas, local_heads),
        out_shape=[
            shape((rows, local_heads * HD), bf16),
            shape((rows, local_heads * HD), bf16),
            shape(pool.shape, bf16),
        ],
        in_specs=[SMEM, SMEM, SMEM]
        + [VMEM] * 4
        + [ANY] * (replicas - 1)
        + [VMEM] * (replicas - 1)
        + [VMEM] * (count - 1)
        + [ANY, ANY],
        out_specs=[VMEM, VMEM, ANY],
        scratch_shapes=[
            pltpu.VMEM((2, rows, HD), f32),
            pltpu.VMEM((KV_ROWS, width), f32),
            pltpu.VMEM((rows + replicas - 1, WINDOW, width), bf16),
            pltpu.SemaphoreType.DMA((replicas - 1,)),
            pltpu.SemaphoreType.DMA((rows + replicas - 1,)),
            pltpu.SemaphoreType.DMA((rows + replicas - 1,)),
        ],
        input_output_aliases={7 + 2 * (replicas - 1) + (count - 1) + 1: 2},
        compiler_params=params(),
        name="finish",
    )(moves, table_after, lengths, kv, messages[0], num, den, *pages_in, *tokens_in, *sums_in, pool, pool_copy)
    return first, second, pool_after[None, None]


def solution(mesh):
    return jax.shard_map(
        body,
        mesh=mesh,
        in_specs=(
            P(None, ("groups", "replica"), "mp"),
            P("mp", None),
            P(None, ("groups", "replica"), "mp"),
            P(("groups", "replica"), "mp", None, None, None),
            P(("groups", "replica")),
            P(("groups", "replica"), None),
            P(("groups", "replica"), None),
            P("groups", None),
        ),
        out_specs=(
            P(("groups", "replica"), "mp"),
            P(("groups", "replica"), "mp"),
            P(("groups", "replica"), "mp", None, None, None),
        ),
        check_vma=False,
    )
```

time: 51.7 us -> 39.2 us (0.76)
  Pallas kernels: 18.6 us -> 9.89 us
  waiting for transfers between devices: 11.2 us -> 9.27 us
  starting transfers between devices: 15.1 us -> 14 us
    pallas_call x1, Pallas kernels: 7.86 us -> 2.7 us  [body(): pl.pallas_call(functools.partial(attend_kernel, count, local_heads), out_...]
    ppermute x12, waiting for transfers between devices: 11.2 us -> 9.27 us  [swap(): return lax.ppermute(value, axis, [(i, i ^ distance) for i in range(size)])]
    pallas_call x1, Pallas kernels: 2.9 us -> 1.15 us  [body(): pl.pallas_call(functools.partial(arrive_kernel, count, replicas, local_he...]
    ppermute x12, starting transfers between devices: 15.1 us -> 14 us  [swap(): return lax.ppermute(value, axis, [(i, i ^ distance) for i in range(size)])]
    pallas_call x1, Pallas kernels: 1.81 us -> 0.76 us  [body(): pl.pallas_call(functools.partial(leave_kernel, rows), out_shape=[shape((p...]
    unnamed x17 -> x22, local copies, waits for them, and re-layouts: 5.39 us -> 5.16 us
  transfers between devices with their start and end apart: 12 -> 12, of which waited for: 6 -> 5; matrix products, arithmetic and copies ran while one was open for 0% -> 0% of each run, Pallas kernels for 20% -> 11%
where the time goes in v2:
time: 39.2 us; the launch traced here: 39 us
  starting transfers between devices  14 us (36%)
  Pallas kernels  9.89 us (25%)
  waiting for transfers between devices  9.27 us (24%)
  local copies, waits for them, and re-layouts  5.16 us (13%)
  between operations  0.77 us (2%)
    ppermute x12, starting transfers between devices, swap(): return lax.ppermute(value, axis, [(i, i ^ distance) for i in range(size)])  14 us
    ppermute x12, waiting for transfers between devices, swap(): return lax.ppermute(value, axis, [(i, i ^ distance) for i in range(size)])  9.27 us
    unnamed x22, local copies, waits for them, and re-layouts  5.16 us
    pallas_call x1, Pallas kernels, body(): pl.pallas_call(functools.partial(finish_kernel, count, replicas, local_he...  3.57 us
    pallas_call x1, Pallas kernels, body(): pl.pallas_call(functools.partial(attend_kernel, count, local_heads), out_...  2.7 us
    pallas_call x1, Pallas kernels, body(): pl.pallas_call(functools.partial(arrive_kernel, count, replicas, local_he...  1.15 us
    pallas_call x1, Pallas kernels, body(): pl.pallas_call(functools.partial(project_kernel, count, local_heads), gri...  1.1 us
  transfers between devices with their start and end apart: 12, of which 5 were waited for; matrix products, arithmetic and copies ran while one was open for 0% of the time, Pallas kernels for 11%

profile of v2, /device:TPU:0, one launch (start us, length us, event | category | flops | bytes accessed | tf_op | source)
XLA Modules:
  0.0 39.0 jit_solution(4734763835164809219)
XLA Ops:
  0.6 0.0 copy-start
  0.6 1.6 %copy-done = bf16[1,1,8,128,1024]{4,3,2,1,0:T(8,128)(2,1)S(1)} copy-done((bf16[1,1,8,128,1024]{4,3,2,1,0:T(8,128)(2,1)S(1)}, bf16[1,1,8,128,1024]{4,3,2,1,0:T(8,128)(2,1)}, u32[]{:S(2)}) %copy-start) | copy-done | bytes 2097176
  2.2 0.7 %copy-done.5 = s32[8,2]{0,1:T(2,128)S(1)} copy-done((s32[8,2]{0,1:T(2,128)S(1)}, s32[8,2]{0,1:T(2,128)}, u32[]{:S(2)}) %copy-start.5) | copy-done | bytes 88
  2.9 0.7 %copy-done.8 = s32[8,4]{0,1:T(4,128)S(1)} copy-done((s32[8,4]{0,1:T(4,128)S(1)}, s32[8,4]{0,1:T(4,128)}, u32[]{:S(2)}) %copy-start.8) | copy-done | bytes 152
  3.6 0.8 %leave.1 = (bf16[128,1024]{1,0:T(8,128)(2,1)S(1)}, bf16[128,1024]{1,0:T(8,128)(2,1)S(1)}, bf16[128,1024]{1,0:T(8,128)(2,1)S(1)}) custom-call(s32[2,8]{1,0:T(2,128)S(1)} %bitcast.10, s32[4,8]{1,0:T(4,128)S(1)} %bitcast.16, bf16[8,128,1024]{2,1,0:T(8,128)(2,1)S(1)} %bitcast.6), custom_call_target="tpu_custom_call" | custom-call | tf_op jit(solution)/shard_map/leave/pallas_call | solution.py:376
  4.4 0.5 %collective-permute-start = (bf16[128,1024]{1,0:T(8,128)(2,1)S(1)}, bf16[128,1024]{1,0:T(8,128)(2,1)S(1)}, u32[]{:S(2)}, u32[]{:S(2)}) collective-permute-start(bf16[128,1024]{1,0:T(8,128)(2,1)S(1)} %get-tuple-element.34), channel_id=1, source_target_pairs={{0,4},{4,0},{8,12},{12,8},{1,5},{5,1},{9,13},{13,9},{2,6},{6,2},{1... | collective-permute-start | bytes 786440 | tf_op jit(solution)/shard_map/ppermute | solution.py:29
  4.9 2.6 %collective-permute-start.4 = (bf16[128,1024]{1,0:T(8,128)(2,1)S(1)}, bf16[128,1024]{1,0:T(8,128)(2,1)S(1)}, u32[]{:S(2)}, u32[]{:S(2)}) collective-permute-start(bf16[128,1024]{1,0:T(8,128)(2,1)S(1)} %get-tuple-element.41), channel_id=1, source_target_pairs={{0,8},{4,12},{8,0},{12,4},{1,9},{5,13},{9,1},{13,5},{2,10},{6,14},... | collective-permute-start | bytes 786440 | tf_op jit(solution)/shard_map/ppermute | solution.py:29
  7.4 0.1 collective-permute-start.5
  7.5 2.2 %copy-done.2 = bf16[2048,1024]{1,0:T(8,128)(2,1)S(1)} copy-done((bf16[2048,1024]{1,0:T(8,128)(2,1)S(1)}, bf16[2048,1024]{1,0:T(8,128)(2,1)}, u32[]{:S(2)}) %copy-start.2) | copy-done | bytes 4194328
  9.7 1.1 %project.1 = (bf16[192,128]{1,0:T(8,128)(2,1)S(1)}, bf16[192,128]{1,0:T(8,128)(2,1)S(1)}, bf16[192,128]{1,0:T(8,128)(2,1)S(1)}, bf16[192,128]{1,0:T(8,128)(2,1)S(1)}) custom-call(bf16[16,2048]{1,0:T(8,128)(2,1)S(1)} %bitcast.9, bf16[2048,1024]{1,0:T(8,128)(2,1)S(1)} %copy-done.2, bf16[2,8,1024]{2,1,0:T(8,128)(2,1)S(1)} %copy-done.4), custom_call_target="tpu_custom_call" | custom-call | tf_op jit(solution)/shard_map/project/pallas_call | solution.py:389
  10.8 0.0 copy-start.7
  10.8 0.0 collective-permute-done.refs_0_
  10.9 1.9 %collective-permute-start.1 = (bf16[192,128]{1,0:T(8,128)(2,1)S(1)}, bf16[192,128]{1,0:T(8,128)(2,1)S(1)}, u32[]{:S(2)}, u32[]{:S(2)}) collective-permute-start(bf16[192,128]{1,0:T(8,128)(2,1)S(1)} %get-tuple-element.36), channel_id=1, source_target_pairs={{0,1},{1,0},{2,3},{3,2},{4,5},{5,4},{6,7},{7,6},{8,9},{9,8},{10,11... | collective-permute-start | bytes 147464 | tf_op jit(solution)/shard_map/ppermute | solution.py:29
  12.7 2.6 %collective-permute-start.2 = (bf16[192,128]{1,0:T(8,128)(2,1)S(1)}, bf16[192,128]{1,0:T(8,128)(2,1)S(1)}, u32[]{:S(2)}, u32[]{:S(2)}) collective-permute-start(bf16[192,128]{1,0:T(8,128)(2,1)S(1)} %get-tuple-element.37), channel_id=1, source_target_pairs={{0,2},{1,3},{2,0},{3,1},{4,6},{5,7},{6,4},{7,5},{8,10},{9,11},{10,... | collective-permute-start | bytes 147464 | tf_op jit(solution)/shard_map/ppermute | solution.py:29
  15.3 0.0 collective-permute-done.1.refs_1_.refs_7_
  15.3 3.5 %collective-permute-done.2.refs_2_.refs_8_ = bf16[192,128]{1,0:T(8,128)(2,1)S(1)} collective-permute-done((bf16[192,128]{1,0:T(8,128)(2,1)S(1)}, bf16[192,128]{1,0:T(8,128)(2,1)S(1)}, u32[]{:S(2)}, u32[]{:S(2)}) %collective-permute-start.2) | collective-permute-done | bytes 49184 | tf_op jit(solution)/shard_map/ppermute | solution.py:29
  18.8 2.4 %collective-permute-done.3.refs_3_.refs_9_ = bf16[192,128]{1,0:T(8,128)(2,1)S(1)} collective-permute-done((bf16[192,128]{1,0:T(8,128)(2,1)S(1)}, bf16[192,128]{1,0:T(8,128)(2,1)S(1)}, u32[]{:S(2)}, u32[]{:S(2)}) %collective-permute-start.3) | collective-permute-done | bytes 49184 | tf_op jit(solution)/shard_map/ppermute | solution.py:29
  21.2 0.6 %token_.1 = (f32[2,16,128]{2,1,0:T(8,128)S(1)}, f32[8,128]{1,0:T(8,128)S(1)}, f32[8,128]{1,0:T(8,128)S(1)}, f32[8,128]{1,0:T(8,128)S(1)}) custom-call(s32[2,8]{1,0:T(2,128)S(1)} %bitcast.11, s32[8]{0:T(128)S(1)} %copy-done.10, bf16[192,128]{1,0:T(8,128)(2,1)S(1)} %get-tuple-element.35.refs_0_.refs_6_.q, ...), custom_call_target="tpu_custom_call" | custom-call | tf_op jit(solution)/shard_map/token/pallas_call | solution.py:406
  21.8 0.1 collective-permute-start.6
  21.9 1.6 %collective-permute-start.7 = (f32[8,128]{1,0:T(8,128)S(1)}, f32[8,128]{1,0:T(8,128)S(1)}, u32[]{:S(2)}, u32[]{:S(2)}) collective-permute-start(f32[8,128]{1,0:T(8,128)S(1)} %get-tuple-element.44), channel_id=1, source_target_pairs={{0,8},{4,12},{8,0},{12,4},{1,9},{5,13},{9,1},{13,5},{2,10},{6,14},... | collective-permute-start | bytes 12296 | tf_op jit(solution)/shard_map/ppermute | solution.py:29
  23.5 0.3 collective-permute-start.8
  23.8 2.7 %attend.1 = (f32[4,128,128]{2,1,0:T(8,128)S(1)}, f32[4,16,128]{2,1,0:T(8,128)S(1)}, bf16[8,128,1024]{2,1,0:T(8,128)(2,1)}) custom-call(s32[4,8]{1,0:T(4,128)S(1)} %bitcast.17, s32[8]{0:T(128)S(1)} %copy-done.10, bf16[8,128,1024]{2,1,0:T(8,128)(2,1)S(1)} %bitcast.7, bf16[192,128]{1,0:T(8,128)(2,1)S(1)} %get-tuple-element.35.refs_0_.refs_6_.q, ...), custom_call_target="tpu_custom_call" | custom-call | tf_op jit(solution)/shard_map/attend/pallas_call | solution.py:416
  26.5 0.0 collective-permute-done.5.refs_2_
  26.5 0.0 collective-permute-done.8.refs_5_
  26.5 1.1 %arrive.1 = (bf16[192,128]{1,0:T(8,128)(2,1)S(1)}, bf16[192,128]{1,0:T(8,128)(2,1)S(1)}, bf16[192,128]{1,0:T(8,128)(2,1)S(1)}, f32[128,128]{1,0:T(8,128)S(1)}, f32[16,128]{1,0:T(8,128)S(1)}) custom-call(s32[2,8]{1,0:T(2,128)S(1)} %bitcast.12, s32[4,8]{1,0:T(4,128)S(1)} %bitcast.14, f32[2,16,128]{2,1,0:T(8,128)S(1)} %get-tuple-element.39.kv, ...), custom_call_target="tpu_custom_call" | custom-call | tf_op jit(solution)/shard_map/arrive/pallas_call | solution.py:434
  27.7 0.0 collective-permute-start.9
  27.7 1.8 %collective-permute-start.10 = (bf16[192,128]{1,0:T(8,128)(2,1)S(1)}, bf16[192,128]{1,0:T(8,128)(2,1)S(1)}, u32[]{:S(2)}, u32[]{:S(2)}) collective-permute-start(bf16[192,128]{1,0:T(8,128)(2,1)S(1)} %get-tuple-element.51), channel_id=1, source_target_pairs={{0,2},{1,3},{2,0},{3,1},{4,6},{5,7},{6,4},{7,5},{8,10},{9,11},{10,... | collective-permute-start | bytes 147464 | tf_op jit(solution)/shard_map/ppermute | solution.py:29
  29.5 2.6 %collective-permute-start.11 = (bf16[192,128]{1,0:T(8,128)(2,1)S(1)}, bf16[192,128]{1,0:T(8,128)(2,1)S(1)}, u32[]{:S(2)}, u32[]{:S(2)}) collective-permute-start(bf16[192,128]{1,0:T(8,128)(2,1)S(1)} %get-tuple-element.52), channel_id=1, source_target_pairs={{0,3},{1,2},{2,1},{3,0},{4,7},{5,6},{6,5},{7,4},{8,11},{9,10},{10,... | collective-permute-start | bytes 147464 | tf_op jit(solution)/shard_map/ppermute | solution.py:29
  32.1 0.5 %collective-permute-done.9.refs_6_ = bf16[192,128]{1,0:T(8,128)(2,1)S(1)} collective-permute-done((bf16[192,128]{1,0:T(8,128)(2,1)S(1)}, bf16[192,128]{1,0:T(8,128)(2,1)S(1)}, u32[]{:S(2)}, u32[]{:S(2)}) %collective-permute-start.9) | collective-permute-done | bytes 49184 | tf_op jit(solution)/shard_map/ppermute | solution.py:29
  32.6 2.1 %collective-permute-done.10.refs_7_ = bf16[192,128]{1,0:T(8,128)(2,1)S(1)} collective-permute-done((bf16[192,128]{1,0:T(8,128)(2,1)S(1)}, bf16[192,128]{1,0:T(8,128)(2,1)S(1)}, u32[]{:S(2)}, u32[]{:S(2)}) %collective-permute-start.10) | collective-permute-done | bytes 49184 | tf_op jit(solution)/shard_map/ppermute | solution.py:29
  34.7 0.8 %collective-permute-done.11.refs_8_ = bf16[192,128]{1,0:T(8,128)(2,1)S(1)} collective-permute-done((bf16[192,128]{1,0:T(8,128)(2,1)S(1)}, bf16[192,128]{1,0:T(8,128)(2,1)S(1)}, u32[]{:S(2)}, u32[]{:S(2)}) %collective-permute-start.11) | collective-permute-done | bytes 49184 | tf_op jit(solution)/shard_map/ppermute | solution.py:29
  35.5 3.6 %finish.1 = (bf16[8,1024]{1,0:T(8,128)(2,1)}, bf16[8,1024]{1,0:T(8,128)(2,1)}, bf16[8,128,1024]{2,1,0:T(8,128)(2,1)}) custom-call(s32[2,8]{1,0:T(2,128)S(1)} %bitcast.13, s32[4,8]{1,0:T(4,128)S(1)} %bitcast.15, s32[8]{0:T(128)S(1)} %copy-done.10, f32[2,16,128]{2,1,0:T(8,128)S(1)} %get-tuple-element.39.kv, ...), custom_call_target="tpu_custom_call", output_to_operand_aliasing={{2}: (17, {})} | custom-call | tf_op jit(solution)/shard_map/finish/pallas_call | solution.py:454
  (20 shorter events, 0.0 us)
Async XLA Ops:
  0.6 1.6 %copy-start = (bf16[1,1,8,128,1024]{4,3,2,1,0:T(8,128)(2,1)S(1)}, bf16[1,1,8,128,1024]{4,3,2,1,0:T(8,128)(2,1)}, u32[]{:S(2)}) copy-start(bf16[1,1,8,128,1024]{4,3,2,1,0:T(8,128)(2,1)} %param.11) | copy-start | bytes 6291460
  2.2 0.7 %copy-start.5 = (s32[8,2]{0,1:T(2,128)S(1)}, s32[8,2]{0,1:T(2,128)}, u32[]{:S(2)}) copy-start(s32[8,2]{0,1:T(2,128)} %param.15) | copy-start | bytes 196
  2.9 0.7 %copy-start.8 = (s32[8,4]{0,1:T(4,128)S(1)}, s32[8,4]{0,1:T(4,128)}, u32[]{:S(2)}) copy-start(s32[8,4]{0,1:T(4,128)} %param.13) | copy-start | bytes 388
  3.6 3.9 %copy-start.3 = (bf16[2,8,2048]{2,1,0:T(8,128)(2,1)S(1)}, bf16[2,8,2048]{2,1,0:T(8,128)(2,1)}, u32[]{:S(2)}) copy-start(bf16[2,8,2048]{2,1,0:T(8,128)(2,1)} %param.8) | copy-start | bytes 196612
  3.6 3.9 %copy-start.4 = (bf16[2,8,1024]{2,1,0:T(8,128)(2,1)S(1)}, bf16[2,8,1024]{2,1,0:T(8,128)(2,1)}, u32[]{:S(2)}) copy-start(bf16[2,8,1024]{2,1,0:T(8,128)(2,1)} %q.1) | copy-start | bytes 98308
  4.4 6.5 %collective-permute-start = (bf16[128,1024]{1,0:T(8,128)(2,1)S(1)}, bf16[128,1024]{1,0:T(8,128)(2,1)S(1)}, u32[]{:S(2)}, u32[]{:S(2)}) collective-permute-start(bf16[128,1024]{1,0:T(8,128)(2,1)S(1)} %get-tuple-element.34), channel_id=1, source_target_pairs={{0,4},{4,0},{8,12},{12,8},{1,5},{5,1},{9,13},{13,9},{2,6},{6,2},{1... | collective-permute-start | bytes 786440 | tf_op jit(solution)/shard_map/ppermute | solution.py:29
  4.9 21.6 %collective-permute-start.4 = (bf16[128,1024]{1,0:T(8,128)(2,1)S(1)}, bf16[128,1024]{1,0:T(8,128)(2,1)S(1)}, u32[]{:S(2)}, u32[]{:S(2)}) collective-permute-start(bf16[128,1024]{1,0:T(8,128)(2,1)S(1)} %get-tuple-element.41), channel_id=1, source_target_pairs={{0,8},{4,12},{8,0},{12,4},{1,9},{5,13},{9,1},{13,5},{2,10},{6,14},... | collective-permute-start | bytes 786440 | tf_op jit(solution)/shard_map/ppermute | solution.py:29
  7.4 19.1 %collective-permute-start.5 = (bf16[128,1024]{1,0:T(8,128)(2,1)S(1)}, bf16[128,1024]{1,0:T(8,128)(2,1)S(1)}, u32[]{:S(2)}, u32[]{:S(2)}) collective-permute-start(bf16[128,1024]{1,0:T(8,128)(2,1)S(1)} %get-tuple-element.42), channel_id=1, source_target_pairs={{0,12},{4,8},{8,4},{12,0},{1,13},{5,9},{9,5},{13,1},{2,14},{6,10},... | collective-permute-start | bytes 786440 | tf_op jit(solution)/shard_map/ppermute | solution.py:29
  7.5 2.2 %copy-start.2 = (bf16[2048,1024]{1,0:T(8,128)(2,1)S(1)}, bf16[2048,1024]{1,0:T(8,128)(2,1)}, u32[]{:S(2)}) copy-start(bf16[2048,1024]{1,0:T(8,128)(2,1)} %weight.1) | copy-start | bytes 12582916
  9.7 11.5 %copy-start.6 = (s32[8,2]{0,1:T(2,128)S(1)}, s32[8,2]{0,1:T(2,128)}, u32[]{:S(2)}) copy-start(s32[8,2]{0,1:T(2,128)} %param.15) | copy-start | bytes 196
  9.7 11.5 %copy-start.10 = (s32[8]{0:T(128)S(1)}, s32[8]{0:T(128)}, u32[]{:S(2)}) copy-start(s32[8]{0:T(128)} %lengths.5) | copy-start | bytes 100
  9.7 14.1 %copy-start.1 = (bf16[1,1,8,128,1024]{4,3,2,1,0:T(8,128)(2,1)S(1)}, bf16[1,1,8,128,1024]{4,3,2,1,0:T(8,128)(2,1)}, u32[]{:S(2)}) copy-start(bf16[1,1,8,128,1024]{4,3,2,1,0:T(8,128)(2,1)} %param.11) | copy-start | bytes 6291460
  9.7 14.1 %copy-start.9 = (s32[8,4]{0,1:T(4,128)S(1)}, s32[8,4]{0,1:T(4,128)}, u32[]{:S(2)}) copy-start(s32[8,4]{0,1:T(4,128)} %param.13) | copy-start | bytes 388
  10.8 15.7 %copy-start.7 = (s32[8,4]{0,1:T(4,128)S(1)}, s32[8,4]{0,1:T(4,128)}, u32[]{:S(2)}) copy-start(s32[8,4]{0,1:T(4,128)} %param.14) | copy-start | bytes 388
  10.9 4.5 %collective-permute-start.1 = (bf16[192,128]{1,0:T(8,128)(2,1)S(1)}, bf16[192,128]{1,0:T(8,128)(2,1)S(1)}, u32[]{:S(2)}, u32[]{:S(2)}) collective-permute-start(bf16[192,128]{1,0:T(8,128)(2,1)S(1)} %get-tuple-element.36), channel_id=1, source_target_pairs={{0,1},{1,0},{2,3},{3,2},{4,5},{5,4},{6,7},{7,6},{8,9},{9,8},{10,11... | collective-permute-start | bytes 147464 | tf_op jit(solution)/shard_map/ppermute | solution.py:29
  12.7 6.1 %collective-permute-start.2 = (bf16[192,128]{1,0:T(8,128)(2,1)S(1)}, bf16[192,128]{1,0:T(8,128)(2,1)S(1)}, u32[]{:S(2)}, u32[]{:S(2)}) collective-permute-start(bf16[192,128]{1,0:T(8,128)(2,1)S(1)} %get-tuple-element.37), channel_id=1, source_target_pairs={{0,2},{1,3},{2,0},{3,1},{4,6},{5,7},{6,4},{7,5},{8,10},{9,11},{10,... | collective-permute-start | bytes 147464 | tf_op jit(solution)/shard_map/ppermute | solution.py:29
  15.3 5.9 %collective-permute-start.3 = (bf16[192,128]{1,0:T(8,128)(2,1)S(1)}, bf16[192,128]{1,0:T(8,128)(2,1)S(1)}, u32[]{:S(2)}, u32[]{:S(2)}) collective-permute-start(bf16[192,128]{1,0:T(8,128)(2,1)S(1)} %get-tuple-element.38), channel_id=1, source_target_pairs={{0,3},{1,2},{2,1},{3,0},{4,7},{5,6},{6,5},{7,4},{8,11},{9,10},{10,... | collective-permute-start | bytes 147464 | tf_op jit(solution)/shard_map/ppermute | solution.py:29
  21.8 4.7 %collective-permute-start.6 = (f32[8,128]{1,0:T(8,128)S(1)}, f32[8,128]{1,0:T(8,128)S(1)}, u32[]{:S(2)}, u32[]{:S(2)}) collective-permute-start(f32[8,128]{1,0:T(8,128)S(1)} %get-tuple-element.43), channel_id=1, source_target_pairs={{0,4},{4,0},{8,12},{12,8},{1,5},{5,1},{9,13},{13,9},{2,6},{6,2},{1... | collective-permute-start | bytes 12296 | tf_op jit(solution)/shard_map/ppermute | solution.py:29
  21.9 4.6 %collective-permute-start.7 = (f32[8,128]{1,0:T(8,128)S(1)}, f32[8,128]{1,0:T(8,128)S(1)}, u32[]{:S(2)}, u32[]{:S(2)}) collective-permute-start(f32[8,128]{1,0:T(8,128)S(1)} %get-tuple-element.44), channel_id=1, source_target_pairs={{0,8},{4,12},{8,0},{12,4},{1,9},{5,13},{9,1},{13,5},{2,10},{6,14},... | collective-permute-start | bytes 12296 | tf_op jit(solution)/shard_map/ppermute | solution.py:29
  23.5 3.1 %collective-permute-start.8 = (f32[8,128]{1,0:T(8,128)S(1)}, f32[8,128]{1,0:T(8,128)S(1)}, u32[]{:S(2)}, u32[]{:S(2)}) collective-permute-start(f32[8,128]{1,0:T(8,128)S(1)} %get-tuple-element.45), channel_id=1, source_target_pairs={{0,12},{4,8},{8,4},{12,0},{1,13},{5,9},{9,5},{13,1},{2,14},{6,10},... | collective-permute-start | bytes 12296 | tf_op jit(solution)/shard_map/ppermute | solution.py:29
  27.7 4.9 %collective-permute-start.9 = (bf16[192,128]{1,0:T(8,128)(2,1)S(1)}, bf16[192,128]{1,0:T(8,128)(2,1)S(1)}, u32[]{:S(2)}, u32[]{:S(2)}) collective-permute-start(bf16[192,128]{1,0:T(8,128)(2,1)S(1)} %get-tuple-element.50), channel_id=1, source_target_pairs={{0,1},{1,0},{2,3},{3,2},{4,5},{5,4},{6,7},{7,6},{8,9},{9,8},{10,11... | collective-permute-start | bytes 147464 | tf_op jit(solution)/shard_map/ppermute | solution.py:29
  27.7 7.0 %collective-permute-start.10 = (bf16[192,128]{1,0:T(8,128)(2,1)S(1)}, bf16[192,128]{1,0:T(8,128)(2,1)S(1)}, u32[]{:S(2)}, u32[]{:S(2)}) collective-permute-start(bf16[192,128]{1,0:T(8,128)(2,1)S(1)} %get-tuple-element.51), channel_id=1, source_target_pairs={{0,2},{1,3},{2,0},{3,1},{4,6},{5,7},{6,4},{7,5},{8,10},{9,11},{10,... | collective-permute-start | bytes 147464 | tf_op jit(solution)/shard_map/ppermute | solution.py:29
  29.5 5.9 %collective-permute-start.11 = (bf16[192,128]{1,0:T(8,128)(2,1)S(1)}, bf16[192,128]{1,0:T(8,128)(2,1)S(1)}, u32[]{:S(2)}, u32[]{:S(2)}) collective-permute-start(bf16[192,128]{1,0:T(8,128)(2,1)S(1)} %get-tuple-element.52), channel_id=1, source_target_pairs={{0,3},{1,2},{2,1},{3,0},{4,7},{5,6},{6,5},{7,4},{8,11},{9,10},{10,... | collective-permute-start | bytes 147464 | tf_op jit(solution)/shard_map/ppermute | solution.py:29

commit v3 on v2

--- a/solution.py
+++ b/solution.py
@@ -16,6 +16,7 @@
 SCALE = 1.0 / math.sqrt(HD)
 WINDOW = 32
 KV_ROWS = 24
+OPEN_MB = 32
 
 SMEM = pl.BlockSpec(memory_space=pltpu.SMEM)
 VMEM = pl.BlockSpec(memory_space=pltpu.VMEM)
@@ -30,7 +31,8 @@
 
 
 def exchange(messages, axis):
-    return [swap(message, axis, d + 1) for d, message in enumerate(messages)]
+    received = [swap(messages[d], axis, d + 1) for d in reversed(range(len(messages)))]
+    return received[::-1]
 
 
 def partner(axis, distance):
@@ -80,50 +82,65 @@
     return jnp.exp(CAP * jnp.tanh(score * (SCALE / CAP)))
 
 
-def leave_kernel(rows, moves, table, pool, *refs):
-    outs, sems = refs[:-1], refs[-1]
+def open_kernel(count, replicas, local_heads, moves_all, table_all, x_all, q_all, weight, pool, *refs):
+    outs, pages = refs[:count], refs[count : count + replicas - 1]
+    held, x, q, moves, table, weight_sems, page_sems, rest_sems = refs[count + replicas - 1 :]
     me, column = lax.axis_index("replica"), lax.axis_index("mp")
+    rows = q.shape[1]
+    tokens, depth = x.shape
+    chunks = weight_sems.shape[0]
+    loads = []
+    pairs = ((moves_all, moves), (table_all, table), (x_all, x), (q_all, q))
+    rest = [pltpu.make_async_copy(*pair, rest_sems.at[i]) for i, pair in enumerate(pairs)]
+    for copy in rest:
+        copy.start()
+    for c in range(chunks):
+        span = pl.ds(c * (depth // chunks), depth // chunks)
+        loads.append(pltpu.make_async_copy(weight.at[span], held.at[span], weight_sems.at[c]))
+        loads[-1].start()
     copies = []
-    for s, out in enumerate(outs):
+    for copy in rest[:2]:
+        copy.wait()
+    for s, page in enumerate(pages):
         _, row = pair_row(moves, me, partner("replica", s + 1), rows, 0)
         _, slot = locate(table, row, column, pool.shape[0])
-        copies.append(pltpu.make_async_copy(pool.at[slot], out, sems.at[s]))
+        copies.append(pltpu.make_async_copy(pool.at[slot], page, page_sems.at[s]))
         copies[-1].start()
+
+    for copy in rest[2:]:
+        copy.wait()
+    wide = [q[i].astype(jnp.float32) for i in range(2)]
+    blocks = [wide[i][:, h * HD : (h + 1) * HD] for i in range(2) for h in range(local_heads)]
+    packed = jnp.concatenate(blocks, axis=0).astype(jnp.bfloat16)
+    query_rows = packed.shape[0]
+    for out in outs:
+        out[:query_rows, :] = packed
+    total = jnp.zeros((tokens, held.shape[1]), jnp.float32)
+    for c, load in enumerate(loads):
+        load.wait()
+        span = pl.ds(c * (depth // chunks), depth // chunks)
+        total += jnp.dot(x[:, span], held[span, :], preferred_element_type=jnp.float32)
+    for j in range(KVH):
+        parts = []
+        for half in range(2):
+            start = (half * KVH + j) * HD
+            part = total[:, start : start + HD]
+            high = part.astype(jnp.bfloat16)
+            parts += [high, (part - high.astype(jnp.float32)).astype(jnp.bfloat16)]
+        parts = jnp.concatenate(parts, axis=0)
+        for s, out in enumerate(outs):
+
+            @pl.when(split(partner("mp", s) * local_heads, GROUP)[0] == j)
+            def _(out=out, parts=parts):
+                out[query_rows:, :] = parts
+
     for copy in copies:
         copy.wait()
 
 
-def project_kernel(count, local_heads, x, weight, q, *refs):
-    outs, total = refs[:-1], refs[-1]
-    step = pl.program_id(0)
-    rows = q.shape[1]
-    query_rows = 2 * local_heads * rows
-
-    @pl.when(step == 0)
-    def _():
-        total[...] = jnp.zeros_like(total)
-        wide = [q[i].astype(jnp.float32) for i in range(2)]
-        blocks = [wide[i][:, h * HD : (h + 1) * HD] for i in range(2) for h in range(local_heads)]
-        packed = jnp.concatenate(blocks, axis=0).astype(jnp.bfloat16)
-        for out in outs:
-            out[:query_rows, :] = packed
-
-    total[...] += jnp.dot(x[...], weight[...], preferred_element_type=jnp.float32)
-
-    @pl.when(step == pl.num_programs(0) - 1)
-    def _():
-        for s, out in enumerate(outs):
-            columns = head_columns(partner("mp", s), local_heads)
-            parts = []
-            for half in range(2):
-                part = total.at[:, pl.ds(half * KVH * HD, KVH * HD)][:, columns]
-                high = part.astype(jnp.bfloat16)
-                parts += [high, (part - high.astype(jnp.float32)).astype(jnp.bfloat16)]
-            out[query_rows:, :] = jnp.concatenate(parts, axis=0)
-
-
-def token_kernel(count, replicas, rows, moves, lengths, *refs):
-    messages, kv, outs = refs[:count], refs[count], refs[count + 1 :]
+def token_kernel(count, moves, lengths, *refs):
+    messages, kv, outs = refs[:count][::-1], refs[count], refs[count + 1 :]
+    rows = lengths.shape[0]
     tokens = 2 * rows
     base = messages[0].shape[0] - 4 * tokens
     me = lax.axis_index("replica")
@@ -134,12 +151,17 @@
             total += message[start : start + tokens, :].astype(jnp.float32)
             total += message[start + tokens : start + 2 * tokens, :].astype(jnp.float32)
         kv[half] = total.astype(jnp.bfloat16).astype(jnp.float32)
+    sublane = lax.broadcasted_iota(jnp.int32, (8, HD), 0)
     for s, out in enumerate(outs):
         _, row = pair_row(moves, me, partner("replica", s + 1), rows, 0)
-        out[...] = jnp.zeros_like(out)
-        out[0:1, :] = kv[0, pl.ds(row, 1), :]
-        out[1:2, :] = kv[1, pl.ds(row, 1), :]
-        out[2:3, :] = jnp.full((1, HD), lengths[row], jnp.int32).astype(jnp.float32)
+        value = jnp.full((8, HD), lengths[row], jnp.int32).astype(jnp.float32)
+        for half in range(2):
+            value = jnp.where(sublane == half, kv[half, pl.ds(row, 1), :], value)
+        out[...] = value
+
+
+def arrived_token(part):
+    return part[0:1], part[1:2], part[2:3]
 
 
 def scores_of(q, keys):
@@ -147,7 +169,7 @@
 
 
 def attend_kernel(count, local_heads, table, lengths, pool, *refs):
-    messages = refs[:count]
+    messages = refs[:count][::-1]
     num, den, pool_out, wide, sem = refs[count:]
     column = lax.axis_index("mp")
     rows = lengths.shape[0]
@@ -185,16 +207,19 @@
     store.wait()
 
 
-def arrive_kernel(count, replicas, local_heads, slots, moves, table, kv, *refs):
-    rows = table.shape[1]
+def arrive_kernel(count, replicas, local_heads, slots, *refs):
     refs = list(refs)
     take = lambda n: [refs.pop(0) for _ in range(n)]
-    pages_in, tokens_in, messages = take(replicas - 1), take(replicas - 1), take(count)
+    pages_in = take(replicas - 2)
+    moves, table, kv = take(3)
+    pages_in, tokens_in, messages = take(1) + pages_in, take(replicas - 1), take(count)[::-1]
+    rows = table.shape[1]
+    page_size, width = pages_in[0].shape
+    tokens_in = [arrived_token(part) for part in tokens_in]
     num_in, den_in = take(2)
     outs = take(count - 1)
     own_num, own_den, num, den, wide = refs
     me, column = lax.axis_index("replica"), lax.axis_index("mp")
-    page_size, width = pages_in[0].shape
     half_rows = local_heads * rows
     num[...] = num_in[...]
     den[...] = den_in[...]
@@ -212,7 +237,7 @@
         scores[d, s] = scores_of(q, pages_in[d - 1].at[:, pl.ds(0, width // 2)][:, columns[s]])
     for d, s in cases:
         index, _ = locate(table, arrivals[d - 1][1], column, slots)
-        inside = (token + index * page_size).astype(jnp.float32) < tokens_in[d - 1][2:3, :]
+        inside = (token + index * page_size).astype(jnp.float32) < tokens_in[d - 1][2]
         weight = jnp.where(inside, weight_of(scores[d, s]), 0.0)
         weights[d, s] = weight.astype(jnp.bfloat16)
         totals[d, s] = jnp.sum(weight, axis=1, keepdims=True)
@@ -233,7 +258,7 @@
     filler = jnp.zeros((KV_ROWS - 2 * rows - (replicas - 1), HD), jnp.float32)
     all_kv = []
     for half in range(2):
-        all_kv += [kv[half]] + [arrived[half : half + 1, :] for arrived in tokens_in] + [filler]
+        all_kv += [kv[half]] + [arrived[half] for arrived in tokens_in] + [filler]
     all_kv = jnp.concatenate(all_kv, axis=0)
     for s, out in enumerate(outs):
         at = s + 1
@@ -243,11 +268,14 @@
         out[...] = jnp.concatenate([num[at], parts, all_kv], axis=0).astype(SEND)
 
 
-def finish_kernel(count, replicas, local_heads, moves, table, lengths, kv, q, num, den, *refs):
+def finish_kernel(count, replicas, local_heads, *refs):
     refs = list(refs)
     take = lambda n: [refs.pop(0) for _ in range(n)]
-    pages_in, tokens_in, messages = take(replicas - 1), take(replicas - 1), take(count - 1)
+    pages_in = take(replicas - 2)
+    moves, table, lengths, kv, q, num, den = take(7)
+    pages_in, tokens_in, messages = take(1) + pages_in, take(replicas - 1), take(count - 1)[::-1]
     pool_raw, _, first, second, pool = take(5)
+    tokens_in = [arrived_token(part) for part in tokens_in]
     held, full, windows, page_sems, read_sems, write_sems = refs
     me, column = lax.axis_index("replica"), lax.axis_index("mp")
     rows = lengths.shape[0]
@@ -273,7 +301,7 @@
     for s, page in enumerate(pages_in):
         valid, row = pair_row(moves, partner("replica", s + 1), me, rows, 1)
         valid = valid == 1
-        length = jnp.max(tokens_in[s][2:3, :]).astype(jnp.int32)
+        length = jnp.max(tokens_in[s][2]).astype(jnp.int32)
         slot = add_plan(valid, row, length, 2 * rows + s, page)
         copies.append(pltpu.make_async_copy(page, pool.at[slot], page_sems.at[s]))
         pl.when(valid)(copies[-1].start)
@@ -288,7 +316,7 @@
 
             @pl.when(valid)
             def _(half=half, s=s, row=row):
-                held[half, pl.ds(row, 1), :] = tokens_in[s][half : half + 1, :]
+                held[half, pl.ds(row, 1), :] = tokens_in[s][half]
 
     query_rows = both * rows
     kv_base = messages[0].shape[0] - 2 * KV_ROWS
@@ -298,7 +326,7 @@
         for half in range(2):
             if s == 0:
                 chunk = jnp.concatenate(
-                    [kv[half]] + [arrived[half : half + 1, :] for arrived in tokens_in] + [filler],
+                    [kv[half]] + [arrived[half] for arrived in tokens_in] + [filler],
                     axis=0,
                 )
             else:
@@ -356,6 +384,14 @@
         pl.when(touched)(write.wait)
 
 
+def cost(microseconds):
+    return pl.CostEstimate(flops=0, transcendentals=0, bytes_accessed=int(microseconds * 3.5e6))
+
+
+def in_hbm(value):
+    return pltpu.with_memory_space_constraint(value, pltpu.HBM)
+
+
 def params(megabytes=32, **rest):
     return pltpu.CompilerParams(vmem_limit_bytes=megabytes << 20, **rest)
 
@@ -373,44 +409,41 @@
     moves, old_table, table_after = migrations.T, block_table.T, new_table.T
     shape = jax.ShapeDtypeStruct
 
-    leaving = pl.pallas_call(
-        functools.partial(leave_kernel, rows),
-        out_shape=[shape((page_size, width), bf16)] * (replicas - 1),
-        in_specs=[SMEM, SMEM, HBM],
-        out_specs=[ANY] * (replicas - 1),
-        scratch_shapes=[pltpu.SemaphoreType.DMA((replicas - 1,))],
-        compiler_params=params(),
-        name="leave",
-    )(moves, old_table, pool)
-    pages_in = exchange(leaving, "replica")
-
-    block = math.gcd(depth, 512)
     message_rows = query_rows + 8 * rows
+    chunks = 8
     sent = pl.pallas_call(
-        functools.partial(project_kernel, count, local_heads),
-        grid=(depth // block,),
-        out_shape=[shape((message_rows, HD), bf16)] * count,
-        in_specs=[
-            pl.BlockSpec((2 * rows, block), lambda k: (0, k)),
-            pl.BlockSpec((block, width), lambda k: (k, 0), memory_space=pltpu.VMEM),
-            pl.BlockSpec(queries.shape, lambda k: (0, 0, 0)),
+        functools.partial(open_kernel, count, replicas, local_heads),
+        out_shape=[shape((message_rows, HD), bf16)] * count
+        + [shape((page_size, width), bf16)] * (replicas - 1),
+        in_specs=[HBM] * 6,
+        out_specs=[VMEM] * count + [ANY] * (replicas - 1),
+        scratch_shapes=[
+            pltpu.VMEM((depth, width), bf16),
+            pltpu.VMEM((2 * rows, depth), bf16),
+            pltpu.VMEM(queries.shape, bf16),
+            pltpu.SMEM(moves.shape, jnp.int32),
+            pltpu.SMEM(old_table.shape, jnp.int32),
+            pltpu.SemaphoreType.DMA((chunks,)),
+            pltpu.SemaphoreType.DMA((replicas - 1,)),
+            pltpu.SemaphoreType.DMA((4,)),
         ],
-        out_specs=[pl.BlockSpec((message_rows, HD), lambda k: (0, 0))] * count,
-        scratch_shapes=[pltpu.VMEM((2 * rows, width), f32)],
-        compiler_params=params(),
-        name="project",
-    )(layer_input.reshape(2 * rows, depth), kv_weight, queries)
-    sent, pages_in[0] = lax.optimization_barrier((sent, pages_in[0]))
+        compiler_params=params(OPEN_MB),
+        cost_estimate=cost(2.8),
+        name="open",
+    )(*map(in_hbm, (moves, old_table, layer_input.reshape(2 * rows, depth), queries, kv_weight, pool)))
+    sent, leaving = list(sent[:count]), list(sent[count:])
     messages = [sent[0]] + exchange(sent[1:], "mp")
+    pages_in = [swap(page, "replica", d + 1) for d, page in enumerate(leaving) if d > 0]
 
     kv, *tokens = pl.pallas_call(
-        functools.partial(token_kernel, count, replicas, rows),
+        functools.partial(token_kernel, count),
         out_shape=[shape((2, 2 * rows, HD), f32)] + [shape((8, HD), f32)] * (replicas - 1),
         in_specs=[SMEM, SMEM] + [VMEM] * count,
         out_specs=[VMEM] * replicas,
         compiler_params=params(),
+        cost_estimate=cost(0.6),
         name="token",
-    )(moves, lengths, *messages)
+    )(moves, lengths, *messages[::-1])
     tokens_in = exchange(tokens, "replica")
 
     num, den, pool_copy = pl.pallas_call(
@@ -427,17 +460,21 @@
             pltpu.SemaphoreType.DMA(()),
         ],
         compiler_params=params(),
+        cost_estimate=cost(2.7),
         name="attend",
-    )(old_table, lengths, pool, *messages)
+    )(old_table, lengths, pool, *messages[::-1])
+
+    near, num = lax.optimization_barrier((leaving[0], num))
+    pages_in.insert(0, swap(near, "replica", 1))
 
     sum_rows = query_rows + both + 2 * KV_ROWS
     *sums, num, den = pl.pallas_call(
         functools.partial(arrive_kernel, count, replicas, local_heads, slots),
         out_shape=[shape((sum_rows, HD), SEND)] * (count - 1)
         + [shape((query_rows, HD), f32), shape((both, HD), f32)],
-        in_specs=[SMEM, SMEM, VMEM]
-        + [VMEM] * (replicas - 1)
-        + [VMEM] * (replicas - 1)
+        in_specs=[VMEM] * (replicas - 2)
+        + [SMEM, SMEM, VMEM]
+        + [VMEM] * replicas
         + [VMEM] * count
         + [VMEM] * 2,
         out_specs=[VMEM] * (count + 1),
@@ -447,8 +484,9 @@
             pltpu.VMEM((count, query_rows // 2, HD), f32),
         ],
         compiler_params=params(),
+        cost_estimate=cost(1.2),
         name="arrive",
-    )(moves, table_after, kv, *pages_in, *tokens_in, *messages, num, den)
+    )(*pages_in[1:], moves, table_after, kv, pages_in[0], *tokens_in, *messages[::-1], num, den)
     sums_in = exchange(sums, "mp")
 
     first, second, pool_after = pl.pallas_call(
@@ -458,10 +496,10 @@
             shape((rows, local_heads * HD), bf16),
             shape(pool.shape, bf16),
         ],
-        in_specs=[SMEM, SMEM, SMEM]
+        in_specs=[VMEM] * (replicas - 2)
+        + [SMEM, SMEM, SMEM]
         + [VMEM] * 4
-        + [ANY] * (replicas - 1)
-        + [VMEM] * (replicas - 1)
+        + [VMEM] * replicas
         + [VMEM] * (count - 1)
         + [ANY, ANY],
         out_specs=[VMEM, VMEM, ANY],
@@ -473,10 +511,11 @@
             pltpu.SemaphoreType.DMA((rows + replicas - 1,)),
             pltpu.SemaphoreType.DMA((rows + replicas - 1,)),
         ],
-        input_output_aliases={7 + 2 * (replicas - 1) + (count - 1) + 1: 2},
+        input_output_aliases={7 + 2 * replicas - 2 + (count - 1) + 1: 2},
         compiler_params=params(),
+        cost_estimate=cost(3.4),
         name="finish",
-    )(moves, table_after, lengths, kv, messages[0], num, den, *pages_in, *tokens_in, *sums_in, pool, pool_copy)
+    )(*pages_in[1:], moves, table_after, lengths, kv, messages[0], num, den, pages_in[0], *tokens_in, *sums_in[::-1], pool, pool_copy)
     return first, second, pool_after[None, None]
 
 

time: 39.2 us -> 35.6 us (0.908); the launches traced: 39 us -> 35 us
  local copies, waits for them, and re-layouts: 5.16 us -> 0.03 us
  starting transfers between devices: 14 us -> 14.7 us
    unnamed x22 -> x10, local copies, waits for them, and re-layouts: 5.16 us -> 0.03 us
    pallas_call x3 -> x2, Pallas kernels: 2.47 us -> 3.53 us  [the longest x1 2.93 us: body(): pl.pallas_call(functools.partial(open_kernel, count, replicas, local_head...]
    pallas_call x1, Pallas kernels: 3.57 us -> 2.6 us  [body(): pl.pallas_call(functools.partial(finish_kernel, count, replicas, local_he...]
    ppermute x12, starting transfers between devices: 14 us -> 14.7 us  [swap(): return lax.ppermute(value, axis, [(i, i ^ distance) for i in range(size)])]
  transfers between devices with their start and end apart: 12 -> 12, of which waited for: 5 -> 5; matrix products, arithmetic and copies ran while one was open for 0% -> 0% of each run, Pallas kernels for 11% -> 9%
where the time goes in v3:
time: 35.6 us; the launch traced here: 35 us
  starting transfers between devices  14.7 us (41%)
  Pallas kernels  9.99 us (28%)
  waiting for transfers between devices  9.59 us (27%)
  between operations  0.75 us (2%)
    ppermute x12, starting transfers between devices, swap(): return lax.ppermute(value, axis, [(i, i ^ distance) for i in range(size)])  14.7 us
    ppermute x12, waiting for transfers between devices, swap(): return lax.ppermute(value, axis, [(i, i ^ distance) for i in range(size)])  9.59 us
    pallas_call x1, Pallas kernels, body(): pl.pallas_call(functools.partial(open_kernel, count, replicas, local_head...  2.93 us
    pallas_call x1, Pallas kernels, body(): pl.pallas_call(functools.partial(attend_kernel, count, local_heads), out_...  2.71 us
    pallas_call x1, Pallas kernels, body(): pl.pallas_call(functools.partial(finish_kernel, count, replicas, local_he...  2.6 us
    pallas_call x1, Pallas kernels, body(): pl.pallas_call(functools.partial(arrive_kernel, count, replicas, local_he...  1.16 us
  transfers between devices with their start and end apart: 12, of which 5 were waited for; matrix products, arithmetic and copies ran while one was open for 0% of the time, Pallas kernels for 9%

profile of v3, /device:TPU:0, one launch (start us, length us, event | category | flops | bytes accessed | tf_op | source)
XLA Modules:
  0.0 35.0 jit_solution(14912126434716258799)
XLA Ops:
  0.6 0.0 copy-start
  0.7 2.9 %open.1 = (bf16[192,128]{1,0:T(8,128)(2,1)S(1)}, bf16[192,128]{1,0:T(8,128)(2,1)S(1)}, bf16[192,128]{1,0:T(8,128)(2,1)S(1)}, bf16[192,128]{1,0:T(8,128)(2,1)S(1)...) custom-call(s32[2,8]{1,0:T(2,128)} %bitcast.9, s32[4,8]{1,0:T(4,128)} %bitcast.15, ...), custom_call_target="tpu_custom_call" | custom-call | bytes 9800000 | tf_op jit(solution)/shard_map/open/pallas_call | solution.py:414
  3.6 0.0 copy-start.1
  3.6 0.0 copy-start.2
  3.6 5.1 %collective-permute-start.2 = (bf16[192,128]{1,0:T(8,128)(2,1)S(1)}, bf16[192,128]{1,0:T(8,128)(2,1)S(1)}, u32[]{:S(2)}, u32[]{:S(2)}) collective-permute-start(bf16[192,128]{1,0:T(8,128)(2,1)S(1)} %get-tuple-element.29), channel_id=1, source_target_pairs={{0,3},{1,2},{2,1},{3,0},{4,7},{5,6},{6,5},{7,4},{8,11},{9,10},{10,... | collective-permute-start | bytes 147464 | tf_op jit(solution)/shard_map/ppermute | solution.py:30
  8.7 0.0 collective-permute-start.3
  8.7 0.6 %collective-permute-start.4 = (bf16[192,128]{1,0:T(8,128)(2,1)S(1)}, bf16[192,128]{1,0:T(8,128)(2,1)S(1)}, u32[]{:S(2)}, u32[]{:S(2)}) collective-permute-start(bf16[192,128]{1,0:T(8,128)(2,1)S(1)} %get-tuple-element.31), channel_id=1, source_target_pairs={{0,1},{1,0},{2,3},{3,2},{4,5},{5,4},{6,7},{7,6},{8,9},{9,8},{10,11... | collective-permute-start | bytes 147464 | tf_op jit(solution)/shard_map/ppermute | solution.py:30
  9.4 1.6 %collective-permute-start = (bf16[128,1024]{1,0:T(8,128)(2,1)S(1)}, bf16[128,1024]{1,0:T(8,128)(2,1)S(1)}, u32[]{:S(2)}, u32[]{:S(2)}) collective-permute-start(bf16[128,1024]{1,0:T(8,128)(2,1)S(1)} %get-tuple-element.27), channel_id=1, source_target_pairs={{0,8},{4,12},{8,0},{12,4},{1,9},{5,13},{9,1},{13,5},{2,10},{6,14},... | collective-permute-start | bytes 786440 | tf_op jit(solution)/shard_map/ppermute | solution.py:30
  11.0 0.0 collective-permute-start.1
  11.0 0.0 collective-permute-done.2.refs_0_.refs_9_
  11.0 2.7 %collective-permute-done.3.refs_1_.refs_10_ = bf16[192,128]{1,0:T(8,128)(2,1)S(1)} collective-permute-done((bf16[192,128]{1,0:T(8,128)(2,1)S(1)}, bf16[192,128]{1,0:T(8,128)(2,1)S(1)}, u32[]{:S(2)}, u32[]{:S(2)}) %collective-permute-start.3) | collective-permute-done | bytes 49184 | tf_op jit(solution)/shard_map/ppermute | solution.py:30
  13.7 0.0 collective-permute-done.4.refs_2_.refs_11_
  13.8 2.7 %attend.1 = (f32[4,128,128]{2,1,0:T(8,128)S(1)}, f32[4,16,128]{2,1,0:T(8,128)S(1)}, bf16[8,128,1024]{2,1,0:T(8,128)(2,1)}) custom-call(s32[4,8]{1,0:T(4,128)S(1)} %bitcast.16, s32[8]{0:T(128)S(1)} %copy-done.4, bf16[8,128,1024]{2,1,0:T(8,128)(2,1)S(1)} %bitcast.7, bf16[192,128]{1,0:T(8,128)(2,1)S(1)} %collective-permute-done.2.refs_0_.refs_9_, ...), custom_call_target="tpu_custom_call" | custom-call | bytes 9450000 | tf_op jit(solution)/shard_map/attend/pallas_call | solution.py:449
  16.5 0.1 collective-permute-start.5
  16.6 0.6 %token_.1 = (f32[2,16,128]{2,1,0:T(8,128)S(1)}, f32[8,128]{1,0:T(8,128)S(1)}, f32[8,128]{1,0:T(8,128)S(1)}, f32[8,128]{1,0:T(8,128)S(1)}) custom-call(s32[2,8]{1,0:T(2,128)S(1)} %bitcast.10, s32[8]{0:T(128)S(1)} %copy-done.4, bf16[192,128]{1,0:T(8,128)(2,1)S(1)} %collective-permute-done.2.refs_0_.refs_9_, ...), custom_call_target="tpu_custom_call" | custom-call | bytes 2100000 | tf_op jit(solution)/shard_map/token/pallas_call | solution.py:438
  17.2 0.6 %collective-permute-start.6 = (f32[8,128]{1,0:T(8,128)S(1)}, f32[8,128]{1,0:T(8,128)S(1)}, u32[]{:S(2)}, u32[]{:S(2)}) collective-permute-start(f32[8,128]{1,0:T(8,128)S(1)} %get-tuple-element.37), channel_id=1, source_target_pairs={{0,4},{4,0},{8,12},{12,8},{1,5},{5,1},{9,13},{13,9},{2,6},{6,2},{1... | collective-permute-start | bytes 12296 | tf_op jit(solution)/shard_map/ppermute | solution.py:30
  17.7 1.5 %collective-permute-start.7 = (f32[8,128]{1,0:T(8,128)S(1)}, f32[8,128]{1,0:T(8,128)S(1)}, u32[]{:S(2)}, u32[]{:S(2)}) collective-permute-start(f32[8,128]{1,0:T(8,128)S(1)} %get-tuple-element.38), channel_id=1, source_target_pairs={{0,8},{4,12},{8,0},{12,4},{1,9},{5,13},{9,1},{13,5},{2,10},{6,14},... | collective-permute-start | bytes 12296 | tf_op jit(solution)/shard_map/ppermute | solution.py:30
  19.2 0.0 collective-permute-done.6.refs_6_.refs_10_
  19.2 0.8 %collective-permute-start.8 = (f32[8,128]{1,0:T(8,128)S(1)}, f32[8,128]{1,0:T(8,128)S(1)}, u32[]{:S(2)}, u32[]{:S(2)}) collective-permute-start(f32[8,128]{1,0:T(8,128)S(1)} %get-tuple-element.39), channel_id=1, source_target_pairs={{0,12},{4,8},{8,4},{12,0},{1,13},{5,9},{9,5},{13,1},{2,14},{6,10},... | collective-permute-start | bytes 12296 | tf_op jit(solution)/shard_map/ppermute | solution.py:30
  20.0 2.6 %collective-permute-done.7.refs_7_.refs_11_ = f32[8,128]{1,0:T(8,128)S(1)} collective-permute-done((f32[8,128]{1,0:T(8,128)S(1)}, f32[8,128]{1,0:T(8,128)S(1)}, u32[]{:S(2)}, u32[]{:S(2)}) %collective-permute-start.7) | collective-permute-done | bytes 4128 | tf_op jit(solution)/shard_map/ppermute | solution.py:30
  22.6 0.0 collective-permute-done.8.refs_8_.refs_12_
  22.6 0.0 collective-permute-done.refs_0_
  22.6 0.0 collective-permute-done.1.refs_1_
  22.6 0.0 collective-permute-done.5.refs_5_.refs_9_
  22.7 1.2 %arrive.1 = (bf16[192,128]{1,0:T(8,128)(2,1)S(1)}, bf16[192,128]{1,0:T(8,128)(2,1)S(1)}, bf16[192,128]{1,0:T(8,128)(2,1)S(1)}, f32[128,128]{1,0:T(8,128)S(1)}, f32[16,128]{1,0:T(8,128)S(1)}) custom-call(bf16[128,1024]{1,0:T(8,128)(2,1)S(1)} %collective-permute-done.refs_0_, bf16[128,1024]{1,0:T(8,128)(2,1)S(1)} %collective-permute-done.1.refs_1_, ...), custom_call_target="tpu_custom_call" | custom-call | bytes 4200000 | tf_op jit(solution)/shard_map/arrive/pallas_call | solution.py:471
  23.8 3.5 %collective-permute-start.9 = (bf16[192,128]{1,0:T(8,128)(2,1)S(1)}, bf16[192,128]{1,0:T(8,128)(2,1)S(1)}, u32[]{:S(2)}, u32[]{:S(2)}) collective-permute-start(bf16[192,128]{1,0:T(8,128)(2,1)S(1)} %get-tuple-element.44), channel_id=1, source_target_pairs={{0,3},{1,2},{2,1},{3,0},{4,7},{5,6},{6,5},{7,4},{8,11},{9,10},{10,... | collective-permute-start | bytes 147464 | tf_op jit(solution)/shard_map/ppermute | solution.py:30
  27.3 0.0 collective-permute-start.10
  27.3 0.9 %collective-permute-start.11 = (bf16[192,128]{1,0:T(8,128)(2,1)S(1)}, bf16[192,128]{1,0:T(8,128)(2,1)S(1)}, u32[]{:S(2)}, u32[]{:S(2)}) collective-permute-start(bf16[192,128]{1,0:T(8,128)(2,1)S(1)} %get-tuple-element.46), channel_id=1, source_target_pairs={{0,1},{1,0},{2,3},{3,2},{4,5},{5,4},{6,7},{7,6},{8,9},{9,8},{10,11... | collective-permute-start | bytes 147464 | tf_op jit(solution)/shard_map/ppermute | solution.py:30
  28.2 1.8 %collective-permute-done.9.refs_13_ = bf16[192,128]{1,0:T(8,128)(2,1)S(1)} collective-permute-done((bf16[192,128]{1,0:T(8,128)(2,1)S(1)}, bf16[192,128]{1,0:T(8,128)(2,1)S(1)}, u32[]{:S(2)}, u32[]{:S(2)}) %collective-permute-start.9) | collective-permute-done | bytes 49184 | tf_op jit(solution)/shard_map/ppermute | solution.py:30
  30.1 2.3 %collective-permute-done.10.refs_14_ = bf16[192,128]{1,0:T(8,128)(2,1)S(1)} collective-permute-done((bf16[192,128]{1,0:T(8,128)(2,1)S(1)}, bf16[192,128]{1,0:T(8,128)(2,1)S(1)}, u32[]{:S(2)}, u32[]{:S(2)}) %collective-permute-start.10) | collective-permute-done | bytes 49184 | tf_op jit(solution)/shard_map/ppermute | solution.py:30
  32.3 0.1 collective-permute-done.11.refs_15_
  32.4 2.6 %finish.1 = (bf16[8,1024]{1,0:T(8,128)(2,1)}, bf16[8,1024]{1,0:T(8,128)(2,1)}, bf16[8,128,1024]{2,1,0:T(8,128)(2,1)}) custom-call(bf16[128,1024]{1,0:T(8,128)(2,1)S(1)} %collective-permute-done.refs_0_, bf16[128,1024]{1,0:T(8,128)(2,1)S(1)} %collective-permute-done.1.refs_1_, s32[2,8]{1,0:T(2,128)S(1)} %bitcast.12, ...), custom_call_target="tpu_custom_call", output_to_operand_aliasing={{2}: (17, {})} | custom-call | bytes 11900000 | tf_op jit(solution)/shard_map/finish/pallas_call | solution.py:492
  (7 shorter events, 0.0 us)
Async XLA Ops:
  0.6 13.1 %copy-start = (bf16[1,1,8,128,1024]{4,3,2,1,0:T(8,128)(2,1)S(1)}, bf16[1,1,8,128,1024]{4,3,2,1,0:T(8,128)(2,1)}, u32[]{:S(2)}) copy-start(bf16[1,1,8,128,1024]{4,3,2,1,0:T(8,128)(2,1)} %param.11) | copy-start | bytes 6291460
  0.6 13.1 %copy-start.3 = (s32[8,4]{0,1:T(4,128)S(1)}, s32[8,4]{0,1:T(4,128)}, u32[]{:S(2)}) copy-start(s32[8,4]{0,1:T(4,128)} %param.13) | copy-start | bytes 388
  0.7 13.1 %copy-start.4 = (s32[8]{0:T(128)S(1)}, s32[8]{0:T(128)}, u32[]{:S(2)}) copy-start(s32[8]{0:T(128)} %refs_4_.1) | copy-start | bytes 100
  3.6 12.9 %copy-start.1 = (s32[8,2]{0,1:T(2,128)S(1)}, s32[8,2]{0,1:T(2,128)}, u32[]{:S(2)}) copy-start(s32[8,2]{0,1:T(2,128)} %param.15) | copy-start | bytes 196
  3.6 19.0 %copy-start.2 = (s32[8,4]{0,1:T(4,128)S(1)}, s32[8,4]{0,1:T(4,128)}, u32[]{:S(2)}) copy-start(s32[8,4]{0,1:T(4,128)} %param.14) | copy-start | bytes 388
  3.6 7.4 %collective-permute-start.2 = (bf16[192,128]{1,0:T(8,128)(2,1)S(1)}, bf16[192,128]{1,0:T(8,128)(2,1)S(1)}, u32[]{:S(2)}, u32[]{:S(2)}) collective-permute-start(bf16[192,128]{1,0:T(8,128)(2,1)S(1)} %get-tuple-element.29), channel_id=1, source_target_pairs={{0,3},{1,2},{2,1},{3,0},{4,7},{5,6},{6,5},{7,4},{8,11},{9,10},{10,... | collective-permute-start | bytes 147464 | tf_op jit(solution)/shard_map/ppermute | solution.py:30
  8.7 5.0 %collective-permute-start.3 = (bf16[192,128]{1,0:T(8,128)(2,1)S(1)}, bf16[192,128]{1,0:T(8,128)(2,1)S(1)}, u32[]{:S(2)}, u32[]{:S(2)}) collective-permute-start(bf16[192,128]{1,0:T(8,128)(2,1)S(1)} %get-tuple-element.30), channel_id=1, source_target_pairs={{0,2},{1,3},{2,0},{3,1},{4,6},{5,7},{6,4},{7,5},{8,10},{9,11},{10,... | collective-permute-start | bytes 147464 | tf_op jit(solution)/shard_map/ppermute | solution.py:30
  8.7 5.0 %collective-permute-start.4 = (bf16[192,128]{1,0:T(8,128)(2,1)S(1)}, bf16[192,128]{1,0:T(8,128)(2,1)S(1)}, u32[]{:S(2)}, u32[]{:S(2)}) collective-permute-start(bf16[192,128]{1,0:T(8,128)(2,1)S(1)} %get-tuple-element.31), channel_id=1, source_target_pairs={{0,1},{1,0},{2,3},{3,2},{4,5},{5,4},{6,7},{7,6},{8,9},{9,8},{10,11... | collective-permute-start | bytes 147464 | tf_op jit(solution)/shard_map/ppermute | solution.py:30
  9.4 13.2 %collective-permute-start = (bf16[128,1024]{1,0:T(8,128)(2,1)S(1)}, bf16[128,1024]{1,0:T(8,128)(2,1)S(1)}, u32[]{:S(2)}, u32[]{:S(2)}) collective-permute-start(bf16[128,1024]{1,0:T(8,128)(2,1)S(1)} %get-tuple-element.27), channel_id=1, source_target_pairs={{0,8},{4,12},{8,0},{12,4},{1,9},{5,13},{9,1},{13,5},{2,10},{6,14},... | collective-permute-start | bytes 786440 | tf_op jit(solution)/shard_map/ppermute | solution.py:30
  11.0 11.6 %collective-permute-start.1 = (bf16[128,1024]{1,0:T(8,128)(2,1)S(1)}, bf16[128,1024]{1,0:T(8,128)(2,1)S(1)}, u32[]{:S(2)}, u32[]{:S(2)}) collective-permute-start(bf16[128,1024]{1,0:T(8,128)(2,1)S(1)} %get-tuple-element.28), channel_id=1, source_target_pairs={{0,12},{4,8},{8,4},{12,0},{1,13},{5,9},{9,5},{13,1},{2,14},{6,10},... | collective-permute-start | bytes 786440 | tf_op jit(solution)/shard_map/ppermute | solution.py:30
  16.5 6.2 %collective-permute-start.5 = (bf16[128,1024]{1,0:T(8,128)(2,1)S(1)}, bf16[128,1024]{1,0:T(8,128)(2,1)S(1)}, u32[]{:S(2)}, u32[]{:S(2)}) collective-permute-start(bf16[128,1024]{1,0:T(8,128)(2,1)S(1)} %get-tuple-element.36), channel_id=1, source_target_pairs={{0,4},{4,0},{8,12},{12,8},{1,5},{5,1},{9,13},{13,9},{2,6},{6,2},{1... | collective-permute-start | bytes 786440 | tf_op jit(solution)/shard_map/ppermute | solution.py:30
  17.2 2.0 %collective-permute-start.6 = (f32[8,128]{1,0:T(8,128)S(1)}, f32[8,128]{1,0:T(8,128)S(1)}, u32[]{:S(2)}, u32[]{:S(2)}) collective-permute-start(f32[8,128]{1,0:T(8,128)S(1)} %get-tuple-element.37), channel_id=1, source_target_pairs={{0,4},{4,0},{8,12},{12,8},{1,5},{5,1},{9,13},{13,9},{2,6},{6,2},{1... | collective-permute-start | bytes 12296 | tf_op jit(solution)/shard_map/ppermute | solution.py:30
  17.7 4.9 %collective-permute-start.7 = (f32[8,128]{1,0:T(8,128)S(1)}, f32[8,128]{1,0:T(8,128)S(1)}, u32[]{:S(2)}, u32[]{:S(2)}) collective-permute-start(f32[8,128]{1,0:T(8,128)S(1)} %get-tuple-element.38), channel_id=1, source_target_pairs={{0,8},{4,12},{8,0},{12,4},{1,9},{5,13},{9,1},{13,5},{2,10},{6,14},... | collective-permute-start | bytes 12296 | tf_op jit(solution)/shard_map/ppermute | solution.py:30
  19.2 3.4 %collective-permute-start.8 = (f32[8,128]{1,0:T(8,128)S(1)}, f32[8,128]{1,0:T(8,128)S(1)}, u32[]{:S(2)}, u32[]{:S(2)}) collective-permute-start(f32[8,128]{1,0:T(8,128)S(1)} %get-tuple-element.39), channel_id=1, source_target_pairs={{0,12},{4,8},{8,4},{12,0},{1,13},{5,9},{9,5},{13,1},{2,14},{6,10},... | collective-permute-start | bytes 12296 | tf_op jit(solution)/shard_map/ppermute | solution.py:30
  23.8 6.3 %collective-permute-start.9 = (bf16[192,128]{1,0:T(8,128)(2,1)S(1)}, bf16[192,128]{1,0:T(8,128)(2,1)S(1)}, u32[]{:S(2)}, u32[]{:S(2)}) collective-permute-start(bf16[192,128]{1,0:T(8,128)(2,1)S(1)} %get-tuple-element.44), channel_id=1, source_target_pairs={{0,3},{1,2},{2,1},{3,0},{4,7},{5,6},{6,5},{7,4},{8,11},{9,10},{10,... | collective-permute-start | bytes 147464 | tf_op jit(solution)/shard_map/ppermute | solution.py:30
  27.3 5.0 %collective-permute-start.10 = (bf16[192,128]{1,0:T(8,128)(2,1)S(1)}, bf16[192,128]{1,0:T(8,128)(2,1)S(1)}, u32[]{:S(2)}, u32[]{:S(2)}) collective-permute-start(bf16[192,128]{1,0:T(8,128)(2,1)S(1)} %get-tuple-element.45), channel_id=1, source_target_pairs={{0,2},{1,3},{2,0},{3,1},{4,6},{5,7},{6,4},{7,5},{8,10},{9,11},{10,... | collective-permute-start | bytes 147464 | tf_op jit(solution)/shard_map/ppermute | solution.py:30
  27.3 5.1 %collective-permute-start.11 = (bf16[192,128]{1,0:T(8,128)(2,1)S(1)}, bf16[192,128]{1,0:T(8,128)(2,1)S(1)}, u32[]{:S(2)}, u32[]{:S(2)}) collective-permute-start(bf16[192,128]{1,0:T(8,128)(2,1)S(1)} %get-tuple-element.46), channel_id=1, source_target_pairs={{0,1},{1,0},{2,3},{3,2},{4,5},{5,4},{6,7},{7,6},{8,9},{9,8},{10,11... | collective-permute-start | bytes 147464 | tf_op jit(solution)/shard_map/ppermute | solution.py:30

commit v4 on v3

v4 whole, which is shorter than its diff:
```python
import functools
import math

import jax
import jax.numpy as jnp
from jax import lax
from jax.experimental import pallas as pl
from jax.experimental.pallas import tpu as pltpu
from jax.sharding import PartitionSpec as P

H = 32
KVH = 4
HD = 128
GROUP = H // KVH
CAP = 20.0
SCALE = 1.0 / math.sqrt(HD)
WINDOW = 32
KV_ROWS = 24
EXTRA = 8

SMEM = pl.BlockSpec(memory_space=pltpu.SMEM)
VMEM = pl.BlockSpec(memory_space=pltpu.VMEM)
ANY = pl.BlockSpec(memory_space=pl.ANY)
HBM = pl.BlockSpec(memory_space=pltpu.HBM)
SEND = jnp.bfloat16


def swap(value, axis, distance):
    size = lax.axis_size(axis)
    return lax.ppermute(value, axis, [(i, i ^ distance) for i in range(size)])


def exchange(messages, axis):
    received = [swap(messages[d], axis, d + 1) for d in reversed(range(len(messages)))]
    return received[::-1]


def partner(axis, distance):
    return lax.axis_index(axis) ^ distance


def split(value, size):
    if size & (size - 1) == 0:
        return lax.shift_right_logical(value, size.bit_length() - 1), value & (size - 1)
    return lax.div(value, size), lax.rem(value, size)


def count_up(limit, step, state):
    if limit > 8:
        return lax.fori_loop(0, limit, step, state)
    for i in range(limit):
        state = step(i, state)
    return state


def locate(table, row, column, slots):
    def step(p, found):
        device, slot = split(table[p, row], slots)
        here = device == column
        return jnp.where(here, p, found[0]), jnp.where(here, slot, found[1])

    return count_up(table.shape[0], step, (jnp.int32(0), jnp.int32(0)))


def pair_row(moves, source, target, rows, side):
    def step(j, found):
        valid, row, order, number = found
        ends = [split(moves[i, j], rows) for i in range(2)]
        match = (ends[0][0] == source) & (ends[1][0] == target)
        return (
            jnp.where(match, jnp.int32(1), valid),
            jnp.where(match, ends[side][1], row),
            jnp.where(match, number, order),
            number + jnp.where(ends[side][0] == (source, target)[side], 1, 0),
        )

    return count_up(moves.shape[1], step, (jnp.int32(0),) * 4)[:3]


def head_columns(device, local_heads):
    return pl.ds(pl.multiple_of(split(device * local_heads, GROUP)[0] * HD, HD), HD)


def weight_of(score):
    return jnp.exp(CAP * jnp.tanh(score * (SCALE / CAP)))


def pieces_of(depth, width):
    return [slice(at, min(at + width, depth)) for at in range(0, depth, width)]


def start_copies(pairs, sems):
    copies = [pltpu.make_async_copy(*pair, sems.at[i]) for i, pair in enumerate(pairs)]
    for copy in copies:
        copy.start()
    return copies


def wait_for(copies):
    for copy in copies:
        copy.wait()


def leave_kernel(rows, moves_all, table_all, lengths_all, x_all, pool, *refs):
    pages, (moves, table, lengths, x, sems, page_sems) = refs[:-6], refs[-6:]
    me, column = lax.axis_index("replica"), lax.axis_index("mp")
    page_size, width = pool.shape[1:]
    depth = x.shape[1]
    rest = start_copies(
        ((moves_all, moves), (table_all, table), (lengths_all, lengths), (x_all, x)), sems
    )
    wait_for(rest[:2])
    found = [pair_row(moves, me, partner("replica", s + 1), rows, 0)[1] for s in range(len(pages))]
    copies = start_copies(
        [
            (pool.at[locate(table, row, column, pool.shape[0])[1]], page.at[pl.ds(0, page_size)])
            for row, page in zip(found, pages)
        ],
        page_sems,
    )
    wait_for(rest[2:])
    sublane = lax.broadcasted_iota(jnp.int32, (EXTRA, width), 0)
    first_rows = x[:rows, :].astype(jnp.float32)
    row_ids = lax.broadcasted_iota(jnp.int32, (rows, depth), 0)
    for row, page in zip(found, pages):
        high, low = split(lengths[row], 64)
        extra = jnp.where(sublane == 0, high, low).astype(jnp.float32)
        picked = jnp.sum(jnp.where(row_ids == row, first_rows, 0.0), axis=0, keepdims=True)
        for i, piece in enumerate(pieces_of(depth, width)):
            value = picked[:, piece]
            if value.shape[1] < width:
                value = jnp.concatenate([value, jnp.zeros((1, width - value.shape[1]), jnp.float32)], axis=1)
            extra = jnp.where(sublane == 2 + i, value, extra)
        page[page_size:, :] = extra.astype(jnp.bfloat16)
    wait_for(copies)


def open_kernel(count, local_heads, x, q, weight, *outs):
    rows = q.shape[1]
    wide = [q[i].astype(jnp.float32) for i in range(2)]
    blocks = [wide[i][:, h * HD : (h + 1) * HD] for i in range(2) for h in range(local_heads)]
    packed = jnp.concatenate(blocks, axis=0).astype(jnp.bfloat16)
    query_rows = packed.shape[0]
    for out in outs:
        out[:query_rows, :] = packed
    total = jnp.dot(x[...], weight[...], preferred_element_type=jnp.float32)
    for j in range(KVH):
        parts = []
        for half in range(2):
            start = (half * KVH + j) * HD
            part = total[:, start : start + HD]
            high = part.astype(jnp.bfloat16)
            parts += [high, (part - high.astype(jnp.float32)).astype(jnp.bfloat16)]
        parts = jnp.concatenate(parts, axis=0)
        for s, out in enumerate(outs):

            @pl.when(split(partner("mp", s) * local_heads, GROUP)[0] == j)
            def _(out=out, parts=parts):
                out[query_rows:, :] = parts


def keep_kernel(pool, pool_out, sem):
    pltpu.make_async_copy(pool, pool_out, sem).start()
    pltpu.make_async_copy(pool, pool_out, sem).wait()


def length_of(page, page_size):
    part = page[page_size:, :HD].astype(jnp.float32)
    return part[0:1] * 64.0 + part[1:2]


def own_tokens(messages, rows, query_rows, half):
    tokens = 2 * rows
    start = query_rows + 2 * half * tokens
    total = jnp.zeros((tokens, HD), jnp.float32)
    for message in messages:
        total += message[start : start + tokens, :].astype(jnp.float32)
        total += message[start + tokens : start + 2 * tokens, :].astype(jnp.float32)
    return total.astype(jnp.bfloat16).astype(jnp.float32)


def scores_of(q, keys):
    return lax.dot_general(q, keys, (((1,), (1,)), ((), ())), preferred_element_type=jnp.float32)


def attend_kernel(count, local_heads, table, lengths, pool, *refs):
    messages = refs[:count][::-1]
    num, den, wide = refs[count:]
    column = lax.axis_index("mp")
    rows = lengths.shape[0]
    slots, page_size, width = pool.shape
    both = 2 * local_heads
    for s, message in enumerate(messages):
        wide[s] = message[: both * rows, :].astype(jnp.float32)
    lane = lax.broadcasted_iota(jnp.int32, (both, HD), 1)
    token = lax.broadcasted_iota(jnp.int32, (both, page_size), 1)
    places = [locate(table, r, column, slots) for r in range(rows)]
    columns = [head_columns(partner("mp", s), local_heads) for s in range(count)]
    keys = pool.at[:, :, pl.ds(0, width // 2)]
    values = pool.at[:, :, pl.ds(width // 2, width // 2)]
    cases = [(r, s) for r in range(rows) for s in range(count)]
    scores = {}
    for r, s in cases:
        q = wide[s, pl.ds(r, both, stride=rows), :].astype(jnp.bfloat16)
        scores[r, s] = scores_of(q, keys[places[r][1], :, columns[s]])
    weights = {}
    denominators = [jnp.zeros((both, HD), jnp.float32) for _ in range(count)]
    for r, s in cases:
        inside = token < lengths[r] - places[r][0] * page_size
        weight = jnp.where(inside, weight_of(scores[r, s]), 0.0)
        weights[r, s] = weight.astype(jnp.bfloat16)
        total = jnp.sum(weight, axis=1, keepdims=True)
        denominators[s] += jnp.where(lane == r, total, 0.0)
    for r, s in cases:
        num[s, pl.ds(r, both, stride=rows), :] = jnp.dot(
            weights[r, s], values[places[r][1], :, columns[s]], preferred_element_type=jnp.float32
        )
    for s in range(count):
        den[s] = denominators[s]


def arrive_kernel(count, replicas, local_heads, slots, *refs):
    refs = list(refs)
    take = lambda n: [refs.pop(0) for _ in range(n)]
    pages_in = take(replicas - 2)
    moves, table, projection = take(3)
    pages_in, messages = take(1) + pages_in, take(count)[::-1]
    num_in, den_in = take(2)
    outs = take(count - 1)
    own_num, own_den, own_kv, own_share, num, den, wide = refs
    me, column = lax.axis_index("replica"), lax.axis_index("mp")
    rows = table.shape[1]
    page_size, width = pages_in[0].shape[0] - EXTRA, pages_in[0].shape[1]
    half_rows = local_heads * rows
    num[...] = num_in[...]
    den[...] = den_in[...]
    for s, message in enumerate(messages):
        wide[s] = message[half_rows : 2 * half_rows, :].astype(jnp.float32)
    lane = lax.broadcasted_iota(jnp.int32, (local_heads, HD), 1)
    token = lax.broadcasted_iota(jnp.int32, (local_heads, page_size), 1)
    columns = [head_columns(partner("mp", s), local_heads) for s in range(count)]
    cases = [(d, s) for d in range(1, replicas) for s in range(count)]
    arrivals = [pair_row(moves, partner("replica", d), me, rows, 1) for d in range(1, replicas)]
    movers = moves.shape[1] // replicas
    scores, weights, totals = {}, {}, {}
    for d, s in cases:
        row = arrivals[d - 1][1]
        q = wide[s, pl.ds(row, local_heads, stride=rows), :].astype(jnp.bfloat16)
        keys = pages_in[d - 1].at[pl.ds(0, page_size), pl.ds(0, width // 2)]
        scores[d, s] = scores_of(q, keys[:, columns[s]])
    for d, s in cases:
        index, _ = locate(table, arrivals[d - 1][1], column, slots)
        length = length_of(pages_in[d - 1], page_size)
        inside = (token + index * page_size).astype(jnp.float32) < length
        weight = jnp.where(inside, weight_of(scores[d, s]), 0.0)
        weights[d, s] = weight.astype(jnp.bfloat16)
        totals[d, s] = jnp.sum(weight, axis=1, keepdims=True)
    for d, s in cases:
        values = pages_in[d - 1].at[pl.ds(0, page_size), pl.ds(width // 2, width // 2)]
        scores[d, s] = jnp.dot(weights[d, s], values[:, columns[s]], preferred_element_type=jnp.float32)
    for d, (valid, row, _) in enumerate(arrivals, 1):

        @pl.when(valid == 1)
        def _(d=d, row=row):
            for s in range(count):
                num[s, pl.ds(half_rows + row, local_heads, stride=rows), :] = scores[d, s]
                old = den[s, pl.ds(local_heads, local_heads), :]
                den[s, pl.ds(local_heads, local_heads), :] = jnp.where(lane == row, totals[d, s], old)

    own_num[...] = num[0]
    own_den[...] = den[0]
    depth = projection.shape[0]
    extra = [page[page_size:, :].astype(jnp.float32) for page in pages_in]
    inputs = [
        jnp.concatenate(
            [part[2 + i : 3 + i, : piece.stop - piece.start] for i, piece in enumerate(pieces_of(depth, width))],
            axis=1,
        )
        for part in extra
    ]
    inputs += [jnp.zeros((8 - len(inputs), depth), jnp.float32)]
    inputs = jnp.concatenate(inputs, axis=0).astype(jnp.bfloat16)
    share = jnp.dot(inputs, projection[...], preferred_element_type=jnp.float32)
    arrived = []
    for number in range(movers):
        row = jnp.zeros((1, width), jnp.float32)
        for d, (valid, _, order) in enumerate(arrivals):
            row = jnp.where((valid == 1) & (order == number), share[d : d + 1], row)
        part = jnp.concatenate([row[:, j * HD : (j + 1) * HD] for j in range(2 * KVH)], axis=0)
        high = part.astype(jnp.bfloat16).astype(jnp.float32)
        arrived += [high, part - high]
        own_share[number] = part
    all_kv = []
    for half in range(2):
        own_kv[half] = own_tokens(messages, rows, 2 * half_rows, half)
        all_kv.append(own_kv[half])
    filler = [jnp.zeros((-2 * local_heads % 16, HD), jnp.float32)] if local_heads % 8 else []
    for s, out in enumerate(outs):
        at = s + 1
        parts = den[at]
        high = parts.astype(SEND).astype(jnp.float32)
        parts = high + pltpu.roll(parts - high, HD // 2, 1)
        out[...] = jnp.concatenate([num[at], parts] + filler + all_kv + arrived, axis=0).astype(SEND)


def finish_kernel(count, replicas, local_heads, *refs):
    refs = list(refs)
    take = lambda n: [refs.pop(0) for _ in range(n)]
    pages_in = take(replicas - 2)
    moves_all, table_all, lengths_all, kv, share, q, num, den = take(8)
    pages_in, messages = take(1) + pages_in, take(count - 1)[::-1]
    pool_raw, _, first, second, pool = take(5)
    moves, table, lengths, held, full, arrived, windows, results, sems, page_sems, write_sems, out_sems = refs
    tables = start_copies(((moves_all, moves), (table_all, table), (lengths_all, lengths)), sems)
    me, column = lax.axis_index("replica"), lax.axis_index("mp")
    rows = lengths.shape[0]
    slots, page_size, width = pool_raw.shape
    both = 2 * local_heads
    query_rows = both * rows
    movers = moves.shape[1] // replicas
    head = split(column * local_heads, GROUP)[0]

    kv_base = messages[0].shape[0] - 4 * rows - 16 * movers
    for s in range(count):
        device = partner("mp", s)
        for half in range(2):
            if s == 0:
                chunk = kv[half]
            else:
                start = kv_base + half * 2 * rows
                chunk = messages[s - 1][start : start + 2 * rows, :].astype(jnp.float32)

            def place(half=half, device=device, chunk=chunk):
                columns = head_columns(device, local_heads)
                full.at[pl.ds(0, 2 * rows), pl.ds(half * (width // 2), width // 2)][:, columns] = chunk

            if local_heads == GROUP:
                place()
            else:
                pl.when(split(device * local_heads, GROUP)[1] == 0)(place)
    for number in range(movers):
        total = share[number]
        for message in messages:
            start = kv_base + 4 * rows + 16 * number
            part = message[start : start + 16, :].astype(jnp.float32)
            total += part[: 2 * KVH] + part[2 * KVH :]
        total = total.astype(jnp.bfloat16).astype(jnp.float32)
        arrived[number] = total
        for j in range(2 * KVH):
            full[2 * rows + number : 2 * rows + number + 1, j * HD : (j + 1) * HD] = total[j : j + 1, :]
    sums = den[...]
    for message in messages:
        part = message[query_rows : query_rows + both, :].astype(jnp.float32)
        sums += part + pltpu.roll(part, HD // 2, 1)
    sums = jnp.transpose(sums)[:rows, :]

    wait_for(tables)
    arrivals, copies, kept, plans = [], [], [jnp.bool_(True)] * rows, []

    def add_plan(active, row, length, first_token, source, r=None):
        index, slot = locate(table, row, column, slots)
        at = length - index * page_size
        touched = active & (at >= -1) & (at < page_size)
        start = jnp.clip(at, 0, page_size - WINDOW) & -16
        span = pl.ds(pl.multiple_of(start, 16), WINDOW)
        n = len(plans)
        source = source.at[slot] if r is not None else source
        write = pltpu.make_async_copy(windows.at[n], pool.at[slot, span], write_sems.at[n])
        plans.append((touched, source, span, write, first_token, rows + row, at - start))
        return slot

    for s, page in enumerate(pages_in):
        valid, row, order = pair_row(moves, partner("replica", s + 1), me, rows, 1)
        valid = valid == 1
        length = jnp.max(length_of(page, page_size)).astype(jnp.int32)
        page = page.at[pl.ds(0, page_size)]
        slot = add_plan(valid, row, length, 2 * rows + order, page)
        copies.append(pltpu.make_async_copy(page, pool.at[slot], page_sems.at[s]))
        pl.when(valid)(copies[-1].start)
        arrivals.append((valid, row, order))
        kept = [stays & ~(valid & (row == r)) for r, stays in enumerate(kept)]
    for r in range(rows):
        add_plan(kept[r], r, lengths[r], r, pool_raw, r)

    for half in range(2):
        held[half] = kv[half, :rows, :]
        for valid, row, order in arrivals:

            @pl.when(valid)
            def _(half=half, row=row, order=order):
                held[half, pl.ds(row, 1), :] = arrived[order, pl.ds(head + half * KVH, 1), :]

    outs = []
    for step, out in enumerate((first, second)):
        pieces = []
        for h in range(local_heads):
            at = (step * local_heads + h) * rows
            query = q[at : at + rows, :].astype(jnp.float32)
            numerator = num[at : at + rows, :]
            for message in messages:
                numerator += message[at : at + rows, :].astype(jnp.float32)
            denominator = sums[:, step * local_heads + h : step * local_heads + h + 1]
            extra = [(kv[0, :rows, :], kv[1, :rows, :])]
            if step == 1:
                extra = [(held[0], held[1]), (kv[0, rows:, :], kv[1, rows:, :])]
            for key, value in extra:
                weight = weight_of(jnp.sum(query * key, axis=1, keepdims=True))
                numerator += weight.astype(jnp.bfloat16).astype(jnp.float32) * value
                denominator += weight
            pieces.append(numerator / denominator)
        results[step] = jnp.concatenate(pieces, axis=1).astype(out.dtype)
        outs.append(pltpu.make_async_copy(results.at[step], out, out_sems.at[step]))
        outs[-1].start()

    for (valid, _, _), copy in zip(arrivals, copies):
        pl.when(valid)(copy.wait)
    place_ids = lax.broadcasted_iota(jnp.int32, (WINDOW, width), 0)
    for n, (touched, source, span, write, token, next_token, offset) in enumerate(plans):

        @pl.when(touched)
        def _(n=n, source=source, span=span, write=write, token=token, next_token=next_token, offset=offset):
            old = source[span, :].astype(jnp.float32)
            new = jnp.where(place_ids == offset, full[pl.ds(token, 1), :], old)
            new = jnp.where(place_ids == offset + 1, full[pl.ds(next_token, 1), :], new)
            windows[n] = new.astype(jnp.bfloat16)
            write.start()

    for plan in plans:
        pl.when(plan[0])(plan[3].wait)
    wait_for(outs)


def cost(microseconds):
    return pl.CostEstimate(flops=0, transcendentals=0, bytes_accessed=int(microseconds * 3.5e6))


def in_vmem(value):
    return pltpu.with_memory_space_constraint(value, pltpu.VMEM)


def in_hbm(value):
    return pltpu.with_memory_space_constraint(value, pltpu.HBM)


def params(megabytes=32, **rest):
    return pltpu.CompilerParams(vmem_limit_bytes=megabytes << 20, **rest)


def body(layer_input, kv_weight, queries, kv_pool, lengths, block_table, new_table, migrations):
    replicas, count = lax.axis_size("replica"), lax.axis_size("mp")
    rows = lengths.shape[0]
    pool = kv_pool[0, 0]
    slots, page_size, width = pool.shape
    local_heads = queries.shape[2] // HD
    both = 2 * local_heads
    query_rows = both * rows
    depth = layer_input.shape[2]
    f32, bf16 = jnp.float32, jnp.bfloat16
    moves, old_table, table_after = migrations.T, block_table.T, new_table.T
    shape = jax.ShapeDtypeStruct

    message_rows = query_rows + 8 * rows
    movers = migrations.shape[0] // replicas
    inputs = layer_input.reshape(2 * rows, depth)
    leaving = pl.pallas_call(
        functools.partial(leave_kernel, rows),
        out_shape=[shape((page_size + EXTRA, width), bf16)] * (replicas - 1),
        in_specs=[HBM] * 5,
        out_specs=[VMEM] * (replicas - 1),
        scratch_shapes=[
            pltpu.SMEM(moves.shape, jnp.int32),
            pltpu.SMEM(old_table.shape, jnp.int32),
            pltpu.SMEM(lengths.shape, jnp.int32),
            pltpu.VMEM((2 * rows, depth), bf16),
            pltpu.SemaphoreType.DMA((4,)),
            pltpu.SemaphoreType.DMA((replicas - 1,)),
        ],
        compiler_params=params(),
        cost_estimate=cost(2.0),
        name="leave",
    )(*map(in_hbm, (moves, old_table, lengths, inputs, pool)))
    pages_in = exchange(leaving, "replica")

    weight_near, inputs_near, queries_near = map(in_vmem, (kv_weight, inputs, queries))
    sent = pl.pallas_call(
        functools.partial(open_kernel, count, local_heads),
        out_shape=[shape((message_rows, HD), bf16)] * count,
        in_specs=[VMEM] * 3,
        out_specs=[VMEM] * count,
        compiler_params=params(),
        cost_estimate=cost(1.2),
        name="open",
    )(inputs_near, queries_near, weight_near)
    sent, pages_in[0] = lax.optimization_barrier((list(sent), pages_in[0]))
    messages = [sent[0]] + exchange(sent[1:], "mp")

    pool_near = in_vmem(pool)
    pool_copy = pl.pallas_call(
        keep_kernel,
        out_shape=shape(pool.shape, bf16),
        in_specs=[VMEM],
        out_specs=ANY,
        scratch_shapes=[pltpu.SemaphoreType.DMA(())],
        compiler_params=params(),
        cost_estimate=cost(1.6),
        name="keep",
    )(pool_near)
    num, den = pl.pallas_call(
        functools.partial(attend_kernel, count, local_heads),
        out_shape=[shape((count, query_rows, HD), f32), shape((count, both, HD), f32)],
        in_specs=[SMEM, SMEM, VMEM] + [VMEM] * count,
        out_specs=[VMEM, VMEM],
        scratch_shapes=[pltpu.VMEM((count, query_rows, HD), f32)],
        compiler_params=params(),
        cost_estimate=cost(1.5),
        name="attend",
    )(old_table, lengths, pool_near, *messages[::-1])

    sum_rows = query_rows + -(-both // 16) * 16 + 4 * rows + 16 * movers
    *sums, num, den, kv, share = pl.pallas_call(
        functools.partial(arrive_kernel, count, replicas, local_heads, slots),
        out_shape=[shape((sum_rows, HD), SEND)] * (count - 1)
        + [shape((query_rows, HD), f32), shape((both, HD), f32)]
        + [shape((2, 2 * rows, HD), f32), shape((movers, 2 * KVH, HD), f32)],
        in_specs=[VMEM] * (replicas - 2)
        + [SMEM, SMEM, VMEM, VMEM]
        + [VMEM] * count
        + [VMEM] * 2,
        out_specs=[VMEM] * (count + 3),
        scratch_shapes=[
            pltpu.VMEM((count, query_rows, HD), f32),
            pltpu.VMEM((count, both, HD), f32),
            pltpu.VMEM((count, query_rows // 2, HD), f32),
        ],
        compiler_params=params(),
        cost_estimate=cost(1.2),
        name="arrive",
    )(*pages_in[1:], moves, table_after, weight_near, pages_in[0], *messages[::-1], num, den)
    sums_in = exchange(sums, "mp")

    first, second, pool_after = pl.pallas_call(
        functools.partial(finish_kernel, count, replicas, local_heads),
        out_shape=[
            shape((rows, local_heads * HD), bf16),
            shape((rows, local_heads * HD), bf16),
            shape(pool.shape, bf16),
        ],
        in_specs=[VMEM] * (replicas - 2) + [ANY] * 3 + [VMEM] * (6 + count - 1) + [VMEM, ANY],
        out_specs=[ANY] * 3,
        scratch_shapes=[
            pltpu.SMEM(moves.shape, jnp.int32),
            pltpu.SMEM(table_after.shape, jnp.int32),
            pltpu.SMEM(lengths.shape, jnp.int32),
            pltpu.VMEM((2, rows, HD), f32),
            pltpu.VMEM((KV_ROWS, width), f32),
            pltpu.VMEM((movers, 2 * KVH, HD), f32),
            pltpu.VMEM((rows + replicas - 1, WINDOW, width), bf16),
            pltpu.VMEM((2, rows, local_heads * HD), bf16),
            pltpu.SemaphoreType.DMA((3,)),
            pltpu.SemaphoreType.DMA((replicas - 1,)),
            pltpu.SemaphoreType.DMA((rows + replicas - 1,)),
            pltpu.SemaphoreType.DMA((2,)),
        ],
        input_output_aliases={8 + replicas - 1 + (count - 1) + 1: 2},
        compiler_params=params(),
        cost_estimate=cost(2.5),
        name="finish",
    )(
        *pages_in[1:],
        *(moves, table_after, lengths),
        *(kv, share, messages[0], num, den, pages_in[0]),
        *sums_in[::-1],
        *(pool_near, pool_copy),
    )
    return first, second, pool_after[None, None]


def solution(mesh):
    return jax.shard_map(
        body,
        mesh=mesh,
        in_specs=(
            P(None, ("groups", "replica"), "mp"),
            P("mp", None),
            P(None, ("groups", "replica"), "mp"),
            P(("groups", "replica"), "mp", None, None, None),
            P(("groups", "replica")),
            P(("groups", "replica"), None),
            P(("groups", "replica"), None),
            P("groups", None),
        ),
        out_specs=(
            P(("groups", "replica"), "mp"),
            P(("groups", "replica"), "mp"),
            P(("groups", "replica"), "mp", None, None, None),
        ),
        check_vma=False,
    )
```

time: 35.6 us -> 32.3 us (0.907); the launches traced: 35 us -> 32.2 us
  waiting for transfers between devices: 9.59 us -> 7.04 us
  starting transfers between devices: 14.7 us -> 12.2 us
  local copies, waits for them, and re-layouts: 0.03 us -> 2.36 us
    ppermute x12 -> x9, waiting for transfers between devices: 9.59 us -> 7.04 us  [swap(): return lax.ppermute(value, axis, [(i, i ^ distance) for i in range(size)])]
    ppermute x12 -> x9, starting transfers between devices: 14.7 us -> 12.2 us  [swap(): return lax.ppermute(value, axis, [(i, i ^ distance) for i in range(size)])]
    unnamed x10 -> x18, local copies, waits for them, and re-layouts: 0.03 us -> 2.36 us
    pallas_call x1, Pallas kernels: 2.71 us -> 1.53 us  [body(): pl.pallas_call(functools.partial(attend_kernel, count, local_heads), out_...]
    pallas_call x1, Pallas kernels: 1.16 us -> 1.75 us  [body(): pl.pallas_call(functools.partial(arrive_kernel, count, replicas, local_he...]
    pallas_call x2 -> x3, Pallas kernels: 3.53 us -> 4.07 us  [the longest x1 2.06 us: body(): pl.pallas_call(functools.partial(leave_kernel, rows), out_shape=[shape((p...]
  transfers between devices with their start and end apart: 12 -> 9, of which waited for: 5 -> 4; matrix products, arithmetic and copies ran while one was open for 0% -> 0% of each run, Pallas kernels for 9% -> 11%
where the time goes in v4:
time: 32.3 us; the launch traced here: 32.2 us
  starting transfers between devices  12.2 us (38%)
  Pallas kernels  9.83 us (30%)
  waiting for transfers between devices  7.04 us (22%)
  local copies, waits for them, and re-layouts  2.36 us (7%)
  between operations  0.76 us (2%)
    ppermute x9, starting transfers between devices, swap(): return lax.ppermute(value, axis, [(i, i ^ distance) for i in range(size)])  12.2 us
    ppermute x9, waiting for transfers between devices, swap(): return lax.ppermute(value, axis, [(i, i ^ distance) for i in range(size)])  7.04 us
    pallas_call x1, Pallas kernels, body(): pl.pallas_call(functools.partial(finish_kernel, count, replicas, local_he...  2.49 us
    unnamed x18, local copies, waits for them, and re-layouts  2.36 us
    pallas_call x1, Pallas kernels, body(): pl.pallas_call(functools.partial(leave_kernel, rows), out_shape=[shape((p...  2.06 us
    pallas_call x1, Pallas kernels, body(): pl.pallas_call(functools.partial(arrive_kernel, count, replicas, local_he...  1.75 us
    pallas_call x1, Pallas kernels, body(): pl.pallas_call(functools.partial(attend_kernel, count, local_heads), out_...  1.53 us
    pallas_call x1, Pallas kernels, body(): pl.pallas_call(keep_kernel, out_shape=shape(pool.shape, bf16), in_specs=[...  1.33 us
  transfers between devices with their start and end apart: 9, of which 4 were waited for; matrix products, arithmetic and copies ran while one was open for 0% of the time, Pallas kernels for 11%

profile of v4, /device:TPU:0, one launch (start us, length us, event | category | flops | bytes accessed | tf_op | source)
XLA Modules:
  0.0 32.2 jit_solution(9992851879208322001)
XLA Ops:
  0.6 0.0 copy-start.3
  0.6 0.0 copy-start.4
  0.7 0.0 copy-start.7
  0.7 2.1 %leave.1 = (bf16[136,1024]{1,0:T(8,128)(2,1)S(1)}, bf16[136,1024]{1,0:T(8,128)(2,1)S(1)}, bf16[136,1024]{1,0:T(8,128)(2,1)S(1)}) custom-call(s32[2,8]{1,0:T(2,128)} %bitcast.12, s32[4,8]{1,0:T(4,128)} %bitcast.17, s32[8]{0:T(128)} %refs_4_.3, bf16[16,2048]{1,0:T(8,128)(2,1)} %bitcast.10, bf16[8,128,1024]{2,1,0:T(8,128)(2,1)} %bitcast.6), custom_call_target="tpu_custom_call" | custom-call | bytes 7000000 | tf_op jit(solution)/shard_map/leave/pallas_call | solution.py:465
  2.7 0.5 %collective-permute-start.2 = (bf16[136,1024]{1,0:T(8,128)(2,1)S(1)}, bf16[136,1024]{1,0:T(8,128)(2,1)S(1)}, u32[]{:S(2)}, u32[]{:S(2)}) collective-permute-start(bf16[136,1024]{1,0:T(8,128)(2,1)S(1)} %get-tuple-element.33), channel_id=1, source_target_pairs={{0,4},{4,0},{8,12},{12,8},{1,5},{5,1},{9,13},{13,9},{2,6},{6,2},{1... | collective-permute-start | bytes 835592 | tf_op jit(solution)/shard_map/ppermute | solution.py:30
  3.2 2.6 %collective-permute-start = (bf16[136,1024]{1,0:T(8,128)(2,1)S(1)}, bf16[136,1024]{1,0:T(8,128)(2,1)S(1)}, u32[]{:S(2)}, u32[]{:S(2)}) collective-permute-start(bf16[136,1024]{1,0:T(8,128)(2,1)S(1)} %get-tuple-element.27), channel_id=1, source_target_pairs={{0,8},{4,12},{8,0},{12,4},{1,9},{5,13},{9,1},{13,5},{2,10},{6,14},... | collective-permute-start | bytes 835592 | tf_op jit(solution)/shard_map/ppermute | solution.py:30
  5.8 0.1 collective-permute-start.1
  5.9 0.0 copy-done.4
  5.9 2.3 %copy-done.1 = bf16[2048,1024]{1,0:T(8,128)(2,1)S(1)} copy-done((bf16[2048,1024]{1,0:T(8,128)(2,1)S(1)}, bf16[2048,1024]{1,0:T(8,128)(2,1)}, u32[]{:S(2)}) %copy-start.1) | copy-done | bytes 4194328
  8.2 0.7 %open.1 = (bf16[192,128]{1,0:T(8,128)(2,1)S(1)}, bf16[192,128]{1,0:T(8,128)(2,1)S(1)}, bf16[192,128]{1,0:T(8,128)(2,1)S(1)}, bf16[192,128]{1,0:T(8,128)(2,1)S(1)}) custom-call(bf16[16,2048]{1,0:T(8,128)(2,1)S(1)} %bitcast.11, bf16[2,8,1024]{2,1,0:T(8,128)(2,1)S(1)} %copy-done.4, bf16[2048,1024]{1,0:T(8,128)(2,1)S(1)} %copy-done.1), custom_call_target="tpu_custom_call" | custom-call | bytes 4200000 | tf_op jit(solution)/shard_map/open/pallas_call | solution.py:485
  8.9 0.0 copy-start.5
  8.9 0.0 copy-start.6
  8.9 0.0 collective-permute-done.2.refs_5_.refs_10_
  8.9 3.9 %collective-permute-start.3 = (bf16[192,128]{1,0:T(8,128)(2,1)S(1)}, bf16[192,128]{1,0:T(8,128)(2,1)S(1)}, u32[]{:S(2)}, u32[]{:S(2)}) collective-permute-start(bf16[192,128]{1,0:T(8,128)(2,1)S(1)} %get-tuple-element.35), channel_id=1, source_target_pairs={{0,3},{1,2},{2,1},{3,0},{4,7},{5,6},{6,5},{7,4},{8,11},{9,10},{10,... | collective-permute-start | bytes 147464 | tf_op jit(solution)/shard_map/ppermute | solution.py:30
  12.9 0.0 collective-permute-start.4
  12.9 0.6 %collective-permute-start.5 = (bf16[192,128]{1,0:T(8,128)(2,1)S(1)}, bf16[192,128]{1,0:T(8,128)(2,1)S(1)}, u32[]{:S(2)}, u32[]{:S(2)}) collective-permute-start(bf16[192,128]{1,0:T(8,128)(2,1)S(1)} %get-tuple-element.37), channel_id=1, source_target_pairs={{0,1},{1,0},{2,3},{3,2},{4,5},{5,4},{6,7},{7,6},{8,9},{9,8},{10,11... | collective-permute-start | bytes 147464 | tf_op jit(solution)/shard_map/ppermute | solution.py:30
  13.5 1.7 %collective-permute-done.3.refs_0_.refs_6_ = bf16[192,128]{1,0:T(8,128)(2,1)S(1)} collective-permute-done((bf16[192,128]{1,0:T(8,128)(2,1)S(1)}, bf16[192,128]{1,0:T(8,128)(2,1)S(1)}, u32[]{:S(2)}, u32[]{:S(2)}) %collective-permute-start.3) | collective-permute-done | bytes 49184 | tf_op jit(solution)/shard_map/ppermute | solution.py:30
  15.2 2.8 %collective-permute-done.4.refs_1_.refs_7_ = bf16[192,128]{1,0:T(8,128)(2,1)S(1)} collective-permute-done((bf16[192,128]{1,0:T(8,128)(2,1)S(1)}, bf16[192,128]{1,0:T(8,128)(2,1)S(1)}, u32[]{:S(2)}, u32[]{:S(2)}) %collective-permute-start.4) | collective-permute-done | bytes 49184 | tf_op jit(solution)/shard_map/ppermute | solution.py:30
  18.0 0.0 collective-permute-done.5.refs_2_.refs_8_
  18.0 0.0 copy-done.8
  18.0 1.5 %attend.1 = (f32[4,128,128]{2,1,0:T(8,128)S(1)}, f32[4,16,128]{2,1,0:T(8,128)S(1)}) custom-call(s32[4,8]{1,0:T(4,128)S(1)} %bitcast.18, s32[8]{0:T(128)S(1)} %copy-done.8, bf16[8,128,1024]{2,1,0:T(8,128)(2,1)S(1)} %bitcast.7, bf16[192,128]{1,0:T(8,128)(2,1)S(1)} %collective-permute-done.3.refs_0_.refs_6_, ...), custom_call_target="tpu_custom_call" | custom-call | bytes 5250000 | tf_op jit(solution)/shard_map/attend/pallas_call | solution.py:508
  19.6 0.0 collective-permute-done.refs_0_
  19.6 0.0 collective-permute-done.1.refs_1_
  19.6 1.7 %arrive.1 = (bf16[208,128]{1,0:T(8,128)(2,1)S(1)}, bf16[208,128]{1,0:T(8,128)(2,1)S(1)}, bf16[208,128]{1,0:T(8,128)(2,1)S(1)}, f32[128,128]{1,0:T(8,128)S(1)}, f...) custom-call(bf16[136,1024]{1,0:T(8,128)(2,1)S(1)} %collective-permute-done.refs_0_, ...), custom_call_target="tpu_custom_call" | custom-call | bytes 4200000 | tf_op jit(solution)/shard_map/arrive/pallas_call | solution.py:520
  21.4 2.9 %collective-permute-start.6 = (bf16[208,128]{1,0:T(8,128)(2,1)S(1)}, bf16[208,128]{1,0:T(8,128)(2,1)S(1)}, u32[]{:S(2)}, u32[]{:S(2)}) collective-permute-start(bf16[208,128]{1,0:T(8,128)(2,1)S(1)} %get-tuple-element.45), channel_id=1, source_target_pairs={{0,3},{1,2},{2,1},{3,0},{4,7},{5,6},{6,5},{7,4},{8,11},{9,10},{10,... | collective-permute-start | bytes 159752 | tf_op jit(solution)/shard_map/ppermute | solution.py:30
  24.3 0.0 collective-permute-start.7
  24.3 1.5 %collective-permute-start.8 = (bf16[208,128]{1,0:T(8,128)(2,1)S(1)}, bf16[208,128]{1,0:T(8,128)(2,1)S(1)}, u32[]{:S(2)}, u32[]{:S(2)}) collective-permute-start(bf16[208,128]{1,0:T(8,128)(2,1)S(1)} %get-tuple-element.47), channel_id=1, source_target_pairs={{0,1},{1,0},{2,3},{3,2},{4,5},{5,4},{6,7},{7,6},{8,9},{9,8},{10,11... | collective-permute-start | bytes 159752 | tf_op jit(solution)/shard_map/ppermute | solution.py:30
  25.8 1.3 %keep.1.refs_15_ = bf16[8,128,1024]{2,1,0:T(8,128)(2,1)} custom-call(bf16[8,128,1024]{2,1,0:T(8,128)(2,1)S(1)} %bitcast.8), custom_call_target="tpu_custom_call" | custom-call | bytes 5600000 | tf_op jit(solution)/shard_map/keep/pallas_call | solution.py:498
  27.1 0.8 %collective-permute-done.6.refs_11_ = bf16[208,128]{1,0:T(8,128)(2,1)S(1)} collective-permute-done((bf16[208,128]{1,0:T(8,128)(2,1)S(1)}, bf16[208,128]{1,0:T(8,128)(2,1)S(1)}, u32[]{:S(2)}, u32[]{:S(2)}) %collective-permute-start.6) | collective-permute-done | bytes 53280 | tf_op jit(solution)/shard_map/ppermute | solution.py:30
  28.0 1.7 %collective-permute-done.7.refs_12_ = bf16[208,128]{1,0:T(8,128)(2,1)S(1)} collective-permute-done((bf16[208,128]{1,0:T(8,128)(2,1)S(1)}, bf16[208,128]{1,0:T(8,128)(2,1)S(1)}, u32[]{:S(2)}, u32[]{:S(2)}) %collective-permute-start.7) | collective-permute-done | bytes 53280 | tf_op jit(solution)/shard_map/ppermute | solution.py:30
  29.7 0.0 collective-permute-done.8.refs_13_
  29.7 2.5 %finish.1 = (bf16[8,1024]{1,0:T(8,128)(2,1)}, bf16[8,1024]{1,0:T(8,128)(2,1)}, bf16[8,128,1024]{2,1,0:T(8,128)(2,1)}) custom-call(bf16[136,1024]{1,0:T(8,128)(2,1)S(1)} %collective-permute-done.refs_0_, bf16[136,1024]{1,0:T(8,128)(2,1)S(1)} %collective-permute-done.1.refs_1_, s32[2,8]{1,0:T(2,128)S(1)} %bitcast.14, ...), custom_call_target="tpu_custom_call", output_to_operand_aliasing={{2}: (15, {})} | custom-call | bytes 8750000 | tf_op jit(solution)/shard_map/finish/pallas_call | solution.py:541
  (10 shorter events, 0.0 us)
Async XLA Ops:
  0.6 5.3 %copy-start.3 = (bf16[2,8,2048]{2,1,0:T(8,128)(2,1)S(1)}, bf16[2,8,2048]{2,1,0:T(8,128)(2,1)}, u32[]{:S(2)}) copy-start(bf16[2,8,2048]{2,1,0:T(8,128)(2,1)} %param.8) | copy-start | bytes 196612
  0.6 5.2 %copy-start.4 = (bf16[2,8,1024]{2,1,0:T(8,128)(2,1)S(1)}, bf16[2,8,1024]{2,1,0:T(8,128)(2,1)}, u32[]{:S(2)}) copy-start(bf16[2,8,1024]{2,1,0:T(8,128)(2,1)} %q.1) | copy-start | bytes 98308
  0.7 17.4 %copy-start.7 = (s32[8,4]{0,1:T(4,128)S(1)}, s32[8,4]{0,1:T(4,128)}, u32[]{:S(2)}) copy-start(s32[8,4]{0,1:T(4,128)} %param.13) | copy-start | bytes 388
  2.7 6.2 %collective-permute-start.2 = (bf16[136,1024]{1,0:T(8,128)(2,1)S(1)}, bf16[136,1024]{1,0:T(8,128)(2,1)S(1)}, u32[]{:S(2)}, u32[]{:S(2)}) collective-permute-start(bf16[136,1024]{1,0:T(8,128)(2,1)S(1)} %get-tuple-element.33), channel_id=1, source_target_pairs={{0,4},{4,0},{8,12},{12,8},{1,5},{5,1},{9,13},{13,9},{2,6},{6,2},{1... | collective-permute-start | bytes 835592 | tf_op jit(solution)/shard_map/ppermute | solution.py:30
  3.2 16.3 %collective-permute-start = (bf16[136,1024]{1,0:T(8,128)(2,1)S(1)}, bf16[136,1024]{1,0:T(8,128)(2,1)S(1)}, u32[]{:S(2)}, u32[]{:S(2)}) collective-permute-start(bf16[136,1024]{1,0:T(8,128)(2,1)S(1)} %get-tuple-element.27), channel_id=1, source_target_pairs={{0,8},{4,12},{8,0},{12,4},{1,9},{5,13},{9,1},{13,5},{2,10},{6,14},... | collective-permute-start | bytes 835592 | tf_op jit(solution)/shard_map/ppermute | solution.py:30
  5.8 12.2 %copy-start.8 = (s32[8]{0:T(128)S(1)}, s32[8]{0:T(128)}, u32[]{:S(2)}) copy-start(s32[8]{0:T(128)} %refs_4_.3) | copy-start | bytes 100
  5.8 12.2 %copy-start = (bf16[1,1,8,128,1024]{4,3,2,1,0:T(8,128)(2,1)S(1)}, bf16[1,1,8,128,1024]{4,3,2,1,0:T(8,128)(2,1)}, u32[]{:S(2)}) copy-start(bf16[1,1,8,128,1024]{4,3,2,1,0:T(8,128)(2,1)} %param.11) | copy-start | bytes 6291460
  5.8 13.8 %collective-permute-start.1 = (bf16[136,1024]{1,0:T(8,128)(2,1)S(1)}, bf16[136,1024]{1,0:T(8,128)(2,1)S(1)}, u32[]{:S(2)}, u32[]{:S(2)}) collective-permute-start(bf16[136,1024]{1,0:T(8,128)(2,1)S(1)} %get-tuple-element.28), channel_id=1, source_target_pairs={{0,12},{4,8},{8,4},{12,0},{1,13},{5,9},{9,5},{13,1},{2,14},{6,10},... | collective-permute-start | bytes 835592 | tf_op jit(solution)/shard_map/ppermute | solution.py:30
  5.9 2.3 %copy-start.1 = (bf16[2048,1024]{1,0:T(8,128)(2,1)S(1)}, bf16[2048,1024]{1,0:T(8,128)(2,1)}, u32[]{:S(2)}) copy-start(bf16[2048,1024]{1,0:T(8,128)(2,1)} %refs_4_.2) | copy-start | bytes 12582916
  8.2 11.4 %copy-start.2 = (bf16[2048,1024]{1,0:T(8,128)(2,1)S(1)}, bf16[2048,1024]{1,0:T(8,128)(2,1)}, u32[]{:S(2)}) copy-start(bf16[2048,1024]{1,0:T(8,128)(2,1)} %refs_4_.2) | copy-start | bytes 12582916
  8.9 10.7 %copy-start.5 = (s32[8,2]{0,1:T(2,128)S(1)}, s32[8,2]{0,1:T(2,128)}, u32[]{:S(2)}) copy-start(s32[8,2]{0,1:T(2,128)} %param.15) | copy-start | bytes 196
  8.9 10.7 %copy-start.6 = (s32[8,4]{0,1:T(4,128)S(1)}, s32[8,4]{0,1:T(4,128)}, u32[]{:S(2)}) copy-start(s32[8,4]{0,1:T(4,128)} %param.14) | copy-start | bytes 388
  8.9 6.3 %collective-permute-start.3 = (bf16[192,128]{1,0:T(8,128)(2,1)S(1)}, bf16[192,128]{1,0:T(8,128)(2,1)S(1)}, u32[]{:S(2)}, u32[]{:S(2)}) collective-permute-start(bf16[192,128]{1,0:T(8,128)(2,1)S(1)} %get-tuple-element.35), channel_id=1, source_target_pairs={{0,3},{1,2},{2,1},{3,0},{4,7},{5,6},{6,5},{7,4},{8,11},{9,10},{10,... | collective-permute-start | bytes 147464 | tf_op jit(solution)/shard_map/ppermute | solution.py:30
  12.9 5.1 %collective-permute-start.4 = (bf16[192,128]{1,0:T(8,128)(2,1)S(1)}, bf16[192,128]{1,0:T(8,128)(2,1)S(1)}, u32[]{:S(2)}, u32[]{:S(2)}) collective-permute-start(bf16[192,128]{1,0:T(8,128)(2,1)S(1)} %get-tuple-element.36), channel_id=1, source_target_pairs={{0,2},{1,3},{2,0},{3,1},{4,6},{5,7},{6,4},{7,5},{8,10},{9,11},{10,... | collective-permute-start | bytes 147464 | tf_op jit(solution)/shard_map/ppermute | solution.py:30
  12.9 5.1 %collective-permute-start.5 = (bf16[192,128]{1,0:T(8,128)(2,1)S(1)}, bf16[192,128]{1,0:T(8,128)(2,1)S(1)}, u32[]{:S(2)}, u32[]{:S(2)}) collective-permute-start(bf16[192,128]{1,0:T(8,128)(2,1)S(1)} %get-tuple-element.37), channel_id=1, source_target_pairs={{0,1},{1,0},{2,3},{3,2},{4,5},{5,4},{6,7},{7,6},{8,9},{9,8},{10,11... | collective-permute-start | bytes 147464 | tf_op jit(solution)/shard_map/ppermute | solution.py:30
  21.4 6.6 %collective-permute-start.6 = (bf16[208,128]{1,0:T(8,128)(2,1)S(1)}, bf16[208,128]{1,0:T(8,128)(2,1)S(1)}, u32[]{:S(2)}, u32[]{:S(2)}) collective-permute-start(bf16[208,128]{1,0:T(8,128)(2,1)S(1)} %get-tuple-element.45), channel_id=1, source_target_pairs={{0,3},{1,2},{2,1},{3,0},{4,7},{5,6},{6,5},{7,4},{8,11},{9,10},{10,... | collective-permute-start | bytes 159752 | tf_op jit(solution)/shard_map/ppermute | solution.py:30
  24.3 5.4 %collective-permute-start.7 = (bf16[208,128]{1,0:T(8,128)(2,1)S(1)}, bf16[208,128]{1,0:T(8,128)(2,1)S(1)}, u32[]{:S(2)}, u32[]{:S(2)}) collective-permute-start(bf16[208,128]{1,0:T(8,128)(2,1)S(1)} %get-tuple-element.46), channel_id=1, source_target_pairs={{0,2},{1,3},{2,0},{3,1},{4,6},{5,7},{6,4},{7,5},{8,10},{9,11},{10,... | collective-permute-start | bytes 159752 | tf_op jit(solution)/shard_map/ppermute | solution.py:30
  24.3 5.4 %collective-permute-start.8 = (bf16[208,128]{1,0:T(8,128)(2,1)S(1)}, bf16[208,128]{1,0:T(8,128)(2,1)S(1)}, u32[]{:S(2)}, u32[]{:S(2)}) collective-permute-start(bf16[208,128]{1,0:T(8,128)(2,1)S(1)} %get-tuple-element.47), channel_id=1, source_target_pairs={{0,1},{1,0},{2,3},{3,2},{4,5},{5,4},{6,7},{7,6},{8,9},{9,8},{10,11... | collective-permute-start | bytes 159752 | tf_op jit(solution)/shard_map/ppermute | solution.py:30

commit v5 on v4

--- a/solution.py
+++ b/solution.py
@@ -33,6 +33,22 @@
 def exchange(messages, axis):
     received = [swap(messages[d], axis, d + 1) for d in reversed(range(len(messages)))]
     return received[::-1]
+
+
+def start_order(count):
+    return [count // 2] + [d for d in range(count - 1, 0, -1) if d != count // 2]
+
+
+def by_start(values):
+    own = len(values) & 1 ^ 1
+    order = start_order(len(values) + 1 - own)
+    return [values[d - 1 + own] for d in order] + list(values[:own])
+
+
+def by_distance(values):
+    own = len(values) & 1 ^ 1
+    order = start_order(len(values) + 1 - own)
+    return list(values[len(order) :]) + [values[order.index(d)] for d in range(1, len(order) + 1)]
 
 
 def partner(axis, distance):
@@ -159,9 +175,29 @@
                 out[query_rows:, :] = parts
 
 
-def keep_kernel(pool, pool_out, sem):
-    pltpu.make_async_copy(pool, pool_out, sem).start()
-    pltpu.make_async_copy(pool, pool_out, sem).wait()
+def keep_kernel(replicas, *refs):
+    pages_in, (pool, moves_all, table_all, pool_out, moves, table, sems, page_sems) = (
+        refs[: replicas - 1],
+        refs[replicas - 1 :],
+    )
+    wait_for(start_copies(((moves_all, moves), (table_all, table)), sems))
+    me, column = lax.axis_index("replica"), lax.axis_index("mp")
+    rows = table.shape[1]
+    slots, page_size, _ = pool.shape
+    kept, copies = [jnp.bool_(True)] * rows, []
+    for s, page in enumerate(pages_in):
+        valid, row, _ = pair_row(moves, partner("replica", s + 1), me, rows, 1)
+        kept = [stays & ~((valid == 1) & (row == r)) for r, stays in enumerate(kept)]
+        copies.append((valid == 1, row, lambda slot, page=page: page.at[pl.ds(0, page_size)]))
+    copies += [(stays, r, lambda slot: pool.at[slot]) for r, stays in enumerate(kept)]
+    started = []
+    for n, (active, row, source) in enumerate(copies):
+        _, slot = locate(table, row, column, slots)
+        copy = pltpu.make_async_copy(source(slot), pool_out.at[slot], page_sems.at[n])
+        started.append((active, copy))
+        pl.when(active)(copy.start)
+    for active, copy in started:
+        pl.when(active)(copy.wait)
 
 
 def length_of(page, page_size):
@@ -184,7 +220,7 @@
 
 
 def attend_kernel(count, local_heads, table, lengths, pool, *refs):
-    messages = refs[:count][::-1]
+    messages = by_distance(refs[:count])
     num, den, wide = refs[count:]
     column = lax.axis_index("mp")
     rows = lengths.shape[0]
@@ -223,52 +259,18 @@
     refs = list(refs)
     take = lambda n: [refs.pop(0) for _ in range(n)]
     pages_in = take(replicas - 2)
-    moves, table, projection = take(3)
-    pages_in, messages = take(1) + pages_in, take(count)[::-1]
+    moves_all, table_all, projection = take(3)
+    pages_in, messages = take(1) + pages_in, by_distance(take(count))
     num_in, den_in = take(2)
     outs = take(count - 1)
-    own_num, own_den, own_kv, own_share, num, den, wide = refs
+    own_num, own_den, own_kv, own_share, marks, num, den, wide, moves, table, sems = refs
+    tables = start_copies(((moves_all, moves), (table_all, table)), sems)
     me, column = lax.axis_index("replica"), lax.axis_index("mp")
     rows = table.shape[1]
     page_size, width = pages_in[0].shape[0] - EXTRA, pages_in[0].shape[1]
     half_rows = local_heads * rows
-    num[...] = num_in[...]
-    den[...] = den_in[...]
-    for s, message in enumerate(messages):
-        wide[s] = message[half_rows : 2 * half_rows, :].astype(jnp.float32)
-    lane = lax.broadcasted_iota(jnp.int32, (local_heads, HD), 1)
-    token = lax.broadcasted_iota(jnp.int32, (local_heads, page_size), 1)
-    columns = [head_columns(partner("mp", s), local_heads) for s in range(count)]
-    cases = [(d, s) for d in range(1, replicas) for s in range(count)]
-    arrivals = [pair_row(moves, partner("replica", d), me, rows, 1) for d in range(1, replicas)]
     movers = moves.shape[1] // replicas
-    scores, weights, totals = {}, {}, {}
-    for d, s in cases:
-        row = arrivals[d - 1][1]
-        q = wide[s, pl.ds(row, local_heads, stride=rows), :].astype(jnp.bfloat16)
-        keys = pages_in[d - 1].at[pl.ds(0, page_size), pl.ds(0, width // 2)]
-        scores[d, s] = scores_of(q, keys[:, columns[s]])
-    for d, s in cases:
-        index, _ = locate(table, arrivals[d - 1][1], column, slots)
-        length = length_of(pages_in[d - 1], page_size)
-        inside = (token + index * page_size).astype(jnp.float32) < length
-        weight = jnp.where(inside, weight_of(scores[d, s]), 0.0)
-        weights[d, s] = weight.astype(jnp.bfloat16)
-        totals[d, s] = jnp.sum(weight, axis=1, keepdims=True)
-    for d, s in cases:
-        values = pages_in[d - 1].at[pl.ds(0, page_size), pl.ds(width // 2, width // 2)]
-        scores[d, s] = jnp.dot(weights[d, s], values[:, columns[s]], preferred_element_type=jnp.float32)
-    for d, (valid, row, _) in enumerate(arrivals, 1):
-
-        @pl.when(valid == 1)
-        def _(d=d, row=row):
-            for s in range(count):
-                num[s, pl.ds(half_rows + row, local_heads, stride=rows), :] = scores[d, s]
-                old = den[s, pl.ds(local_heads, local_heads), :]
-                den[s, pl.ds(local_heads, local_heads), :] = jnp.where(lane == row, totals[d, s], old)
-
-    own_num[...] = num[0]
-    own_den[...] = den[0]
+
     depth = projection.shape[0]
     extra = [page[page_size:, :].astype(jnp.float32) for page in pages_in]
     inputs = [
@@ -281,15 +283,58 @@
     inputs += [jnp.zeros((8 - len(inputs), depth), jnp.float32)]
     inputs = jnp.concatenate(inputs, axis=0).astype(jnp.bfloat16)
     share = jnp.dot(inputs, projection[...], preferred_element_type=jnp.float32)
+    num[...] = num_in[...]
+    den[...] = den_in[...]
+    for s, message in enumerate(messages):
+        wide[s] = message[half_rows : 2 * half_rows, :].astype(jnp.float32)
+    lengths = [length_of(page, page_size) for page in pages_in]
+
+    wait_for(tables)
+    lane = lax.broadcasted_iota(jnp.int32, (local_heads, HD), 1)
+    token = lax.broadcasted_iota(jnp.int32, (local_heads, page_size), 1)
+    columns = [head_columns(partner("mp", s), local_heads) for s in range(count)]
+    cases = [(d, s) for d in range(1, replicas) for s in range(count)]
+    arrivals = [pair_row(moves, partner("replica", d), me, rows, 1) for d in range(1, replicas)]
+    places = [locate(table, row, column, slots) for _, row, _ in arrivals]
+    scores, weights, totals = {}, {}, {}
+    for d, s in cases:
+        row = arrivals[d - 1][1]
+        q = wide[s, pl.ds(row, local_heads, stride=rows), :].astype(jnp.bfloat16)
+        keys = pages_in[d - 1].at[pl.ds(0, page_size), pl.ds(0, width // 2)]
+        scores[d, s] = scores_of(q, keys[:, columns[s]])
+    for d, s in cases:
+        inside = (token + places[d - 1][0] * page_size).astype(jnp.float32) < lengths[d - 1]
+        weight = jnp.where(inside, weight_of(scores[d, s]), 0.0)
+        weights[d, s] = weight.astype(jnp.bfloat16)
+        totals[d, s] = jnp.sum(weight, axis=1, keepdims=True)
+    for d, s in cases:
+        values = pages_in[d - 1].at[pl.ds(0, page_size), pl.ds(width // 2, width // 2)]
+        scores[d, s] = jnp.dot(weights[d, s], values[:, columns[s]], preferred_element_type=jnp.float32)
+    for d, (valid, row, _) in enumerate(arrivals, 1):
+
+        @pl.when(valid == 1)
+        def _(d=d, row=row):
+            for s in range(count):
+                num[s, pl.ds(half_rows + row, local_heads, stride=rows), :] = scores[d, s]
+                old = den[s, pl.ds(local_heads, local_heads), :]
+                den[s, pl.ds(local_heads, local_heads), :] = jnp.where(lane == row, totals[d, s], old)
+
     arrived = []
+    row_ids = lax.broadcasted_iota(jnp.int32, (rows, HD), 0)
     for number in range(movers):
-        row = jnp.zeros((1, width), jnp.float32)
-        for d, (valid, _, order) in enumerate(arrivals):
-            row = jnp.where((valid == 1) & (order == number), share[d : d + 1], row)
-        part = jnp.concatenate([row[:, j * HD : (j + 1) * HD] for j in range(2 * KVH)], axis=0)
+        picked = jnp.zeros((1, width), jnp.float32)
+        mark = jnp.zeros((rows, HD), jnp.float32)
+        for d, (valid, row, order) in enumerate(arrivals):
+            here = (valid == 1) & (order == number)
+            picked = jnp.where(here, share[d : d + 1], picked)
+            mark = jnp.where(here & (row_ids == row), 1.0, mark)
+        part = jnp.concatenate([picked[:, j * HD : (j + 1) * HD] for j in range(2 * KVH)], axis=0)
         high = part.astype(jnp.bfloat16).astype(jnp.float32)
         arrived += [high, part - high]
         own_share[number] = part
+        marks[number] = mark
+    own_num[...] = num[0]
+    own_den[...] = den[0]
     all_kv = []
     for half in range(2):
         own_kv[half] = own_tokens(messages, rows, 2 * half_rows, half)
@@ -307,10 +352,10 @@
     refs = list(refs)
     take = lambda n: [refs.pop(0) for _ in range(n)]
     pages_in = take(replicas - 2)
-    moves_all, table_all, lengths_all, kv, share, q, num, den = take(8)
-    pages_in, messages = take(1) + pages_in, take(count - 1)[::-1]
+    moves_all, table_all, lengths_all, kv, share, marks, q, num, den = take(9)
+    pages_in, messages = take(1) + pages_in, by_distance(take(count - 1))
     pool_raw, _, first, second, pool = take(5)
-    moves, table, lengths, held, full, arrived, windows, results, sems, page_sems, write_sems, out_sems = refs
+    moves, table, lengths, full, arrived, windows, results, sems, write_sems, out_sems = refs
     tables = start_copies(((moves_all, moves), (table_all, table), (lengths_all, lengths)), sems)
     me, column = lax.axis_index("replica"), lax.axis_index("mp")
     rows = lengths.shape[0]
@@ -354,8 +399,39 @@
         sums += part + pltpu.roll(part, HD // 2, 1)
     sums = jnp.transpose(sums)[:rows, :]
 
+    held = []
+    for half in range(2):
+        value = kv[half, :rows, :]
+        for number in range(movers):
+            moved = arrived[number, pl.ds(head + half * KVH, 1), :]
+            value = jnp.where(marks[number] > 0.5, moved, value)
+        held.append(value)
+    outs = []
+
+    def finish_step(step, out):
+        pieces = []
+        for h in range(local_heads):
+            at = (step * local_heads + h) * rows
+            query = q[at : at + rows, :].astype(jnp.float32)
+            numerator = num[at : at + rows, :]
+            for message in messages:
+                numerator += message[at : at + rows, :].astype(jnp.float32)
+            denominator = sums[:, step * local_heads + h : step * local_heads + h + 1]
+            extra = [(kv[0, :rows, :], kv[1, :rows, :])]
+            if step == 1:
+                extra = [held, (kv[0, rows:, :], kv[1, rows:, :])]
+            for key, value in extra:
+                weight = weight_of(jnp.sum(query * key, axis=1, keepdims=True))
+                numerator += weight.astype(jnp.bfloat16).astype(jnp.float32) * value
+                denominator += weight
+            pieces.append(numerator / denominator)
+        results[step] = jnp.concatenate(pieces, axis=1).astype(out.dtype)
+        outs.append(pltpu.make_async_copy(results.at[step], out, out_sems.at[step]))
+        outs[-1].start()
+
+    finish_step(0, first)
     wait_for(tables)
-    arrivals, copies, kept, plans = [], [], [jnp.bool_(True)] * rows, []
+    kept, plans = [jnp.bool_(True)] * rows, []
 
     def add_plan(active, row, length, first_token, source, r=None):
         index, slot = locate(table, row, column, slots)
@@ -367,53 +443,17 @@
         source = source.at[slot] if r is not None else source
         write = pltpu.make_async_copy(windows.at[n], pool.at[slot, span], write_sems.at[n])
         plans.append((touched, source, span, write, first_token, rows + row, at - start))
-        return slot
 
     for s, page in enumerate(pages_in):
         valid, row, order = pair_row(moves, partner("replica", s + 1), me, rows, 1)
         valid = valid == 1
         length = jnp.max(length_of(page, page_size)).astype(jnp.int32)
         page = page.at[pl.ds(0, page_size)]
-        slot = add_plan(valid, row, length, 2 * rows + order, page)
-        copies.append(pltpu.make_async_copy(page, pool.at[slot], page_sems.at[s]))
-        pl.when(valid)(copies[-1].start)
-        arrivals.append((valid, row, order))
+        add_plan(valid, row, length, 2 * rows + order, page)
         kept = [stays & ~(valid & (row == r)) for r, stays in enumerate(kept)]
     for r in range(rows):
         add_plan(kept[r], r, lengths[r], r, pool_raw, r)
 
-    for half in range(2):
-        held[half] = kv[half, :rows, :]
-        for valid, row, order in arrivals:
-
-            @pl.when(valid)
-            def _(half=half, row=row, order=order):
-                held[half, pl.ds(row, 1), :] = arrived[order, pl.ds(head + half * KVH, 1), :]
-
-    outs = []
-    for step, out in enumerate((first, second)):
-        pieces = []
-        for h in range(local_heads):
-            at = (step * local_heads + h) * rows
-            query = q[at : at + rows, :].astype(jnp.float32)
-            numerator = num[at : at + rows, :]
-            for message in messages:
-                numerator += message[at : at + rows, :].astype(jnp.float32)
-            denominator = sums[:, step * local_heads + h : step * local_heads + h + 1]
-            extra = [(kv[0, :rows, :], kv[1, :rows, :])]
-            if step == 1:
-                extra = [(held[0], held[1]), (kv[0, rows:, :], kv[1, rows:, :])]
-            for key, value in extra:
-                weight = weight_of(jnp.sum(query * key, axis=1, keepdims=True))
-                numerator += weight.astype(jnp.bfloat16).astype(jnp.float32) * value
-                denominator += weight
-            pieces.append(numerator / denominator)
-        results[step] = jnp.concatenate(pieces, axis=1).astype(out.dtype)
-        outs.append(pltpu.make_async_copy(results.at[step], out, out_sems.at[step]))
-        outs[-1].start()
-
-    for (valid, _, _), copy in zip(arrivals, copies):
-        pl.when(valid)(copy.wait)
     place_ids = lax.broadcasted_iota(jnp.int32, (WINDOW, width), 0)
     for n, (touched, source, span, write, token, next_token, offset) in enumerate(plans):
 
@@ -425,6 +465,7 @@
             windows[n] = new.astype(jnp.bfloat16)
             write.start()
 
+    finish_step(1, second)
     for plan in plans:
         pl.when(plan[0])(plan[3].wait)
     wait_for(outs)
@@ -495,16 +536,6 @@
     messages = [sent[0]] + exchange(sent[1:], "mp")
 
     pool_near = in_vmem(pool)
-    pool_copy = pl.pallas_call(
-        keep_kernel,
-        out_shape=shape(pool.shape, bf16),
-        in_specs=[VMEM],
-        out_specs=ANY,
-        scratch_shapes=[pltpu.SemaphoreType.DMA(())],
-        compiler_params=params(),
-        cost_estimate=cost(1.6),
-        name="keep",
-    )(pool_near)
     num, den = pl.pallas_call(
         functools.partial(attend_kernel, count, local_heads),
         out_shape=[shape((count, query_rows, HD), f32), shape((count, both, HD), f32)],
@@ -514,29 +545,51 @@
         compiler_params=params(),
         cost_estimate=cost(1.5),
         name="attend",
-    )(old_table, lengths, pool_near, *messages[::-1])
+    )(old_table, lengths, pool_near, *by_start(messages))
 
     sum_rows = query_rows + -(-both // 16) * 16 + 4 * rows + 16 * movers
-    *sums, num, den, kv, share = pl.pallas_call(
+    *sums, num, den, kv, share, marks = pl.pallas_call(
         functools.partial(arrive_kernel, count, replicas, local_heads, slots),
         out_shape=[shape((sum_rows, HD), SEND)] * (count - 1)
         + [shape((query_rows, HD), f32), shape((both, HD), f32)]
-        + [shape((2, 2 * rows, HD), f32), shape((movers, 2 * KVH, HD), f32)],
+        + [shape((2, 2 * rows, HD), f32), shape((movers, 2 * KVH, HD), f32)]
+        + [shape((movers, rows, HD), f32)],
         in_specs=[VMEM] * (replicas - 2)
-        + [SMEM, SMEM, VMEM, VMEM]
+        + [ANY, ANY, VMEM, VMEM]
         + [VMEM] * count
         + [VMEM] * 2,
-        out_specs=[VMEM] * (count + 3),
+        out_specs=[VMEM] * (count + 4),
         scratch_shapes=[
             pltpu.VMEM((count, query_rows, HD), f32),
             pltpu.VMEM((count, both, HD), f32),
             pltpu.VMEM((count, query_rows // 2, HD), f32),
+            pltpu.SMEM(moves.shape, jnp.int32),
+            pltpu.SMEM(table_after.shape, jnp.int32),
+            pltpu.SemaphoreType.DMA((2,)),
         ],
         compiler_params=params(),
         cost_estimate=cost(1.2),
         name="arrive",
-    )(*pages_in[1:], moves, table_after, weight_near, pages_in[0], *messages[::-1], num, den)
+    )(*pages_in[1:], moves, table_after, weight_near, pages_in[0], *by_start(messages), num, den)
     sums_in = exchange(sums, "mp")
+
+    moves_then, _ = lax.optimization_barrier((moves, marks))
+
+    pool_copy = pl.pallas_call(
+        functools.partial(keep_kernel, replicas),
+        out_shape=shape(pool.shape, bf16),
+        in_specs=[VMEM] * replicas + [ANY] * 2,
+        out_specs=ANY,
+        scratch_shapes=[
+            pltpu.SMEM(moves.shape, jnp.int32),
+            pltpu.SMEM(table_after.shape, jnp.int32),
+            pltpu.SemaphoreType.DMA((2,)),
+            pltpu.SemaphoreType.DMA((rows + replicas - 1,)),
+        ],
+        compiler_params=params(),
+        cost_estimate=cost(1.6),
+        name="keep",
+    )(*pages_in, pool_near, moves_then, table_after)
 
     first, second, pool_after = pl.pallas_call(
         functools.partial(finish_kernel, count, replicas, local_heads),
@@ -545,31 +598,29 @@
             shape((rows, local_heads * HD), bf16),
             shape(pool.shape, bf16),
         ],
-        in_specs=[VMEM] * (replicas - 2) + [ANY] * 3 + [VMEM] * (6 + count - 1) + [VMEM, ANY],
+        in_specs=[VMEM] * (replicas - 2) + [ANY] * 3 + [VMEM] * (7 + count - 1) + [VMEM, ANY],
         out_specs=[ANY] * 3,
         scratch_shapes=[
             pltpu.SMEM(moves.shape, jnp.int32),
             pltpu.SMEM(table_after.shape, jnp.int32),
             pltpu.SMEM(lengths.shape, jnp.int32),
-            pltpu.VMEM((2, rows, HD), f32),
             pltpu.VMEM((KV_ROWS, width), f32),
             pltpu.VMEM((movers, 2 * KVH, HD), f32),
             pltpu.VMEM((rows + replicas - 1, WINDOW, width), bf16),
             pltpu.VMEM((2, rows, local_heads * HD), bf16),
             pltpu.SemaphoreType.DMA((3,)),
-            pltpu.SemaphoreType.DMA((replicas - 1,)),
             pltpu.SemaphoreType.DMA((rows + replicas - 1,)),
             pltpu.SemaphoreType.DMA((2,)),
         ],
-        input_output_aliases={8 + replicas - 1 + (count - 1) + 1: 2},
+        input_output_aliases={9 + replicas - 1 + (count - 1) + 1: 2},
         compiler_params=params(),
         cost_estimate=cost(2.5),
         name="finish",
     )(
         *pages_in[1:],
         *(moves, table_after, lengths),
-        *(kv, share, messages[0], num, den, pages_in[0]),
-        *sums_in[::-1],
+        *(kv, share, marks, messages[0], num, den, pages_in[0]),
+        *by_start(sums_in),
         *(pool_near, pool_copy),
     )
     return first, second, pool_after[None, None]

time: 32.3 us -> 31.2 us (0.966)
  starting transfers between devices: 12.2 us -> 11.2 us
    ppermute x9, starting transfers between devices: 12.2 us -> 11.2 us  [swap(): return lax.ppermute(value, axis, [(i, i ^ distance) for i in range(size)])]
    pallas_call x1, Pallas kernels: 1.33 us -> 2.06 us  [body(): pl.pallas_call(functools.partial(keep_kernel, replicas), out_shape=shape(...]
    pallas_call x1, Pallas kernels: 2.49 us -> 1.97 us  [body(): pl.pallas_call(functools.partial(finish_kernel, count, replicas, local_he...]
    pallas_call x1, Pallas kernels: 1.75 us -> 1.26 us  [body(): pl.pallas_call(functools.partial(arrive_kernel, count, replicas, local_he...]
  transfers between devices with their start and end apart: 9 -> 9, of which waited for: 4 -> 5; matrix products, arithmetic and copies ran while one was open for 0% -> 0% of each run, Pallas kernels for 11% -> 14%
where the time goes in v5:
time: 31.2 us; the launch traced here: 31 us
  starting transfers between devices  11.2 us (36%)
  Pallas kernels  9.55 us (31%)
  waiting for transfers between devices  7.05 us (23%)
  local copies, waits for them, and re-layouts  2.36 us (8%)
  between operations  0.77 us (2%)
    ppermute x9, starting transfers between devices, swap(): return lax.ppermute(value, axis, [(i, i ^ distance) for i in range(size)])  11.2 us
    ppermute x9, waiting for transfers between devices, swap(): return lax.ppermute(value, axis, [(i, i ^ distance) for i in range(size)])  7.05 us
    unnamed x18, local copies, waits for them, and re-layouts  2.36 us
    pallas_call x1, Pallas kernels, body(): pl.pallas_call(functools.partial(keep_kernel, replicas), out_shape=shape(...  2.06 us
    pallas_call x1, Pallas kernels, body(): pl.pallas_call(functools.partial(leave_kernel, rows), out_shape=[shape((p...  2.06 us
    pallas_call x1, Pallas kernels, body(): pl.pallas_call(functools.partial(finish_kernel, count, replicas, local_he...  1.97 us
    pallas_call x1, Pallas kernels, body(): pl.pallas_call(functools.partial(attend_kernel, count, local_heads), out_...  1.52 us
    pallas_call x1, Pallas kernels, body(): pl.pallas_call(functools.partial(arrive_kernel, count, replicas, local_he...  1.26 us
  transfers between devices with their start and end apart: 9, of which 5 were waited for; matrix products, arithmetic and copies ran while one was open for 0% of the time, Pallas kernels for 14%

profile of v5, /device:TPU:0, one launch (start us, length us, event | category | flops | bytes accessed | tf_op | source)
XLA Modules:
  0.0 31.0 jit_solution(13021593810484713032)
XLA Ops:
  0.6 0.0 copy-start.3
  0.6 0.0 copy-start.4
  0.7 0.0 copy-start.7
  0.7 2.1 %leave.1 = (bf16[136,1024]{1,0:T(8,128)(2,1)S(1)}, bf16[136,1024]{1,0:T(8,128)(2,1)S(1)}, bf16[136,1024]{1,0:T(8,128)(2,1)S(1)}) custom-call(s32[2,8]{1,0:T(2,128)} %bitcast.15, s32[4,8]{1,0:T(4,128)} %bitcast.19, s32[8]{0:T(128)} %refs_4_.3, bf16[16,2048]{1,0:T(8,128)(2,1)} %bitcast.10, bf16[8,128,1024]{2,1,0:T(8,128)(2,1)} %bitcast.6), custom_call_target="tpu_custom_call" | custom-call | bytes 7000000 | tf_op jit(solution)/shard_map/leave/pallas_call | solution.py:506
  2.7 0.5 %collective-permute-start.2 = (bf16[136,1024]{1,0:T(8,128)(2,1)S(1)}, bf16[136,1024]{1,0:T(8,128)(2,1)S(1)}, u32[]{:S(2)}, u32[]{:S(2)}) collective-permute-start(bf16[136,1024]{1,0:T(8,128)(2,1)S(1)} %get-tuple-element.35), channel_id=1, source_target_pairs={{0,4},{4,0},{8,12},{12,8},{1,5},{5,1},{9,13},{13,9},{2,6},{6,2},{1... | collective-permute-start | bytes 835592 | tf_op jit(solution)/shard_map/ppermute | solution.py:30
  3.2 2.6 %collective-permute-start = (bf16[136,1024]{1,0:T(8,128)(2,1)S(1)}, bf16[136,1024]{1,0:T(8,128)(2,1)S(1)}, u32[]{:S(2)}, u32[]{:S(2)}) collective-permute-start(bf16[136,1024]{1,0:T(8,128)(2,1)S(1)} %get-tuple-element.29), channel_id=1, source_target_pairs={{0,8},{4,12},{8,0},{12,4},{1,9},{5,13},{9,1},{13,5},{2,10},{6,14},... | collective-permute-start | bytes 835592 | tf_op jit(solution)/shard_map/ppermute | solution.py:30
  5.8 0.1 collective-permute-start.1
  5.9 0.0 copy-done.4
  5.9 2.3 %copy-done.1 = bf16[2048,1024]{1,0:T(8,128)(2,1)S(1)} copy-done((bf16[2048,1024]{1,0:T(8,128)(2,1)S(1)}, bf16[2048,1024]{1,0:T(8,128)(2,1)}, u32[]{:S(2)}) %copy-start.1) | copy-done | bytes 4194328
  8.2 0.7 %open.1 = (bf16[192,128]{1,0:T(8,128)(2,1)S(1)}, bf16[192,128]{1,0:T(8,128)(2,1)S(1)}, bf16[192,128]{1,0:T(8,128)(2,1)S(1)}, bf16[192,128]{1,0:T(8,128)(2,1)S(1)}) custom-call(bf16[16,2048]{1,0:T(8,128)(2,1)S(1)} %bitcast.11, bf16[2,8,1024]{2,1,0:T(8,128)(2,1)S(1)} %copy-done.4, bf16[2048,1024]{1,0:T(8,128)(2,1)S(1)} %copy-done.1), custom_call_target="tpu_custom_call" | custom-call | bytes 4200000 | tf_op jit(solution)/shard_map/open/pallas_call | solution.py:526
  8.9 0.0 copy-start.5
  8.9 0.0 copy-start.6
  8.9 0.0 collective-permute-done.2.refs_5_.refs_0_.refs_11_
  8.9 2.9 %collective-permute-start.3 = (bf16[192,128]{1,0:T(8,128)(2,1)S(1)}, bf16[192,128]{1,0:T(8,128)(2,1)S(1)}, u32[]{:S(2)}, u32[]{:S(2)}) collective-permute-start(bf16[192,128]{1,0:T(8,128)(2,1)S(1)} %get-tuple-element.37), channel_id=1, source_target_pairs={{0,2},{1,3},{2,0},{3,1},{4,6},{5,7},{6,4},{7,5},{8,10},{9,11},{10,... | collective-permute-start | bytes 147464 | tf_op jit(solution)/shard_map/ppermute | solution.py:30
  11.9 1.3 %collective-permute-start.4 = (bf16[192,128]{1,0:T(8,128)(2,1)S(1)}, bf16[192,128]{1,0:T(8,128)(2,1)S(1)}, u32[]{:S(2)}, u32[]{:S(2)}) collective-permute-start(bf16[192,128]{1,0:T(8,128)(2,1)S(1)} %get-tuple-element.38), channel_id=1, source_target_pairs={{0,3},{1,2},{2,1},{3,0},{4,7},{5,6},{6,5},{7,4},{8,11},{9,10},{10,... | collective-permute-start | bytes 147464 | tf_op jit(solution)/shard_map/ppermute | solution.py:30
  13.2 0.2 collective-permute-start.5
  13.4 0.7 %collective-permute-done.3.refs_0_.refs_6_ = bf16[192,128]{1,0:T(8,128)(2,1)S(1)} collective-permute-done((bf16[192,128]{1,0:T(8,128)(2,1)S(1)}, bf16[192,128]{1,0:T(8,128)(2,1)S(1)}, u32[]{:S(2)}, u32[]{:S(2)}) %collective-permute-start.3) | collective-permute-done | bytes 49184 | tf_op jit(solution)/shard_map/ppermute | solution.py:30
  14.1 3.8 %collective-permute-done.4.refs_1_.refs_7_ = bf16[192,128]{1,0:T(8,128)(2,1)S(1)} collective-permute-done((bf16[192,128]{1,0:T(8,128)(2,1)S(1)}, bf16[192,128]{1,0:T(8,128)(2,1)S(1)}, u32[]{:S(2)}, u32[]{:S(2)}) %collective-permute-start.4) | collective-permute-done | bytes 49184 | tf_op jit(solution)/shard_map/ppermute | solution.py:30
  17.9 0.0 collective-permute-done.5.refs_2_.refs_8_
  17.9 0.0 copy-done
  17.9 1.5 %attend.1 = (f32[4,128,128]{2,1,0:T(8,128)S(1)}, f32[4,16,128]{2,1,0:T(8,128)S(1)}) custom-call(s32[4,8]{1,0:T(4,128)S(1)} %bitcast.20, s32[8]{0:T(128)S(1)} %copy-done.8, bf16[8,128,1024]{2,1,0:T(8,128)(2,1)S(1)} %bitcast.7, bf16[192,128]{1,0:T(8,128)(2,1)S(1)} %collective-permute-done.3.refs_0_.refs_6_, ...), custom_call_target="tpu_custom_call" | custom-call | bytes 5250000 | tf_op jit(solution)/shard_map/attend/pallas_call | solution.py:539
  19.5 0.0 collective-permute-done.refs_0_.refs_1_
  19.5 0.0 collective-permute-done.1.refs_1_.refs_2_
  19.5 1.3 %arrive.1 = (bf16[208,128]{1,0:T(8,128)(2,1)S(1)}, bf16[208,128]{1,0:T(8,128)(2,1)S(1)}, bf16[208,128]{1,0:T(8,128)(2,1)S(1)}, f32[128,128]{1,0:T(8,128)S(1)}, f...) custom-call(bf16[136,1024]{1,0:T(8,128)(2,1)S(1)} %collective-permute-don, ...), custom_call_target="tpu_custom_call" | custom-call | bytes 4200000 | tf_op jit(solution)/shard_map/arrive/pallas_call | solution.py:551
  20.8 2.1 %collective-permute-start.6 = (bf16[208,128]{1,0:T(8,128)(2,1)S(1)}, bf16[208,128]{1,0:T(8,128)(2,1)S(1)}, u32[]{:S(2)}, u32[]{:S(2)}) collective-permute-start(bf16[208,128]{1,0:T(8,128)(2,1)S(1)} %get-tuple-element.48), channel_id=1, source_target_pairs={{0,2},{1,3},{2,0},{3,1},{4,6},{5,7},{6,4},{7,5},{8,10},{9,11},{10,... | collective-permute-start | bytes 159752 | tf_op jit(solution)/shard_map/ppermute | solution.py:30
  22.8 1.3 %collective-permute-start.7 = (bf16[208,128]{1,0:T(8,128)(2,1)S(1)}, bf16[208,128]{1,0:T(8,128)(2,1)S(1)}, u32[]{:S(2)}, u32[]{:S(2)}) collective-permute-start(bf16[208,128]{1,0:T(8,128)(2,1)S(1)} %get-tuple-element.49), channel_id=1, source_target_pairs={{0,3},{1,2},{2,1},{3,0},{4,7},{5,6},{6,5},{7,4},{8,11},{9,10},{10,... | collective-permute-start | bytes 159752 | tf_op jit(solution)/shard_map/ppermute | solution.py:30
  24.1 0.2 collective-permute-start.8
  24.4 2.1 %keep.1.refs_16_ = bf16[8,128,1024]{2,1,0:T(8,128)(2,1)} custom-call(bf16[136,1024]{1,0:T(8,128)(2,1)S(1)} %collective-permute-done.2.refs_5_.refs_0_.refs_11_, bf16[136,1024]{1,0:T(8,128)(2,1)S(1)} %collective-permute-done.refs_0_.refs_1_, bf16[136,1024]{1,0:T(8,128)(2,1)S(1)} %collective-permute-done.1.refs_1_.refs_2_, bf16[8,128,1024]{2,1,0:T(8,128)(2,1)S(1)} %bitcast.8, ...), custom_call_target="tpu_custom_call" | custom-call | bytes 5600000 | tf_op jit(solution)/shard_map/keep/pallas_call | solution.py:578
  26.4 0.6 %collective-permute-done.6.refs_12_ = bf16[208,128]{1,0:T(8,128)(2,1)S(1)} collective-permute-done((bf16[208,128]{1,0:T(8,128)(2,1)S(1)}, bf16[208,128]{1,0:T(8,128)(2,1)S(1)}, u32[]{:S(2)}, u32[]{:S(2)}) %collective-permute-start.6) | collective-permute-done | bytes 53280 | tf_op jit(solution)/shard_map/ppermute | solution.py:30
  27.0 2.0 %collective-permute-done.7.refs_13_ = bf16[208,128]{1,0:T(8,128)(2,1)S(1)} collective-permute-done((bf16[208,128]{1,0:T(8,128)(2,1)S(1)}, bf16[208,128]{1,0:T(8,128)(2,1)S(1)}, u32[]{:S(2)}, u32[]{:S(2)}) %collective-permute-start.7) | collective-permute-done | bytes 53280 | tf_op jit(solution)/shard_map/ppermute | solution.py:30
  28.9 0.1 collective-permute-done.8.refs_14_
  29.0 2.0 %finish.1 = (bf16[8,1024]{1,0:T(8,128)(2,1)}, bf16[8,1024]{1,0:T(8,128)(2,1)}, bf16[8,128,1024]{2,1,0:T(8,128)(2,1)}) custom-call(bf16[136,1024]{1,0:T(8,128)(2,1)S(1)} %collective-permute-done.refs_0_.refs_1_, bf16[136,1024]{1,0:T(8,128)(2,1)S(1)} %collective-permute-done.1.refs_1_.refs_2_, s32[2,8]{1,0:T(2,128)S(1)} %bitcast.18, ...), custom_call_target="tpu_custom_call", output_to_operand_aliasing={{2}: (16, {})} | custom-call | bytes 8750000 | tf_op jit(solution)/shard_map/finish/pallas_call | solution.py:594
  (10 shorter events, 0.0 us)
Async XLA Ops:
  0.6 5.3 %copy-start.3 = (bf16[2,8,2048]{2,1,0:T(8,128)(2,1)S(1)}, bf16[2,8,2048]{2,1,0:T(8,128)(2,1)}, u32[]{:S(2)}) copy-start(bf16[2,8,2048]{2,1,0:T(8,128)(2,1)} %param.8) | copy-start | bytes 196612
  0.6 5.2 %copy-start.4 = (bf16[2,8,1024]{2,1,0:T(8,128)(2,1)S(1)}, bf16[2,8,1024]{2,1,0:T(8,128)(2,1)}, u32[]{:S(2)}) copy-start(bf16[2,8,1024]{2,1,0:T(8,128)(2,1)} %q.1) | copy-start | bytes 98308
  0.7 17.3 %copy-start.7 = (s32[8,4]{0,1:T(4,128)S(1)}, s32[8,4]{0,1:T(4,128)}, u32[]{:S(2)}) copy-start(s32[8,4]{0,1:T(4,128)} %param.13) | copy-start | bytes 388
  2.7 6.2 %collective-permute-start.2 = (bf16[136,1024]{1,0:T(8,128)(2,1)S(1)}, bf16[136,1024]{1,0:T(8,128)(2,1)S(1)}, u32[]{:S(2)}, u32[]{:S(2)}) collective-permute-start(bf16[136,1024]{1,0:T(8,128)(2,1)S(1)} %get-tuple-element.35), channel_id=1, source_target_pairs={{0,4},{4,0},{8,12},{12,8},{1,5},{5,1},{9,13},{13,9},{2,6},{6,2},{1... | collective-permute-start | bytes 835592 | tf_op jit(solution)/shard_map/ppermute | solution.py:30
  3.2 16.2 %collective-permute-start = (bf16[136,1024]{1,0:T(8,128)(2,1)S(1)}, bf16[136,1024]{1,0:T(8,128)(2,1)S(1)}, u32[]{:S(2)}, u32[]{:S(2)}) collective-permute-start(bf16[136,1024]{1,0:T(8,128)(2,1)S(1)} %get-tuple-element.29), channel_id=1, source_target_pairs={{0,8},{4,12},{8,0},{12,4},{1,9},{5,13},{9,1},{13,5},{2,10},{6,14},... | collective-permute-start | bytes 835592 | tf_op jit(solution)/shard_map/ppermute | solution.py:30
  5.8 12.1 %copy-start.8 = (s32[8]{0:T(128)S(1)}, s32[8]{0:T(128)}, u32[]{:S(2)}) copy-start(s32[8]{0:T(128)} %refs_4_.3) | copy-start | bytes 100
  5.8 12.1 %copy-start = (bf16[1,1,8,128,1024]{4,3,2,1,0:T(8,128)(2,1)S(1)}, bf16[1,1,8,128,1024]{4,3,2,1,0:T(8,128)(2,1)}, u32[]{:S(2)}) copy-start(bf16[1,1,8,128,1024]{4,3,2,1,0:T(8,128)(2,1)} %param.11) | copy-start | bytes 6291460
  5.8 13.7 %collective-permute-start.1 = (bf16[136,1024]{1,0:T(8,128)(2,1)S(1)}, bf16[136,1024]{1,0:T(8,128)(2,1)S(1)}, u32[]{:S(2)}, u32[]{:S(2)}) collective-permute-start(bf16[136,1024]{1,0:T(8,128)(2,1)S(1)} %get-tuple-element.30), channel_id=1, source_target_pairs={{0,12},{4,8},{8,4},{12,0},{1,13},{5,9},{9,5},{13,1},{2,14},{6,10},... | collective-permute-start | bytes 835592 | tf_op jit(solution)/shard_map/ppermute | solution.py:30
  5.9 2.3 %copy-start.1 = (bf16[2048,1024]{1,0:T(8,128)(2,1)S(1)}, bf16[2048,1024]{1,0:T(8,128)(2,1)}, u32[]{:S(2)}) copy-start(bf16[2048,1024]{1,0:T(8,128)(2,1)} %refs_4_.2) | copy-start | bytes 12582916
  8.2 11.3 %copy-start.2 = (bf16[2048,1024]{1,0:T(8,128)(2,1)S(1)}, bf16[2048,1024]{1,0:T(8,128)(2,1)}, u32[]{:S(2)}) copy-start(bf16[2048,1024]{1,0:T(8,128)(2,1)} %refs_4_.2) | copy-start | bytes 12582916
  8.9 10.6 %copy-start.5 = (s32[8,4]{0,1:T(4,128)S(1)}, s32[8,4]{0,1:T(4,128)}, u32[]{:S(2)}) copy-start(s32[8,4]{0,1:T(4,128)} %param.14) | copy-start | bytes 388
  8.9 10.6 %copy-start.6 = (s32[8,2]{0,1:T(2,128)S(1)}, s32[8,2]{0,1:T(2,128)}, u32[]{:S(2)}) copy-start(s32[8,2]{0,1:T(2,128)} %param.15) | copy-start | bytes 196
  8.9 5.2 %collective-permute-start.3 = (bf16[192,128]{1,0:T(8,128)(2,1)S(1)}, bf16[192,128]{1,0:T(8,128)(2,1)S(1)}, u32[]{:S(2)}, u32[]{:S(2)}) collective-permute-start(bf16[192,128]{1,0:T(8,128)(2,1)S(1)} %get-tuple-element.37), channel_id=1, source_target_pairs={{0,2},{1,3},{2,0},{3,1},{4,6},{5,7},{6,4},{7,5},{8,10},{9,11},{10,... | collective-permute-start | bytes 147464 | tf_op jit(solution)/shard_map/ppermute | solution.py:30
  11.9 6.0 %collective-permute-start.4 = (bf16[192,128]{1,0:T(8,128)(2,1)S(1)}, bf16[192,128]{1,0:T(8,128)(2,1)S(1)}, u32[]{:S(2)}, u32[]{:S(2)}) collective-permute-start(bf16[192,128]{1,0:T(8,128)(2,1)S(1)} %get-tuple-element.38), channel_id=1, source_target_pairs={{0,3},{1,2},{2,1},{3,0},{4,7},{5,6},{6,5},{7,4},{8,11},{9,10},{10,... | collective-permute-start | bytes 147464 | tf_op jit(solution)/shard_map/ppermute | solution.py:30
  13.2 4.7 %collective-permute-start.5 = (bf16[192,128]{1,0:T(8,128)(2,1)S(1)}, bf16[192,128]{1,0:T(8,128)(2,1)S(1)}, u32[]{:S(2)}, u32[]{:S(2)}) collective-permute-start(bf16[192,128]{1,0:T(8,128)(2,1)S(1)} %get-tuple-element.39), channel_id=1, source_target_pairs={{0,1},{1,0},{2,3},{3,2},{4,5},{5,4},{6,7},{7,6},{8,9},{9,8},{10,11... | collective-permute-start | bytes 147464 | tf_op jit(solution)/shard_map/ppermute | solution.py:30
  20.8 6.2 %collective-permute-start.6 = (bf16[208,128]{1,0:T(8,128)(2,1)S(1)}, bf16[208,128]{1,0:T(8,128)(2,1)S(1)}, u32[]{:S(2)}, u32[]{:S(2)}) collective-permute-start(bf16[208,128]{1,0:T(8,128)(2,1)S(1)} %get-tuple-element.48), channel_id=1, source_target_pairs={{0,2},{1,3},{2,0},{3,1},{4,6},{5,7},{6,4},{7,5},{8,10},{9,11},{10,... | collective-permute-start | bytes 159752 | tf_op jit(solution)/shard_map/ppermute | solution.py:30
  22.8 6.1 %collective-permute-start.7 = (bf16[208,128]{1,0:T(8,128)(2,1)S(1)}, bf16[208,128]{1,0:T(8,128)(2,1)S(1)}, u32[]{:S(2)}, u32[]{:S(2)}) collective-permute-start(bf16[208,128]{1,0:T(8,128)(2,1)S(1)} %get-tuple-element.49), channel_id=1, source_target_pairs={{0,3},{1,2},{2,1},{3,0},{4,7},{5,6},{6,5},{7,4},{8,11},{9,10},{10,... | collective-permute-start | bytes 159752 | tf_op jit(solution)/shard_map/ppermute | solution.py:30
  24.1 4.9 %collective-permute-start.8 = (bf16[208,128]{1,0:T(8,128)(2,1)S(1)}, bf16[208,128]{1,0:T(8,128)(2,1)S(1)}, u32[]{:S(2)}, u32[]{:S(2)}) collective-permute-start(bf16[208,128]{1,0:T(8,128)(2,1)S(1)} %get-tuple-element.50), channel_id=1, source_target_pairs={{0,1},{1,0},{2,3},{3,2},{4,5},{5,4},{6,7},{7,6},{8,9},{9,8},{10,11... | collective-permute-start | bytes 159752 | tf_op jit(solution)/shard_map/ppermute | solution.py:30

commit v6 on v5

--- a/solution.py
+++ b/solution.py
@@ -118,22 +118,17 @@
 
 
 def leave_kernel(rows, moves_all, table_all, lengths_all, x_all, pool, *refs):
-    pages, (moves, table, lengths, x, sems, page_sems) = refs[:-6], refs[-6:]
+    held, pages, (moves, table, lengths, x, sems, pool_sems) = refs[0], refs[1:-6], refs[-6:]
     me, column = lax.axis_index("replica"), lax.axis_index("mp")
     page_size, width = pool.shape[1:]
     depth = x.shape[1]
     rest = start_copies(
         ((moves_all, moves), (table_all, table), (lengths_all, lengths), (x_all, x)), sems
     )
+    copies = start_copies([(pool.at[i], held.at[i]) for i in range(pool.shape[0])], pool_sems)
     wait_for(rest[:2])
     found = [pair_row(moves, me, partner("replica", s + 1), rows, 0)[1] for s in range(len(pages))]
-    copies = start_copies(
-        [
-            (pool.at[locate(table, row, column, pool.shape[0])[1]], page.at[pl.ds(0, page_size)])
-            for row, page in zip(found, pages)
-        ],
-        page_sems,
-    )
+    picks = [locate(table, row, column, pool.shape[0])[1] for row in found]
     wait_for(rest[2:])
     sublane = lax.broadcasted_iota(jnp.int32, (EXTRA, width), 0)
     first_rows = x[:rows, :].astype(jnp.float32)
@@ -149,9 +144,15 @@
             extra = jnp.where(sublane == 2 + i, value, extra)
         page[page_size:, :] = extra.astype(jnp.bfloat16)
     wait_for(copies)
-
-
-def open_kernel(count, local_heads, x, q, weight, *outs):
+    for slot, page in zip(picks, pages):
+        page[:page_size, :] = held[slot]
+
+
+def open_kernel(count, local_heads, x, q, weight, *refs):
+    outs, (held, weight_sems) = refs[:-2], refs[-2:]
+    depth, chunks = weight.shape[0], weight_sems.shape[0]
+    spans = [pl.ds(c * (depth // chunks), depth // chunks) for c in range(chunks)]
+    loads = start_copies([(weight.at[span], held.at[span]) for span in spans], weight_sems)
     rows = q.shape[1]
     wide = [q[i].astype(jnp.float32) for i in range(2)]
     blocks = [wide[i][:, h * HD : (h + 1) * HD] for i in range(2) for h in range(local_heads)]
@@ -159,7 +160,10 @@
     query_rows = packed.shape[0]
     for out in outs:
         out[:query_rows, :] = packed
-    total = jnp.dot(x[...], weight[...], preferred_element_type=jnp.float32)
+    total = jnp.zeros((x.shape[0], weight.shape[1]), jnp.float32)
+    for span, load in zip(spans, loads):
+        load.wait()
+        total += jnp.dot(x[:, span], held[span, :], preferred_element_type=jnp.float32)
     for j in range(KVH):
         parts = []
         for half in range(2):
@@ -503,21 +507,21 @@
     message_rows = query_rows + 8 * rows
     movers = migrations.shape[0] // replicas
     inputs = layer_input.reshape(2 * rows, depth)
-    leaving = pl.pallas_call(
+    pool_near, *leaving = pl.pallas_call(
         functools.partial(leave_kernel, rows),
-        out_shape=[shape((page_size + EXTRA, width), bf16)] * (replicas - 1),
+        out_shape=[shape(pool.shape, bf16)] + [shape((page_size + EXTRA, width), bf16)] * (replicas - 1),
         in_specs=[HBM] * 5,
-        out_specs=[VMEM] * (replicas - 1),
+        out_specs=[VMEM] * replicas,
         scratch_shapes=[
             pltpu.SMEM(moves.shape, jnp.int32),
             pltpu.SMEM(old_table.shape, jnp.int32),
             pltpu.SMEM(lengths.shape, jnp.int32),
             pltpu.VMEM((2 * rows, depth), bf16),
             pltpu.SemaphoreType.DMA((4,)),
-            pltpu.SemaphoreType.DMA((replicas - 1,)),
+            pltpu.SemaphoreType.DMA((slots,)),
         ],
         compiler_params=params(),
-        cost_estimate=cost(2.0),
+        cost_estimate=cost(1.8),
         name="leave",
     )(*map(in_hbm, (moves, old_table, lengths, inputs, pool)))
     pages_in = exchange(leaving, "replica")
@@ -526,16 +530,16 @@
     sent = pl.pallas_call(
         functools.partial(open_kernel, count, local_heads),
         out_shape=[shape((message_rows, HD), bf16)] * count,
-        in_specs=[VMEM] * 3,
+        in_specs=[VMEM] * 2 + [HBM],
         out_specs=[VMEM] * count,
+        scratch_shapes=[pltpu.VMEM((depth, width), bf16), pltpu.SemaphoreType.DMA((8,))],
         compiler_params=params(),
         cost_estimate=cost(1.2),
         name="open",
-    )(inputs_near, queries_near, weight_near)
+    )(inputs_near, queries_near, in_hbm(kv_weight))
     sent, pages_in[0] = lax.optimization_barrier((list(sent), pages_in[0]))
     messages = [sent[0]] + exchange(sent[1:], "mp")
 
-    pool_near = in_vmem(pool)
     num, den = pl.pallas_call(
         functools.partial(attend_kernel, count, local_heads),
         out_shape=[shape((count, query_rows, HD), f32), shape((count, both, HD), f32)],

time: 31.2 us -> 30.6 us (0.981)
  local copies, waits for them, and re-layouts: 2.36 us -> 0.03 us
  Pallas kernels: 9.55 us -> 11 us
  starting transfers between devices: 11.2 us -> 11.7 us
    unnamed x18 -> x14, local copies, waits for them, and re-layouts: 2.36 us -> 0.03 us
    pallas_call x1, Pallas kernels: 0.68 us -> 2.57 us  [body(): pl.pallas_call(functools.partial(open_kernel, count, local_heads), out_sh...]
    ppermute x9, starting transfers between devices: 11.2 us -> 11.7 us  [swap(): return lax.ppermute(value, axis, [(i, i ^ distance) for i in range(size)])]
    pallas_call x1, Pallas kernels: 2.06 us -> 1.71 us  [body(): pl.pallas_call(functools.partial(leave_kernel, rows), out_shape=[shape(po...]
  transfers between devices with their start and end apart: 9 -> 9, of which waited for: 5 -> 4; matrix products, arithmetic and copies ran while one was open for 0% -> 0% of each run, Pallas kernels for 14% -> 20%
where the time goes in v6:
time: 30.6 us; the launch traced here: 30.5 us
  starting transfers between devices  11.7 us (38%)
  Pallas kernels  11 us (36%)
  waiting for transfers between devices  6.98 us (23%)
  between operations  0.75 us (2%)
    ppermute x9, starting transfers between devices, swap(): return lax.ppermute(value, axis, [(i, i ^ distance) for i in range(size)])  11.7 us
    ppermute x9, waiting for transfers between devices, swap(): return lax.ppermute(value, axis, [(i, i ^ distance) for i in range(size)])  6.98 us
    pallas_call x1, Pallas kernels, body(): pl.pallas_call(functools.partial(open_kernel, count, local_heads), out_sh...  2.57 us
    pallas_call x1, Pallas kernels, body(): pl.pallas_call(functools.partial(keep_kernel, replicas), out_shape=shape(...  2.06 us
    pallas_call x1, Pallas kernels, body(): pl.pallas_call(functools.partial(finish_kernel, count, replicas, local_he...  1.91 us
    pallas_call x1, Pallas kernels, body(): pl.pallas_call(functools.partial(leave_kernel, rows), out_shape=[shape(po...  1.71 us
    pallas_call x1, Pallas kernels, body(): pl.pallas_call(functools.partial(attend_kernel, count, local_heads), out_...  1.52 us
    pallas_call x1, Pallas kernels, body(): pl.pallas_call(functools.partial(arrive_kernel, count, replicas, local_he...  1.26 us
  transfers between devices with their start and end apart: 9, of which 4 were waited for; matrix products, arithmetic and copies ran while one was open for 0% of the time, Pallas kernels for 20%

profile of v6, /device:TPU:0, one launch (start us, length us, event | category | flops | bytes accessed | tf_op | source)
XLA Modules:
  0.0 30.5 jit_solution(6843225609407971381)
XLA Ops:
  0.6 0.0 copy-start.1
  0.6 0.0 copy-start.2
  0.7 1.7 %leave.1 = (bf16[8,128,1024]{2,1,0:T(8,128)(2,1)S(1)}, bf16[136,1024]{1,0:T(8,128)(2,1)S(1)}, bf16[136,1024]{1,0:T(8,128)(2,1)S(1)}, bf16[136,1024]{1,0:T(8,128)(2,1)S(1)}) custom-call(s32[2,8]{1,0:T(2,128)} %bitcast.11, s32[4,8]{1,0:T(4,128)} %bitcast.15, s32[8]{0:T(128)} %refs_4_.3, bf16[16,2048]{1,0:T(8,128)(2,1)} %bitcast.6, bf16[8,128,1024]{2,1,0:T(8,128)(2,1)} %bitcast.18), custom_call_target="tpu_custom_call" | custom-call | bytes 6300000 | tf_op jit(solution)/shard_map/leave/pallas_call | solution.py:510
  2.4 0.5 %collective-permute-start.2 = (bf16[136,1024]{1,0:T(8,128)(2,1)S(1)}, bf16[136,1024]{1,0:T(8,128)(2,1)S(1)}, u32[]{:S(2)}, u32[]{:S(2)}) collective-permute-start(bf16[136,1024]{1,0:T(8,128)(2,1)S(1)} %get-tuple-element.36), channel_id=1, source_target_pairs={{0,4},{4,0},{8,12},{12,8},{1,5},{5,1},{9,13},{13,9},{2,6},{6,2},{1... | collective-permute-start | bytes 835592 | tf_op jit(solution)/shard_map/ppermute | solution.py:30
  2.9 2.6 %collective-permute-start = (bf16[136,1024]{1,0:T(8,128)(2,1)S(1)}, bf16[136,1024]{1,0:T(8,128)(2,1)S(1)}, u32[]{:S(2)}, u32[]{:S(2)}) collective-permute-start(bf16[136,1024]{1,0:T(8,128)(2,1)S(1)} %get-tuple-element.30), channel_id=1, source_target_pairs={{0,8},{4,12},{8,0},{12,4},{1,9},{5,13},{9,1},{13,5},{2,10},{6,14},... | collective-permute-start | bytes 835592 | tf_op jit(solution)/shard_map/ppermute | solution.py:30
  5.5 0.1 collective-permute-start.1
  5.5 0.0 copy-done.1
  5.5 2.6 %open.1 = (bf16[192,128]{1,0:T(8,128)(2,1)S(1)}, bf16[192,128]{1,0:T(8,128)(2,1)S(1)}, bf16[192,128]{1,0:T(8,128)(2,1)S(1)}, bf16[192,128]{1,0:T(8,128)(2,1)S(1)}) custom-call(bf16[16,2048]{1,0:T(8,128)(2,1)S(1)} %bitcast.7, bf16[2,8,1024]{2,1,0:T(8,128)(2,1)S(1)} %copy-done.2, bf16[2048,1024]{1,0:T(8,128)(2,1)} %refs_4_.2), custom_call_target="tpu_custom_call" | custom-call | bytes 4200000 | tf_op jit(solution)/shard_map/open/pallas_call | solution.py:530
  8.1 0.0 copy-start.3
  8.1 0.0 copy-start.4
  8.1 0.0 collective-permute-done.2.refs_5_.refs_0_.refs_11_
  8.1 2.9 %collective-permute-start.3 = (bf16[192,128]{1,0:T(8,128)(2,1)S(1)}, bf16[192,128]{1,0:T(8,128)(2,1)S(1)}, u32[]{:S(2)}, u32[]{:S(2)}) collective-permute-start(bf16[192,128]{1,0:T(8,128)(2,1)S(1)} %get-tuple-element.38), channel_id=1, source_target_pairs={{0,2},{1,3},{2,0},{3,1},{4,6},{5,7},{6,4},{7,5},{8,10},{9,11},{10,... | collective-permute-start | bytes 147464 | tf_op jit(solution)/shard_map/ppermute | solution.py:30
  11.0 1.3 %collective-permute-start.4 = (bf16[192,128]{1,0:T(8,128)(2,1)S(1)}, bf16[192,128]{1,0:T(8,128)(2,1)S(1)}, u32[]{:S(2)}, u32[]{:S(2)}) collective-permute-start(bf16[192,128]{1,0:T(8,128)(2,1)S(1)} %get-tuple-element.39), channel_id=1, source_target_pairs={{0,3},{1,2},{2,1},{3,0},{4,7},{5,6},{6,5},{7,4},{8,11},{9,10},{10,... | collective-permute-start | bytes 147464 | tf_op jit(solution)/shard_map/ppermute | solution.py:30
  12.4 0.2 collective-permute-start.5
  12.6 0.7 %collective-permute-done.3.refs_0_.refs_6_ = bf16[192,128]{1,0:T(8,128)(2,1)S(1)} collective-permute-done((bf16[192,128]{1,0:T(8,128)(2,1)S(1)}, bf16[192,128]{1,0:T(8,128)(2,1)S(1)}, u32[]{:S(2)}, u32[]{:S(2)}) %collective-permute-start.3) | collective-permute-done | bytes 49184 | tf_op jit(solution)/shard_map/ppermute | solution.py:30
  13.3 3.8 %collective-permute-done.4.refs_1_.refs_7_ = bf16[192,128]{1,0:T(8,128)(2,1)S(1)} collective-permute-done((bf16[192,128]{1,0:T(8,128)(2,1)S(1)}, bf16[192,128]{1,0:T(8,128)(2,1)S(1)}, u32[]{:S(2)}, u32[]{:S(2)}) %collective-permute-start.4) | collective-permute-done | bytes 49184 | tf_op jit(solution)/shard_map/ppermute | solution.py:30
  17.1 0.0 collective-permute-done.5.refs_2_.refs_8_
  17.1 1.5 %attend.1 = (f32[4,128,128]{2,1,0:T(8,128)S(1)}, f32[4,16,128]{2,1,0:T(8,128)S(1)}) custom-call(s32[4,8]{1,0:T(4,128)S(1)} %bitcast.16, s32[8]{0:T(128)S(1)} %copy-done.6, bf16[8,128,1024]{2,1,0:T(8,128)(2,1)S(1)} %get-tuple-element.42.pool.refs_3_.refs_15_, bf16[192,128]{1,0:T(8,128)(2,1)S(1)} %collective-permute-done.3.refs_0_.refs_6_, ...), custom_call_target="tpu_custom_call" | custom-call | bytes 5250000 | tf_op jit(solution)/shard_map/attend/pallas_call | solution.py:543
  18.6 0.0 collective-permute-done.refs_0_.refs_1_
  18.6 0.0 collective-permute-done.1.refs_1_.refs_2_
  18.7 0.0 copy-done
  18.7 0.0 copy-done.3
  18.7 0.0 copy-done.4
  18.7 1.3 %arrive.1 = (bf16[208,128]{1,0:T(8,128)(2,1)S(1)}, bf16[208,128]{1,0:T(8,128)(2,1)S(1)}, bf16[208,128]{1,0:T(8,128)(2,1)S(1)}, f32[128,128]{1,0:T(8,128)S(1)}, f...) custom-call(bf16[136,1024]{1,0:T(8,128)(2,1)S(1)} %collective-permute-don, ...), custom_call_target="tpu_custom_call" | custom-call | bytes 4200000 | tf_op jit(solution)/shard_map/arrive/pallas_call | solution.py:555
  20.0 2.5 %collective-permute-start.6 = (bf16[208,128]{1,0:T(8,128)(2,1)S(1)}, bf16[208,128]{1,0:T(8,128)(2,1)S(1)}, u32[]{:S(2)}, u32[]{:S(2)}) collective-permute-start(bf16[208,128]{1,0:T(8,128)(2,1)S(1)} %get-tuple-element.50), channel_id=1, source_target_pairs={{0,2},{1,3},{2,0},{3,1},{4,6},{5,7},{6,4},{7,5},{8,10},{9,11},{10,... | collective-permute-start | bytes 159752 | tf_op jit(solution)/shard_map/ppermute | solution.py:30
  22.4 1.3 %collective-permute-start.7 = (bf16[208,128]{1,0:T(8,128)(2,1)S(1)}, bf16[208,128]{1,0:T(8,128)(2,1)S(1)}, u32[]{:S(2)}, u32[]{:S(2)}) collective-permute-start(bf16[208,128]{1,0:T(8,128)(2,1)S(1)} %get-tuple-element.51), channel_id=1, source_target_pairs={{0,3},{1,2},{2,1},{3,0},{4,7},{5,6},{6,5},{7,4},{8,11},{9,10},{10,... | collective-permute-start | bytes 159752 | tf_op jit(solution)/shard_map/ppermute | solution.py:30
  23.8 0.2 collective-permute-start.8
  24.0 2.1 %keep.1.refs_16_ = bf16[8,128,1024]{2,1,0:T(8,128)(2,1)} custom-call(bf16[136,1024]{1,0:T(8,128)(2,1)S(1)} %collective-permute-done.2.refs_5_.refs_0_.refs_11_, bf16[136,1024]{1,0:T(8,128)(2,1)S(1)} %collective-permute-done.refs_0_.refs_1_, bf16[136,1024]{1,0:T(8,128)(2,1)S(1)} %collective-permute-done.1.refs_1_.refs_2_, ...), custom_call_target="tpu_custom_call" | custom-call | bytes 5600000 | tf_op jit(solution)/shard_map/keep/pallas_call | solution.py:582
  26.1 0.2 collective-permute-done.6.refs_12_
  26.3 2.3 %collective-permute-done.7.refs_13_ = bf16[208,128]{1,0:T(8,128)(2,1)S(1)} collective-permute-done((bf16[208,128]{1,0:T(8,128)(2,1)S(1)}, bf16[208,128]{1,0:T(8,128)(2,1)S(1)}, u32[]{:S(2)}, u32[]{:S(2)}) %collective-permute-start.7) | collective-permute-done | bytes 53280 | tf_op jit(solution)/shard_map/ppermute | solution.py:30
  28.6 0.0 collective-permute-done.8.refs_14_
  28.6 1.9 %finish.1 = (bf16[8,1024]{1,0:T(8,128)(2,1)}, bf16[8,1024]{1,0:T(8,128)(2,1)}, bf16[8,128,1024]{2,1,0:T(8,128)(2,1)}) custom-call(bf16[136,1024]{1,0:T(8,128)(2,1)S(1)} %collective-permute-done.refs_0_.refs_1_, bf16[136,1024]{1,0:T(8,128)(2,1)S(1)} %collective-permute-done.1.refs_1_.refs_2_, s32[2,8]{1,0:T(2,128)S(1)} %bitcast.14, ...), custom_call_target="tpu_custom_call", output_to_operand_aliasing={{2}: (16, {})} | custom-call | bytes 8750000 | tf_op jit(solution)/shard_map/finish/pallas_call | solution.py:598
  (6 shorter events, 0.0 us)
Async XLA Ops:
  0.6 4.9 %copy-start.1 = (bf16[2,8,2048]{2,1,0:T(8,128)(2,1)S(1)}, bf16[2,8,2048]{2,1,0:T(8,128)(2,1)}, u32[]{:S(2)}) copy-start(bf16[2,8,2048]{2,1,0:T(8,128)(2,1)} %param.8) | copy-start | bytes 196612
  0.6 4.9 %copy-start.2 = (bf16[2,8,1024]{2,1,0:T(8,128)(2,1)S(1)}, bf16[2,8,1024]{2,1,0:T(8,128)(2,1)}, u32[]{:S(2)}) copy-start(bf16[2,8,1024]{2,1,0:T(8,128)(2,1)} %q.1) | copy-start | bytes 98308
  2.4 5.8 %collective-permute-start.2 = (bf16[136,1024]{1,0:T(8,128)(2,1)S(1)}, bf16[136,1024]{1,0:T(8,128)(2,1)S(1)}, u32[]{:S(2)}, u32[]{:S(2)}) collective-permute-start(bf16[136,1024]{1,0:T(8,128)(2,1)S(1)} %get-tuple-element.36), channel_id=1, source_target_pairs={{0,4},{4,0},{8,12},{12,8},{1,5},{5,1},{9,13},{13,9},{2,6},{6,2},{1... | collective-permute-start | bytes 835592 | tf_op jit(solution)/shard_map/ppermute | solution.py:30
  2.9 15.8 %collective-permute-start = (bf16[136,1024]{1,0:T(8,128)(2,1)S(1)}, bf16[136,1024]{1,0:T(8,128)(2,1)S(1)}, u32[]{:S(2)}, u32[]{:S(2)}) collective-permute-start(bf16[136,1024]{1,0:T(8,128)(2,1)S(1)} %get-tuple-element.30), channel_id=1, source_target_pairs={{0,8},{4,12},{8,0},{12,4},{1,9},{5,13},{9,1},{13,5},{2,10},{6,14},... | collective-permute-start | bytes 835592 | tf_op jit(solution)/shard_map/ppermute | solution.py:30
  5.5 11.7 %copy-start.5 = (s32[8,4]{0,1:T(4,128)S(1)}, s32[8,4]{0,1:T(4,128)}, u32[]{:S(2)}) copy-start(s32[8,4]{0,1:T(4,128)} %param.13) | copy-start | bytes 388
  5.5 11.7 %copy-start.6 = (s32[8]{0:T(128)S(1)}, s32[8]{0:T(128)}, u32[]{:S(2)}) copy-start(s32[8]{0:T(128)} %refs_4_.3) | copy-start | bytes 100
  5.5 13.2 %collective-permute-start.1 = (bf16[136,1024]{1,0:T(8,128)(2,1)S(1)}, bf16[136,1024]{1,0:T(8,128)(2,1)S(1)}, u32[]{:S(2)}, u32[]{:S(2)}) collective-permute-start(bf16[136,1024]{1,0:T(8,128)(2,1)S(1)} %get-tuple-element.31), channel_id=1, source_target_pairs={{0,12},{4,8},{8,4},{12,0},{1,13},{5,9},{9,5},{13,1},{2,14},{6,10},... | collective-permute-start | bytes 835592 | tf_op jit(solution)/shard_map/ppermute | solution.py:30
  5.5 13.1 %copy-start = (bf16[2048,1024]{1,0:T(8,128)(2,1)S(1)}, bf16[2048,1024]{1,0:T(8,128)(2,1)}, u32[]{:S(2)}) copy-start(bf16[2048,1024]{1,0:T(8,128)(2,1)} %refs_4_.2) | copy-start | bytes 12582916
  8.1 10.6 %copy-start.3 = (s32[8,4]{0,1:T(4,128)S(1)}, s32[8,4]{0,1:T(4,128)}, u32[]{:S(2)}) copy-start(s32[8,4]{0,1:T(4,128)} %param.14) | copy-start | bytes 388
  8.1 10.6 %copy-start.4 = (s32[8,2]{0,1:T(2,128)S(1)}, s32[8,2]{0,1:T(2,128)}, u32[]{:S(2)}) copy-start(s32[8,2]{0,1:T(2,128)} %param.15) | copy-start | bytes 196
  8.1 5.1 %collective-permute-start.3 = (bf16[192,128]{1,0:T(8,128)(2,1)S(1)}, bf16[192,128]{1,0:T(8,128)(2,1)S(1)}, u32[]{:S(2)}, u32[]{:S(2)}) collective-permute-start(bf16[192,128]{1,0:T(8,128)(2,1)S(1)} %get-tuple-element.38), channel_id=1, source_target_pairs={{0,2},{1,3},{2,0},{3,1},{4,6},{5,7},{6,4},{7,5},{8,10},{9,11},{10,... | collective-permute-start | bytes 147464 | tf_op jit(solution)/shard_map/ppermute | solution.py:30
  11.0 6.1 %collective-permute-start.4 = (bf16[192,128]{1,0:T(8,128)(2,1)S(1)}, bf16[192,128]{1,0:T(8,128)(2,1)S(1)}, u32[]{:S(2)}, u32[]{:S(2)}) collective-permute-start(bf16[192,128]{1,0:T(8,128)(2,1)S(1)} %get-tuple-element.39), channel_id=1, source_target_pairs={{0,3},{1,2},{2,1},{3,0},{4,7},{5,6},{6,5},{7,4},{8,11},{9,10},{10,... | collective-permute-start | bytes 147464 | tf_op jit(solution)/shard_map/ppermute | solution.py:30
  12.4 4.7 %collective-permute-start.5 = (bf16[192,128]{1,0:T(8,128)(2,1)S(1)}, bf16[192,128]{1,0:T(8,128)(2,1)S(1)}, u32[]{:S(2)}, u32[]{:S(2)}) collective-permute-start(bf16[192,128]{1,0:T(8,128)(2,1)S(1)} %get-tuple-element.40), channel_id=1, source_target_pairs={{0,1},{1,0},{2,3},{3,2},{4,5},{5,4},{6,7},{7,6},{8,9},{9,8},{10,11... | collective-permute-start | bytes 147464 | tf_op jit(solution)/shard_map/ppermute | solution.py:30
  20.0 6.3 %collective-permute-start.6 = (bf16[208,128]{1,0:T(8,128)(2,1)S(1)}, bf16[208,128]{1,0:T(8,128)(2,1)S(1)}, u32[]{:S(2)}, u32[]{:S(2)}) collective-permute-start(bf16[208,128]{1,0:T(8,128)(2,1)S(1)} %get-tuple-element.50), channel_id=1, source_target_pairs={{0,2},{1,3},{2,0},{3,1},{4,6},{5,7},{6,4},{7,5},{8,10},{9,11},{10,... | collective-permute-start | bytes 159752 | tf_op jit(solution)/shard_map/ppermute | solution.py:30
  22.4 6.1 %collective-permute-start.7 = (bf16[208,128]{1,0:T(8,128)(2,1)S(1)}, bf16[208,128]{1,0:T(8,128)(2,1)S(1)}, u32[]{:S(2)}, u32[]{:S(2)}) collective-permute-start(bf16[208,128]{1,0:T(8,128)(2,1)S(1)} %get-tuple-element.51), channel_id=1, source_target_pairs={{0,3},{1,2},{2,1},{3,0},{4,7},{5,6},{6,5},{7,4},{8,11},{9,10},{10,... | collective-permute-start | bytes 159752 | tf_op jit(solution)/shard_map/ppermute | solution.py:30
  23.8 4.8 %collective-permute-start.8 = (bf16[208,128]{1,0:T(8,128)(2,1)S(1)}, bf16[208,128]{1,0:T(8,128)(2,1)S(1)}, u32[]{:S(2)}, u32[]{:S(2)}) collective-permute-start(bf16[208,128]{1,0:T(8,128)(2,1)S(1)} %get-tuple-element.52), channel_id=1, source_target_pairs={{0,1},{1,0},{2,3},{3,2},{4,5},{5,4},{6,7},{7,6},{8,9},{9,8},{10,11... | collective-permute-start | bytes 159752 | tf_op jit(solution)/shard_map/ppermute | solution.py:30

commit v7 on v6

--- a/solution.py
+++ b/solution.py
@@ -16,7 +16,6 @@
 SCALE = 1.0 / math.sqrt(HD)
 WINDOW = 32
 KV_ROWS = 24
-EXTRA = 8
 
 SMEM = pl.BlockSpec(memory_space=pltpu.SMEM)
 VMEM = pl.BlockSpec(memory_space=pltpu.VMEM)
@@ -101,8 +100,16 @@
     return jnp.exp(CAP * jnp.tanh(score * (SCALE / CAP)))
 
 
-def pieces_of(depth, width):
-    return [slice(at, min(at + width, depth)) for at in range(0, depth, width)]
+def pieces_of(width):
+    return [slice(at, at + HD) for at in range(0, width, HD)]
+
+
+def page_lines(width, page_size):
+    return [j * page_size for j in range(width // HD)]
+
+
+def extra_lines(depth):
+    return -(-(2 + depth // HD) // 8) * 8
 
 
 def start_copies(pairs, sems):
@@ -130,22 +137,24 @@
     found = [pair_row(moves, me, partner("replica", s + 1), rows, 0)[1] for s in range(len(pages))]
     picks = [locate(table, row, column, pool.shape[0])[1] for row in found]
     wait_for(rest[2:])
-    sublane = lax.broadcasted_iota(jnp.int32, (EXTRA, width), 0)
+    lines = extra_lines(depth)
+    sublane = lax.broadcasted_iota(jnp.int32, (lines, HD), 0)
     first_rows = x[:rows, :].astype(jnp.float32)
     row_ids = lax.broadcasted_iota(jnp.int32, (rows, depth), 0)
     for row, page in zip(found, pages):
         high, low = split(lengths[row], 64)
-        extra = jnp.where(sublane == 0, high, low).astype(jnp.float32)
         picked = jnp.sum(jnp.where(row_ids == row, first_rows, 0.0), axis=0, keepdims=True)
-        for i, piece in enumerate(pieces_of(depth, width)):
-            value = picked[:, piece]
-            if value.shape[1] < width:
-                value = jnp.concatenate([value, jnp.zeros((1, width - value.shape[1]), jnp.float32)], axis=1)
-            extra = jnp.where(sublane == 2 + i, value, extra)
-        page[page_size:, :] = extra.astype(jnp.bfloat16)
+        parts = [jnp.zeros((2, HD), jnp.float32)] + [picked[:, piece] for piece in pieces_of(depth)]
+        spare = lines - 2 - depth // HD
+        parts += [jnp.zeros((spare, HD), jnp.float32)] if spare else []
+        extra = jnp.concatenate(parts, axis=0)
+        extra = jnp.where(sublane == 0, high.astype(jnp.float32), extra)
+        extra = jnp.where(sublane == 1, low.astype(jnp.float32), extra)
+        page[page_size * width // HD :, :] = extra.astype(jnp.bfloat16)
     wait_for(copies)
     for slot, page in zip(picks, pages):
-        page[:page_size, :] = held[slot]
+        for line, piece in zip(page_lines(width, page_size), pieces_of(width)):
+            page[line : line + page_size, :] = held[slot, :, piece]
 
 
 def open_kernel(count, local_heads, x, q, weight, *refs):
@@ -187,26 +196,40 @@
     wait_for(start_copies(((moves_all, moves), (table_all, table)), sems))
     me, column = lax.axis_index("replica"), lax.axis_index("mp")
     rows = table.shape[1]
-    slots, page_size, _ = pool.shape
+    slots, page_size, width = pool.shape
     kept, copies = [jnp.bool_(True)] * rows, []
     for s, page in enumerate(pages_in):
         valid, row, _ = pair_row(moves, partner("replica", s + 1), me, rows, 1)
         kept = [stays & ~((valid == 1) & (row == r)) for r, stays in enumerate(kept)]
-        copies.append((valid == 1, row, lambda slot, page=page: page.at[pl.ds(0, page_size)]))
-    copies += [(stays, r, lambda slot: pool.at[slot]) for r, stays in enumerate(kept)]
+        copies.append((valid == 1, row, page))
+    copies += [(stays, r, None) for r, stays in enumerate(kept)]
     started = []
-    for n, (active, row, source) in enumerate(copies):
+    for n, (active, row, page) in enumerate(copies):
         _, slot = locate(table, row, column, slots)
-        copy = pltpu.make_async_copy(source(slot), pool_out.at[slot], page_sems.at[n])
-        started.append((active, copy))
-        pl.when(active)(copy.start)
-    for active, copy in started:
-        pl.when(active)(copy.wait)
-
-
-def length_of(page, page_size):
-    part = page[page_size:, :HD].astype(jnp.float32)
-    return part[0:1] * 64.0 + part[1:2]
+        pairs = [(pool.at[slot], pool_out.at[slot])]
+        if page is not None:
+            pairs = [
+                (page.at[pl.ds(line, page_size)], pool_out.at[slot, :, piece])
+                for line, piece in zip(page_lines(width, page_size), pieces_of(width))
+            ]
+        parts = [pltpu.make_async_copy(*pair, page_sems.at[n, i]) for i, pair in enumerate(pairs)]
+        started.append((active, parts))
+
+        @pl.when(active)
+        def _(parts=parts):
+            for copy in parts:
+                copy.start()
+
+    for active, parts in started:
+        pl.when(active)(functools.partial(wait_for, parts))
+
+
+def extra_of(page, page_size, width):
+    return page[page_size * width // HD :, :].astype(jnp.float32)
+
+
+def length_of(extra):
+    return extra[0:1] * 64.0 + extra[1:2]
 
 
 def own_tokens(messages, rows, query_rows, half):
@@ -259,7 +282,7 @@
         den[s] = denominators[s]
 
 
-def arrive_kernel(count, replicas, local_heads, slots, *refs):
+def arrive_kernel(count, replicas, local_heads, slots, page_size, *refs):
     refs = list(refs)
     take = lambda n: [refs.pop(0) for _ in range(n)]
     pages_in = take(replicas - 2)
@@ -271,18 +294,13 @@
     tables = start_copies(((moves_all, moves), (table_all, table)), sems)
     me, column = lax.axis_index("replica"), lax.axis_index("mp")
     rows = table.shape[1]
-    page_size, width = pages_in[0].shape[0] - EXTRA, pages_in[0].shape[1]
+    depth, width = projection.shape
     half_rows = local_heads * rows
     movers = moves.shape[1] // replicas
 
-    depth = projection.shape[0]
-    extra = [page[page_size:, :].astype(jnp.float32) for page in pages_in]
+    extra = [extra_of(page, page_size, width) for page in pages_in]
     inputs = [
-        jnp.concatenate(
-            [part[2 + i : 3 + i, : piece.stop - piece.start] for i, piece in enumerate(pieces_of(depth, width))],
-            axis=1,
-        )
-        for part in extra
+        jnp.concatenate([part[2 + i : 3 + i] for i in range(depth // HD)], axis=1) for part in extra
     ]
     inputs += [jnp.zeros((8 - len(inputs), depth), jnp.float32)]
     inputs = jnp.concatenate(inputs, axis=0).astype(jnp.bfloat16)
@@ -291,12 +309,14 @@
     den[...] = den_in[...]
     for s, message in enumerate(messages):
         wide[s] = message[half_rows : 2 * half_rows, :].astype(jnp.float32)
-    lengths = [length_of(page, page_size) for page in pages_in]
+    lengths = [length_of(part) for part in extra]
 
     wait_for(tables)
     lane = lax.broadcasted_iota(jnp.int32, (local_heads, HD), 1)
     token = lax.broadcasted_iota(jnp.int32, (local_heads, page_size), 1)
-    columns = [head_columns(partner("mp", s), local_heads) for s in range(count)]
+    lines = [
+        pl.multiple_of(split(partner("mp", s) * local_heads, GROUP)[0] * page_size, page_size) for s in range(count)
+    ]
     cases = [(d, s) for d in range(1, replicas) for s in range(count)]
     arrivals = [pair_row(moves, partner("replica", d), me, rows, 1) for d in range(1, replicas)]
     places = [locate(table, row, column, slots) for _, row, _ in arrivals]
@@ -304,16 +324,15 @@
     for d, s in cases:
         row = arrivals[d - 1][1]
         q = wide[s, pl.ds(row, local_heads, stride=rows), :].astype(jnp.bfloat16)
-        keys = pages_in[d - 1].at[pl.ds(0, page_size), pl.ds(0, width // 2)]
-        scores[d, s] = scores_of(q, keys[:, columns[s]])
+        scores[d, s] = scores_of(q, pages_in[d - 1][pl.ds(lines[s], page_size), :])
     for d, s in cases:
         inside = (token + places[d - 1][0] * page_size).astype(jnp.float32) < lengths[d - 1]
         weight = jnp.where(inside, weight_of(scores[d, s]), 0.0)
         weights[d, s] = weight.astype(jnp.bfloat16)
         totals[d, s] = jnp.sum(weight, axis=1, keepdims=True)
     for d, s in cases:
-        values = pages_in[d - 1].at[pl.ds(0, page_size), pl.ds(width // 2, width // 2)]
-        scores[d, s] = jnp.dot(weights[d, s], values[:, columns[s]], preferred_element_type=jnp.float32)
+        values = pages_in[d - 1][pl.ds(lines[s] + KVH * page_size, page_size), :]
+        scores[d, s] = jnp.dot(weights[d, s], values, preferred_element_type=jnp.float32)
     for d, (valid, row, _) in enumerate(arrivals, 1):
 
         @pl.when(valid == 1)
@@ -444,26 +463,31 @@
         start = jnp.clip(at, 0, page_size - WINDOW) & -16
         span = pl.ds(pl.multiple_of(start, 16), WINDOW)
         n = len(plans)
-        source = source.at[slot] if r is not None else source
+        if r is None:
+            read = lambda: jnp.concatenate(
+                [source[pl.ds(pl.multiple_of(line + start, 16), WINDOW), :] for line in page_lines(width, page_size)],
+                axis=1,
+            )
+        else:
+            read = lambda: source[slot, span, :]
         write = pltpu.make_async_copy(windows.at[n], pool.at[slot, span], write_sems.at[n])
-        plans.append((touched, source, span, write, first_token, rows + row, at - start))
+        plans.append((touched, read, write, first_token, rows + row, at - start))
 
     for s, page in enumerate(pages_in):
         valid, row, order = pair_row(moves, partner("replica", s + 1), me, rows, 1)
         valid = valid == 1
-        length = jnp.max(length_of(page, page_size)).astype(jnp.int32)
-        page = page.at[pl.ds(0, page_size)]
+        length = jnp.max(length_of(extra_of(page, page_size, width))).astype(jnp.int32)
         add_plan(valid, row, length, 2 * rows + order, page)
         kept = [stays & ~(valid & (row == r)) for r, stays in enumerate(kept)]
     for r in range(rows):
         add_plan(kept[r], r, lengths[r], r, pool_raw, r)
 
     place_ids = lax.broadcasted_iota(jnp.int32, (WINDOW, width), 0)
-    for n, (touched, source, span, write, token, next_token, offset) in enumerate(plans):
+    for n, (touched, read, write, token, next_token, offset) in enumerate(plans):
 
         @pl.when(touched)
-        def _(n=n, source=source, span=span, write=write, token=token, next_token=next_token, offset=offset):
-            old = source[span, :].astype(jnp.float32)
+        def _(n=n, read=read, write=write, token=token, next_token=next_token, offset=offset):
+            old = read().astype(jnp.float32)
             new = jnp.where(place_ids == offset, full[pl.ds(token, 1), :], old)
             new = jnp.where(place_ids == offset + 1, full[pl.ds(next_token, 1), :], new)
             windows[n] = new.astype(jnp.bfloat16)
@@ -471,7 +495,7 @@
 
     finish_step(1, second)
     for plan in plans:
-        pl.when(plan[0])(plan[3].wait)
+        pl.when(plan[0])(plan[2].wait)
     wait_for(outs)
 
 
@@ -509,7 +533,7 @@
     inputs = layer_input.reshape(2 * rows, depth)
     pool_near, *leaving = pl.pallas_call(
         functools.partial(leave_kernel, rows),
-        out_shape=[shape(pool.shape, bf16)] + [shape((page_size + EXTRA, width), bf16)] * (replicas - 1),
+        out_shape=[shape(pool.shape, bf16)] + [shape((page_size * width // HD + extra_lines(depth), HD), bf16)] * (replicas - 1),
         in_specs=[HBM] * 5,
         out_specs=[VMEM] * replicas,
         scratch_shapes=[
@@ -553,7 +577,7 @@
 
     sum_rows = query_rows + -(-both // 16) * 16 + 4 * rows + 16 * movers
     *sums, num, den, kv, share, marks = pl.pallas_call(
-        functools.partial(arrive_kernel, count, replicas, local_heads, slots),
+        functools.partial(arrive_kernel, count, replicas, local_heads, slots, page_size),
         out_shape=[shape((sum_rows, HD), SEND)] * (count - 1)
         + [shape((query_rows, HD), f32), shape((both, HD), f32)]
         + [shape((2, 2 * rows, HD), f32), shape((movers, 2 * KVH, HD), f32)]
@@ -588,7 +612,7 @@
             pltpu.SMEM(moves.shape, jnp.int32),
             pltpu.SMEM(table_after.shape, jnp.int32),
             pltpu.SemaphoreType.DMA((2,)),
-            pltpu.SemaphoreType.DMA((rows + replicas - 1,)),
+            pltpu.SemaphoreType.DMA((rows + replicas - 1, width // HD)),
         ],
         compiler_params=params(),
         cost_estimate=cost(1.6),

time: 30.6 us -> 30.4 us (level)
  Pallas kernels: 11 us -> 11.8 us
  waiting for transfers between devices: 6.98 us -> 6.4 us
  starting transfers between devices: 11.7 us -> 11.2 us
    pallas_call x1, Pallas kernels: 2.06 us -> 2.72 us  [body(): pl.pallas_call(functools.partial(keep_kernel, replicas), out_shape=shape(...]
    ppermute x9, waiting for transfers between devices: 6.98 us -> 6.4 us  [swap(): return lax.ppermute(value, axis, [(i, i ^ distance) for i in range(size)])]
    ppermute x9, starting transfers between devices: 11.7 us -> 11.2 us  [swap(): return lax.ppermute(value, axis, [(i, i ^ distance) for i in range(size)])]
  transfers between devices with their start and end apart: 9 -> 9, of which waited for: 4 -> 4; matrix products, arithmetic and copies ran while one was open for 0% -> 0% of each run, Pallas kernels for 20% -> 23%
where the time goes in v7:
time: 30.4 us; the launch traced here: 30.2 us
  Pallas kernels  11.8 us (39%)
  starting transfers between devices  11.2 us (37%)
  waiting for transfers between devices  6.4 us (21%)
  between operations  0.76 us (2%)
    ppermute x9, starting transfers between devices, swap(): return lax.ppermute(value, axis, [(i, i ^ distance) for i in range(size)])  11.2 us
    ppermute x9, waiting for transfers between devices, swap(): return lax.ppermute(value, axis, [(i, i ^ distance) for i in range(size)])  6.4 us
    pallas_call x1, Pallas kernels, body(): pl.pallas_call(functools.partial(keep_kernel, replicas), out_shape=shape(...  2.72 us
    pallas_call x1, Pallas kernels, body(): pl.pallas_call(functools.partial(open_kernel, count, local_heads), out_sh...  2.57 us
    pallas_call x1, Pallas kernels, body(): pl.pallas_call(functools.partial(finish_kernel, count, replicas, local_he...  1.95 us
    pallas_call x1, Pallas kernels, body(): pl.pallas_call(functools.partial(leave_kernel, rows), out_shape=[shape(po...  1.8 us
    pallas_call x1, Pallas kernels, body(): pl.pallas_call(functools.partial(attend_kernel, count, local_heads), out_...  1.53 us
    pallas_call x1, Pallas kernels, body(): pl.pallas_call(functools.partial(arrive_kernel, count, replicas, local_he...  1.26 us
  transfers between devices with their start and end apart: 9, of which 4 were waited for; matrix products, arithmetic and copies ran while one was open for 0% of the time, Pallas kernels for 23%

profile of v7, /device:TPU:0, one launch (start us, length us, event | category | flops | bytes accessed | tf_op | source)
XLA Modules:
  0.0 30.2 jit_solution(7361242768859124734)
XLA Ops:
  0.6 0.0 copy-start.1
  0.6 0.0 copy-start.2
  0.7 1.8 %leave.1 = (bf16[8,128,1024]{2,1,0:T(8,128)(2,1)S(1)}, bf16[1048,128]{1,0:T(8,128)(2,1)S(1)}, bf16[1048,128]{1,0:T(8,128)(2,1)S(1)}, bf16[1048,128]{1,0:T(8,128)(2,1)S(1)}) custom-call(s32[2,8]{1,0:T(2,128)} %bitcast.11, s32[4,8]{1,0:T(4,128)} %bitcast.15, s32[8]{0:T(128)} %refs_4_.3, bf16[16,2048]{1,0:T(8,128)(2,1)} %bitcast.6, bf16[8,128,1024]{2,1,0:T(8,128)(2,1)} %bitcast.18), custom_call_target="tpu_custom_call" | custom-call | bytes 6300000 | tf_op jit(solution)/shard_map/leave/pallas_call | solution.py:534
  2.5 0.5 %collective-permute-start.2 = (bf16[1048,128]{1,0:T(8,128)(2,1)S(1)}, bf16[1048,128]{1,0:T(8,128)(2,1)S(1)}, u32[]{:S(2)}, u32[]{:S(2)}) collective-permute-start(bf16[1048,128]{1,0:T(8,128)(2,1)S(1)} %get-tuple-element.36), channel_id=1, source_target_pairs={{0,4},{4,0},{8,12},{12,8},{1,5},{5,1},{9,13},{13,9},{2,6},{6,2},{1... | collective-permute-start | bytes 804872 | tf_op jit(solution)/shard_map/ppermute | solution.py:29
  3.0 2.6 %collective-permute-start = (bf16[1048,128]{1,0:T(8,128)(2,1)S(1)}, bf16[1048,128]{1,0:T(8,128)(2,1)S(1)}, u32[]{:S(2)}, u32[]{:S(2)}) collective-permute-start(bf16[1048,128]{1,0:T(8,128)(2,1)S(1)} %get-tuple-element.30), channel_id=1, source_target_pairs={{0,8},{4,12},{8,0},{12,4},{1,9},{5,13},{9,1},{13,5},{2,10},{6,14},... | collective-permute-start | bytes 804872 | tf_op jit(solution)/shard_map/ppermute | solution.py:29
  5.5 0.1 collective-permute-start.1
  5.6 0.0 copy-done.1
  5.6 2.6 %open.1 = (bf16[192,128]{1,0:T(8,128)(2,1)S(1)}, bf16[192,128]{1,0:T(8,128)(2,1)S(1)}, bf16[192,128]{1,0:T(8,128)(2,1)S(1)}, bf16[192,128]{1,0:T(8,128)(2,1)S(1)}) custom-call(bf16[16,2048]{1,0:T(8,128)(2,1)S(1)} %bitcast.7, bf16[2,8,1024]{2,1,0:T(8,128)(2,1)S(1)} %copy-done.2, bf16[2048,1024]{1,0:T(8,128)(2,1)} %refs_4_.2), custom_call_target="tpu_custom_call" | custom-call | bytes 4200000 | tf_op jit(solution)/shard_map/open/pallas_call | solution.py:554
  8.2 0.0 copy-start.3
  8.2 0.0 copy-start.4
  8.2 0.0 collective-permute-done.2.refs_5_.refs_0_.refs_11_
  8.2 2.9 %collective-permute-start.3 = (bf16[192,128]{1,0:T(8,128)(2,1)S(1)}, bf16[192,128]{1,0:T(8,128)(2,1)S(1)}, u32[]{:S(2)}, u32[]{:S(2)}) collective-permute-start(bf16[192,128]{1,0:T(8,128)(2,1)S(1)} %get-tuple-element.38), channel_id=1, source_target_pairs={{0,2},{1,3},{2,0},{3,1},{4,6},{5,7},{6,4},{7,5},{8,10},{9,11},{10,... | collective-permute-start | bytes 147464 | tf_op jit(solution)/shard_map/ppermute | solution.py:29
  11.1 1.3 %collective-permute-start.4 = (bf16[192,128]{1,0:T(8,128)(2,1)S(1)}, bf16[192,128]{1,0:T(8,128)(2,1)S(1)}, u32[]{:S(2)}, u32[]{:S(2)}) collective-permute-start(bf16[192,128]{1,0:T(8,128)(2,1)S(1)} %get-tuple-element.39), channel_id=1, source_target_pairs={{0,3},{1,2},{2,1},{3,0},{4,7},{5,6},{6,5},{7,4},{8,11},{9,10},{10,... | collective-permute-start | bytes 147464 | tf_op jit(solution)/shard_map/ppermute | solution.py:29
  12.5 0.2 collective-permute-start.5
  12.7 0.7 %collective-permute-done.3.refs_0_.refs_6_ = bf16[192,128]{1,0:T(8,128)(2,1)S(1)} collective-permute-done((bf16[192,128]{1,0:T(8,128)(2,1)S(1)}, bf16[192,128]{1,0:T(8,128)(2,1)S(1)}, u32[]{:S(2)}, u32[]{:S(2)}) %collective-permute-start.3) | collective-permute-done | bytes 49184 | tf_op jit(solution)/shard_map/ppermute | solution.py:29
  13.4 3.8 %collective-permute-done.4.refs_1_.refs_7_ = bf16[192,128]{1,0:T(8,128)(2,1)S(1)} collective-permute-done((bf16[192,128]{1,0:T(8,128)(2,1)S(1)}, bf16[192,128]{1,0:T(8,128)(2,1)S(1)}, u32[]{:S(2)}, u32[]{:S(2)}) %collective-permute-start.4) | collective-permute-done | bytes 49184 | tf_op jit(solution)/shard_map/ppermute | solution.py:29
  17.2 0.0 collective-permute-done.5.refs_2_.refs_8_
  17.2 1.5 %attend.1 = (f32[4,128,128]{2,1,0:T(8,128)S(1)}, f32[4,16,128]{2,1,0:T(8,128)S(1)}) custom-call(s32[4,8]{1,0:T(4,128)S(1)} %bitcast.16, s32[8]{0:T(128)S(1)} %copy-done.6, bf16[8,128,1024]{2,1,0:T(8,128)(2,1)S(1)} %get-tuple-element.42.pool.refs_3_.refs_15_, bf16[192,128]{1,0:T(8,128)(2,1)S(1)} %collective-permute-done.3.refs_0_.refs_6_, ...), custom_call_target="tpu_custom_call" | custom-call | bytes 5250000 | tf_op jit(solution)/shard_map/attend/pallas_call | solution.py:567
  18.7 0.0 collective-permute-done.refs_0_.refs_1_
  18.7 0.0 collective-permute-done.1.refs_1_.refs_2_
  18.7 0.0 copy-done
  18.8 0.0 copy-done.3
  18.8 0.0 copy-done.4
  18.8 1.3 %arrive.1 = (bf16[208,128]{1,0:T(8,128)(2,1)S(1)}, bf16[208,128]{1,0:T(8,128)(2,1)S(1)}, bf16[208,128]{1,0:T(8,128)(2,1)S(1)}, f32[128,128]{1,0:T(8,128)S(1)}, f...) custom-call(bf16[1048,128]{1,0:T(8,128)(2,1)S(1)} %collective-permute-don, ...), custom_call_target="tpu_custom_call" | custom-call | bytes 4200000 | tf_op jit(solution)/shard_map/arrive/pallas_call | solution.py:579
  20.0 2.1 %collective-permute-start.6 = (bf16[208,128]{1,0:T(8,128)(2,1)S(1)}, bf16[208,128]{1,0:T(8,128)(2,1)S(1)}, u32[]{:S(2)}, u32[]{:S(2)}) collective-permute-start(bf16[208,128]{1,0:T(8,128)(2,1)S(1)} %get-tuple-element.50), channel_id=1, source_target_pairs={{0,2},{1,3},{2,0},{3,1},{4,6},{5,7},{6,4},{7,5},{8,10},{9,11},{10,... | collective-permute-start | bytes 159752 | tf_op jit(solution)/shard_map/ppermute | solution.py:29
  22.1 1.3 %collective-permute-start.7 = (bf16[208,128]{1,0:T(8,128)(2,1)S(1)}, bf16[208,128]{1,0:T(8,128)(2,1)S(1)}, u32[]{:S(2)}, u32[]{:S(2)}) collective-permute-start(bf16[208,128]{1,0:T(8,128)(2,1)S(1)} %get-tuple-element.51), channel_id=1, source_target_pairs={{0,3},{1,2},{2,1},{3,0},{4,7},{5,6},{6,5},{7,4},{8,11},{9,10},{10,... | collective-permute-start | bytes 159752 | tf_op jit(solution)/shard_map/ppermute | solution.py:29
  23.4 0.2 collective-permute-start.8
  23.6 2.7 %keep.1.refs_16_ = bf16[8,128,1024]{2,1,0:T(8,128)(2,1)} custom-call(bf16[1048,128]{1,0:T(8,128)(2,1)S(1)} %collective-permute-done.2.refs_5_.refs_0_.refs_11_, bf16[1048,128]{1,0:T(8,128)(2,1)S(1)} %collective-permute-done.refs_0_.refs_1_, bf16[1048,128]{1,0:T(8,128)(2,1)S(1)} %collective-permute-done.1.refs_1_.refs_2_, ...), custom_call_target="tpu_custom_call" | custom-call | bytes 5600000 | tf_op jit(solution)/shard_map/keep/pallas_call | solution.py:606
  26.4 0.0 collective-permute-done.6.refs_12_
  26.4 1.8 %collective-permute-done.7.refs_13_ = bf16[208,128]{1,0:T(8,128)(2,1)S(1)} collective-permute-done((bf16[208,128]{1,0:T(8,128)(2,1)S(1)}, bf16[208,128]{1,0:T(8,128)(2,1)S(1)}, u32[]{:S(2)}, u32[]{:S(2)}) %collective-permute-start.7) | collective-permute-done | bytes 53280 | tf_op jit(solution)/shard_map/ppermute | solution.py:29
  28.2 0.1 collective-permute-done.8.refs_14_
  28.3 1.9 %finish.1 = (bf16[8,1024]{1,0:T(8,128)(2,1)}, bf16[8,1024]{1,0:T(8,128)(2,1)}, bf16[8,128,1024]{2,1,0:T(8,128)(2,1)}) custom-call(bf16[1048,128]{1,0:T(8,128)(2,1)S(1)} %collective-permute-done.refs_0_.refs_1_, bf16[1048,128]{1,0:T(8,128)(2,1)S(1)} %collective-permute-done.1.refs_1_.refs_2_, s32[2,8]{1,0:T(2,128)S(1)} %bitcast.14, ...), custom_call_target="tpu_custom_call", output_to_operand_aliasing={{2}: (16, {})} | custom-call | bytes 8750000 | tf_op jit(solution)/shard_map/finish/pallas_call | solution.py:622
  (6 shorter events, 0.0 us)
Async XLA Ops:
  0.6 5.0 %copy-start.1 = (bf16[2,8,2048]{2,1,0:T(8,128)(2,1)S(1)}, bf16[2,8,2048]{2,1,0:T(8,128)(2,1)}, u32[]{:S(2)}) copy-start(bf16[2,8,2048]{2,1,0:T(8,128)(2,1)} %param.8) | copy-start | bytes 196612
  0.6 5.0 %copy-start.2 = (bf16[2,8,1024]{2,1,0:T(8,128)(2,1)S(1)}, bf16[2,8,1024]{2,1,0:T(8,128)(2,1)}, u32[]{:S(2)}) copy-start(bf16[2,8,1024]{2,1,0:T(8,128)(2,1)} %q.1) | copy-start | bytes 98308
  2.5 5.8 %collective-permute-start.2 = (bf16[1048,128]{1,0:T(8,128)(2,1)S(1)}, bf16[1048,128]{1,0:T(8,128)(2,1)S(1)}, u32[]{:S(2)}, u32[]{:S(2)}) collective-permute-start(bf16[1048,128]{1,0:T(8,128)(2,1)S(1)} %get-tuple-element.36), channel_id=1, source_target_pairs={{0,4},{4,0},{8,12},{12,8},{1,5},{5,1},{9,13},{13,9},{2,6},{6,2},{1... | collective-permute-start | bytes 804872 | tf_op jit(solution)/shard_map/ppermute | solution.py:29
  3.0 15.8 %collective-permute-start = (bf16[1048,128]{1,0:T(8,128)(2,1)S(1)}, bf16[1048,128]{1,0:T(8,128)(2,1)S(1)}, u32[]{:S(2)}, u32[]{:S(2)}) collective-permute-start(bf16[1048,128]{1,0:T(8,128)(2,1)S(1)} %get-tuple-element.30), channel_id=1, source_target_pairs={{0,8},{4,12},{8,0},{12,4},{1,9},{5,13},{9,1},{13,5},{2,10},{6,14},... | collective-permute-start | bytes 804872 | tf_op jit(solution)/shard_map/ppermute | solution.py:29
  5.5 11.7 %copy-start.5 = (s32[8,4]{0,1:T(4,128)S(1)}, s32[8,4]{0,1:T(4,128)}, u32[]{:S(2)}) copy-start(s32[8,4]{0,1:T(4,128)} %param.13) | copy-start | bytes 388
  5.5 11.7 %copy-start.6 = (s32[8]{0:T(128)S(1)}, s32[8]{0:T(128)}, u32[]{:S(2)}) copy-start(s32[8]{0:T(128)} %refs_4_.3) | copy-start | bytes 100
  5.5 13.2 %collective-permute-start.1 = (bf16[1048,128]{1,0:T(8,128)(2,1)S(1)}, bf16[1048,128]{1,0:T(8,128)(2,1)S(1)}, u32[]{:S(2)}, u32[]{:S(2)}) collective-permute-start(bf16[1048,128]{1,0:T(8,128)(2,1)S(1)} %get-tuple-element.31), channel_id=1, source_target_pairs={{0,12},{4,8},{8,4},{12,0},{1,13},{5,9},{9,5},{13,1},{2,14},{6,10},... | collective-permute-start | bytes 804872 | tf_op jit(solution)/shard_map/ppermute | solution.py:29
  5.6 13.1 %copy-start = (bf16[2048,1024]{1,0:T(8,128)(2,1)S(1)}, bf16[2048,1024]{1,0:T(8,128)(2,1)}, u32[]{:S(2)}) copy-start(bf16[2048,1024]{1,0:T(8,128)(2,1)} %refs_4_.2) | copy-start | bytes 12582916
  8.2 10.6 %copy-start.3 = (s32[8,4]{0,1:T(4,128)S(1)}, s32[8,4]{0,1:T(4,128)}, u32[]{:S(2)}) copy-start(s32[8,4]{0,1:T(4,128)} %param.14) | copy-start | bytes 388
  8.2 10.6 %copy-start.4 = (s32[8,2]{0,1:T(2,128)S(1)}, s32[8,2]{0,1:T(2,128)}, u32[]{:S(2)}) copy-start(s32[8,2]{0,1:T(2,128)} %param.15) | copy-start | bytes 196
  8.2 5.1 %collective-permute-start.3 = (bf16[192,128]{1,0:T(8,128)(2,1)S(1)}, bf16[192,128]{1,0:T(8,128)(2,1)S(1)}, u32[]{:S(2)}, u32[]{:S(2)}) collective-permute-start(bf16[192,128]{1,0:T(8,128)(2,1)S(1)} %get-tuple-element.38), channel_id=1, source_target_pairs={{0,2},{1,3},{2,0},{3,1},{4,6},{5,7},{6,4},{7,5},{8,10},{9,11},{10,... | collective-permute-start | bytes 147464 | tf_op jit(solution)/shard_map/ppermute | solution.py:29
  11.1 6.1 %collective-permute-start.4 = (bf16[192,128]{1,0:T(8,128)(2,1)S(1)}, bf16[192,128]{1,0:T(8,128)(2,1)S(1)}, u32[]{:S(2)}, u32[]{:S(2)}) collective-permute-start(bf16[192,128]{1,0:T(8,128)(2,1)S(1)} %get-tuple-element.39), channel_id=1, source_target_pairs={{0,3},{1,2},{2,1},{3,0},{4,7},{5,6},{6,5},{7,4},{8,11},{9,10},{10,... | collective-permute-start | bytes 147464 | tf_op jit(solution)/shard_map/ppermute | solution.py:29
  12.5 4.7 %collective-permute-start.5 = (bf16[192,128]{1,0:T(8,128)(2,1)S(1)}, bf16[192,128]{1,0:T(8,128)(2,1)S(1)}, u32[]{:S(2)}, u32[]{:S(2)}) collective-permute-start(bf16[192,128]{1,0:T(8,128)(2,1)S(1)} %get-tuple-element.40), channel_id=1, source_target_pairs={{0,1},{1,0},{2,3},{3,2},{4,5},{5,4},{6,7},{7,6},{8,9},{9,8},{10,11... | collective-permute-start | bytes 147464 | tf_op jit(solution)/shard_map/ppermute | solution.py:29
  20.0 6.3 %collective-permute-start.6 = (bf16[208,128]{1,0:T(8,128)(2,1)S(1)}, bf16[208,128]{1,0:T(8,128)(2,1)S(1)}, u32[]{:S(2)}, u32[]{:S(2)}) collective-permute-start(bf16[208,128]{1,0:T(8,128)(2,1)S(1)} %get-tuple-element.50), channel_id=1, source_target_pairs={{0,2},{1,3},{2,0},{3,1},{4,6},{5,7},{6,4},{7,5},{8,10},{9,11},{10,... | collective-permute-start | bytes 159752 | tf_op jit(solution)/shard_map/ppermute | solution.py:29
  22.1 6.1 %collective-permute-start.7 = (bf16[208,128]{1,0:T(8,128)(2,1)S(1)}, bf16[208,128]{1,0:T(8,128)(2,1)S(1)}, u32[]{:S(2)}, u32[]{:S(2)}) collective-permute-start(bf16[208,128]{1,0:T(8,128)(2,1)S(1)} %get-tuple-element.51), channel_id=1, source_target_pairs={{0,3},{1,2},{2,1},{3,0},{4,7},{5,6},{6,5},{7,4},{8,11},{9,10},{10,... | collective-permute-start | bytes 159752 | tf_op jit(solution)/shard_map/ppermute | solution.py:29
  23.4 4.9 %collective-permute-start.8 = (bf16[208,128]{1,0:T(8,128)(2,1)S(1)}, bf16[208,128]{1,0:T(8,128)(2,1)S(1)}, u32[]{:S(2)}, u32[]{:S(2)}) collective-permute-start(bf16[208,128]{1,0:T(8,128)(2,1)S(1)} %get-tuple-element.52), channel_id=1, source_target_pairs={{0,1},{1,0},{2,3},{3,2},{4,5},{5,4},{6,7},{7,6},{8,9},{9,8},{10,11... | collective-permute-start | bytes 159752 | tf_op jit(solution)/shard_map/ppermute | solution.py:29

commit v8 on v7

--- a/solution.py
+++ b/solution.py
@@ -305,10 +305,10 @@
     inputs += [jnp.zeros((8 - len(inputs), depth), jnp.float32)]
     inputs = jnp.concatenate(inputs, axis=0).astype(jnp.bfloat16)
     share = jnp.dot(inputs, projection[...], preferred_element_type=jnp.float32)
-    num[...] = num_in[...]
+    num[:, : 2 * half_rows, :] = num_in[...]
     den[...] = den_in[...]
     for s, message in enumerate(messages):
-        wide[s] = message[half_rows : 2 * half_rows, :].astype(jnp.float32)
+        wide[s, :half_rows, :] = message[half_rows : 2 * half_rows, :].astype(jnp.float32)
     lengths = [length_of(part) for part in extra]
 
     wait_for(tables)
@@ -356,7 +356,7 @@
         arrived += [high, part - high]
         own_share[number] = part
         marks[number] = mark
-    own_num[...] = num[0]
+    own_num[...] = num[0, : 2 * half_rows, :]
     own_den[...] = den[0]
     all_kv = []
     for half in range(2):
@@ -368,7 +368,7 @@
         parts = den[at]
         high = parts.astype(SEND).astype(jnp.float32)
         parts = high + pltpu.roll(parts - high, HD // 2, 1)
-        out[...] = jnp.concatenate([num[at], parts] + filler + all_kv + arrived, axis=0).astype(SEND)
+        out[...] = jnp.concatenate([num[at, : 2 * half_rows, :], parts] + filler + all_kv + arrived, axis=0).astype(SEND)
 
 
 def finish_kernel(count, replicas, local_heads, *refs):
@@ -588,9 +588,9 @@
         + [VMEM] * 2,
         out_specs=[VMEM] * (count + 4),
         scratch_shapes=[
-            pltpu.VMEM((count, query_rows, HD), f32),
+            pltpu.VMEM((count, query_rows + rows, HD), f32),
             pltpu.VMEM((count, both, HD), f32),
-            pltpu.VMEM((count, query_rows // 2, HD), f32),
+            pltpu.VMEM((count, query_rows // 2 + rows, HD), f32),
             pltpu.SMEM(moves.shape, jnp.int32),
             pltpu.SMEM(table_after.shape, jnp.int32),
             pltpu.SemaphoreType.DMA((2,)),

time: 30.4 us -> 30.4 us (level)
  no operation moved by 1% of the time
where the time goes in v8:
time: 30.4 us; the launch traced here: 30.2 us
  Pallas kernels  11.8 us (39%)
  starting transfers between devices  11.2 us (37%)
  waiting for transfers between devices  6.4 us (21%)
  between operations  0.76 us (2%)
    ppermute x9, starting transfers between devices, swap(): return lax.ppermute(value, axis, [(i, i ^ distance) for i in range(size)])  11.2 us
    ppermute x9, waiting for transfers between devices, swap(): return lax.ppermute(value, axis, [(i, i ^ distance) for i in range(size)])  6.4 us
    pallas_call x1, Pallas kernels, body(): pl.pallas_call(functools.partial(keep_kernel, replicas), out_shape=shape(...  2.72 us
    pallas_call x1, Pallas kernels, body(): pl.pallas_call(functools.partial(open_kernel, count, local_heads), out_sh...  2.57 us
    pallas_call x1, Pallas kernels, body(): pl.pallas_call(functools.partial(finish_kernel, count, replicas, local_he...  1.94 us
    pallas_call x1, Pallas kernels, body(): pl.pallas_call(functools.partial(leave_kernel, rows), out_shape=[shape(po...  1.8 us
    pallas_call x1, Pallas kernels, body(): pl.pallas_call(functools.partial(attend_kernel, count, local_heads), out_...  1.53 us
    pallas_call x1, Pallas kernels, body(): pl.pallas_call(functools.partial(arrive_kernel, count, replicas, local_he...  1.26 us
  transfers between devices with their start and end apart: 9, of which 4 were waited for; matrix products, arithmetic and copies ran while one was open for 0% of the time, Pallas kernels for 23%

profile of v8, /device:TPU:0, one launch (start us, length us, event | category | flops | bytes accessed | tf_op | source)
XLA Modules:
  0.0 30.2 jit_solution(13503141056771555758)
XLA Ops:
  0.6 0.0 copy-start.1
  0.6 0.0 copy-start.2
  0.7 1.8 %leave.1 = (bf16[8,128,1024]{2,1,0:T(8,128)(2,1)S(1)}, bf16[1048,128]{1,0:T(8,128)(2,1)S(1)}, bf16[1048,128]{1,0:T(8,128)(2,1)S(1)}, bf16[1048,128]{1,0:T(8,128)(2,1)S(1)}) custom-call(s32[2,8]{1,0:T(2,128)} %bitcast.11, s32[4,8]{1,0:T(4,128)} %bitcast.15, s32[8]{0:T(128)} %refs_4_.3, bf16[16,2048]{1,0:T(8,128)(2,1)} %bitcast.6, bf16[8,128,1024]{2,1,0:T(8,128)(2,1)} %bitcast.18), custom_call_target="tpu_custom_call" | custom-call | bytes 6300000 | tf_op jit(solution)/shard_map/leave/pallas_call | solution.py:534
  2.5 0.5 %collective-permute-start.2 = (bf16[1048,128]{1,0:T(8,128)(2,1)S(1)}, bf16[1048,128]{1,0:T(8,128)(2,1)S(1)}, u32[]{:S(2)}, u32[]{:S(2)}) collective-permute-start(bf16[1048,128]{1,0:T(8,128)(2,1)S(1)} %get-tuple-element.36), channel_id=1, source_target_pairs={{0,4},{4,0},{8,12},{12,8},{1,5},{5,1},{9,13},{13,9},{2,6},{6,2},{1... | collective-permute-start | bytes 804872 | tf_op jit(solution)/shard_map/ppermute | solution.py:29
  3.0 2.6 %collective-permute-start = (bf16[1048,128]{1,0:T(8,128)(2,1)S(1)}, bf16[1048,128]{1,0:T(8,128)(2,1)S(1)}, u32[]{:S(2)}, u32[]{:S(2)}) collective-permute-start(bf16[1048,128]{1,0:T(8,128)(2,1)S(1)} %get-tuple-element.30), channel_id=1, source_target_pairs={{0,8},{4,12},{8,0},{12,4},{1,9},{5,13},{9,1},{13,5},{2,10},{6,14},... | collective-permute-start | bytes 804872 | tf_op jit(solution)/shard_map/ppermute | solution.py:29
  5.5 0.1 collective-permute-start.1
  5.6 0.0 copy-done.1
  5.6 0.0 copy-done.2
  5.6 2.6 %open.1 = (bf16[192,128]{1,0:T(8,128)(2,1)S(1)}, bf16[192,128]{1,0:T(8,128)(2,1)S(1)}, bf16[192,128]{1,0:T(8,128)(2,1)S(1)}, bf16[192,128]{1,0:T(8,128)(2,1)S(1)}) custom-call(bf16[16,2048]{1,0:T(8,128)(2,1)S(1)} %bitcast.7, bf16[2,8,1024]{2,1,0:T(8,128)(2,1)S(1)} %copy-done.2, bf16[2048,1024]{1,0:T(8,128)(2,1)} %refs_4_.2), custom_call_target="tpu_custom_call" | custom-call | bytes 4200000 | tf_op jit(solution)/shard_map/open/pallas_call | solution.py:554
  8.2 0.0 copy-start.3
  8.2 0.0 copy-start.4
  8.2 0.0 collective-permute-done.2.refs_5_.refs_0_.refs_11_
  8.2 2.9 %collective-permute-start.3 = (bf16[192,128]{1,0:T(8,128)(2,1)S(1)}, bf16[192,128]{1,0:T(8,128)(2,1)S(1)}, u32[]{:S(2)}, u32[]{:S(2)}) collective-permute-start(bf16[192,128]{1,0:T(8,128)(2,1)S(1)} %get-tuple-element.38), channel_id=1, source_target_pairs={{0,2},{1,3},{2,0},{3,1},{4,6},{5,7},{6,4},{7,5},{8,10},{9,11},{10,... | collective-permute-start | bytes 147464 | tf_op jit(solution)/shard_map/ppermute | solution.py:29
  11.1 1.3 %collective-permute-start.4 = (bf16[192,128]{1,0:T(8,128)(2,1)S(1)}, bf16[192,128]{1,0:T(8,128)(2,1)S(1)}, u32[]{:S(2)}, u32[]{:S(2)}) collective-permute-start(bf16[192,128]{1,0:T(8,128)(2,1)S(1)} %get-tuple-element.39), channel_id=1, source_target_pairs={{0,3},{1,2},{2,1},{3,0},{4,7},{5,6},{6,5},{7,4},{8,11},{9,10},{10,... | collective-permute-start | bytes 147464 | tf_op jit(solution)/shard_map/ppermute | solution.py:29
  12.5 0.2 collective-permute-start.5
  12.7 0.7 %collective-permute-done.3.refs_0_.refs_6_ = bf16[192,128]{1,0:T(8,128)(2,1)S(1)} collective-permute-done((bf16[192,128]{1,0:T(8,128)(2,1)S(1)}, bf16[192,128]{1,0:T(8,128)(2,1)S(1)}, u32[]{:S(2)}, u32[]{:S(2)}) %collective-permute-start.3) | collective-permute-done | bytes 49184 | tf_op jit(solution)/shard_map/ppermute | solution.py:29
  13.4 3.8 %collective-permute-done.4.refs_1_.refs_7_ = bf16[192,128]{1,0:T(8,128)(2,1)S(1)} collective-permute-done((bf16[192,128]{1,0:T(8,128)(2,1)S(1)}, bf16[192,128]{1,0:T(8,128)(2,1)S(1)}, u32[]{:S(2)}, u32[]{:S(2)}) %collective-permute-start.4) | collective-permute-done | bytes 49184 | tf_op jit(solution)/shard_map/ppermute | solution.py:29
  17.2 0.0 collective-permute-done.5.refs_2_.refs_8_
  17.2 0.0 copy-done.5
  17.2 0.0 copy-done.6
  17.2 1.5 %attend.1 = (f32[4,128,128]{2,1,0:T(8,128)S(1)}, f32[4,16,128]{2,1,0:T(8,128)S(1)}) custom-call(s32[4,8]{1,0:T(4,128)S(1)} %bitcast.16, s32[8]{0:T(128)S(1)} %copy-done.6, bf16[8,128,1024]{2,1,0:T(8,128)(2,1)S(1)} %get-tuple-element.42.pool.refs_3_.refs_15_, bf16[192,128]{1,0:T(8,128)(2,1)S(1)} %collective-permute-done.3.refs_0_.refs_6_, ...), custom_call_target="tpu_custom_call" | custom-call | bytes 5250000 | tf_op jit(solution)/shard_map/attend/pallas_call | solution.py:567
  18.7 0.0 collective-permute-done.refs_0_.refs_1_
  18.7 0.0 collective-permute-done.1.refs_1_.refs_2_
  18.8 1.3 %arrive.1 = (bf16[208,128]{1,0:T(8,128)(2,1)S(1)}, bf16[208,128]{1,0:T(8,128)(2,1)S(1)}, bf16[208,128]{1,0:T(8,128)(2,1)S(1)}, f32[128,128]{1,0:T(8,128)S(1)}, f...) custom-call(bf16[1048,128]{1,0:T(8,128)(2,1)S(1)} %collective-permute-don, ...), custom_call_target="tpu_custom_call" | custom-call | bytes 4200000 | tf_op jit(solution)/shard_map/arrive/pallas_call | solution.py:579
  20.0 2.1 %collective-permute-start.6 = (bf16[208,128]{1,0:T(8,128)(2,1)S(1)}, bf16[208,128]{1,0:T(8,128)(2,1)S(1)}, u32[]{:S(2)}, u32[]{:S(2)}) collective-permute-start(bf16[208,128]{1,0:T(8,128)(2,1)S(1)} %get-tuple-element.50), channel_id=1, source_target_pairs={{0,2},{1,3},{2,0},{3,1},{4,6},{5,7},{6,4},{7,5},{8,10},{9,11},{10,... | collective-permute-start | bytes 159752 | tf_op jit(solution)/shard_map/ppermute | solution.py:29
  22.1 1.3 %collective-permute-start.7 = (bf16[208,128]{1,0:T(8,128)(2,1)S(1)}, bf16[208,128]{1,0:T(8,128)(2,1)S(1)}, u32[]{:S(2)}, u32[]{:S(2)}) collective-permute-start(bf16[208,128]{1,0:T(8,128)(2,1)S(1)} %get-tuple-element.51), channel_id=1, source_target_pairs={{0,3},{1,2},{2,1},{3,0},{4,7},{5,6},{6,5},{7,4},{8,11},{9,10},{10,... | collective-permute-start | bytes 159752 | tf_op jit(solution)/shard_map/ppermute | solution.py:29
  23.4 0.2 collective-permute-start.8
  23.6 2.7 %keep.1.refs_16_ = bf16[8,128,1024]{2,1,0:T(8,128)(2,1)} custom-call(bf16[1048,128]{1,0:T(8,128)(2,1)S(1)} %collective-permute-done.2.refs_5_.refs_0_.refs_11_, bf16[1048,128]{1,0:T(8,128)(2,1)S(1)} %collective-permute-done.refs_0_.refs_1_, bf16[1048,128]{1,0:T(8,128)(2,1)S(1)} %collective-permute-done.1.refs_1_.refs_2_, ...), custom_call_target="tpu_custom_call" | custom-call | bytes 5600000 | tf_op jit(solution)/shard_map/keep/pallas_call | solution.py:606
  26.4 0.0 collective-permute-done.6.refs_12_
  26.4 1.8 %collective-permute-done.7.refs_13_ = bf16[208,128]{1,0:T(8,128)(2,1)S(1)} collective-permute-done((bf16[208,128]{1,0:T(8,128)(2,1)S(1)}, bf16[208,128]{1,0:T(8,128)(2,1)S(1)}, u32[]{:S(2)}, u32[]{:S(2)}) %collective-permute-start.7) | collective-permute-done | bytes 53280 | tf_op jit(solution)/shard_map/ppermute | solution.py:29
  28.2 0.1 collective-permute-done.8.refs_14_
  28.3 1.9 %finish.1 = (bf16[8,1024]{1,0:T(8,128)(2,1)}, bf16[8,1024]{1,0:T(8,128)(2,1)}, bf16[8,128,1024]{2,1,0:T(8,128)(2,1)}) custom-call(bf16[1048,128]{1,0:T(8,128)(2,1)S(1)} %collective-permute-done.refs_0_.refs_1_, bf16[1048,128]{1,0:T(8,128)(2,1)S(1)} %collective-permute-done.1.refs_1_.refs_2_, s32[2,8]{1,0:T(2,128)S(1)} %bitcast.14, ...), custom_call_target="tpu_custom_call", output_to_operand_aliasing={{2}: (16, {})} | custom-call | bytes 8750000 | tf_op jit(solution)/shard_map/finish/pallas_call | solution.py:622
  (6 shorter events, 0.0 us)
Async XLA Ops:
  0.6 5.0 %copy-start.1 = (bf16[2,8,2048]{2,1,0:T(8,128)(2,1)S(1)}, bf16[2,8,2048]{2,1,0:T(8,128)(2,1)}, u32[]{:S(2)}) copy-start(bf16[2,8,2048]{2,1,0:T(8,128)(2,1)} %param.8) | copy-start | bytes 196612
  0.6 5.0 %copy-start.2 = (bf16[2,8,1024]{2,1,0:T(8,128)(2,1)S(1)}, bf16[2,8,1024]{2,1,0:T(8,128)(2,1)}, u32[]{:S(2)}) copy-start(bf16[2,8,1024]{2,1,0:T(8,128)(2,1)} %q.1) | copy-start | bytes 98308
  2.5 5.8 %collective-permute-start.2 = (bf16[1048,128]{1,0:T(8,128)(2,1)S(1)}, bf16[1048,128]{1,0:T(8,128)(2,1)S(1)}, u32[]{:S(2)}, u32[]{:S(2)}) collective-permute-start(bf16[1048,128]{1,0:T(8,128)(2,1)S(1)} %get-tuple-element.36), channel_id=1, source_target_pairs={{0,4},{4,0},{8,12},{12,8},{1,5},{5,1},{9,13},{13,9},{2,6},{6,2},{1... | collective-permute-start | bytes 804872 | tf_op jit(solution)/shard_map/ppermute | solution.py:29
  3.0 15.8 %collective-permute-start = (bf16[1048,128]{1,0:T(8,128)(2,1)S(1)}, bf16[1048,128]{1,0:T(8,128)(2,1)S(1)}, u32[]{:S(2)}, u32[]{:S(2)}) collective-permute-start(bf16[1048,128]{1,0:T(8,128)(2,1)S(1)} %get-tuple-element.30), channel_id=1, source_target_pairs={{0,8},{4,12},{8,0},{12,4},{1,9},{5,13},{9,1},{13,5},{2,10},{6,14},... | collective-permute-start | bytes 804872 | tf_op jit(solution)/shard_map/ppermute | solution.py:29
  5.5 11.7 %copy-start.5 = (s32[8,4]{0,1:T(4,128)S(1)}, s32[8,4]{0,1:T(4,128)}, u32[]{:S(2)}) copy-start(s32[8,4]{0,1:T(4,128)} %param.13) | copy-start | bytes 388
  5.5 11.7 %copy-start.6 = (s32[8]{0:T(128)S(1)}, s32[8]{0:T(128)}, u32[]{:S(2)}) copy-start(s32[8]{0:T(128)} %refs_4_.3) | copy-start | bytes 100
  5.5 13.2 %collective-permute-start.1 = (bf16[1048,128]{1,0:T(8,128)(2,1)S(1)}, bf16[1048,128]{1,0:T(8,128)(2,1)S(1)}, u32[]{:S(2)}, u32[]{:S(2)}) collective-permute-start(bf16[1048,128]{1,0:T(8,128)(2,1)S(1)} %get-tuple-element.31), channel_id=1, source_target_pairs={{0,12},{4,8},{8,4},{12,0},{1,13},{5,9},{9,5},{13,1},{2,14},{6,10},... | collective-permute-start | bytes 804872 | tf_op jit(solution)/shard_map/ppermute | solution.py:29
  5.6 13.1 %copy-start = (bf16[2048,1024]{1,0:T(8,128)(2,1)S(1)}, bf16[2048,1024]{1,0:T(8,128)(2,1)}, u32[]{:S(2)}) copy-start(bf16[2048,1024]{1,0:T(8,128)(2,1)} %refs_4_.2) | copy-start | bytes 12582916
  8.2 10.6 %copy-start.3 = (s32[8,4]{0,1:T(4,128)S(1)}, s32[8,4]{0,1:T(4,128)}, u32[]{:S(2)}) copy-start(s32[8,4]{0,1:T(4,128)} %param.14) | copy-start | bytes 388
  8.2 10.6 %copy-start.4 = (s32[8,2]{0,1:T(2,128)S(1)}, s32[8,2]{0,1:T(2,128)}, u32[]{:S(2)}) copy-start(s32[8,2]{0,1:T(2,128)} %param.15) | copy-start | bytes 196
  8.2 5.1 %collective-permute-start.3 = (bf16[192,128]{1,0:T(8,128)(2,1)S(1)}, bf16[192,128]{1,0:T(8,128)(2,1)S(1)}, u32[]{:S(2)}, u32[]{:S(2)}) collective-permute-start(bf16[192,128]{1,0:T(8,128)(2,1)S(1)} %get-tuple-element.38), channel_id=1, source_target_pairs={{0,2},{1,3},{2,0},{3,1},{4,6},{5,7},{6,4},{7,5},{8,10},{9,11},{10,... | collective-permute-start | bytes 147464 | tf_op jit(solution)/shard_map/ppermute | solution.py:29
  11.1 6.1 %collective-permute-start.4 = (bf16[192,128]{1,0:T(8,128)(2,1)S(1)}, bf16[192,128]{1,0:T(8,128)(2,1)S(1)}, u32[]{:S(2)}, u32[]{:S(2)}) collective-permute-start(bf16[192,128]{1,0:T(8,128)(2,1)S(1)} %get-tuple-element.39), channel_id=1, source_target_pairs={{0,3},{1,2},{2,1},{3,0},{4,7},{5,6},{6,5},{7,4},{8,11},{9,10},{10,... | collective-permute-start | bytes 147464 | tf_op jit(solution)/shard_map/ppermute | solution.py:29
  12.5 4.7 %collective-permute-start.5 = (bf16[192,128]{1,0:T(8,128)(2,1)S(1)}, bf16[192,128]{1,0:T(8,128)(2,1)S(1)}, u32[]{:S(2)}, u32[]{:S(2)}) collective-permute-start(bf16[192,128]{1,0:T(8,128)(2,1)S(1)} %get-tuple-element.40), channel_id=1, source_target_pairs={{0,1},{1,0},{2,3},{3,2},{4,5},{5,4},{6,7},{7,6},{8,9},{9,8},{10,11... | collective-permute-start | bytes 147464 | tf_op jit(solution)/shard_map/ppermute | solution.py:29
  20.0 6.3 %collective-permute-start.6 = (bf16[208,128]{1,0:T(8,128)(2,1)S(1)}, bf16[208,128]{1,0:T(8,128)(2,1)S(1)}, u32[]{:S(2)}, u32[]{:S(2)}) collective-permute-start(bf16[208,128]{1,0:T(8,128)(2,1)S(1)} %get-tuple-element.50), channel_id=1, source_target_pairs={{0,2},{1,3},{2,0},{3,1},{4,6},{5,7},{6,4},{7,5},{8,10},{9,11},{10,... | collective-permute-start | bytes 159752 | tf_op jit(solution)/shard_map/ppermute | solution.py:29
  22.1 6.1 %collective-permute-start.7 = (bf16[208,128]{1,0:T(8,128)(2,1)S(1)}, bf16[208,128]{1,0:T(8,128)(2,1)S(1)}, u32[]{:S(2)}, u32[]{:S(2)}) collective-permute-start(bf16[208,128]{1,0:T(8,128)(2,1)S(1)} %get-tuple-element.51), channel_id=1, source_target_pairs={{0,3},{1,2},{2,1},{3,0},{4,7},{5,6},{6,5},{7,4},{8,11},{9,10},{10,... | collective-permute-start | bytes 159752 | tf_op jit(solution)/shard_map/ppermute | solution.py:29
  23.4 4.9 %collective-permute-start.8 = (bf16[208,128]{1,0:T(8,128)(2,1)S(1)}, bf16[208,128]{1,0:T(8,128)(2,1)S(1)}, u32[]{:S(2)}, u32[]{:S(2)}) collective-permute-start(bf16[208,128]{1,0:T(8,128)(2,1)S(1)} %get-tuple-element.52), channel_id=1, source_target_pairs={{0,1},{1,0},{2,3},{3,2},{4,5},{5,4},{6,7},{7,6},{8,9},{9,8},{10,11... | collective-permute-start | bytes 159752 | tf_op jit(solution)/shard_map/ppermute | solution.py:29

commit v9 on v8

--- a/solution.py
+++ b/solution.py
@@ -34,20 +34,49 @@
     return received[::-1]
 
 
+def turns(size):
+    if size == 4:
+        return [[1, 3, 0, 2], [3, 2, 1, 0], [2, 0, 3, 1]]
+    return [[(i + s) % size for i in range(size)] for s in range(1, size)]
+
+
+def rotate(messages, axis):
+    steps = turns(lax.axis_size(axis))
+    return [lax.ppermute(message, axis, list(enumerate(step))) for message, step in zip(messages, steps)]
+
+
+def pick(values, index):
+    found = jnp.int32(values[0])
+    for i, value in enumerate(values[1:], 1):
+        found = jnp.where(index == i, value, found)
+    return found
+
+
+def turn_target(axis, k):
+    return pick(turns(lax.axis_size(axis))[k - 1], lax.axis_index(axis))
+
+
+def turn_source(axis, k):
+    if k == 0:
+        return lax.axis_index(axis)
+    step = turns(lax.axis_size(axis))[k - 1]
+    return pick([step.index(i) for i in range(len(step))], lax.axis_index(axis))
+
+
 def start_order(count):
     return [count // 2] + [d for d in range(count - 1, 0, -1) if d != count // 2]
 
 
 def by_start(values):
     own = len(values) & 1 ^ 1
-    order = start_order(len(values) + 1 - own)
+    order = start_order(len(values)) if own else range(1, len(values) + 1)
     return [values[d - 1 + own] for d in order] + list(values[:own])
 
 
 def by_distance(values):
     own = len(values) & 1 ^ 1
-    order = start_order(len(values) + 1 - own)
-    return list(values[len(order) :]) + [values[order.index(d)] for d in range(1, len(order) + 1)]
+    order = start_order(len(values)) if own else range(1, len(values) + 1)
+    return list(values[len(order) :]) + [values[list(order).index(d)] for d in range(1, len(order) + 1)]
 
 
 def partner(axis, distance):
@@ -364,7 +393,7 @@
         all_kv.append(own_kv[half])
     filler = [jnp.zeros((-2 * local_heads % 16, HD), jnp.float32)] if local_heads % 8 else []
     for s, out in enumerate(outs):
-        at = s + 1
+        at = lax.axis_index("mp") ^ turn_target("mp", s + 1)
         parts = den[at]
         high = parts.astype(SEND).astype(jnp.float32)
         parts = high + pltpu.roll(parts - high, HD // 2, 1)
@@ -390,7 +419,7 @@
 
     kv_base = messages[0].shape[0] - 4 * rows - 16 * movers
     for s in range(count):
-        device = partner("mp", s)
+        device = turn_source("mp", s)
         for half in range(2):
             if s == 0:
                 chunk = kv[half]
@@ -599,7 +628,7 @@
         cost_estimate=cost(1.2),
         name="arrive",
     )(*pages_in[1:], moves, table_after, weight_near, pages_in[0], *by_start(messages), num, den)
-    sums_in = exchange(sums, "mp")
+    sums_in = rotate(sums, "mp")
 
     moves_then, _ = lax.optimization_barrier((moves, marks))
 

time: 30.4 us -> 30 us (0.987)
  waiting for transfers between devices: 6.4 us -> 4.53 us
  starting transfers between devices: 11.2 us -> 12.7 us
    ppermute x0 -> x3, starting transfers between devices: none -> 5.05 us  [rotate(): lax.ppermute(message, axis, list(enumerate(step)))]
    ppermute x9 -> x6, starting transfers between devices: 11.2 us -> 7.62 us  [swap(): return lax.ppermute(value, axis, [(i, i ^ distance) for i in range(size)])]
    ppermute x9 -> x6, waiting for transfers between devices: 6.4 us -> 4.49 us  [swap(): return lax.ppermute(value, axis, [(i, i ^ distance) for i in range(size)])]
  transfers between devices with their start and end apart: 9 -> 9, of which waited for: 4 -> 2; matrix products, arithmetic and copies ran while one was open for 0% -> 0% of each run, Pallas kernels for 23% -> 23%
where the time goes in v9:
time: 30 us; the launch traced here: 29.8 us
  starting transfers between devices  12.7 us (42%)
  Pallas kernels  11.8 us (39%)
  waiting for transfers between devices  4.53 us (15%)
  between operations  0.77 us (3%)
    ppermute x6, starting transfers between devices, swap(): return lax.ppermute(value, axis, [(i, i ^ distance) for i in range(size)])  7.62 us
    ppermute x3, starting transfers between devices, rotate(): lax.ppermute(message, axis, list(enumerate(step)))  5.05 us
    ppermute x6, waiting for transfers between devices, swap(): return lax.ppermute(value, axis, [(i, i ^ distance) for i in range(size)])  4.49 us
    pallas_call x1, Pallas kernels, body(): pl.pallas_call(functools.partial(keep_kernel, replicas), out_shape=shape(...  2.72 us
    pallas_call x1, Pallas kernels, body(): pl.pallas_call(functools.partial(open_kernel, count, local_heads), out_sh...  2.57 us
    pallas_call x1, Pallas kernels, body(): pl.pallas_call(functools.partial(finish_kernel, count, replicas, local_he...  1.96 us
    pallas_call x1, Pallas kernels, body(): pl.pallas_call(functools.partial(leave_kernel, rows), out_shape=[shape(po...  1.8 us
    pallas_call x1, Pallas kernels, body(): pl.pallas_call(functools.partial(attend_kernel, count, local_heads), out_...  1.53 us
  transfers between devices with their start and end apart: 9, of which 2 were waited for; matrix products, arithmetic and copies ran while one was open for 0% of the time, Pallas kernels for 23%

profile of v9, /device:TPU:0, one launch (start us, length us, event | category | flops | bytes accessed | tf_op | source)
XLA Modules:
  0.0 29.8 jit_solution(7744965075239231456)
XLA Ops:
  0.6 0.0 copy-start.1
  0.6 0.0 copy-start.2
  0.7 1.8 %leave.1 = (bf16[8,128,1024]{2,1,0:T(8,128)(2,1)S(1)}, bf16[1048,128]{1,0:T(8,128)(2,1)S(1)}, bf16[1048,128]{1,0:T(8,128)(2,1)S(1)}, bf16[1048,128]{1,0:T(8,128)(2,1)S(1)}) custom-call(s32[2,8]{1,0:T(2,128)} %bitcast.11, s32[4,8]{1,0:T(4,128)} %bitcast.15, s32[8]{0:T(128)} %refs_4_.3, bf16[16,2048]{1,0:T(8,128)(2,1)} %bitcast.6, bf16[8,128,1024]{2,1,0:T(8,128)(2,1)} %bitcast.18), custom_call_target="tpu_custom_call" | custom-call | bytes 6300000 | tf_op jit(solution)/shard_map/leave/pallas_call | solution.py:563
  2.5 0.5 %collective-permute-start.2 = (bf16[1048,128]{1,0:T(8,128)(2,1)S(1)}, bf16[1048,128]{1,0:T(8,128)(2,1)S(1)}, u32[]{:S(2)}, u32[]{:S(2)}) collective-permute-start(bf16[1048,128]{1,0:T(8,128)(2,1)S(1)} %get-tuple-element.36), channel_id=1, source_target_pairs={{0,4},{4,0},{8,12},{12,8},{1,5},{5,1},{9,13},{13,9},{2,6},{6,2},{1... | collective-permute-start | bytes 804872 | tf_op jit(solution)/shard_map/ppermute | solution.py:29
  3.0 2.6 %collective-permute-start = (bf16[1048,128]{1,0:T(8,128)(2,1)S(1)}, bf16[1048,128]{1,0:T(8,128)(2,1)S(1)}, u32[]{:S(2)}, u32[]{:S(2)}) collective-permute-start(bf16[1048,128]{1,0:T(8,128)(2,1)S(1)} %get-tuple-element.30), channel_id=1, source_target_pairs={{0,8},{4,12},{8,0},{12,4},{1,9},{5,13},{9,1},{13,5},{2,10},{6,14},... | collective-permute-start | bytes 804872 | tf_op jit(solution)/shard_map/ppermute | solution.py:29
  5.5 0.1 collective-permute-start.1
  5.6 0.0 copy-done.1
  5.6 0.0 copy-done.2
  5.6 2.6 %open.1 = (bf16[192,128]{1,0:T(8,128)(2,1)S(1)}, bf16[192,128]{1,0:T(8,128)(2,1)S(1)}, bf16[192,128]{1,0:T(8,128)(2,1)S(1)}, bf16[192,128]{1,0:T(8,128)(2,1)S(1)}) custom-call(bf16[16,2048]{1,0:T(8,128)(2,1)S(1)} %bitcast.7, bf16[2,8,1024]{2,1,0:T(8,128)(2,1)S(1)} %copy-done.2, bf16[2048,1024]{1,0:T(8,128)(2,1)} %refs_4_.2), custom_call_target="tpu_custom_call" | custom-call | bytes 4200000 | tf_op jit(solution)/shard_map/open/pallas_call | solution.py:583
  8.2 0.0 copy-start.3
  8.2 0.0 copy-start.4
  8.2 0.0 collective-permute-done.2.refs_5_.refs_0_.refs_11_
  8.2 2.9 %collective-permute-start.3 = (bf16[192,128]{1,0:T(8,128)(2,1)S(1)}, bf16[192,128]{1,0:T(8,128)(2,1)S(1)}, u32[]{:S(2)}, u32[]{:S(2)}) collective-permute-start(bf16[192,128]{1,0:T(8,128)(2,1)S(1)} %get-tuple-element.38), channel_id=1, source_target_pairs={{0,2},{1,3},{2,0},{3,1},{4,6},{5,7},{6,4},{7,5},{8,10},{9,11},{10,... | collective-permute-start | bytes 147464 | tf_op jit(solution)/shard_map/ppermute | solution.py:29
  11.1 1.3 %collective-permute-start.4 = (bf16[192,128]{1,0:T(8,128)(2,1)S(1)}, bf16[192,128]{1,0:T(8,128)(2,1)S(1)}, u32[]{:S(2)}, u32[]{:S(2)}) collective-permute-start(bf16[192,128]{1,0:T(8,128)(2,1)S(1)} %get-tuple-element.39), channel_id=1, source_target_pairs={{0,3},{1,2},{2,1},{3,0},{4,7},{5,6},{6,5},{7,4},{8,11},{9,10},{10,... | collective-permute-start | bytes 147464 | tf_op jit(solution)/shard_map/ppermute | solution.py:29
  12.5 0.2 collective-permute-start.5
  12.7 0.7 %collective-permute-done.3.refs_0_.refs_6_ = bf16[192,128]{1,0:T(8,128)(2,1)S(1)} collective-permute-done((bf16[192,128]{1,0:T(8,128)(2,1)S(1)}, bf16[192,128]{1,0:T(8,128)(2,1)S(1)}, u32[]{:S(2)}, u32[]{:S(2)}) %collective-permute-start.3) | collective-permute-done | bytes 49184 | tf_op jit(solution)/shard_map/ppermute | solution.py:29
  13.4 3.8 %collective-permute-done.4.refs_1_.refs_7_ = bf16[192,128]{1,0:T(8,128)(2,1)S(1)} collective-permute-done((bf16[192,128]{1,0:T(8,128)(2,1)S(1)}, bf16[192,128]{1,0:T(8,128)(2,1)S(1)}, u32[]{:S(2)}, u32[]{:S(2)}) %collective-permute-start.4) | collective-permute-done | bytes 49184 | tf_op jit(solution)/shard_map/ppermute | solution.py:29
  17.2 0.0 collective-permute-done.5.refs_2_.refs_8_
  17.2 0.0 copy-done.5
  17.2 0.0 copy-done.6
  17.2 1.5 %attend.1 = (f32[4,128,128]{2,1,0:T(8,128)S(1)}, f32[4,16,128]{2,1,0:T(8,128)S(1)}) custom-call(s32[4,8]{1,0:T(4,128)S(1)} %bitcast.16, s32[8]{0:T(128)S(1)} %copy-done.6, bf16[8,128,1024]{2,1,0:T(8,128)(2,1)S(1)} %get-tuple-element.42.pool.refs_3_.refs_15_, bf16[192,128]{1,0:T(8,128)(2,1)S(1)} %collective-permute-done.3.refs_0_.refs_6_, ...), custom_call_target="tpu_custom_call" | custom-call | bytes 5250000 | tf_op jit(solution)/shard_map/attend/pallas_call | solution.py:596
  18.7 0.0 collective-permute-done.refs_0_.refs_1_
  18.7 0.0 collective-permute-done.1.refs_1_.refs_2_
  18.8 1.3 %arrive.1 = (bf16[208,128]{1,0:T(8,128)(2,1)S(1)}, bf16[208,128]{1,0:T(8,128)(2,1)S(1)}, bf16[208,128]{1,0:T(8,128)(2,1)S(1)}, f32[128,128]{1,0:T(8,128)S(1)}, f...) custom-call(bf16[1048,128]{1,0:T(8,128)(2,1)S(1)} %collective-permute-don, ...), custom_call_target="tpu_custom_call" | custom-call | bytes 4200000 | tf_op jit(solution)/shard_map/arrive/pallas_call | solution.py:608
  20.0 1.0 %collective-permute-start.6 = (bf16[208,128]{1,0:T(8,128)(2,1)S(1)}, bf16[208,128]{1,0:T(8,128)(2,1)S(1)}, u32[]{:S(2)}, u32[]{:S(2)}) collective-permute-start(bf16[208,128]{1,0:T(8,128)(2,1)S(1)} %get-tuple-element.50), channel_id=1, source_target_pairs={{0,1},{1,3},{2,0},{3,2},{4,5},{5,7},{6,4},{7,6},{8,9},{9,11},{10,8... | collective-permute-start | bytes 159752 | tf_op jit(solution)/shard_map/ppermute | solution.py:45
  21.0 2.5 %collective-permute-start.7 = (bf16[208,128]{1,0:T(8,128)(2,1)S(1)}, bf16[208,128]{1,0:T(8,128)(2,1)S(1)}, u32[]{:S(2)}, u32[]{:S(2)}) collective-permute-start(bf16[208,128]{1,0:T(8,128)(2,1)S(1)} %get-tuple-element.51), channel_id=1, source_target_pairs={{0,3},{1,2},{2,1},{3,0},{4,7},{5,6},{6,5},{7,4},{8,11},{9,10},{10,... | collective-permute-start | bytes 159752 | tf_op jit(solution)/shard_map/ppermute | solution.py:45
  23.6 1.5 %collective-permute-start.8 = (bf16[208,128]{1,0:T(8,128)(2,1)S(1)}, bf16[208,128]{1,0:T(8,128)(2,1)S(1)}, u32[]{:S(2)}, u32[]{:S(2)}) collective-permute-start(bf16[208,128]{1,0:T(8,128)(2,1)S(1)} %get-tuple-element.52), channel_id=1, source_target_pairs={{0,2},{1,0},{2,3},{3,1},{4,6},{5,4},{6,7},{7,5},{8,10},{9,8},{10,1... | collective-permute-start | bytes 159752 | tf_op jit(solution)/shard_map/ppermute | solution.py:45
  25.1 2.7 %keep.1.refs_16_ = bf16[8,128,1024]{2,1,0:T(8,128)(2,1)} custom-call(bf16[1048,128]{1,0:T(8,128)(2,1)S(1)} %collective-permute-done.2.refs_5_.refs_0_.refs_11_, bf16[1048,128]{1,0:T(8,128)(2,1)S(1)} %collective-permute-done.refs_0_.refs_1_, bf16[1048,128]{1,0:T(8,128)(2,1)S(1)} %collective-permute-done.1.refs_1_.refs_2_, ...), custom_call_target="tpu_custom_call" | custom-call | bytes 5600000 | tf_op jit(solution)/shard_map/keep/pallas_call | solution.py:635
  27.8 0.0 collective-permute-done.6.refs_12_
  27.8 0.0 collective-permute-done.7.refs_13_
  27.8 0.0 collective-permute-done.8.refs_14_
  27.9 2.0 %finish.1 = (bf16[8,1024]{1,0:T(8,128)(2,1)}, bf16[8,1024]{1,0:T(8,128)(2,1)}, bf16[8,128,1024]{2,1,0:T(8,128)(2,1)}) custom-call(bf16[1048,128]{1,0:T(8,128)(2,1)S(1)} %collective-permute-done.refs_0_.refs_1_, bf16[1048,128]{1,0:T(8,128)(2,1)S(1)} %collective-permute-done.1.refs_1_.refs_2_, s32[2,8]{1,0:T(2,128)S(1)} %bitcast.14, ...), custom_call_target="tpu_custom_call", output_to_operand_aliasing={{2}: (16, {})} | custom-call | bytes 8750000 | tf_op jit(solution)/shard_map/finish/pallas_call | solution.py:651
  (6 shorter events, 0.0 us)
Async XLA Ops:
  0.6 5.0 %copy-start.1 = (bf16[2,8,2048]{2,1,0:T(8,128)(2,1)S(1)}, bf16[2,8,2048]{2,1,0:T(8,128)(2,1)}, u32[]{:S(2)}) copy-start(bf16[2,8,2048]{2,1,0:T(8,128)(2,1)} %param.8) | copy-start | bytes 196612
  0.6 5.0 %copy-start.2 = (bf16[2,8,1024]{2,1,0:T(8,128)(2,1)S(1)}, bf16[2,8,1024]{2,1,0:T(8,128)(2,1)}, u32[]{:S(2)}) copy-start(bf16[2,8,1024]{2,1,0:T(8,128)(2,1)} %q.1) | copy-start | bytes 98308
  2.5 5.8 %collective-permute-start.2 = (bf16[1048,128]{1,0:T(8,128)(2,1)S(1)}, bf16[1048,128]{1,0:T(8,128)(2,1)S(1)}, u32[]{:S(2)}, u32[]{:S(2)}) collective-permute-start(bf16[1048,128]{1,0:T(8,128)(2,1)S(1)} %get-tuple-element.36), channel_id=1, source_target_pairs={{0,4},{4,0},{8,12},{12,8},{1,5},{5,1},{9,13},{13,9},{2,6},{6,2},{1... | collective-permute-start | bytes 804872 | tf_op jit(solution)/shard_map/ppermute | solution.py:29
  3.0 15.8 %collective-permute-start = (bf16[1048,128]{1,0:T(8,128)(2,1)S(1)}, bf16[1048,128]{1,0:T(8,128)(2,1)S(1)}, u32[]{:S(2)}, u32[]{:S(2)}) collective-permute-start(bf16[1048,128]{1,0:T(8,128)(2,1)S(1)} %get-tuple-element.30), channel_id=1, source_target_pairs={{0,8},{4,12},{8,0},{12,4},{1,9},{5,13},{9,1},{13,5},{2,10},{6,14},... | collective-permute-start | bytes 804872 | tf_op jit(solution)/shard_map/ppermute | solution.py:29
  5.5 11.7 %copy-start.5 = (s32[8,4]{0,1:T(4,128)S(1)}, s32[8,4]{0,1:T(4,128)}, u32[]{:S(2)}) copy-start(s32[8,4]{0,1:T(4,128)} %param.13) | copy-start | bytes 388
  5.5 11.7 %copy-start.6 = (s32[8]{0:T(128)S(1)}, s32[8]{0:T(128)}, u32[]{:S(2)}) copy-start(s32[8]{0:T(128)} %refs_4_.3) | copy-start | bytes 100
  5.5 13.2 %collective-permute-start.1 = (bf16[1048,128]{1,0:T(8,128)(2,1)S(1)}, bf16[1048,128]{1,0:T(8,128)(2,1)S(1)}, u32[]{:S(2)}, u32[]{:S(2)}) collective-permute-start(bf16[1048,128]{1,0:T(8,128)(2,1)S(1)} %get-tuple-element.31), channel_id=1, source_target_pairs={{0,12},{4,8},{8,4},{12,0},{1,13},{5,9},{9,5},{13,1},{2,14},{6,10},... | collective-permute-start | bytes 804872 | tf_op jit(solution)/shard_map/ppermute | solution.py:29
  5.6 13.1 %copy-start = (bf16[2048,1024]{1,0:T(8,128)(2,1)S(1)}, bf16[2048,1024]{1,0:T(8,128)(2,1)}, u32[]{:S(2)}) copy-start(bf16[2048,1024]{1,0:T(8,128)(2,1)} %refs_4_.2) | copy-start | bytes 12582916
  8.2 10.6 %copy-start.3 = (s32[8,4]{0,1:T(4,128)S(1)}, s32[8,4]{0,1:T(4,128)}, u32[]{:S(2)}) copy-start(s32[8,4]{0,1:T(4,128)} %param.14) | copy-start | bytes 388
  8.2 10.6 %copy-start.4 = (s32[8,2]{0,1:T(2,128)S(1)}, s32[8,2]{0,1:T(2,128)}, u32[]{:S(2)}) copy-start(s32[8,2]{0,1:T(2,128)} %param.15) | copy-start | bytes 196
  8.2 5.1 %collective-permute-start.3 = (bf16[192,128]{1,0:T(8,128)(2,1)S(1)}, bf16[192,128]{1,0:T(8,128)(2,1)S(1)}, u32[]{:S(2)}, u32[]{:S(2)}) collective-permute-start(bf16[192,128]{1,0:T(8,128)(2,1)S(1)} %get-tuple-element.38), channel_id=1, source_target_pairs={{0,2},{1,3},{2,0},{3,1},{4,6},{5,7},{6,4},{7,5},{8,10},{9,11},{10,... | collective-permute-start | bytes 147464 | tf_op jit(solution)/shard_map/ppermute | solution.py:29
  11.1 6.1 %collective-permute-start.4 = (bf16[192,128]{1,0:T(8,128)(2,1)S(1)}, bf16[192,128]{1,0:T(8,128)(2,1)S(1)}, u32[]{:S(2)}, u32[]{:S(2)}) collective-permute-start(bf16[192,128]{1,0:T(8,128)(2,1)S(1)} %get-tuple-element.39), channel_id=1, source_target_pairs={{0,3},{1,2},{2,1},{3,0},{4,7},{5,6},{6,5},{7,4},{8,11},{9,10},{10,... | collective-permute-start | bytes 147464 | tf_op jit(solution)/shard_map/ppermute | solution.py:29
  12.5 4.7 %collective-permute-start.5 = (bf16[192,128]{1,0:T(8,128)(2,1)S(1)}, bf16[192,128]{1,0:T(8,128)(2,1)S(1)}, u32[]{:S(2)}, u32[]{:S(2)}) collective-permute-start(bf16[192,128]{1,0:T(8,128)(2,1)S(1)} %get-tuple-element.40), channel_id=1, source_target_pairs={{0,1},{1,0},{2,3},{3,2},{4,5},{5,4},{6,7},{7,6},{8,9},{9,8},{10,11... | collective-permute-start | bytes 147464 | tf_op jit(solution)/shard_map/ppermute | solution.py:29
  20.0 7.8 %collective-permute-start.6 = (bf16[208,128]{1,0:T(8,128)(2,1)S(1)}, bf16[208,128]{1,0:T(8,128)(2,1)S(1)}, u32[]{:S(2)}, u32[]{:S(2)}) collective-permute-start(bf16[208,128]{1,0:T(8,128)(2,1)S(1)} %get-tuple-element.50), channel_id=1, source_target_pairs={{0,1},{1,3},{2,0},{3,2},{4,5},{5,7},{6,4},{7,6},{8,9},{9,11},{10,8... | collective-permute-start | bytes 159752 | tf_op jit(solution)/shard_map/ppermute | solution.py:45
  21.0 6.8 %collective-permute-start.7 = (bf16[208,128]{1,0:T(8,128)(2,1)S(1)}, bf16[208,128]{1,0:T(8,128)(2,1)S(1)}, u32[]{:S(2)}, u32[]{:S(2)}) collective-permute-start(bf16[208,128]{1,0:T(8,128)(2,1)S(1)} %get-tuple-element.51), channel_id=1, source_target_pairs={{0,3},{1,2},{2,1},{3,0},{4,7},{5,6},{6,5},{7,4},{8,11},{9,10},{10,... | collective-permute-start | bytes 159752 | tf_op jit(solution)/shard_map/ppermute | solution.py:45
  23.6 4.3 %collective-permute-start.8 = (bf16[208,128]{1,0:T(8,128)(2,1)S(1)}, bf16[208,128]{1,0:T(8,128)(2,1)S(1)}, u32[]{:S(2)}, u32[]{:S(2)}) collective-permute-start(bf16[208,128]{1,0:T(8,128)(2,1)S(1)} %get-tuple-element.52), channel_id=1, source_target_pairs={{0,2},{1,0},{2,3},{3,1},{4,6},{5,4},{6,7},{7,5},{8,10},{9,8},{10,1... | collective-permute-start | bytes 159752 | tf_op jit(solution)/shard_map/ppermute | solution.py:45

commit v10 on v9

--- a/solution.py
+++ b/solution.py
@@ -186,8 +186,26 @@
             page[line : line + page_size, :] = held[slot, :, piece]
 
 
-def open_kernel(count, local_heads, x, q, weight, *refs):
-    outs, (held, weight_sems) = refs[:-2], refs[-2:]
+INDEX, SLOT, KEPT, VALID, ROW, ORDER, NEW_INDEX, NEW_SLOT = range(8)
+
+
+def make_plan(plan, moves, old_table, new_table, replicas, slots):
+    me, column = lax.axis_index("replica"), lax.axis_index("mp")
+    rows = old_table.shape[1]
+    kept = [jnp.int32(1)] * rows
+    for s in range(replicas - 1):
+        valid, row, order = pair_row(moves, partner("replica", s + 1), me, rows, 1)
+        plan[VALID, s], plan[ROW, s], plan[ORDER, s] = valid, row, order
+        plan[NEW_INDEX, s], plan[NEW_SLOT, s] = locate(new_table, row, column, slots)
+        kept = [jnp.where((valid == 1) & (row == r), 0, stays) for r, stays in enumerate(kept)]
+    for r in range(rows):
+        plan[KEPT, r] = kept[r]
+        plan[INDEX, r], plan[SLOT, r] = locate(old_table, r, column, slots)
+
+
+def open_kernel(count, local_heads, replicas, slots, x, q, weight, moves_all, old_all, new_all, *refs):
+    outs, (plan_out, held, plan, moves, old_table, new_table, weight_sems, sems) = refs[:-8], refs[-8:]
+    tables = start_copies(((moves_all, moves), (old_all, old_table), (new_all, new_table)), sems)
     depth, chunks = weight.shape[0], weight_sems.shape[0]
     spans = [pl.ds(c * (depth // chunks), depth // chunks) for c in range(chunks)]
     loads = start_copies([(weight.at[span], held.at[span]) for span in spans], weight_sems)
@@ -198,6 +216,10 @@
     query_rows = packed.shape[0]
     for out in outs:
         out[:query_rows, :] = packed
+    wait_for(tables)
+    make_plan(plan, moves, old_table, new_table, replicas, slots)
+    plan_copy = pltpu.make_async_copy(plan, plan_out, sems.at[3])
+    plan_copy.start()
     total = jnp.zeros((x.shape[0], weight.shape[1]), jnp.float32)
     for span, load in zip(spans, loads):
         load.wait()
@@ -216,25 +238,19 @@
             def _(out=out, parts=parts):
                 out[query_rows:, :] = parts
 
+    plan_copy.wait()
+
 
 def keep_kernel(replicas, *refs):
-    pages_in, (pool, moves_all, table_all, pool_out, moves, table, sems, page_sems) = (
-        refs[: replicas - 1],
-        refs[replicas - 1 :],
-    )
-    wait_for(start_copies(((moves_all, moves), (table_all, table)), sems))
-    me, column = lax.axis_index("replica"), lax.axis_index("mp")
-    rows = table.shape[1]
+    pages_in, (pool, plan_all, pool_out, plan, sem, page_sems) = refs[: replicas - 1], refs[replicas - 1 :]
+    load = pltpu.make_async_copy(plan_all, plan, sem)
+    load.start()
+    load.wait()
     slots, page_size, width = pool.shape
-    kept, copies = [jnp.bool_(True)] * rows, []
-    for s, page in enumerate(pages_in):
-        valid, row, _ = pair_row(moves, partner("replica", s + 1), me, rows, 1)
-        kept = [stays & ~((valid == 1) & (row == r)) for r, stays in enumerate(kept)]
-        copies.append((valid == 1, row, page))
-    copies += [(stays, r, None) for r, stays in enumerate(kept)]
+    copies = [(plan[VALID, s] == 1, plan[NEW_SLOT, s], page) for s, page in enumerate(pages_in)]
+    copies += [(plan[KEPT, r] == 1, plan[SLOT, r], None) for r in range(slots)]
     started = []
-    for n, (active, row, page) in enumerate(copies):
-        _, slot = locate(table, row, column, slots)
+    for n, (active, slot, page) in enumerate(copies):
         pairs = [(pool.at[slot], pool_out.at[slot])]
         if page is not None:
             pairs = [
@@ -275,10 +291,10 @@
     return lax.dot_general(q, keys, (((1,), (1,)), ((), ())), preferred_element_type=jnp.float32)
 
 
-def attend_kernel(count, local_heads, table, lengths, pool, *refs):
+def attend_kernel(count, local_heads, plan_all, lengths_all, pool, *refs):
     messages = by_distance(refs[:count])
-    num, den, wide = refs[count:]
-    column = lax.axis_index("mp")
+    num, den, wide, plan, lengths, sems = refs[count:]
+    tables = start_copies(((plan_all, plan), (lengths_all, lengths)), sems)
     rows = lengths.shape[0]
     slots, page_size, width = pool.shape
     both = 2 * local_heads
@@ -286,7 +302,8 @@
         wide[s] = message[: both * rows, :].astype(jnp.float32)
     lane = lax.broadcasted_iota(jnp.int32, (both, HD), 1)
     token = lax.broadcasted_iota(jnp.int32, (both, page_size), 1)
-    places = [locate(table, r, column, slots) for r in range(rows)]
+    wait_for(tables)
+    places = [(plan[INDEX, r], plan[SLOT, r]) for r in range(rows)]
     columns = [head_columns(partner("mp", s), local_heads) for s in range(count)]
     keys = pool.at[:, :, pl.ds(0, width // 2)]
     values = pool.at[:, :, pl.ds(width // 2, width // 2)]
@@ -311,21 +328,19 @@
         den[s] = denominators[s]
 
 
-def arrive_kernel(count, replicas, local_heads, slots, page_size, *refs):
+def arrive_kernel(count, replicas, local_heads, rows, movers, page_size, *refs):
     refs = list(refs)
     take = lambda n: [refs.pop(0) for _ in range(n)]
     pages_in = take(replicas - 2)
-    moves_all, table_all, projection = take(3)
+    plan_all, projection = take(2)
     pages_in, messages = take(1) + pages_in, by_distance(take(count))
     num_in, den_in = take(2)
     outs = take(count - 1)
-    own_num, own_den, own_kv, own_share, marks, num, den, wide, moves, table, sems = refs
-    tables = start_copies(((moves_all, moves), (table_all, table)), sems)
-    me, column = lax.axis_index("replica"), lax.axis_index("mp")
-    rows = table.shape[1]
+    own_num, own_den, own_kv, own_share, marks, num, den, wide, plan, sem = refs
+    load = pltpu.make_async_copy(plan_all, plan, sem)
+    load.start()
     depth, width = projection.shape
     half_rows = local_heads * rows
-    movers = moves.shape[1] // replicas
 
     extra = [extra_of(page, page_size, width) for page in pages_in]
     inputs = [
@@ -340,22 +355,22 @@
         wide[s, :half_rows, :] = message[half_rows : 2 * half_rows, :].astype(jnp.float32)
     lengths = [length_of(part) for part in extra]
 
-    wait_for(tables)
+    load.wait()
     lane = lax.broadcasted_iota(jnp.int32, (local_heads, HD), 1)
     token = lax.broadcasted_iota(jnp.int32, (local_heads, page_size), 1)
     lines = [
         pl.multiple_of(split(partner("mp", s) * local_heads, GROUP)[0] * page_size, page_size) for s in range(count)
     ]
     cases = [(d, s) for d in range(1, replicas) for s in range(count)]
-    arrivals = [pair_row(moves, partner("replica", d), me, rows, 1) for d in range(1, replicas)]
-    places = [locate(table, row, column, slots) for _, row, _ in arrivals]
+    arrivals = [(plan[VALID, d], plan[ROW, d], plan[ORDER, d]) for d in range(replicas - 1)]
+    indices = [plan[NEW_INDEX, d] for d in range(replicas - 1)]
     scores, weights, totals = {}, {}, {}
     for d, s in cases:
         row = arrivals[d - 1][1]
         q = wide[s, pl.ds(row, local_heads, stride=rows), :].astype(jnp.bfloat16)
         scores[d, s] = scores_of(q, pages_in[d - 1][pl.ds(lines[s], page_size), :])
     for d, s in cases:
-        inside = (token + places[d - 1][0] * page_size).astype(jnp.float32) < lengths[d - 1]
+        inside = (token + indices[d - 1] * page_size).astype(jnp.float32) < lengths[d - 1]
         weight = jnp.where(inside, weight_of(scores[d, s]), 0.0)
         weights[d, s] = weight.astype(jnp.bfloat16)
         totals[d, s] = jnp.sum(weight, axis=1, keepdims=True)
@@ -400,21 +415,20 @@
         out[...] = jnp.concatenate([num[at, : 2 * half_rows, :], parts] + filler + all_kv + arrived, axis=0).astype(SEND)
 
 
-def finish_kernel(count, replicas, local_heads, *refs):
+def finish_kernel(count, replicas, local_heads, movers, *refs):
     refs = list(refs)
     take = lambda n: [refs.pop(0) for _ in range(n)]
     pages_in = take(replicas - 2)
-    moves_all, table_all, lengths_all, kv, share, marks, q, num, den = take(9)
+    plan_all, lengths_all, kv, share, marks, q, num, den = take(8)
     pages_in, messages = take(1) + pages_in, by_distance(take(count - 1))
     pool_raw, _, first, second, pool = take(5)
-    moves, table, lengths, full, arrived, windows, results, sems, write_sems, out_sems = refs
-    tables = start_copies(((moves_all, moves), (table_all, table), (lengths_all, lengths)), sems)
-    me, column = lax.axis_index("replica"), lax.axis_index("mp")
+    plan, lengths, full, arrived, windows, results, sems, write_sems, out_sems = refs
+    tables = start_copies(((plan_all, plan), (lengths_all, lengths)), sems)
+    column = lax.axis_index("mp")
     rows = lengths.shape[0]
     slots, page_size, width = pool_raw.shape
     both = 2 * local_heads
     query_rows = both * rows
-    movers = moves.shape[1] // replicas
     head = split(column * local_heads, GROUP)[0]
 
     kv_base = messages[0].shape[0] - 4 * rows - 16 * movers
@@ -483,10 +497,9 @@
 
     finish_step(0, first)
     wait_for(tables)
-    kept, plans = [jnp.bool_(True)] * rows, []
-
-    def add_plan(active, row, length, first_token, source, r=None):
-        index, slot = locate(table, row, column, slots)
+    plans = []
+
+    def add_plan(active, index, slot, row, length, first_token, source, r=None):
         at = length - index * page_size
         touched = active & (at >= -1) & (at < page_size)
         start = jnp.clip(at, 0, page_size - WINDOW) & -16
@@ -503,13 +516,11 @@
         plans.append((touched, read, write, first_token, rows + row, at - start))
 
     for s, page in enumerate(pages_in):
-        valid, row, order = pair_row(moves, partner("replica", s + 1), me, rows, 1)
-        valid = valid == 1
         length = jnp.max(length_of(extra_of(page, page_size, width))).astype(jnp.int32)
-        add_plan(valid, row, length, 2 * rows + order, page)
-        kept = [stays & ~(valid & (row == r)) for r, stays in enumerate(kept)]
+        place = plan[NEW_INDEX, s], plan[NEW_SLOT, s]
+        add_plan(plan[VALID, s] == 1, *place, plan[ROW, s], length, 2 * rows + plan[ORDER, s], page)
     for r in range(rows):
-        add_plan(kept[r], r, lengths[r], r, pool_raw, r)
+        add_plan(plan[KEPT, r] == 1, plan[INDEX, r], plan[SLOT, r], r, lengths[r], r, pool_raw, r)
 
     place_ids = lax.broadcasted_iota(jnp.int32, (WINDOW, width), 0)
     for n, (touched, read, write, token, next_token, offset) in enumerate(plans):
@@ -580,39 +591,52 @@
     pages_in = exchange(leaving, "replica")
 
     weight_near, inputs_near, queries_near = map(in_vmem, (kv_weight, inputs, queries))
-    sent = pl.pallas_call(
-        functools.partial(open_kernel, count, local_heads),
-        out_shape=[shape((message_rows, HD), bf16)] * count,
-        in_specs=[VMEM] * 2 + [HBM],
-        out_specs=[VMEM] * count,
-        scratch_shapes=[pltpu.VMEM((depth, width), bf16), pltpu.SemaphoreType.DMA((8,))],
+    *sent, plan = pl.pallas_call(
+        functools.partial(open_kernel, count, local_heads, replicas, slots),
+        out_shape=[shape((message_rows, HD), bf16)] * count + [shape((8, 128), jnp.int32)],
+        in_specs=[VMEM] * 2 + [HBM] + [ANY] * 3,
+        out_specs=[VMEM] * count + [ANY],
+        scratch_shapes=[
+            pltpu.VMEM((depth, width), bf16),
+            pltpu.SMEM((8, 128), jnp.int32),
+            pltpu.SMEM(moves.shape, jnp.int32),
+            pltpu.SMEM(old_table.shape, jnp.int32),
+            pltpu.SMEM(table_after.shape, jnp.int32),
+            pltpu.SemaphoreType.DMA((8,)),
+            pltpu.SemaphoreType.DMA((4,)),
+        ],
         compiler_params=params(),
         cost_estimate=cost(1.2),
         name="open",
-    )(inputs_near, queries_near, in_hbm(kv_weight))
+    )(inputs_near, queries_near, in_hbm(kv_weight), moves, old_table, table_after)
     sent, pages_in[0] = lax.optimization_barrier((list(sent), pages_in[0]))
     messages = [sent[0]] + exchange(sent[1:], "mp")
 
     num, den = pl.pallas_call(
         functools.partial(attend_kernel, count, local_heads),
         out_shape=[shape((count, query_rows, HD), f32), shape((count, both, HD), f32)],
-        in_specs=[SMEM, SMEM, VMEM] + [VMEM] * count,
+        in_specs=[ANY, ANY, VMEM] + [VMEM] * count,
         out_specs=[VMEM, VMEM],
-        scratch_shapes=[pltpu.VMEM((count, query_rows, HD), f32)],
+        scratch_shapes=[
+            pltpu.VMEM((count, query_rows, HD), f32),
+            pltpu.SMEM(plan.shape, jnp.int32),
+            pltpu.SMEM(lengths.shape, jnp.int32),
+            pltpu.SemaphoreType.DMA((2,)),
+        ],
         compiler_params=params(),
         cost_estimate=cost(1.5),
         name="attend",
-    )(old_table, lengths, pool_near, *by_start(messages))
+    )(plan, lengths, pool_near, *by_start(messages))
 
     sum_rows = query_rows + -(-both // 16) * 16 + 4 * rows + 16 * movers
     *sums, num, den, kv, share, marks = pl.pallas_call(
-        functools.partial(arrive_kernel, count, replicas, local_heads, slots, page_size),
+        functools.partial(arrive_kernel, count, replicas, local_heads, rows, movers, page_size),
         out_shape=[shape((sum_rows, HD), SEND)] * (count - 1)
         + [shape((query_rows, HD), f32), shape((both, HD), f32)]
         + [shape((2, 2 * rows, HD), f32), shape((movers, 2 * KVH, HD), f32)]
         + [shape((movers, rows, HD), f32)],
         in_specs=[VMEM] * (replicas - 2)
-        + [ANY, ANY, VMEM, VMEM]
+        + [ANY, VMEM, VMEM]
         + [VMEM] * count
         + [VMEM] * 2,
         out_specs=[VMEM] * (count + 4),
@@ -620,62 +644,59 @@
             pltpu.VMEM((count, query_rows + rows, HD), f32),
             pltpu.VMEM((count, both, HD), f32),
             pltpu.VMEM((count, query_rows // 2 + rows, HD), f32),
-            pltpu.SMEM(moves.shape, jnp.int32),
-            pltpu.SMEM(table_after.shape, jnp.int32),
-            pltpu.SemaphoreType.DMA((2,)),
+            pltpu.SMEM(plan.shape, jnp.int32),
+            pltpu.SemaphoreType.DMA(()),
         ],
         compiler_params=params(),
         cost_estimate=cost(1.2),
         name="arrive",
-    )(*pages_in[1:], moves, table_after, weight_near, pages_in[0], *by_start(messages), num, den)
+    )(*pages_in[1:], plan, weight_near, pages_in[0], *by_start(messages), num, den)
     sums_in = rotate(sums, "mp")
 
-    moves_then, _ = lax.optimization_barrier((moves, marks))
+    plan_then, _ = lax.optimization_barrier((plan, marks))
 
     pool_copy = pl.pallas_call(
         functools.partial(keep_kernel, replicas),
         out_shape=shape(pool.shape, bf16),
-        in_specs=[VMEM] * replicas + [ANY] * 2,
+        in_specs=[VMEM] * replicas + [ANY],
         out_specs=ANY,
         scratch_shapes=[
-            pltpu.SMEM(moves.shape, jnp.int32),
-            pltpu.SMEM(table_after.shape, jnp.int32),
-            pltpu.SemaphoreType.DMA((2,)),
+            pltpu.SMEM(plan.shape, jnp.int32),
+            pltpu.SemaphoreType.DMA(()),
             pltpu.SemaphoreType.DMA((rows + replicas - 1, width // HD)),
         ],
         compiler_params=params(),
         cost_estimate=cost(1.6),
         name="keep",
-    )(*pages_in, pool_near, moves_then, table_after)
+    )(*pages_in, pool_near, plan_then)
 
     first, second, pool_after = pl.pallas_call(
-        functools.partial(finish_kernel, count, replicas, local_heads),
+        functools.partial(finish_kernel, count, replicas, local_heads, movers),
         out_shape=[
             shape((rows, local_heads * HD), bf16),
             shape((rows, local_heads * HD), bf16),
             shape(pool.shape, bf16),
         ],
-        in_specs=[VMEM] * (replicas - 2) + [ANY] * 3 + [VMEM] * (7 + count - 1) + [VMEM, ANY],
+        in_specs=[VMEM] * (replicas - 2) + [ANY] * 2 + [VMEM] * (7 + count - 1) + [VMEM, ANY],
         out_specs=[ANY] * 3,
         scratch_shapes=[
-            pltpu.SMEM(moves.shape, jnp.int32),
-            pltpu.SMEM(table_after.shape, jnp.int32),
+            pltpu.SMEM(plan.shape, jnp.int32),
             pltpu.SMEM(lengths.shape, jnp.int32),
             pltpu.VMEM((KV_ROWS, width), f32),
             pltpu.VMEM((movers, 2 * KVH, HD), f32),
             pltpu.VMEM((rows + replicas - 1, WINDOW, width), bf16),
             pltpu.VMEM((2, rows, local_heads * HD), bf16),
-            pltpu.SemaphoreType.DMA((3,)),
+            pltpu.SemaphoreType.DMA((2,)),
             pltpu.SemaphoreType.DMA((rows + replicas - 1,)),
             pltpu.SemaphoreType.DMA((2,)),
         ],
-        input_output_aliases={9 + replicas - 1 + (count - 1) + 1: 2},
+        input_output_aliases={8 + replicas - 1 + (count - 1) + 1: 2},
         compiler_params=params(),
         cost_estimate=cost(2.5),
         name="finish",
     )(
         *pages_in[1:],
-        *(moves, table_after, lengths),
+        *(plan, lengths),
         *(kv, share, marks, messages[0], num, den, pages_in[0]),
         *by_start(sums_in),
         *(pool_near, pool_copy),

time: 30 us -> 29.9 us (level)
  transfers between devices with their start and end apart: 9 -> 9, of which waited for: 2 -> 3; matrix products, arithmetic and copies ran while one was open for 0% -> 0% of each run, Pallas kernels for 23% -> 23%
where the time goes in v10:
time: 29.9 us; the launch traced here: 29.8 us
  starting transfers between devices  12.6 us (42%)
  Pallas kernels  11.8 us (39%)
  waiting for transfers between devices  4.57 us (15%)
  between operations  0.79 us (3%)
    ppermute x6, starting transfers between devices, swap(): return lax.ppermute(value, axis, [(i, i ^ distance) for i in range(size)])  7.63 us
    ppermute x3, starting transfers between devices, rotate(): lax.ppermute(message, axis, list(enumerate(step)))  4.95 us
    ppermute x6, waiting for transfers between devices, swap(): return lax.ppermute(value, axis, [(i, i ^ distance) for i in range(size)])  4.5 us
    pallas_call x1, Pallas kernels, body(): pl.pallas_call(functools.partial(keep_kernel, replicas), out_shape=shape(...  2.7 us
    pallas_call x1, Pallas kernels, body(): pl.pallas_call(functools.partial(open_kernel, count, local_heads, replica...  2.63 us
    pallas_call x1, Pallas kernels, body(): pl.pallas_call(functools.partial(finish_kernel, count, replicas, local_he...  1.84 us
    pallas_call x1, Pallas kernels, body(): pl.pallas_call(functools.partial(leave_kernel, rows), out_shape=[shape(po...  1.81 us
    pallas_call x1, Pallas kernels, body(): pl.pallas_call(functools.partial(attend_kernel, count, local_heads), out_...  1.59 us
  transfers between devices with their start and end apart: 9, of which 3 were waited for; matrix products, arithmetic and copies ran while one was open for 0% of the time, Pallas kernels for 23%

profile of v10, /device:TPU:0, one launch (start us, length us, event | category | flops | bytes accessed | tf_op | source)
XLA Modules:
  0.0 29.8 jit_solution(17955558323562984202)
XLA Ops:
  0.6 0.0 copy-start.5
  0.6 0.0 copy-start.3
  0.7 0.0 copy-start.1
  0.7 1.8 %leave.1 = (bf16[8,128,1024]{2,1,0:T(8,128)(2,1)S(1)}, bf16[1048,128]{1,0:T(8,128)(2,1)S(1)}, bf16[1048,128]{1,0:T(8,128)(2,1)S(1)}, bf16[1048,128]{1,0:T(8,128)(2,1)S(1)}) custom-call(s32[2,8]{1,0:T(2,128)} %bitcast.10, s32[4,8]{1,0:T(4,128)} %bitcast.8, s32[8]{0:T(128)} %refs_3_.3, bf16[16,2048]{1,0:T(8,128)(2,1)} %bitcast.6, bf16[8,128,1024]{2,1,0:T(8,128)(2,1)} %bitcast.14), custom_call_target="tpu_custom_call" | custom-call | bytes 6300000 | tf_op jit(solution)/shard_map/leave/pallas_call | solution.py:574
  2.5 0.5 %collective-permute-start.2 = (bf16[1048,128]{1,0:T(8,128)(2,1)S(1)}, bf16[1048,128]{1,0:T(8,128)(2,1)S(1)}, u32[]{:S(2)}, u32[]{:S(2)}) collective-permute-start(bf16[1048,128]{1,0:T(8,128)(2,1)S(1)} %get-tuple-element.38), channel_id=1, source_target_pairs={{0,4},{4,0},{8,12},{12,8},{1,5},{5,1},{9,13},{13,9},{2,6},{6,2},{1... | collective-permute-start | bytes 804872 | tf_op jit(solution)/shard_map/ppermute | solution.py:29
  3.0 2.6 %collective-permute-start = (bf16[1048,128]{1,0:T(8,128)(2,1)S(1)}, bf16[1048,128]{1,0:T(8,128)(2,1)S(1)}, u32[]{:S(2)}, u32[]{:S(2)}) collective-permute-start(bf16[1048,128]{1,0:T(8,128)(2,1)S(1)} %get-tuple-element.31), channel_id=1, source_target_pairs={{0,8},{4,12},{8,0},{12,4},{1,9},{5,13},{9,1},{13,5},{2,10},{6,14},... | collective-permute-start | bytes 804872 | tf_op jit(solution)/shard_map/ppermute | solution.py:29
  5.6 0.1 collective-permute-start.1
  5.6 0.0 copy-done.5
  5.7 0.0 copy-done.1
  5.7 0.0 copy-start.4
  5.7 0.0 copy-start
  5.7 2.6 %open.1 = (bf16[192,128]{1,0:T(8,128)(2,1)S(1)}, bf16[192,128]{1,0:T(8,128)(2,1)S(1)}, bf16[192,128]{1,0:T(8,128)(2,1)S(1)}, bf16[192,128]{1,0:T(8,128)(2,1)S(1)}, s32[8,128]{1,0:T(8,128)S(1)}) custom-call(bf16[16,2048]{1,0:T(8,128)(2,1)S(1)} %bitcast.7, bf16[2,8,1024]{2,1,0:T(8,128)(2,1)S(1)} %copy-done.2, bf16[2048,1024]{1,0:T(8,128)(2,1)} %refs_3_.2, ...), custom_call_target="tpu_custom_call" | custom-call | bytes 4200000 | tf_op jit(solution)/shard_map/open/pallas_call | solution.py:594
  8.3 0.0 collective-permute-done.2.refs_4_.refs_0_.refs_10_
  8.3 2.9 %collective-permute-start.3 = (bf16[192,128]{1,0:T(8,128)(2,1)S(1)}, bf16[192,128]{1,0:T(8,128)(2,1)S(1)}, u32[]{:S(2)}, u32[]{:S(2)}) collective-permute-start(bf16[192,128]{1,0:T(8,128)(2,1)S(1)} %get-tuple-element.40), channel_id=1, source_target_pairs={{0,2},{1,3},{2,0},{3,1},{4,6},{5,7},{6,4},{7,5},{8,10},{9,11},{10,... | collective-permute-start | bytes 147464 | tf_op jit(solution)/shard_map/ppermute | solution.py:29
  11.2 1.3 %collective-permute-start.4 = (bf16[192,128]{1,0:T(8,128)(2,1)S(1)}, bf16[192,128]{1,0:T(8,128)(2,1)S(1)}, u32[]{:S(2)}, u32[]{:S(2)}) collective-permute-start(bf16[192,128]{1,0:T(8,128)(2,1)S(1)} %get-tuple-element.41), channel_id=1, source_target_pairs={{0,3},{1,2},{2,1},{3,0},{4,7},{5,6},{6,5},{7,4},{8,11},{9,10},{10,... | collective-permute-start | bytes 147464 | tf_op jit(solution)/shard_map/ppermute | solution.py:29
  12.6 0.2 collective-permute-start.5
  12.8 0.7 %collective-permute-done.3.refs_0_.refs_5_ = bf16[192,128]{1,0:T(8,128)(2,1)S(1)} collective-permute-done((bf16[192,128]{1,0:T(8,128)(2,1)S(1)}, bf16[192,128]{1,0:T(8,128)(2,1)S(1)}, u32[]{:S(2)}, u32[]{:S(2)}) %collective-permute-start.3) | collective-permute-done | bytes 49184 | tf_op jit(solution)/shard_map/ppermute | solution.py:29
  13.5 3.8 %collective-permute-done.4.refs_1_.refs_6_ = bf16[192,128]{1,0:T(8,128)(2,1)S(1)} collective-permute-done((bf16[192,128]{1,0:T(8,128)(2,1)S(1)}, bf16[192,128]{1,0:T(8,128)(2,1)S(1)}, u32[]{:S(2)}, u32[]{:S(2)}) %collective-permute-start.4) | collective-permute-done | bytes 49184 | tf_op jit(solution)/shard_map/ppermute | solution.py:29
  17.3 0.0 collective-permute-done.5.refs_2_.refs_7_
  17.3 0.0 copy-done.4
  17.3 1.6 %attend.1 = (f32[4,128,128]{2,1,0:T(8,128)S(1)}, f32[4,16,128]{2,1,0:T(8,128)S(1)}) custom-call(s32[8,128]{1,0:T(8,128)S(1)} %get-tuple-element.55.plan_all.refs_2_.refs_4_, s32[8]{0:T(128)S(1)} %copy-done.4, bf16[8,128,1024]{2,1,0:T(8,128)(2,1)S(1)} %get-tuple-element.44.pool.refs_3_.refs_14_, bf16[192,128]{1,0:T(8,128)(2,1)S(1)} %collective-permute-done.3.refs_0_.refs_5_, ...), custom_call_target="tpu_custom_call" | custom-call | bytes 5250000 | tf_op jit(solution)/shard_map/attend/pallas_call | solution.py:615
  18.9 0.0 collective-permute-done.refs_0_.refs_1_
  18.9 0.0 collective-permute-done.1.refs_1_.refs_2_
  18.9 1.2 %arrive.1 = (bf16[208,128]{1,0:T(8,128)(2,1)S(1)}, bf16[208,128]{1,0:T(8,128)(2,1)S(1)}, bf16[208,128]{1,0:T(8,128)(2,1)S(1)}, f32[128,128]{1,0:T(8,128)S(1)}, f...) custom-call(bf16[1048,128]{1,0:T(8,128)(2,1)S(1)} %collective-permute-don, ...), custom_call_target="tpu_custom_call" | custom-call | bytes 4200000 | tf_op jit(solution)/shard_map/arrive/pallas_call | solution.py:632
  20.2 0.8 %collective-permute-start.6 = (bf16[208,128]{1,0:T(8,128)(2,1)S(1)}, bf16[208,128]{1,0:T(8,128)(2,1)S(1)}, u32[]{:S(2)}, u32[]{:S(2)}) collective-permute-start(bf16[208,128]{1,0:T(8,128)(2,1)S(1)} %get-tuple-element.52), channel_id=1, source_target_pairs={{0,1},{1,3},{2,0},{3,2},{4,5},{5,7},{6,4},{7,6},{8,9},{9,11},{10,8... | collective-permute-start | bytes 159752 | tf_op jit(solution)/shard_map/ppermute | solution.py:45
  21.0 2.7 %collective-permute-start.7 = (bf16[208,128]{1,0:T(8,128)(2,1)S(1)}, bf16[208,128]{1,0:T(8,128)(2,1)S(1)}, u32[]{:S(2)}, u32[]{:S(2)}) collective-permute-start(bf16[208,128]{1,0:T(8,128)(2,1)S(1)} %get-tuple-element.53), channel_id=1, source_target_pairs={{0,3},{1,2},{2,1},{3,0},{4,7},{5,6},{6,5},{7,4},{8,11},{9,10},{10,... | collective-permute-start | bytes 159752 | tf_op jit(solution)/shard_map/ppermute | solution.py:45
  23.7 1.4 %collective-permute-start.8 = (bf16[208,128]{1,0:T(8,128)(2,1)S(1)}, bf16[208,128]{1,0:T(8,128)(2,1)S(1)}, u32[]{:S(2)}, u32[]{:S(2)}) collective-permute-start(bf16[208,128]{1,0:T(8,128)(2,1)S(1)} %get-tuple-element.54), channel_id=1, source_target_pairs={{0,2},{1,0},{2,3},{3,1},{4,6},{5,4},{6,7},{7,5},{8,10},{9,8},{10,1... | collective-permute-start | bytes 159752 | tf_op jit(solution)/shard_map/ppermute | solution.py:45
  25.1 2.7 %keep.1.refs_15_ = bf16[8,128,1024]{2,1,0:T(8,128)(2,1)} custom-call(bf16[1048,128]{1,0:T(8,128)(2,1)S(1)} %collective-permute-done.2.refs_4_.refs_0_.refs_10_, bf16[1048,128]{1,0:T(8,128)(2,1)S(1)} %collective-permute-done.refs_0_.refs_1_, bf16[1048,128]{1,0:T(8,128)(2,1)S(1)} %collective-permute-done.1.refs_1_.refs_2_, ...), custom_call_target="tpu_custom_call" | custom-call | bytes 5600000 | tf_op jit(solution)/shard_map/keep/pallas_call | solution.py:658
  27.8 0.0 collective-permute-done.6.refs_11_
  27.9 0.0 collective-permute-done.7.refs_12_
  27.9 0.1 collective-permute-done.8.refs_13_
  27.9 1.8 %finish.1 = (bf16[8,1024]{1,0:T(8,128)(2,1)}, bf16[8,1024]{1,0:T(8,128)(2,1)}, bf16[8,128,1024]{2,1,0:T(8,128)(2,1)}) custom-call(bf16[1048,128]{1,0:T(8,128)(2,1)S(1)} %collective-permute-done.refs_0_.refs_1_, bf16[1048,128]{1,0:T(8,128)(2,1)S(1)} %collective-permute-done.1.refs_1_.refs_2_, ...), custom_call_target="tpu_custom_call", output_to_operand_aliasing={{2}: (15, {})} | custom-call | bytes 8750000 | tf_op jit(solution)/shard_map/finish/pallas_call | solution.py:673
  (6 shorter events, 0.0 us)
Async XLA Ops:
  0.6 5.0 %copy-start.5 = (s32[8,2]{0,1:T(2,128)S(1)}, s32[8,2]{0,1:T(2,128)}, u32[]{:S(2)}) copy-start(s32[8,2]{0,1:T(2,128)} %param.15) | copy-start | bytes 196
  0.6 5.0 %copy-start.3 = (s32[8,4]{0,1:T(4,128)S(1)}, s32[8,4]{0,1:T(4,128)}, u32[]{:S(2)}) copy-start(s32[8,4]{0,1:T(4,128)} %param.13) | copy-start | bytes 388
  0.7 5.0 %copy-start.1 = (bf16[2,8,2048]{2,1,0:T(8,128)(2,1)S(1)}, bf16[2,8,2048]{2,1,0:T(8,128)(2,1)}, u32[]{:S(2)}) copy-start(bf16[2,8,2048]{2,1,0:T(8,128)(2,1)} %param.8) | copy-start | bytes 196612
  0.7 5.0 %copy-start.6 = (s32[8,4]{0,1:T(4,128)S(1)}, s32[8,4]{0,1:T(4,128)}, u32[]{:S(2)}) copy-start(s32[8,4]{0,1:T(4,128)} %param.14) | copy-start | bytes 388
  0.7 5.0 %copy-start.2 = (bf16[2,8,1024]{2,1,0:T(8,128)(2,1)S(1)}, bf16[2,8,1024]{2,1,0:T(8,128)(2,1)}, u32[]{:S(2)}) copy-start(bf16[2,8,1024]{2,1,0:T(8,128)(2,1)} %q.1) | copy-start | bytes 98308
  2.5 5.8 %collective-permute-start.2 = (bf16[1048,128]{1,0:T(8,128)(2,1)S(1)}, bf16[1048,128]{1,0:T(8,128)(2,1)S(1)}, u32[]{:S(2)}, u32[]{:S(2)}) collective-permute-start(bf16[1048,128]{1,0:T(8,128)(2,1)S(1)} %get-tuple-element.38), channel_id=1, source_target_pairs={{0,4},{4,0},{8,12},{12,8},{1,5},{5,1},{9,13},{13,9},{2,6},{6,2},{1... | collective-permute-start | bytes 804872 | tf_op jit(solution)/shard_map/ppermute | solution.py:29
  3.0 15.9 %collective-permute-start = (bf16[1048,128]{1,0:T(8,128)(2,1)S(1)}, bf16[1048,128]{1,0:T(8,128)(2,1)S(1)}, u32[]{:S(2)}, u32[]{:S(2)}) collective-permute-start(bf16[1048,128]{1,0:T(8,128)(2,1)S(1)} %get-tuple-element.31), channel_id=1, source_target_pairs={{0,8},{4,12},{8,0},{12,4},{1,9},{5,13},{9,1},{13,5},{2,10},{6,14},... | collective-permute-start | bytes 804872 | tf_op jit(solution)/shard_map/ppermute | solution.py:29
  5.6 13.3 %collective-permute-start.1 = (bf16[1048,128]{1,0:T(8,128)(2,1)S(1)}, bf16[1048,128]{1,0:T(8,128)(2,1)S(1)}, u32[]{:S(2)}, u32[]{:S(2)}) collective-permute-start(bf16[1048,128]{1,0:T(8,128)(2,1)S(1)} %get-tuple-element.32), channel_id=1, source_target_pairs={{0,12},{4,8},{8,4},{12,0},{1,13},{5,9},{9,5},{13,1},{2,14},{6,10},... | collective-permute-start | bytes 804872 | tf_op jit(solution)/shard_map/ppermute | solution.py:29
  5.7 11.6 %copy-start.4 = (s32[8]{0:T(128)S(1)}, s32[8]{0:T(128)}, u32[]{:S(2)}) copy-start(s32[8]{0:T(128)} %refs_3_.3) | copy-start | bytes 100
  5.7 13.3 %copy-start = (bf16[2048,1024]{1,0:T(8,128)(2,1)S(1)}, bf16[2048,1024]{1,0:T(8,128)(2,1)}, u32[]{:S(2)}) copy-start(bf16[2048,1024]{1,0:T(8,128)(2,1)} %refs_3_.2) | copy-start | bytes 12582916
  8.3 5.2 %collective-permute-start.3 = (bf16[192,128]{1,0:T(8,128)(2,1)S(1)}, bf16[192,128]{1,0:T(8,128)(2,1)S(1)}, u32[]{:S(2)}, u32[]{:S(2)}) collective-permute-start(bf16[192,128]{1,0:T(8,128)(2,1)S(1)} %get-tuple-element.40), channel_id=1, source_target_pairs={{0,2},{1,3},{2,0},{3,1},{4,6},{5,7},{6,4},{7,5},{8,10},{9,11},{10,... | collective-permute-start | bytes 147464 | tf_op jit(solution)/shard_map/ppermute | solution.py:29
  11.2 6.1 %collective-permute-start.4 = (bf16[192,128]{1,0:T(8,128)(2,1)S(1)}, bf16[192,128]{1,0:T(8,128)(2,1)S(1)}, u32[]{:S(2)}, u32[]{:S(2)}) collective-permute-start(bf16[192,128]{1,0:T(8,128)(2,1)S(1)} %get-tuple-element.41), channel_id=1, source_target_pairs={{0,3},{1,2},{2,1},{3,0},{4,7},{5,6},{6,5},{7,4},{8,11},{9,10},{10,... | collective-permute-start | bytes 147464 | tf_op jit(solution)/shard_map/ppermute | solution.py:29
  12.6 4.7 %collective-permute-start.5 = (bf16[192,128]{1,0:T(8,128)(2,1)S(1)}, bf16[192,128]{1,0:T(8,128)(2,1)S(1)}, u32[]{:S(2)}, u32[]{:S(2)}) collective-permute-start(bf16[192,128]{1,0:T(8,128)(2,1)S(1)} %get-tuple-element.42), channel_id=1, source_target_pairs={{0,1},{1,0},{2,3},{3,2},{4,5},{5,4},{6,7},{7,6},{8,9},{9,8},{10,11... | collective-permute-start | bytes 147464 | tf_op jit(solution)/shard_map/ppermute | solution.py:29
  20.2 7.7 %collective-permute-start.6 = (bf16[208,128]{1,0:T(8,128)(2,1)S(1)}, bf16[208,128]{1,0:T(8,128)(2,1)S(1)}, u32[]{:S(2)}, u32[]{:S(2)}) collective-permute-start(bf16[208,128]{1,0:T(8,128)(2,1)S(1)} %get-tuple-element.52), channel_id=1, source_target_pairs={{0,1},{1,3},{2,0},{3,2},{4,5},{5,7},{6,4},{7,6},{8,9},{9,11},{10,8... | collective-permute-start | bytes 159752 | tf_op jit(solution)/shard_map/ppermute | solution.py:45
  21.0 6.8 %collective-permute-start.7 = (bf16[208,128]{1,0:T(8,128)(2,1)S(1)}, bf16[208,128]{1,0:T(8,128)(2,1)S(1)}, u32[]{:S(2)}, u32[]{:S(2)}) collective-permute-start(bf16[208,128]{1,0:T(8,128)(2,1)S(1)} %get-tuple-element.53), channel_id=1, source_target_pairs={{0,3},{1,2},{2,1},{3,0},{4,7},{5,6},{6,5},{7,4},{8,11},{9,10},{10,... | collective-permute-start | bytes 159752 | tf_op jit(solution)/shard_map/ppermute | solution.py:45
  23.7 4.2 %collective-permute-start.8 = (bf16[208,128]{1,0:T(8,128)(2,1)S(1)}, bf16[208,128]{1,0:T(8,128)(2,1)S(1)}, u32[]{:S(2)}, u32[]{:S(2)}) collective-permute-start(bf16[208,128]{1,0:T(8,128)(2,1)S(1)} %get-tuple-element.54), channel_id=1, source_target_pairs={{0,2},{1,0},{2,3},{3,1},{4,6},{5,4},{6,7},{7,5},{8,10},{9,8},{10,1... | collective-permute-start | bytes 159752 | tf_op jit(solution)/shard_map/ppermute | solution.py:45

commit v11 on v10

--- a/solution.py
+++ b/solution.py
@@ -291,10 +291,10 @@
     return lax.dot_general(q, keys, (((1,), (1,)), ((), ())), preferred_element_type=jnp.float32)
 
 
-def attend_kernel(count, local_heads, plan_all, lengths_all, pool, *refs):
+def attend_kernel(count, local_heads, table, lengths, pool, *refs):
     messages = by_distance(refs[:count])
-    num, den, wide, plan, lengths, sems = refs[count:]
-    tables = start_copies(((plan_all, plan), (lengths_all, lengths)), sems)
+    num, den, wide = refs[count:]
+    column = lax.axis_index("mp")
     rows = lengths.shape[0]
     slots, page_size, width = pool.shape
     both = 2 * local_heads
@@ -302,8 +302,7 @@
         wide[s] = message[: both * rows, :].astype(jnp.float32)
     lane = lax.broadcasted_iota(jnp.int32, (both, HD), 1)
     token = lax.broadcasted_iota(jnp.int32, (both, page_size), 1)
-    wait_for(tables)
-    places = [(plan[INDEX, r], plan[SLOT, r]) for r in range(rows)]
+    places = [locate(table, r, column, slots) for r in range(rows)]
     columns = [head_columns(partner("mp", s), local_heads) for s in range(count)]
     keys = pool.at[:, :, pl.ds(0, width // 2)]
     values = pool.at[:, :, pl.ds(width // 2, width // 2)]
@@ -615,18 +614,13 @@
     num, den = pl.pallas_call(
         functools.partial(attend_kernel, count, local_heads),
         out_shape=[shape((count, query_rows, HD), f32), shape((count, both, HD), f32)],
-        in_specs=[ANY, ANY, VMEM] + [VMEM] * count,
+        in_specs=[SMEM, SMEM, VMEM] + [VMEM] * count,
         out_specs=[VMEM, VMEM],
-        scratch_shapes=[
-            pltpu.VMEM((count, query_rows, HD), f32),
-            pltpu.SMEM(plan.shape, jnp.int32),
-            pltpu.SMEM(lengths.shape, jnp.int32),
-            pltpu.SemaphoreType.DMA((2,)),
-        ],
+        scratch_shapes=[pltpu.VMEM((count, query_rows, HD), f32)],
         compiler_params=params(),
         cost_estimate=cost(1.5),
         name="attend",
-    )(plan, lengths, pool_near, *by_start(messages))
+    )(old_table, lengths, pool_near, *by_start(messages))
 
     sum_rows = query_rows + -(-both // 16) * 16 + 4 * rows + 16 * movers
     *sums, num, den, kv, share, marks = pl.pallas_call(

time: 29.9 us -> 29.9 us (level)
  no operation moved by 1% of the time
where the time goes in v11:
time: 29.9 us; the launch traced here: 29.8 us
  starting transfers between devices  12.6 us (42%)
  Pallas kernels  11.7 us (39%)
  waiting for transfers between devices  4.61 us (15%)
  between operations  0.78 us (3%)
    ppermute x6, starting transfers between devices, swap(): return lax.ppermute(value, axis, [(i, i ^ distance) for i in range(size)])  7.63 us
    ppermute x3, starting transfers between devices, rotate(): lax.ppermute(message, axis, list(enumerate(step)))  4.98 us
    ppermute x6, waiting for transfers between devices, swap(): return lax.ppermute(value, axis, [(i, i ^ distance) for i in range(size)])  4.5 us
    pallas_call x1, Pallas kernels, body(): pl.pallas_call(functools.partial(keep_kernel, replicas), out_shape=shape(...  2.7 us
    pallas_call x1, Pallas kernels, body(): pl.pallas_call(functools.partial(open_kernel, count, local_heads, replica...  2.63 us
    pallas_call x1, Pallas kernels, body(): pl.pallas_call(functools.partial(finish_kernel, count, replicas, local_he...  1.85 us
    pallas_call x1, Pallas kernels, body(): pl.pallas_call(functools.partial(leave_kernel, rows), out_shape=[shape(po...  1.81 us
    pallas_call x1, Pallas kernels, body(): pl.pallas_call(functools.partial(attend_kernel, count, local_heads), out_...  1.52 us
  transfers between devices with their start and end apart: 9, of which 3 were waited for; matrix products, arithmetic and copies ran while one was open for 0% of the time, Pallas kernels for 23%

profile of v11, /device:TPU:0, one launch (start us, length us, event | category | flops | bytes accessed | tf_op | source)
XLA Modules:
  0.0 29.8 jit_solution(17080167785423588129)
XLA Ops:
  0.6 0.0 copy-start.5
  0.6 0.0 copy-start.3
  0.7 0.0 copy-start.1
  0.7 0.0 copy-start.6
  0.7 1.8 %leave.1 = (bf16[8,128,1024]{2,1,0:T(8,128)(2,1)S(1)}, bf16[1048,128]{1,0:T(8,128)(2,1)S(1)}, bf16[1048,128]{1,0:T(8,128)(2,1)S(1)}, bf16[1048,128]{1,0:T(8,128)(2,1)S(1)}) custom-call(s32[2,8]{1,0:T(2,128)} %bitcast.11, s32[4,8]{1,0:T(4,128)} %bitcast.8, s32[8]{0:T(128)} %refs_3_.3, bf16[16,2048]{1,0:T(8,128)(2,1)} %bitcast.6, bf16[8,128,1024]{2,1,0:T(8,128)(2,1)} %bitcast.15), custom_call_target="tpu_custom_call" | custom-call | bytes 6300000 | tf_op jit(solution)/shard_map/leave/pallas_call | solution.py:573
  2.5 0.5 %collective-permute-start.2 = (bf16[1048,128]{1,0:T(8,128)(2,1)S(1)}, bf16[1048,128]{1,0:T(8,128)(2,1)S(1)}, u32[]{:S(2)}, u32[]{:S(2)}) collective-permute-start(bf16[1048,128]{1,0:T(8,128)(2,1)S(1)} %get-tuple-element.38), channel_id=1, source_target_pairs={{0,4},{4,0},{8,12},{12,8},{1,5},{5,1},{9,13},{13,9},{2,6},{6,2},{1... | collective-permute-start | bytes 804872 | tf_op jit(solution)/shard_map/ppermute | solution.py:29
  3.0 2.6 %collective-permute-start = (bf16[1048,128]{1,0:T(8,128)(2,1)S(1)}, bf16[1048,128]{1,0:T(8,128)(2,1)S(1)}, u32[]{:S(2)}, u32[]{:S(2)}) collective-permute-start(bf16[1048,128]{1,0:T(8,128)(2,1)S(1)} %get-tuple-element.31), channel_id=1, source_target_pairs={{0,8},{4,12},{8,0},{12,4},{1,9},{5,13},{9,1},{13,5},{2,10},{6,14},... | collective-permute-start | bytes 804872 | tf_op jit(solution)/shard_map/ppermute | solution.py:29
  5.6 0.1 collective-permute-start.1
  5.7 0.0 copy-done.6
  5.7 0.0 copy-start.4
  5.7 0.0 copy-start
  5.7 2.6 %open.1 = (bf16[192,128]{1,0:T(8,128)(2,1)S(1)}, bf16[192,128]{1,0:T(8,128)(2,1)S(1)}, bf16[192,128]{1,0:T(8,128)(2,1)S(1)}, bf16[192,128]{1,0:T(8,128)(2,1)S(1)}, s32[8,128]{1,0:T(8,128)S(1)}) custom-call(bf16[16,2048]{1,0:T(8,128)(2,1)S(1)} %bitcast.7, bf16[2,8,1024]{2,1,0:T(8,128)(2,1)S(1)} %copy-done.2, bf16[2048,1024]{1,0:T(8,128)(2,1)} %refs_3_.2, ...), custom_call_target="tpu_custom_call" | custom-call | bytes 4200000 | tf_op jit(solution)/shard_map/open/pallas_call | solution.py:593
  8.3 0.0 collective-permute-done.2.refs_4_.refs_0_.refs_10_
  8.3 2.9 %collective-permute-start.3 = (bf16[192,128]{1,0:T(8,128)(2,1)S(1)}, bf16[192,128]{1,0:T(8,128)(2,1)S(1)}, u32[]{:S(2)}, u32[]{:S(2)}) collective-permute-start(bf16[192,128]{1,0:T(8,128)(2,1)S(1)} %get-tuple-element.40), channel_id=1, source_target_pairs={{0,2},{1,3},{2,0},{3,1},{4,6},{5,7},{6,4},{7,5},{8,10},{9,11},{10,... | collective-permute-start | bytes 147464 | tf_op jit(solution)/shard_map/ppermute | solution.py:29
  11.2 1.3 %collective-permute-start.4 = (bf16[192,128]{1,0:T(8,128)(2,1)S(1)}, bf16[192,128]{1,0:T(8,128)(2,1)S(1)}, u32[]{:S(2)}, u32[]{:S(2)}) collective-permute-start(bf16[192,128]{1,0:T(8,128)(2,1)S(1)} %get-tuple-element.41), channel_id=1, source_target_pairs={{0,3},{1,2},{2,1},{3,0},{4,7},{5,6},{6,5},{7,4},{8,11},{9,10},{10,... | collective-permute-start | bytes 147464 | tf_op jit(solution)/shard_map/ppermute | solution.py:29
  12.6 0.2 collective-permute-start.5
  12.8 0.7 %collective-permute-done.3.refs_0_.refs_5_ = bf16[192,128]{1,0:T(8,128)(2,1)S(1)} collective-permute-done((bf16[192,128]{1,0:T(8,128)(2,1)S(1)}, bf16[192,128]{1,0:T(8,128)(2,1)S(1)}, u32[]{:S(2)}, u32[]{:S(2)}) %collective-permute-start.3) | collective-permute-done | bytes 49184 | tf_op jit(solution)/shard_map/ppermute | solution.py:29
  13.5 3.8 %collective-permute-done.4.refs_1_.refs_6_ = bf16[192,128]{1,0:T(8,128)(2,1)S(1)} collective-permute-done((bf16[192,128]{1,0:T(8,128)(2,1)S(1)}, bf16[192,128]{1,0:T(8,128)(2,1)S(1)}, u32[]{:S(2)}, u32[]{:S(2)}) %collective-permute-start.4) | collective-permute-done | bytes 49184 | tf_op jit(solution)/shard_map/ppermute | solution.py:29
  17.3 0.0 collective-permute-done.5.refs_2_.refs_7_
  17.3 1.5 %attend.1 = (f32[4,128,128]{2,1,0:T(8,128)S(1)}, f32[4,16,128]{2,1,0:T(8,128)S(1)}) custom-call(s32[4,8]{1,0:T(4,128)S(1)} %bitcast.10, s32[8]{0:T(128)S(1)} %copy-done.4, bf16[8,128,1024]{2,1,0:T(8,128)(2,1)S(1)} %get-tuple-element.44.pool.refs_3_.refs_14_, bf16[192,128]{1,0:T(8,128)(2,1)S(1)} %collective-permute-done.3.refs_0_.refs_5_, ...), custom_call_target="tpu_custom_call" | custom-call | bytes 5250000 | tf_op jit(solution)/shard_map/attend/pallas_call | solution.py:614
  18.8 0.0 collective-permute-done.refs_0_.refs_1_
  18.9 0.0 collective-permute-done.1.refs_1_.refs_2_
  18.9 0.0 copy-done
  18.9 1.2 %arrive.1 = (bf16[208,128]{1,0:T(8,128)(2,1)S(1)}, bf16[208,128]{1,0:T(8,128)(2,1)S(1)}, bf16[208,128]{1,0:T(8,128)(2,1)S(1)}, f32[128,128]{1,0:T(8,128)S(1)}, f...) custom-call(bf16[1048,128]{1,0:T(8,128)(2,1)S(1)} %collective-permute-don, ...), custom_call_target="tpu_custom_call" | custom-call | bytes 4200000 | tf_op jit(solution)/shard_map/arrive/pallas_call | solution.py:626
  20.1 0.9 %collective-permute-start.6 = (bf16[208,128]{1,0:T(8,128)(2,1)S(1)}, bf16[208,128]{1,0:T(8,128)(2,1)S(1)}, u32[]{:S(2)}, u32[]{:S(2)}) collective-permute-start(bf16[208,128]{1,0:T(8,128)(2,1)S(1)} %get-tuple-element.52), channel_id=1, source_target_pairs={{0,1},{1,3},{2,0},{3,2},{4,5},{5,7},{6,4},{7,6},{8,9},{9,11},{10,8... | collective-permute-start | bytes 159752 | tf_op jit(solution)/shard_map/ppermute | solution.py:45
  21.0 2.6 %collective-permute-start.7 = (bf16[208,128]{1,0:T(8,128)(2,1)S(1)}, bf16[208,128]{1,0:T(8,128)(2,1)S(1)}, u32[]{:S(2)}, u32[]{:S(2)}) collective-permute-start(bf16[208,128]{1,0:T(8,128)(2,1)S(1)} %get-tuple-element.53), channel_id=1, source_target_pairs={{0,3},{1,2},{2,1},{3,0},{4,7},{5,6},{6,5},{7,4},{8,11},{9,10},{10,... | collective-permute-start | bytes 159752 | tf_op jit(solution)/shard_map/ppermute | solution.py:45
  23.6 1.5 %collective-permute-start.8 = (bf16[208,128]{1,0:T(8,128)(2,1)S(1)}, bf16[208,128]{1,0:T(8,128)(2,1)S(1)}, u32[]{:S(2)}, u32[]{:S(2)}) collective-permute-start(bf16[208,128]{1,0:T(8,128)(2,1)S(1)} %get-tuple-element.54), channel_id=1, source_target_pairs={{0,2},{1,0},{2,3},{3,1},{4,6},{5,4},{6,7},{7,5},{8,10},{9,8},{10,1... | collective-permute-start | bytes 159752 | tf_op jit(solution)/shard_map/ppermute | solution.py:45
  25.1 2.7 %keep.1.refs_15_ = bf16[8,128,1024]{2,1,0:T(8,128)(2,1)} custom-call(bf16[1048,128]{1,0:T(8,128)(2,1)S(1)} %collective-permute-done.2.refs_4_.refs_0_.refs_10_, bf16[1048,128]{1,0:T(8,128)(2,1)S(1)} %collective-permute-done.refs_0_.refs_1_, bf16[1048,128]{1,0:T(8,128)(2,1)S(1)} %collective-permute-done.1.refs_1_.refs_2_, ...), custom_call_target="tpu_custom_call" | custom-call | bytes 5600000 | tf_op jit(solution)/shard_map/keep/pallas_call | solution.py:652
  27.8 0.0 collective-permute-done.6.refs_11_
  27.8 0.0 collective-permute-done.7.refs_12_
  27.8 0.1 collective-permute-done.8.refs_13_
  27.9 1.9 %finish.1 = (bf16[8,1024]{1,0:T(8,128)(2,1)}, bf16[8,1024]{1,0:T(8,128)(2,1)}, bf16[8,128,1024]{2,1,0:T(8,128)(2,1)}) custom-call(bf16[1048,128]{1,0:T(8,128)(2,1)S(1)} %collective-permute-done.refs_0_.refs_1_, bf16[1048,128]{1,0:T(8,128)(2,1)S(1)} %collective-permute-done.1.refs_1_.refs_2_, ...), custom_call_target="tpu_custom_call", output_to_operand_aliasing={{2}: (15, {})} | custom-call | bytes 8750000 | tf_op jit(solution)/shard_map/finish/pallas_call | solution.py:667
  (6 shorter events, 0.0 us)
Async XLA Ops:
  0.6 5.0 %copy-start.5 = (s32[8,2]{0,1:T(2,128)S(1)}, s32[8,2]{0,1:T(2,128)}, u32[]{:S(2)}) copy-start(s32[8,2]{0,1:T(2,128)} %param.15) | copy-start | bytes 196
  0.6 5.0 %copy-start.3 = (s32[8,4]{0,1:T(4,128)S(1)}, s32[8,4]{0,1:T(4,128)}, u32[]{:S(2)}) copy-start(s32[8,4]{0,1:T(4,128)} %param.13) | copy-start | bytes 388
  0.7 5.0 %copy-start.1 = (bf16[2,8,2048]{2,1,0:T(8,128)(2,1)S(1)}, bf16[2,8,2048]{2,1,0:T(8,128)(2,1)}, u32[]{:S(2)}) copy-start(bf16[2,8,2048]{2,1,0:T(8,128)(2,1)} %param.8) | copy-start | bytes 196612
  0.7 5.0 %copy-start.6 = (s32[8,4]{0,1:T(4,128)S(1)}, s32[8,4]{0,1:T(4,128)}, u32[]{:S(2)}) copy-start(s32[8,4]{0,1:T(4,128)} %param.14) | copy-start | bytes 388
  0.7 5.0 %copy-start.2 = (bf16[2,8,1024]{2,1,0:T(8,128)(2,1)S(1)}, bf16[2,8,1024]{2,1,0:T(8,128)(2,1)}, u32[]{:S(2)}) copy-start(bf16[2,8,1024]{2,1,0:T(8,128)(2,1)} %q.1) | copy-start | bytes 98308
  2.5 5.8 %collective-permute-start.2 = (bf16[1048,128]{1,0:T(8,128)(2,1)S(1)}, bf16[1048,128]{1,0:T(8,128)(2,1)S(1)}, u32[]{:S(2)}, u32[]{:S(2)}) collective-permute-start(bf16[1048,128]{1,0:T(8,128)(2,1)S(1)} %get-tuple-element.38), channel_id=1, source_target_pairs={{0,4},{4,0},{8,12},{12,8},{1,5},{5,1},{9,13},{13,9},{2,6},{6,2},{1... | collective-permute-start | bytes 804872 | tf_op jit(solution)/shard_map/ppermute | solution.py:29
  3.0 15.8 %collective-permute-start = (bf16[1048,128]{1,0:T(8,128)(2,1)S(1)}, bf16[1048,128]{1,0:T(8,128)(2,1)S(1)}, u32[]{:S(2)}, u32[]{:S(2)}) collective-permute-start(bf16[1048,128]{1,0:T(8,128)(2,1)S(1)} %get-tuple-element.31), channel_id=1, source_target_pairs={{0,8},{4,12},{8,0},{12,4},{1,9},{5,13},{9,1},{13,5},{2,10},{6,14},... | collective-permute-start | bytes 804872 | tf_op jit(solution)/shard_map/ppermute | solution.py:29
  5.6 13.3 %collective-permute-start.1 = (bf16[1048,128]{1,0:T(8,128)(2,1)S(1)}, bf16[1048,128]{1,0:T(8,128)(2,1)S(1)}, u32[]{:S(2)}, u32[]{:S(2)}) collective-permute-start(bf16[1048,128]{1,0:T(8,128)(2,1)S(1)} %get-tuple-element.32), channel_id=1, source_target_pairs={{0,12},{4,8},{8,4},{12,0},{1,13},{5,9},{9,5},{13,1},{2,14},{6,10},... | collective-permute-start | bytes 804872 | tf_op jit(solution)/shard_map/ppermute | solution.py:29
  5.7 11.6 %copy-start.4 = (s32[8]{0:T(128)S(1)}, s32[8]{0:T(128)}, u32[]{:S(2)}) copy-start(s32[8]{0:T(128)} %refs_3_.3) | copy-start | bytes 100
  5.7 13.2 %copy-start = (bf16[2048,1024]{1,0:T(8,128)(2,1)S(1)}, bf16[2048,1024]{1,0:T(8,128)(2,1)}, u32[]{:S(2)}) copy-start(bf16[2048,1024]{1,0:T(8,128)(2,1)} %refs_3_.2) | copy-start | bytes 12582916
  8.3 5.2 %collective-permute-start.3 = (bf16[192,128]{1,0:T(8,128)(2,1)S(1)}, bf16[192,128]{1,0:T(8,128)(2,1)S(1)}, u32[]{:S(2)}, u32[]{:S(2)}) collective-permute-start(bf16[192,128]{1,0:T(8,128)(2,1)S(1)} %get-tuple-element.40), channel_id=1, source_target_pairs={{0,2},{1,3},{2,0},{3,1},{4,6},{5,7},{6,4},{7,5},{8,10},{9,11},{10,... | collective-permute-start | bytes 147464 | tf_op jit(solution)/shard_map/ppermute | solution.py:29
  11.2 6.1 %collective-permute-start.4 = (bf16[192,128]{1,0:T(8,128)(2,1)S(1)}, bf16[192,128]{1,0:T(8,128)(2,1)S(1)}, u32[]{:S(2)}, u32[]{:S(2)}) collective-permute-start(bf16[192,128]{1,0:T(8,128)(2,1)S(1)} %get-tuple-element.41), channel_id=1, source_target_pairs={{0,3},{1,2},{2,1},{3,0},{4,7},{5,6},{6,5},{7,4},{8,11},{9,10},{10,... | collective-permute-start | bytes 147464 | tf_op jit(solution)/shard_map/ppermute | solution.py:29
  12.6 4.7 %collective-permute-start.5 = (bf16[192,128]{1,0:T(8,128)(2,1)S(1)}, bf16[192,128]{1,0:T(8,128)(2,1)S(1)}, u32[]{:S(2)}, u32[]{:S(2)}) collective-permute-start(bf16[192,128]{1,0:T(8,128)(2,1)S(1)} %get-tuple-element.42), channel_id=1, source_target_pairs={{0,1},{1,0},{2,3},{3,2},{4,5},{5,4},{6,7},{7,6},{8,9},{9,8},{10,11... | collective-permute-start | bytes 147464 | tf_op jit(solution)/shard_map/ppermute | solution.py:29
  20.1 7.7 %collective-permute-start.6 = (bf16[208,128]{1,0:T(8,128)(2,1)S(1)}, bf16[208,128]{1,0:T(8,128)(2,1)S(1)}, u32[]{:S(2)}, u32[]{:S(2)}) collective-permute-start(bf16[208,128]{1,0:T(8,128)(2,1)S(1)} %get-tuple-element.52), channel_id=1, source_target_pairs={{0,1},{1,3},{2,0},{3,2},{4,5},{5,7},{6,4},{7,6},{8,9},{9,11},{10,8... | collective-permute-start | bytes 159752 | tf_op jit(solution)/shard_map/ppermute | solution.py:45
  21.0 6.8 %collective-permute-start.7 = (bf16[208,128]{1,0:T(8,128)(2,1)S(1)}, bf16[208,128]{1,0:T(8,128)(2,1)S(1)}, u32[]{:S(2)}, u32[]{:S(2)}) collective-permute-start(bf16[208,128]{1,0:T(8,128)(2,1)S(1)} %get-tuple-element.53), channel_id=1, source_target_pairs={{0,3},{1,2},{2,1},{3,0},{4,7},{5,6},{6,5},{7,4},{8,11},{9,10},{10,... | collective-permute-start | bytes 159752 | tf_op jit(solution)/shard_map/ppermute | solution.py:45
  23.6 4.3 %collective-permute-start.8 = (bf16[208,128]{1,0:T(8,128)(2,1)S(1)}, bf16[208,128]{1,0:T(8,128)(2,1)S(1)}, u32[]{:S(2)}, u32[]{:S(2)}) collective-permute-start(bf16[208,128]{1,0:T(8,128)(2,1)S(1)} %get-tuple-element.54), channel_id=1, source_target_pairs={{0,2},{1,0},{2,3},{3,1},{4,6},{5,4},{6,7},{7,5},{8,10},{9,8},{10,1... | collective-permute-start | bytes 159752 | tf_op jit(solution)/shard_map/ppermute | solution.py:45
